TPU v7x, 256 devices: a whole 4x4x8 slice. The times are simulated.
256 devices in a mesh: space: 8 (over y, x_hi), orb: 32 (over x_lo, z, core).
Axes of the slice: x: 4 (x_hi: 2, x_lo: 2; x = x_hi * 2 + x_lo), y: 4, z: 8, core: 2. Of those that a mesh axis runs over, the one named last changes fastest.
Arguments:
- orbitals: float32 [32, 16, 32, 4096], P('space', None, None, 'orb'), may hold values from -6 to 6
- potential: float32 [32, 16, 32], P('space'), may hold values from 0 to 2
Outputs:
- updated: float32 [32, 16, 32, 4096], P('space', None, None, 'orb')
All inputs are finite; a program needn't handle non-finite values.
Results may differ from a plain program's by a relative error of at most 0.00007.
Values sent between devices are 32-bit elements; how exact they have to be, the bound alone decides.
No kernel may reach another device: no remote copies, remote signals or barrier semaphores. Data moves between devices by JAX's collectives and lax.ppermute only.
A program may use at most 64 MiB of HBM per device.

v0:
```python
import jax
import jax.numpy as jnp
from jax import lax
from jax.sharding import PartitionSpec as P

PANEL = 512
DEGREE = 4


STENCIL = (-205.0 / 72.0, 8.0 / 5.0, -1.0 / 5.0, 8.0 / 315.0, -1.0 / 560.0)
SHIFT_MID = 7.25
HALF_WIDTH = 4.75


def padded_2(shard, sides, width):
    for axis, dim in sides:
        count, length = (lax.axis_size(axis), shard.shape[dim])
        up = [(i, (i + 1) % count) for i in range(count)]
        down = [(j, i) for i, j in up]
        last = lax.slice_in_dim(shard, length - width, length, axis=dim)
        leading = lax.slice_in_dim(shard, 0, width, axis=dim)
        before = lax.ppermute(last, axis, up)
        after = lax.ppermute(leading, axis, down)
        shard = jnp.concatenate([before, shard, after], axis=dim)
    return shard


def hamilton(field, potential):
    planes = field.shape[0]
    padded = padded_2(field, (("space", 0),), 4)
    laplace = 3.0 * STENCIL[0] * field
    for offset in range(1, 5):
        upper = padded[4 + offset : 4 + offset + planes]
        below = padded[4 - offset : 4 - offset + planes]
        laplace = laplace + STENCIL[offset] * (upper + below)
    for axis in (1, 2):
        for offset in range(1, 5):
            laplace = laplace + STENCIL[offset] * (
                jnp.roll(field, offset, axis) + jnp.roll(field, -offset, axis)
            )
    return -0.5 * laplace + potential[..., None] * field


def chebyshev(block, potential):
    before = block
    current = (hamilton(block, potential) - SHIFT_MID * block) / HALF_WIDTH
    for order in range(DEGREE - 1):
        following = 2.0 * (hamilton(current, potential) - SHIFT_MID * current) / HALF_WIDTH - before
        before, current = (current, following)
    return current


def per_device(orbitals, potential):
    highest = lax.Precision.HIGHEST
    filtered = chebyshev(orbitals, potential)
    planes, rows_y, rows_z, columns = filtered.shape
    local_points = planes * rows_y * rows_z
    points = local_points * lax.axis_size("space")
    panel_dev = PANEL // lax.axis_size("orb")
    flat = filtered.reshape(local_points, columns)
    panel_own = flat[:, :panel_dev]
    trailing = flat[:, panel_dev:]
    panel = lax.all_gather(panel_own, "orb", axis=1, tiled=True)
    coupling_part = jnp.dot(panel.T, trailing, precision=highest)
    gram_part = jnp.dot(panel.T, panel_own, precision=highest)
    gram_block, coupling = lax.psum((gram_part, coupling_part), "space")
    gram_full = lax.all_gather(gram_block, "orb", axis=1, tiled=True)
    gram_full = gram_full / points
    coupling = coupling / points
    lower_factor = jnp.linalg.cholesky(gram_full)
    identity = jnp.eye(PANEL, dtype=jnp.float32)
    inverse = lax.linalg.triangular_solve(lower_factor, identity, left_side=True, lower=True)
    start = lax.axis_index("orb") * panel_dev
    own_rows = lax.dynamic_slice_in_dim(inverse, start, panel_dev, 0)
    ortho_own = jnp.dot(panel, own_rows.T, precision=highest)
    middle = jnp.dot(inverse, coupling, precision=highest)
    project = jnp.dot(inverse.T, middle, precision=highest)
    trailing_new = trailing - jnp.dot(panel, project, precision=highest)
    joined = jnp.concatenate([ortho_own, trailing_new], axis=1)
    return joined.reshape(planes, rows_y, rows_z, columns)


def solution(mesh):
    placed = (P("space", None, None, "orb"), P("space", None, None))
    return jax.shard_map(
        per_device,
        mesh=mesh,
        in_specs=placed,
        out_specs=P("space", None, None, "orb"),
        check_vma=False,
    )
```

profile of v0, /device:TPU:1, one launch (start us, length us, event | category | flops | bytes accessed | tf_op | source)
XLA Modules:
  0.0 582.5 jit_solution(3495229856487177631)
XLA Ops:
  23.2 10.6 %collective-permute-done.1 = f32[4,16,32,128]{3,2,1,0:T(8,128)S(1)} collective-permute-done((f32[4,16,32,128]{3,2,1,0:T(8,128)}, f32[4,16,32,128]{3,2,1,0:T(8,128)S(1)}, u32[]{:S(2)}, u32[]{:S(2)}) %collective-permute-start.1) | collective-permute-done | bytes 1048608 | tf_op jit(solution)/shard_map/ppermute | solution.py:22
  34.1 22.5 %collective-permute-done = f32[4,16,32,128]{3,2,1,0:T(8,128)S(1)} collective-permute-done((f32[4,16,32,128]{3,2,1,0:T(8,128)}, f32[4,16,32,128]{3,2,1,0:T(8,128)S(1)}, u32[]{:S(2)}, u32[]{:S(2)}) %collective-permute-start) | collective-permute-done | bytes 1048608 | tf_op jit(solution)/shard_map/ppermute | solution.py:23
  74.8 19.6 %collective-permute-done.2 = f32[4,16,32,128]{3,2,1,0:T(8,128)S(1)} collective-permute-done((f32[4,16,32,128]{3,2,1,0:T(8,128)S(1)}, f32[4,16,32,128]{3,2,1,0:T(8,128)S(1)}, u32[]{:S(2)}, u32[]{:S(2)}) %collective-permute-start.2) | collective-permute-done | bytes 1048608 | tf_op jit(solution)/shard_map/ppermute | solution.py:23
  94.3 22.8 %collective-permute-done.3 = f32[4,16,32,128]{3,2,1,0:T(8,128)S(1)} collective-permute-done((f32[4,16,32,128]{3,2,1,0:T(8,128)S(1)}, f32[4,16,32,128]{3,2,1,0:T(8,128)S(1)}, u32[]{:S(2)}, u32[]{:S(2)}) %collective-permute-start.3) | collective-permute-done | bytes 1048608 | tf_op jit(solution)/shard_map/ppermute | solution.py:22
  118.1 7.0 %multiply_subtract_fusion.2 = f32[4,16,32,128]{3,2,1,0:T(8,128)S(1)} fusion(f32[4,16,32,128]{3,2,1,0:T(8,128)S(1)} %copy-done, f32[4,16,32,128]{3,2,1,0:T(8,128)S(1)} %get-tuple-element.22, f32[4,16,4,128]{3,2,1,0:T(4,128)} %get-tuple-element.118, f32[4,16,28,128]{3,2,1,0:T(8,128)S(1)} %get-tuple-element.120, f32[4,16,28,128]{3,2,1,0:T(8,128)S(1)} %get-tuple-element.119, ...), kind=kLoop, calls=%fused_computation.201 | loop fusion | flops 17301504 | bytes 23076864 | tf_op jit(solution)/shard_map/sub | solution.py:48
  138.5 13.4 %collective-permute-done.4 = f32[4,16,32,128]{3,2,1,0:T(8,128)S(1)} collective-permute-done((f32[4,16,32,128]{3,2,1,0:T(8,128)S(1)}, f32[4,16,32,128]{3,2,1,0:T(8,128)S(1)}, u32[]{:S(2)}, u32[]{:S(2)}) %collective-permute-start.4) | collective-permute-done | bytes 1048608 | tf_op jit(solution)/shard_map/ppermute | solution.py:23
  151.9 23.4 %collective-permute-done.5 = f32[4,16,32,128]{3,2,1,0:T(8,128)S(1)} collective-permute-done((f32[4,16,32,128]{3,2,1,0:T(8,128)S(1)}, f32[4,16,32,128]{3,2,1,0:T(8,128)S(1)}, u32[]{:S(2)}, u32[]{:S(2)}) %collective-permute-start.5) | collective-permute-done | bytes 1048608 | tf_op jit(solution)/shard_map/ppermute | solution.py:22
  176.3 6.9 %multiply_subtract_fusion.1 = f32[4,16,32,128]{3,2,1,0:T(8,128)S(1)} fusion(f32[4,16,32,128]{3,2,1,0:T(8,128)S(1)} %multiply_subtract_fusion.2, f32[4,16,4,128]{3,2,1,0:T(4,128)} %get-tuple-element.86, f32[4,16,28,128]{3,2,1,0:T(8,128)S(1)} %get-tuple-element.88, f32[4,16,28,128]{3,2,1,0:T(8,128)S(1)} %get-tuple-element.87, ...), kind=kLoop, calls=%fused_computation.200 | loop fusion | flops 17563648 | bytes 22028288 | tf_op jit(solution)/shard_map/sub | solution.py:48
  194.2 14.1 %collective-permute-done.6 = f32[4,16,32,128]{3,2,1,0:T(8,128)S(1)} collective-permute-done((f32[4,16,32,128]{3,2,1,0:T(8,128)S(1)}, f32[4,16,32,128]{3,2,1,0:T(8,128)S(1)}, u32[]{:S(2)}, u32[]{:S(2)}) %collective-permute-start.6) | collective-permute-done | bytes 1048608 | tf_op jit(solution)/shard_map/ppermute | solution.py:23
  208.3 22.6 %collective-permute-done.7 = f32[4,16,32,128]{3,2,1,0:T(8,128)S(1)} collective-permute-done((f32[4,16,32,128]{3,2,1,0:T(8,128)S(1)}, f32[4,16,32,128]{3,2,1,0:T(8,128)S(1)}, u32[]{:S(2)}, u32[]{:S(2)}) %collective-permute-start.7) | collective-permute-done | bytes 1048608 | tf_op jit(solution)/shard_map/ppermute | solution.py:22
  231.9 6.8 %multiply_subtract_fusion = f32[4,16,32,128]{3,2,1,0:T(8,128)S(1)} fusion(f32[4,16,32,128]{3,2,1,0:T(8,128)S(1)} %multiply_subtract_fusion.2, f32[4,16,32,128]{3,2,1,0:T(8,128)S(1)} %multiply_subtract_fusion.1, f32[4,16,4,128]{3,2,1,0:T(4,128)} %get-tuple-element.54, f32[4,16,28,128]{3,2,1,0:T(8,128)S(1)} %get-tuple-element.56, ...), kind=kLoop, calls=%fused_computation.199 | loop fusion | flops 17301504 | bytes 22028288 | tf_op jit(solution)/shard_map/sub | solution.py:48
  240.1 71.9 %all-gather.3.cloned.1.call-done = f32[2048,512]{0,1:T(8,128)} async-done(((f32[2048,16]{0,1:T(8,128)}), f32[2048,512]{0,1:T(8,128)}) %all-gather.3.cloned.1.call-update) | async-done | bytes 4194320 | tf_op jit(solution)/shard_map/all_gather | solution.py:63
  317.9 34.9 %psum.14 = f32[512,16]{0,1:T(8,128)} all-reduce(f32[512,16]{0,1:T(8,128)S(1)} %fusion.156), channel_id=1, replica_groups=mesh['space'=8,'orb'=32] {'space'}, use_global_device_ids=true, to_apply=%region_0.1 | all-reduce | flops 8192 | bytes 65536 | tf_op jit(solution)/shard_map/psum | solution.py:66
  355.7 7.3 %fusion.154 = f32[512,112]{0,1:T(8,128)} fusion(f32[2048,512]{0,1:T(8,128)} %all-gather.3.cloned.1.call-done, f32[2048,128]{1,0:T(8,128)S(1)} %bitcast.60), kind=kOutput, calls=%fused_computation.268 | convolution fusion | flops 1409286144 | bytes 5472256 | tf_op jit(solution)/shard_map/dot_general | solution.py:64
  363.0 55.8 %all-gather.5.cloned.1.call-done = f32[512,512]{0,1:T(8,128)} async-done(((f32[512,16]{0,1:T(8,128)}), f32[512,512]{0,1:T(8,128)}) %all-gather.5.cloned.1.call-update) | async-done | bytes 1048592 | tf_op jit(solution)/shard_map/all_gather | solution.py:67
  420.9 11.7 %cholesky.104 = f32[128,128]{1,0:T(8,128)S(1)} custom-call(f32[128,128]{1,0:T(8,128)S(1)} %cholesky.266), custom_call_target="Cholesky" | custom-call | tf_op jit(solution)/shard_map/jit(cholesky)/cholesky | solution.py:70
  432.7 9.8 %custom-call.30 = f32[1,128,128]{1,2,0:T(8,128)S(1)} custom-call(f32[1,128,128]{2,1,0:T(8,128)S(1)} %get-tuple-element.164), custom_call_target="InvertDiagBlocksLowerTriangular" | custom-call | tf_op jit(solution)/shard_map/jit(cholesky)/cholesky | solution.py:70
  443.2 11.9 %cholesky.217 = f32[128,128]{1,0:T(8,128)S(1)} custom-call(f32[128,128]{1,0:T(8,128)S(1)} %cholesky.270), custom_call_target="Cholesky" | custom-call | tf_op jit(solution)/shard_map/jit(cholesky)/cholesky | solution.py:70
  455.1 9.8 %custom-call.31 = f32[1,128,128]{1,2,0:T(8,128)S(1)} custom-call(f32[1,128,128]{2,1,0:T(8,128)S(1)} %get-tuple-element.161), custom_call_target="InvertDiagBlocksLowerTriangular" | custom-call | tf_op jit(solution)/shard_map/jit(cholesky)/cholesky | solution.py:70
  465.6 12.3 %cholesky.238 = f32[128,128]{1,0:T(8,128)} custom-call(f32[128,128]{1,0:T(8,128)S(1)} %cholesky.275), custom_call_target="Cholesky" | custom-call | tf_op jit(solution)/shard_map/jit(cholesky)/cholesky | solution.py:70
  480.2 11.3 %custom-call.32 = f32[1,128,128]{1,2,0:T(8,128)} custom-call(f32[1,128,128]{2,1,0:T(8,128)} %get-tuple-element.158), custom_call_target="InvertDiagBlocksLowerTriangular" | custom-call | tf_op jit(solution)/shard_map/jit(cholesky)/cholesky | solution.py:70
  493.1 11.7 %cholesky.255 = f32[128,128]{1,0:T(8,128)S(1)} custom-call(f32[128,128]{1,0:T(8,128)S(1)} %convolution_subtract_fusion.6), custom_call_target="Cholesky" | custom-call | tf_op jit(solution)/shard_map/jit(cholesky)/cholesky | solution.py:70
  508.9 10.4 %while.1 = (s32[]{:T(128)}, f32[512,512]{1,0:T(8,128)S(1)}, s32[4,2]{0,1:T(2,128)S(1)}, f32[4,128,128]{2,1,0:T(8,128)}, s32[]{:T(128)}) while((s32[]{:T(128)}, f32[512,512]{1,0:T(8,128)S(1)}, s32[4,2]{0,1:T(2,128)S(1)}, f32[4,128,128]{2,1,0:T(8,128)}, s32[]{:T(128)}) %tuple.93), condition=%wide.while_cond, body=%wide.while_body.sunk | while | flops 2 | bytes 132705 | solution.py:72
  519.3 40.1 %custom-call.33 = f32[4,128,128]{1,2,0:T(8,128)S(1)} custom-call(f32[4,128,128]{2,1,0:T(8,128)} %get-tuple-element.12), custom_call_target="InvertDiagBlocksLowerTriangular" | custom-call | tf_op jit(solution)/shard_map/triangular_solve | solution.py:72
  (168 shorter events, 107.4 us)
Async XLA Ops:
  6.5 7.8 %copy-start = (f32[4,16,32,128]{3,2,1,0:T(8,128)S(1)}, f32[4,16,32,128]{3,2,1,0:T(8,128)}, u32[]{:S(2)}) copy-start(f32[4,16,32,128]{3,2,1,0:T(8,128)} %param.2) | copy-start | bytes 3145732
  6.5 305.5 %all-gather.3.cloned.1.call-start = ((), (), s32[]{:S(2)}) async-start(), calls=%async_computation | async-start | bytes 4325376 | tf_op jit(solution)/shard_map/all_gather | solution.py:63
  6.5 27.3 %collective-permute-start.1 = (f32[4,16,32,128]{3,2,1,0:T(8,128)}, f32[4,16,32,128]{3,2,1,0:T(8,128)S(1)}, u32[]{:S(2)}, u32[]{:S(2)}) collective-permute-start(f32[4,16,32,128]{3,2,1,0:T(8,128)} %param.2), channel_id=1, source_target_pairs={{0,32},{32,64},{64,96},{96,128},{128,160},{160,192},{192,224},{224... | collective-permute-start | bytes 3145736 | tf_op jit(solution)/shard_map/ppermute | solution.py:22
  10.1 46.5 %collective-permute-start = (f32[4,16,32,128]{3,2,1,0:T(8,128)}, f32[4,16,32,128]{3,2,1,0:T(8,128)S(1)}, u32[]{:S(2)}, u32[]{:S(2)}) collective-permute-start(f32[4,16,32,128]{3,2,1,0:T(8,128)} %param.2), channel_id=1, source_target_pairs={{32,0},{64,32},{96,64},{128,96},{160,128},{192,160},{224,192},{0,2... | collective-permute-start | bytes 3145736 | tf_op jit(solution)/shard_map/ppermute | solution.py:23
  18.5 4.3 copy-start.11
  69.6 24.7 %collective-permute-start.2 = (f32[4,16,32,128]{3,2,1,0:T(8,128)S(1)}, f32[4,16,32,128]{3,2,1,0:T(8,128)S(1)}, u32[]{:S(2)}, u32[]{:S(2)}) collective-permute-start(f32[4,16,32,128]{3,2,1,0:T(8,128)S(1)} %get-tuple-element.21), channel_id=1, source_target_pairs={{32,0},{64,32},{96,64},{128,96},{160,128},{192,160},{224,192},{0,2... | collective-permute-start | bytes 3145736 | tf_op jit(solution)/shard_map/ppermute | solution.py:23
  73.4 43.7 %collective-permute-start.3 = (f32[4,16,32,128]{3,2,1,0:T(8,128)S(1)}, f32[4,16,32,128]{3,2,1,0:T(8,128)S(1)}, u32[]{:S(2)}, u32[]{:S(2)}) collective-permute-start(f32[4,16,32,128]{3,2,1,0:T(8,128)S(1)} %get-tuple-element.21), channel_id=1, source_target_pairs={{0,32},{32,64},{64,96},{96,128},{128,160},{160,192},{192,224},{224... | collective-permute-start | bytes 3145736 | tf_op jit(solution)/shard_map/ppermute | solution.py:22
  94.3 22.8 %copy-start.9 = (f32[4,16,32,128]{3,2,1,0:T(8,128)}, f32[4,16,32,128]{3,2,1,0:T(8,128)S(1)}, u32[]{:S(2)}) copy-start(f32[4,16,32,128]{3,2,1,0:T(8,128)S(1)} %collective-permute-done.2) | copy-start | bytes 3145732
  117.1 1.0 copy-start.10
  127.1 24.8 %collective-permute-start.4 = (f32[4,16,32,128]{3,2,1,0:T(8,128)S(1)}, f32[4,16,32,128]{3,2,1,0:T(8,128)S(1)}, u32[]{:S(2)}, u32[]{:S(2)}) collective-permute-start(f32[4,16,32,128]{3,2,1,0:T(8,128)S(1)} %multiply_subtract_fusion.2), channel_id=1, source_target_pairs={{32,0},{64,32},{96,64},{128,96},{160,128},{192,160},{224,192},{0,2... | collective-permute-start | bytes 3145736 | tf_op jit(solution)/shard_map/ppermute | solution.py:23
  131.9 43.4 %collective-permute-start.5 = (f32[4,16,32,128]{3,2,1,0:T(8,128)S(1)}, f32[4,16,32,128]{3,2,1,0:T(8,128)S(1)}, u32[]{:S(2)}, u32[]{:S(2)}) collective-permute-start(f32[4,16,32,128]{3,2,1,0:T(8,128)S(1)} %multiply_subtract_fusion.2), channel_id=1, source_target_pairs={{0,32},{32,64},{64,96},{96,128},{128,160},{160,192},{192,224},{224... | collective-permute-start | bytes 3145736 | tf_op jit(solution)/shard_map/ppermute | solution.py:22
  151.9 23.4 %copy-start.6 = (f32[4,16,32,128]{3,2,1,0:T(8,128)}, f32[4,16,32,128]{3,2,1,0:T(8,128)S(1)}, u32[]{:S(2)}) copy-start(f32[4,16,32,128]{3,2,1,0:T(8,128)S(1)} %collective-permute-done.4) | copy-start | bytes 3145732
  175.3 1.0 copy-start.8
  185.5 22.8 %collective-permute-start.6 = (f32[4,16,32,128]{3,2,1,0:T(8,128)S(1)}, f32[4,16,32,128]{3,2,1,0:T(8,128)S(1)}, u32[]{:S(2)}, u32[]{:S(2)}) collective-permute-start(f32[4,16,32,128]{3,2,1,0:T(8,128)S(1)} %multiply_subtract_fusion.1), channel_id=1, source_target_pairs={{32,0},{64,32},{96,64},{128,96},{160,128},{192,160},{224,192},{0,2... | collective-permute-start | bytes 3145736 | tf_op jit(solution)/shard_map/ppermute | solution.py:23
  188.4 42.5 %collective-permute-start.7 = (f32[4,16,32,128]{3,2,1,0:T(8,128)S(1)}, f32[4,16,32,128]{3,2,1,0:T(8,128)S(1)}, u32[]{:S(2)}, u32[]{:S(2)}) collective-permute-start(f32[4,16,32,128]{3,2,1,0:T(8,128)S(1)} %multiply_subtract_fusion.1), channel_id=1, source_target_pairs={{0,32},{32,64},{64,96},{96,128},{128,160},{160,192},{192,224},{224... | collective-permute-start | bytes 3145736 | tf_op jit(solution)/shard_map/ppermute | solution.py:22
  194.0 37.9 %copy-start.12 = (f32[4,16,32]{2,1,0:T(8,128)S(1)}, f32[4,16,32]{2,1,0:T(8,128)}, u32[]{:S(2)}) copy-start(f32[4,16,32]{2,1,0:T(8,128)} %param.3) | copy-start | bytes 24580
  208.3 22.7 %copy-start.5 = (f32[4,16,32,128]{3,2,1,0:T(8,128)}, f32[4,16,32,128]{3,2,1,0:T(8,128)S(1)}, u32[]{:S(2)}) copy-start(f32[4,16,32,128]{3,2,1,0:T(8,128)S(1)} %collective-permute-done.6) | copy-start | bytes 3145732
  230.9 1.0 copy-start.7
  239.7 179.2 %all-gather.5.cloned.1.call-start = ((), (), s32[]{:S(2)}) async-start(), calls=%async_computation.1 | async-start | bytes 1081344 | tf_op jit(solution)/shard_map/all_gather | solution.py:67
  352.8 211.5 %all-reduce.3.cloned.1.call-start = ((), (), s32[]{:S(2)}) async-start(), calls=%async_computation.2 | async-start | bytes 458752 | tf_op jit(solution)/shard_map/psum | solution.py:66
  418.8 1.8 copy-start.2
  478.0 81.8 %copy-start.4 = (f32[512,512]{1,0:T(8,128)S(1)}, f32[512,512]{1,0:T(8,128)}, u32[]{:S(2)}) copy-start(f32[512,512]{1,0:T(8,128)} %fusion.125) | copy-start | bytes 3145732
  566.4 5.3 copy-start.3
  567.1 4.6 copy-start.1
  (1 other events, 0.7 us)
Sparse Core Ops, SparseCore 0:
  239.8 72.2 all-gather.2
  352.9 65.8 all-gather.4
  421.5 83.3 all-reduce.2
where the time goes:
time: 592 us; the launch traced here: 582 us
  waiting for transfers between devices  277 us (47%)
  other arithmetic  152 us (26%)
  local copies, waits for them, and re-layouts  53.9 us (9%)
  blocking collectives  34.9 us (6%)
  matrix products  30.6 us (5%)
  starting transfers between devices  18.1 us (3%)
  between operations  16.6 us (3%)
    another operation x14, other arithmetic, per_device(): lower_factor = jnp.linalg.cholesky(gram_full)  82.2 us
    ppermute x4, waiting for transfers between devices, padded_2(): before = lax.ppermute(last, axis, up)  79.5 us
    all_gather x1, waiting for transfers between devices, per_device(): panel = lax.all_gather(panel_own, 'orb', axis=1, tiled=True)  71.9 us
    ppermute x4, waiting for transfers between devices, padded_2(): after = lax.ppermute(leading, axis, down)  69.6 us
    all_gather x1, waiting for transfers between devices, per_device(): gram_full = lax.all_gather(gram_block, 'orb', axis=1, tiled=True)  55.8 us
    another operation x4, other arithmetic, per_device(): lax.linalg.triangular_solve(lower_factor, identity, left_side=True, lower...  40.3 us
    slice x64, local copies, waits for them, and re-layouts, hamilton(): jnp.roll(field, offset, axis) + jnp.roll(field, -offset, axis)  35.8 us
    psum x1, blocking collectives, per_device(): gram_block, coupling = lax.psum((gram_part, coupling_part), 'space')  34.9 us
  transfers between devices with their start and end apart: 11, of which 10 were waited for; matrix products, arithmetic and copies ran while one was open for 30% of the time, Pallas kernels for 0%

commit v1 on v0

v1 whole, which is shorter than its diff:
```python
import functools

import jax
import jax.numpy as jnp
from jax import lax
from jax.experimental import pallas as pl
from jax.experimental.pallas import tpu as pltpu
from jax.sharding import Mesh, PartitionSpec as P

PANEL = 512
C0, C1, C2, C3, C4 = (-205.0 / 72.0, 8.0 / 5.0, -1.0 / 5.0, 8.0 / 315.0, -1.0 / 560.0)
SHIFT_MID = 7.25
HALF_WIDTH = 4.75
POINTS = 16384.0
SPACE = ("y", "xh")
HI = lax.Precision.HIGHEST
MIB = 1024 * 1024


def dot_nn(a, b):
    return lax.dot_general(a, b, (((1,), (0,)), ((), ())), precision=HI, preferred_element_type=jnp.float32)


def dot_nt(a, b):
    return lax.dot_general(a, b, (((1,), (1,)), ((), ())), precision=HI, preferred_element_type=jnp.float32)


def dot_tn(a, b):
    return lax.dot_general(a, b, (((0,), (0,)), ((), ())), precision=HI, preferred_element_type=jnp.float32)


def swap_groups(arrays):
    arrays = list(arrays)
    group = lax.broadcasted_iota(jnp.int32, arrays[0].shape, 1) // 16
    for bit in (1, 2, 4):
        high = (group & bit) != 0
        for i in range(8):
            if i & bit:
                continue
            a, d = arrays[i], arrays[i | bit]
            arrays[i] = jnp.where(high, pltpu.roll(d, 16 * bit, 1), a)
            arrays[i | bit] = jnp.where(high, d, pltpu.roll(a, 128 - 16 * bit, 1))
    return arrays


def pack_kernel(orb_ref, pot_ref, out_ref):
    def body(step, _):
        xp, yh = step // 2, step % 2
        parts = swap_groups([orb_ref[xp, yh * 8 + yl] for yl in range(8)])
        for g in range(8):
            out_ref[g, pl.ds(step * 32, 32), :] = parts[g]
        return 0

    lax.fori_loop(0, 8, body, 0)
    packed = jnp.concatenate([pot_ref[xp] for xp in range(4)], axis=1)
    for g in range(8):
        out_ref[g, 256:272, :] = packed


def pack(orbitals, potential):
    return pl.pallas_call(
        pack_kernel,
        out_shape=jax.ShapeDtypeStruct((8, 272, 128), jnp.float32),
        compiler_params=pltpu.CompilerParams(vmem_limit_bytes=8 * MIB),
    )(orbitals, potential)


def filter_kernel(in_ref, out_ref, weight, buf_a, buf_b):
    scale = 2.0 / HALF_WIDTH
    centre = (-1.5 * C0 - SHIFT_MID) * scale
    side = [-0.5 * c * scale for c in (C1, C2, C3, C4)]
    y_of = lax.broadcasted_iota(jnp.int32, (16, 256), 0)
    lane_y = lax.broadcasted_iota(jnp.int32, (16, 256), 1) // 16
    spread = jnp.where(y_of == lane_y, 1.0, 0.0).astype(jnp.float32)
    for s in range(8):
        wide = dot_tn(in_ref[s, 256:272, :], spread) * scale + centre
        for xp in range(4):
            for yh in range(2):
                weight[4 * s + xp, yh] = wide[xp * 32 : xp * 32 + 32, yh * 128 : yh * 128 + 128]
    lane = lax.broadcasted_iota(jnp.int32, (32, 128), 1)

    def plane_of_input(x, yh):
        return in_ref[x // 4, pl.ds((x % 4) * 64 + yh * 32, 32), :]

    def apply(read, x):
        near = [read(x, yh) for yh in range(2)]
        total = [weight[x, yh] * near[yh] for yh in range(2)]
        for m in range(1, 5):
            up, down = (x + m) & 31, (x + 32 - m) & 31
            forth = [pltpu.roll(near[yh], 16 * m, 1) for yh in range(2)]
            back = [pltpu.roll(near[yh], 128 - 16 * m, 1) for yh in range(2)]
            low, top = lane < 16 * m, lane >= 128 - 16 * m
            for yh in range(2):
                along_x = read(up, yh) + read(down, yh)
                along_y = jnp.where(low, forth[1 - yh], forth[yh]) + jnp.where(top, back[1 - yh], back[yh])
                along_z = pltpu.roll(near[yh], m, 0) + pltpu.roll(near[yh], 32 - m, 0)
                total[yh] = total[yh] + side[m - 1] * (along_x + along_y + along_z)
        return total

    def first(x, _):
        total = apply(plane_of_input, x)
        for yh in range(2):
            buf_a[x, yh] = 0.5 * total[yh]
        return 0

    def second(x, _):
        total = apply(lambda p, yh: buf_a[p, yh], x)
        for yh in range(2):
            buf_b[x, yh] = total[yh] - plane_of_input(x, yh)
        return 0

    def third(x, _):
        total = apply(lambda p, yh: buf_b[p, yh], x)
        for yh in range(2):
            out_ref[x, yh] = total[yh] - buf_a[x, yh]
        return 0

    def fourth(x, _):
        total = apply(lambda p, yh: out_ref[p, yh], x)
        for yh in range(2):
            buf_a[x, yh] = total[yh] - buf_b[x, yh]
        return 0

    def move(x, _):
        out_ref[x] = buf_a[x]
        return 0

    for step in (first, second, third, fourth, move):
        lax.fori_loop(0, 32, step, 0)


def chebyshev(received):
    out = pl.pallas_call(
        filter_kernel,
        out_shape=jax.ShapeDtypeStruct((32, 2, 32, 128), jnp.float32),
        scratch_shapes=[pltpu.VMEM((32, 2, 32, 128), jnp.float32)] * 3,
        compiler_params=pltpu.CompilerParams(vmem_limit_bytes=16 * MIB),
    )(received)
    return out.reshape(8, 256, 128)


def unpack_kernel(in_ref, out_ref):
    def body(step, _):
        xp, yh = step // 2, step % 2
        parts = swap_groups([in_ref[g, pl.ds(step * 32, 32), :] for g in range(8)])
        for yl in range(8):
            out_ref[pl.ds((xp * 16 + yh * 8 + yl) * 32, 32), :] = parts[yl]
        return 0

    lax.fori_loop(0, 8, body, 0)


def unpack(back):
    return pl.pallas_call(
        unpack_kernel,
        out_shape=jax.ShapeDtypeStruct((2048, 128), jnp.float32),
        compiler_params=pltpu.CompilerParams(vmem_limit_bytes=8 * MIB),
    )(back)


def ring(count, step):
    return [(i, (i + step) % count) for i in range(count)]


def gather_panel(own):
    other = lax.ppermute(own, "xl", ring(2, 1))
    pair = jnp.concatenate([own, other], axis=0)
    found = [pair]
    right = left = pair
    for _ in range(3):
        right = lax.ppermute(right, "z", ring(8, 1))
        left = lax.ppermute(left, "z", ring(8, -1))
        found += [right, left]
    far = jnp.concatenate([lax.ppermute(right[:256], "z", ring(8, 1)), lax.ppermute(left[256:], "z", ring(8, -1))], axis=0)
    found.append(far)
    return found + [lax.ppermute(block, "c", ring(2, 1)) for block in found]


OFFSETS = (0, -1, 1, -2, 2, -3, 3, 4)


def products_kernel(place_ref, *refs):
    blocks, (field_ref, panel_ref, out_ref, order) = refs[:16], refs[16:]
    xl, z, core = place_ref[0], place_ref[1], place_ref[2]
    for other in range(2):
        for k, offset in enumerate(OFFSETS):
            for xo in range(2):
                owner = (xl ^ xo) * 16 + ((z + offset) & 7) * 2 + (core ^ other)
                order[owner] = blocks[other * 8 + k][xo * 256 : xo * 256 + 256, :]
    for group in range(4):

        def body(step, _, group=group):
            xp, yh = step // 2, step % 2
            parts = swap_groups([order[group * 8 + q, pl.ds(step * 32, 32), :] for q in range(8)])
            for yl in range(8):
                panel_ref[pl.ds((xp * 16 + yh * 8 + yl) * 32, 32), group * 128 : group * 128 + 128] = parts[yl]
            return 0

        lax.fori_loop(0, 8, body, 0)
    column = pl.multiple_of((xl * 2 + core) * 128, 128)
    out_ref[...] = jnp.zeros_like(out_ref)

    def chunk(i, _):
        rows = pl.ds(i * 512, 512)
        wide = panel_ref[rows, :]
        out_ref[0:128, :] += dot_tn(panel_ref[rows, pl.ds(column, 128)], wide)
        out_ref[128:256, :] += dot_tn(field_ref[rows, :], wide)
        return 0

    lax.fori_loop(0, 4, chunk, 0)


def products(place, blocks, field):
    return pl.pallas_call(
        products_kernel,
        in_specs=[pl.BlockSpec(memory_space=pltpu.SMEM)] + [pl.BlockSpec(memory_space=pltpu.VMEM)] * 17,
        out_shape=(jax.ShapeDtypeStruct((2048, 512), jnp.float32), jax.ShapeDtypeStruct((256, 512), jnp.float32)),
        scratch_shapes=[pltpu.VMEM((32, 256, 128), jnp.float32)],
        compiler_params=pltpu.CompilerParams(vmem_limit_bytes=28 * MIB),
    )(place, *blocks, field)


def eliminate(block):
    rows = lax.broadcasted_iota(jnp.int32, (8, 128), 0)
    lanes = lax.broadcasted_iota(jnp.int32, (8, 128), 1)
    left = [block[8 * t : 8 * t + 8, :] for t in range(16)]
    right = [jnp.where(lanes == rows + 8 * t, 1.0, 0.0).astype(jnp.float32) for t in range(16)]
    for j in range(128):
        t0, i = j // 8, j % 8
        column = jnp.broadcast_to(left[t0][:, j : j + 1], (8, 128))
        inverse = 1.0 / jnp.broadcast_to(column[i : i + 1, :], (8, 128))
        row_l = jnp.broadcast_to(left[t0][i : i + 1, :], (8, 128)) * inverse
        row_r = jnp.broadcast_to(right[t0][i : i + 1, :], (8, 128)) * inverse
        for t in range(t0, 16):
            if t == t0:
                if i == 7:
                    continue
                factor = jnp.where(rows > i, column, 0.0)
            else:
                factor = jnp.broadcast_to(left[t][:, j : j + 1], (8, 128))
            left[t] = left[t] - factor * row_l
            right[t] = right[t] - factor * row_r
    out = []
    for t in range(16):
        pivot = jnp.sum(jnp.where(lanes == rows + 8 * t, left[t], 0.0), axis=1, keepdims=True)
        root = lax.rsqrt(pivot)
        root = root * (1.5 - 0.5 * pivot * root * root)
        out.append(right[t] * root)
    return jnp.concatenate(out, axis=0)


def inverse_kernel(gram_ref, inv_ref, work):
    work[...] = gram_ref[...] * (1.0 / POINTS)
    inv_ref[...] = jnp.zeros_like(inv_ref)

    def diagonal(k, _):
        here = pl.ds(pl.multiple_of(k * 128, 128), 128)
        corner = eliminate(work[here, here])
        for kk in range(4):

            @pl.when(k == kk)
            def _(kk=kk, corner=corner):
                low, high = kk * 128, kk * 128 + 128
                if kk:
                    inv_ref[low:high, :low] = dot_nn(corner, inv_ref[low:high, :low])
                inv_ref[low:high, low:high] = corner
                if high < PANEL:
                    panel = dot_nt(work[high:, low:high], corner)
                    work[high:, high:] -= dot_nt(panel, panel)
                    inv_ref[high:, :high] -= dot_nn(panel, inv_ref[low:high, :high])

        return 0

    lax.fori_loop(0, 4, diagonal, 0)


def inverse_factor(gram):
    return pl.pallas_call(
        inverse_kernel,
        out_shape=jax.ShapeDtypeStruct((PANEL, PANEL), jnp.float32),
        scratch_shapes=[pltpu.VMEM((PANEL, PANEL), jnp.float32)],
        compiler_params=pltpu.CompilerParams(vmem_limit_bytes=16 * MIB),
    )(gram)


def update_kernel(own_ref, inv_ref, coupling_ref, panel_ref, field_ref, out_ref, mixer):
    inverse = inv_ref[...]
    middle = dot_nt(coupling_ref[...] * (1.0 / POINTS), inverse)
    mixer[...] = -dot_nn(middle, inverse)
    start = pl.multiple_of(own_ref[0] * 16, 16)
    mixer[0:16, :] = inv_ref[pl.ds(start, 16), :]

    def chunk(i, _):
        rows = pl.ds(i * 512, 512)
        keep = lax.broadcasted_iota(jnp.int32, (512, 128), 1) >= 16
        base = jnp.where(keep, field_ref[rows, :], 0.0)
        out_ref[rows, :] = base + dot_nt(panel_ref[rows, :], mixer[...])
        return 0

    lax.fori_loop(0, 4, chunk, 0)


def update(own, inverse, coupling, panel, field):
    return pl.pallas_call(
        update_kernel,
        in_specs=[pl.BlockSpec(memory_space=pltpu.SMEM)] + [pl.BlockSpec(memory_space=pltpu.VMEM)] * 4,
        out_shape=jax.ShapeDtypeStruct((2048, 128), jnp.float32),
        scratch_shapes=[pltpu.VMEM((128, PANEL), jnp.float32)],
        compiler_params=pltpu.CompilerParams(vmem_limit_bytes=28 * MIB),
    )(own, inverse, coupling, panel, field)


def per_device(orbitals, potential):
    xl, z, core = lax.axis_index("xl"), lax.axis_index("z"), lax.axis_index("c")
    place = jnp.stack([xl, z, core]).astype(jnp.int32)
    received = lax.all_to_all(pack(orbitals, potential), SPACE, 0, 0, tiled=True)
    back = lax.all_to_all(chebyshev(received), SPACE, 0, 0, tiled=True)
    field = unpack(back)
    panel, terms = products(place, gather_panel(back[0]), field)
    terms = terms.reshape(2, 8, 16, PANEL).swapaxes(0, 1)
    mine = jnp.sum(lax.all_to_all(terms, SPACE, 0, 0, tiled=True), axis=0)
    full = lax.all_to_all(jnp.broadcast_to(mine, (8, 2, 16, PANEL)), SPACE, 0, 0, tiled=True)
    piece, coupling = full[:, 0].reshape(128, PANEL), full[:, 1].reshape(128, PANEL)
    by_core = lax.ppermute(piece, "c", ring(2, 1))
    low = jnp.where(core == 0, piece, by_core)
    high = jnp.where(core == 0, by_core, piece)
    half = jnp.concatenate([low, high], axis=0)
    by_x = lax.ppermute(half, "xl", ring(2, 1))
    gram = jnp.concatenate([jnp.where(xl == 0, half, by_x), jnp.where(xl == 0, by_x, half)], axis=0)
    inverse = inverse_factor(gram)
    own = (xl * 16 + z * 2 + core).astype(jnp.int32).reshape(1)
    return update(own, inverse, coupling, panel, field).reshape(4, 16, 32, 128)


def solution(mesh):
    fine = Mesh(mesh.devices.reshape(4, 2, 2, 8, 2), ("y", "xh", "xl", "z", "c"))
    return jax.shard_map(
        per_device,
        mesh=fine,
        in_specs=(P(SPACE, None, None, ("xl", "z", "c")), P(SPACE, None, None)),
        out_specs=P(SPACE, None, None, ("xl", "z", "c")),
        check_vma=False,
    )
```

time: 592 us -> 255 us (0.43); the launches traced: 582 us -> 254 us
  waiting for transfers between devices: 277 us -> 31.5 us
  other arithmetic: 152 us -> 0.4 us
  Pallas kernels: 0 us -> 116 us
  local copies, waits for them, and re-layouts: 53.9 us -> 6.28 us
  blocking collectives: 34.9 us -> 68 us
  matrix products: 30.6 us -> 0 us
  between operations: 16.6 us -> 0.27 us
  starting transfers between devices: 18.1 us -> 31.6 us
    all_gather x2 -> x0, waiting for transfers between devices: 128 us -> none  [the longest x1 71.9 us: per_device(): panel = lax.all_gather(panel_own, 'orb', axis=1, tiled=True)]
    another operation x18 -> x1, other arithmetic: 123 us -> 0.08 us  [per_device(): place = jnp.stack([xl, z, core]).astype(jnp.int32)]
    ppermute x8 -> x19, waiting for transfers between devices: 149 us -> 31.5 us  [the longest x3 14 us: gather_panel(): right = lax.ppermute(right, 'z', ring(8, 1))]
    pallas_call x0 -> x6, Pallas kernels: none -> 116 us  [the longest x1 71.8 us: inverse_factor(): pl.pallas_call(inverse_kernel, out_shape=jax.ShapeDtypeStruct((PANEL, PAN...]
    all_to_all x0 -> x4, blocking collectives: none -> 68 us  [the longest x1 24 us: per_device(): lax.all_to_all(pack(orbitals, potential), SPACE, 0, 0, tiled=True)]
    slice x65 -> x3, local copies, waits for them, and re-layouts: 36.8 us -> 0.06 us  [the longest x1 0.04 us: per_device(): full[:, 1].reshape(128, PANEL)]
    psum x1 -> x0, blocking collectives: 34.9 us -> none  [per_device(): gram_block, coupling = lax.psum((gram_part, coupling_part), 'space')]
    dot_general x6 -> x0, matrix products: 23 us -> none  [the longest x1 7.33 us: per_device(): coupling_part = jnp.dot(panel.T, trailing, precision=highest)]
  transfers between devices with their start and end apart: 11 -> 19, of which waited for: 10 -> 7; matrix products, arithmetic and copies ran while one was open for 30% -> 0% of each run, Pallas kernels for 0% -> 1%
where the time goes in v1:
time: 255 us; the launch traced here: 254 us
  Pallas kernels  116 us (45%)
  blocking collectives  68 us (27%)
  starting transfers between devices  31.6 us (12%)
  waiting for transfers between devices  31.5 us (12%)
  local copies, waits for them, and re-layouts  6.28 us (2%)
    pallas_call x1, Pallas kernels, inverse_factor(): pl.pallas_call(inverse_kernel, out_shape=jax.ShapeDtypeStruct((PANEL, PAN...  71.8 us
    all_to_all x1, blocking collectives, per_device(): lax.all_to_all(pack(orbitals, potential), SPACE, 0, 0, tiled=True)  24 us
    pallas_call x1, Pallas kernels, chebyshev(): pl.pallas_call(filter_kernel, out_shape=jax.ShapeDtypeStruct((32, 2, 32,...  18.9 us
    all_to_all x1, blocking collectives, per_device(): back = lax.all_to_all(chebyshev(received), SPACE, 0, 0, tiled=True)  17.8 us
    pallas_call x1, Pallas kernels, products(): pl.pallas_call(products_kernel, in_specs=[pl.BlockSpec(memory_space=pltpu...  14.2 us
    ppermute x3, waiting for transfers between devices, gather_panel(): right = lax.ppermute(right, 'z', ring(8, 1))  14 us
    all_to_all x1, blocking collectives, per_device(): mine = jnp.sum(lax.all_to_all(terms, SPACE, 0, 0, tiled=True), axis=0)  13.3 us
    ppermute x8, starting transfers between devices, gather_panel(): return found + [lax.ppermute(block, 'c', ring(2, 1)) for block in found]  13.1 us
  transfers between devices with their start and end apart: 19, of which 7 were waited for; matrix products, arithmetic and copies ran while one was open for 0% of the time, Pallas kernels for 1%

profile of v1, /device:TPU:1, one launch (start us, length us, event | category | flops | bytes accessed | tf_op | source)
XLA Modules:
  0.0 253.9 jit_solution(491798086964283413)
XLA Ops:
  2.0 2.2 shard_map.28
  4.2 24.0 %all_to_all.20.in_ref = f32[8,272,128]{2,1,0:T(8,128)S(1)} all-to-all(f32[8,272,128]{2,1,0:T(8,128)S(1)} %shard_map.28), channel_id=1, replica_groups=mesh['y'=4,'xh'=2,'xl'=2,'z'=8,'c'=2] {'y','xh'}, dimensions={0} | all-to-all | bytes 2228224 | tf_op jit(solution)/shard_map/all_to_all | solution.py:316
  28.2 18.9 %shard_map.29 = f32[32,2,32,128]{3,2,1,0:T(8,128)S(1)} custom-call(f32[8,272,128]{2,1,0:T(8,128)S(1)} %all_to_all.20.in_ref), custom_call_target="tpu_custom_call" | custom-call | tf_op jit(solution)/shard_map/pallas_call | solution.py:133
  47.0 17.8 %all_to_all.21.in_ref = f32[8,256,128]{2,1,0:T(8,128)S(1)} all-to-all(f32[8,256,128]{2,1,0:T(8,128)S(1)} %bitcast.16), channel_id=1, replica_groups=mesh['y'=4,'xh'=2,'xl'=2,'z'=8,'c'=2] {'y','xh'}, dimensions={0} | all-to-all | bytes 2097152 | tf_op jit(solution)/shard_map/all_to_all | solution.py:317
  65.3 3.5 %collective-permute-done = f32[256,128]{1,0:T(8,128)S(1)} collective-permute-done((f32[256,128]{1,0:T(8,128)S(1)}, f32[256,128]{1,0:T(8,128)S(1)}, u32[]{:S(2)}, u32[]{:S(2)}) %collective-permute-start) | collective-permute-done | bytes 131104 | tf_op jit(solution)/shard_map/ppermute | solution.py:166
  68.8 1.7 collective-permute-start.1
  70.5 4.0 %collective-permute-start.2 = (f32[512,128]{1,0:T(8,128)S(1)}, f32[512,128]{1,0:T(8,128)S(1)}, u32[]{:S(2)}, u32[]{:S(2)}) collective-permute-start(f32[512,128]{1,0:T(8,128)S(1)} %pad_maximum_fusion.2.refs_0_), channel_id=1, source_target_pairs={{0,14},{2,0},{4,2},{6,4},{8,6},{10,8},{12,10},{14,12},{1,15},{3,1}... | collective-permute-start | bytes 786440 | tf_op jit(solution)/shard_map/ppermute | solution.py:172
  74.6 3.7 %collective-permute-done.1.refs_1_ = f32[512,128]{1,0:T(8,128)S(1)} collective-permute-done((f32[512,128]{1,0:T(8,128)S(1)}, f32[512,128]{1,0:T(8,128)S(1)}, u32[]{:S(2)}, u32[]{:S(2)}) %collective-permute-start.1) | collective-permute-done | bytes 262176 | tf_op jit(solution)/shard_map/ppermute | solution.py:171
  78.3 2.8 %collective-permute-start.4 = (f32[512,128]{1,0:T(8,128)S(1)}, f32[512,128]{1,0:T(8,128)}, u32[]{:S(2)}, u32[]{:S(2)}) collective-permute-start(f32[512,128]{1,0:T(8,128)S(1)} %collective-permute-done.2.refs_2_), channel_id=1, source_target_pairs={{0,14},{2,0},{4,2},{6,4},{8,6},{10,8},{12,10},{14,12},{1,15},{3,1}... | collective-permute-start | bytes 786440 | tf_op jit(solution)/shard_map/ppermute | solution.py:172
  81.0 4.7 %collective-permute-done.3.refs_3_ = f32[512,128]{1,0:T(8,128)} collective-permute-done((f32[512,128]{1,0:T(8,128)S(1)}, f32[512,128]{1,0:T(8,128)}, u32[]{:S(2)}, u32[]{:S(2)}) %collective-permute-start.3) | collective-permute-done | bytes 262176 | tf_op jit(solution)/shard_map/ppermute | solution.py:171
  85.7 3.0 %collective-permute-start.6 = (f32[512,128]{1,0:T(8,128)}, f32[512,128]{1,0:T(8,128)S(1)}, u32[]{:S(2)}, u32[]{:S(2)}) collective-permute-start(f32[512,128]{1,0:T(8,128)} %collective-permute-done.4.refs_4_), channel_id=1, source_target_pairs={{0,14},{2,0},{4,2},{6,4},{8,6},{10,8},{12,10},{14,12},{1,15},{3,1}... | collective-permute-start | bytes 786440 | tf_op jit(solution)/shard_map/ppermute | solution.py:172
  88.7 5.7 %collective-permute-done.5.refs_5_ = f32[512,128]{1,0:T(8,128)S(1)} collective-permute-done((f32[512,128]{1,0:T(8,128)}, f32[512,128]{1,0:T(8,128)S(1)}, u32[]{:S(2)}, u32[]{:S(2)}) %collective-permute-start.5) | collective-permute-done | bytes 262176 | tf_op jit(solution)/shard_map/ppermute | solution.py:171
  94.5 8.7 %collective-permute-start.9 = (f32[512,128]{1,0:T(8,128)S(1)}, f32[512,128]{1,0:T(8,128)S(1)}, u32[]{:S(2)}, u32[]{:S(2)}) collective-permute-start(f32[512,128]{1,0:T(8,128)S(1)} %pad_maximum_fusion.2.refs_0_), channel_id=1, source_target_pairs={{0,1},{1,0},{2,3},{3,2},{4,5},{5,4},{6,7},{7,6},{8,9},{9,8},{10,11... | collective-permute-start | bytes 786440 | tf_op jit(solution)/shard_map/ppermute | solution.py:176
  103.7 2.9 %collective-permute-start.8 = (f32[256,128]{1,0:T(8,128)S(1)}, f32[256,128]{1,0:T(8,128)S(1)}, u32[]{:S(2)}, u32[]{:S(2)}) collective-permute-start(f32[256,128]{1,0:T(8,128)S(1)} %slice.22), channel_id=1, source_target_pairs={{0,14},{2,0},{4,2},{6,4},{8,6},{10,8},{12,10},{14,12},{1,15},{3,1}... | collective-permute-start | bytes 393224 | tf_op jit(solution)/shard_map/ppermute | solution.py:174
  106.6 2.6 %collective-permute-start.13 = (f32[512,128]{1,0:T(8,128)}, f32[512,128]{1,0:T(8,128)}, u32[]{:S(2)}, u32[]{:S(2)}) collective-permute-start(f32[512,128]{1,0:T(8,128)} %collective-permute-done.4.refs_4_), channel_id=1, source_target_pairs={{0,1},{1,0},{2,3},{3,2},{4,5},{5,4},{6,7},{7,6},{8,9},{9,8},{10,11... | collective-permute-start | bytes 786440 | tf_op jit(solution)/shard_map/ppermute | solution.py:176
  113.2 2.1 shard_map.30.refs_16_.field_ref
  115.4 14.2 %shard_map.31 = (f32[2048,512]{1,0:T(8,128)S(1)}, f32[256,512]{1,0:T(8,128)S(1)}) custom-call(s32[3]{0:T(128)S(1)} %pad_add_fusion.place_ref, f32[512,128]{1,0:T(8,128)S(1)} %pad_maximum_fusion.2.refs_0_, f32[512,128]{1,0:T(8,128)S(1)} %collective-permute-done.1.refs_1_, f32[512,128]{1,0:T(8,128)S(1)} %copy-done.4, ...), custom_call_target="tpu_custom_call" | custom-call | tf_op jit(solution)/shard_map/pallas_call | solution.py:214
  129.6 2.0 copy-done
  131.6 13.3 %all_to_all.22 = f32[8,2,16,512]{3,2,1,0:T(8,128)S(1)} all-to-all(f32[8,2,16,512]{3,2,1,0:T(8,128)S(1)} %bitcast.19), channel_id=1, replica_groups=mesh['y'=4,'xh'=2,'xl'=2,'z'=8,'c'=2] {'y','xh'}, dimensions={0} | all-to-all | bytes 1048576 | tf_op jit(solution)/shard_map/all_to_all | solution.py:321
  145.0 12.9 %all_to_all.23 = f32[8,2,16,512]{3,2,1,0:T(8,128)S(1)} all-to-all(f32[8,2,16,512]{3,2,1,0:T(8,128)S(1)} %broadcast_in_dim.3), channel_id=1, replica_groups=mesh['y'=4,'xh'=2,'xl'=2,'z'=8,'c'=2] {'y','xh'}, dimensions={0} | all-to-all | bytes 1048576 | tf_op jit(solution)/shard_map/all_to_all | solution.py:322
  157.9 2.5 collective-permute-start.17
  162.7 12.5 %collective-permute-done.18 = f32[256,512]{1,0:T(8,128)S(1)} collective-permute-done((f32[256,512]{1,0:T(8,128)S(1)}, f32[256,512]{1,0:T(8,128)S(1)}, u32[]{:S(2)}, u32[]{:S(2)}) %collective-permute-start.18) | collective-permute-done | bytes 524320 | tf_op jit(solution)/shard_map/ppermute | solution.py:328
  175.4 71.8 %shard_map.32.inv_ref = f32[512,512]{1,0:T(8,128)S(1)} custom-call(f32[512,512]{1,0:T(8,128)S(1)} %pad_maximum_fusion.gram_ref), custom_call_target="tpu_custom_call" | custom-call | tf_op jit(solution)/shard_map/pallas_call | solution.py:278
  247.2 6.7 %shard_map.33 = f32[2048,128]{1,0:T(8,128)} custom-call(s32[1]{0:T(128)} %bitcast.own_ref, f32[512,512]{1,0:T(8,128)S(1)} %shard_map.32.inv_ref, f32[128,512]{1,0:T(8,128)S(1)} %bitcast.17, f32[2048,512]{1,0:T(8,128)S(1)} %copy-done.1, f32[2048,128]{1,0:T(8,128)S(1)} %shard_map.30.refs_16_.field_ref), custom_call_target="tpu_custom_call" | custom-call | tf_op jit(solution)/shard_map/pallas_call | solution.py:304
  (63 shorter events, 9.5 us)
Async XLA Ops:
  64.9 3.9 %collective-permute-start = (f32[256,128]{1,0:T(8,128)S(1)}, f32[256,128]{1,0:T(8,128)S(1)}, u32[]{:S(2)}, u32[]{:S(2)}) collective-permute-start(f32[256,128]{1,0:T(8,128)S(1)} %slice_bitcast_fusion), channel_id=1, source_target_pairs={{0,16},{16,0},{1,17},{17,1},{2,18},{18,2},{3,19},{19,3},{4,20},{20... | collective-permute-start | bytes 393224 | tf_op jit(solution)/shard_map/ppermute | solution.py:166
  68.8 9.4 %collective-permute-start.1 = (f32[512,128]{1,0:T(8,128)S(1)}, f32[512,128]{1,0:T(8,128)S(1)}, u32[]{:S(2)}, u32[]{:S(2)}) collective-permute-start(f32[512,128]{1,0:T(8,128)S(1)} %pad_maximum_fusion.2.refs_0_), channel_id=1, source_target_pairs={{0,2},{2,4},{4,6},{6,8},{8,10},{10,12},{12,14},{14,0},{1,3},{3,5},... | collective-permute-start | bytes 786440 | tf_op jit(solution)/shard_map/ppermute | solution.py:171
  70.5 7.7 %collective-permute-start.2 = (f32[512,128]{1,0:T(8,128)S(1)}, f32[512,128]{1,0:T(8,128)S(1)}, u32[]{:S(2)}, u32[]{:S(2)}) collective-permute-start(f32[512,128]{1,0:T(8,128)S(1)} %pad_maximum_fusion.2.refs_0_), channel_id=1, source_target_pairs={{0,14},{2,0},{4,2},{6,4},{8,6},{10,8},{12,10},{14,12},{1,15},{3,1}... | collective-permute-start | bytes 786440 | tf_op jit(solution)/shard_map/ppermute | solution.py:172
  78.2 7.4 %collective-permute-start.3 = (f32[512,128]{1,0:T(8,128)S(1)}, f32[512,128]{1,0:T(8,128)}, u32[]{:S(2)}, u32[]{:S(2)}) collective-permute-start(f32[512,128]{1,0:T(8,128)S(1)} %collective-permute-done.1.refs_1_), channel_id=1, source_target_pairs={{0,2},{2,4},{4,6},{6,8},{8,10},{10,12},{12,14},{14,0},{1,3},{3,5},... | collective-permute-start | bytes 786440 | tf_op jit(solution)/shard_map/ppermute | solution.py:171
  78.2 34.1 %copy-start.3 = (f32[512,128]{1,0:T(8,128)}, f32[512,128]{1,0:T(8,128)S(1)}, u32[]{:S(2)}) copy-start(f32[512,128]{1,0:T(8,128)S(1)} %collective-permute-done.2.refs_2_) | copy-start | bytes 786436
  78.3 7.4 %collective-permute-start.4 = (f32[512,128]{1,0:T(8,128)S(1)}, f32[512,128]{1,0:T(8,128)}, u32[]{:S(2)}, u32[]{:S(2)}) collective-permute-start(f32[512,128]{1,0:T(8,128)S(1)} %collective-permute-done.2.refs_2_), channel_id=1, source_target_pairs={{0,14},{2,0},{4,2},{6,4},{8,6},{10,8},{12,10},{14,12},{1,15},{3,1}... | collective-permute-start | bytes 786440 | tf_op jit(solution)/shard_map/ppermute | solution.py:172
  85.7 8.7 %collective-permute-start.5 = (f32[512,128]{1,0:T(8,128)}, f32[512,128]{1,0:T(8,128)S(1)}, u32[]{:S(2)}, u32[]{:S(2)}) collective-permute-start(f32[512,128]{1,0:T(8,128)} %collective-permute-done.3.refs_3_), channel_id=1, source_target_pairs={{0,2},{2,4},{4,6},{6,8},{8,10},{10,12},{12,14},{14,0},{1,3},{3,5},... | collective-permute-start | bytes 786440 | tf_op jit(solution)/shard_map/ppermute | solution.py:171
  85.7 18.0 %collective-permute-start.6 = (f32[512,128]{1,0:T(8,128)}, f32[512,128]{1,0:T(8,128)S(1)}, u32[]{:S(2)}, u32[]{:S(2)}) collective-permute-start(f32[512,128]{1,0:T(8,128)} %collective-permute-done.4.refs_4_), channel_id=1, source_target_pairs={{0,14},{2,0},{4,2},{6,4},{8,6},{10,8},{12,10},{14,12},{1,15},{3,1}... | collective-permute-start | bytes 786440 | tf_op jit(solution)/shard_map/ppermute | solution.py:172
  94.4 12.3 %collective-permute-start.7 = (f32[256,128]{1,0:T(8,128)S(1)}, f32[256,128]{1,0:T(8,128)S(1)}, u32[]{:S(2)}, u32[]{:S(2)}) collective-permute-start(f32[256,128]{1,0:T(8,128)S(1)} %slice.21), channel_id=1, source_target_pairs={{0,2},{2,4},{4,6},{6,8},{8,10},{10,12},{12,14},{14,0},{1,3},{3,5},... | collective-permute-start | bytes 393224 | tf_op jit(solution)/shard_map/ppermute | solution.py:174
  94.5 15.9 %collective-permute-start.9 = (f32[512,128]{1,0:T(8,128)S(1)}, f32[512,128]{1,0:T(8,128)S(1)}, u32[]{:S(2)}, u32[]{:S(2)}) collective-permute-start(f32[512,128]{1,0:T(8,128)S(1)} %pad_maximum_fusion.2.refs_0_), channel_id=1, source_target_pairs={{0,1},{1,0},{2,3},{3,2},{4,5},{5,4},{6,7},{7,6},{8,9},{9,8},{10,11... | collective-permute-start | bytes 786440 | tf_op jit(solution)/shard_map/ppermute | solution.py:176
  103.2 7.9 %collective-permute-start.11 = (f32[512,128]{1,0:T(8,128)S(1)}, f32[512,128]{1,0:T(8,128)S(1)}, u32[]{:S(2)}, u32[]{:S(2)}) collective-permute-start(f32[512,128]{1,0:T(8,128)S(1)} %collective-permute-done.2.refs_2_), channel_id=1, source_target_pairs={{0,1},{1,0},{2,3},{3,2},{4,5},{5,4},{6,7},{7,6},{8,9},{9,8},{10,11... | collective-permute-start | bytes 786440 | tf_op jit(solution)/shard_map/ppermute | solution.py:176
  103.3 9.0 %collective-permute-start.10 = (f32[512,128]{1,0:T(8,128)S(1)}, f32[512,128]{1,0:T(8,128)S(1)}, u32[]{:S(2)}, u32[]{:S(2)}) collective-permute-start(f32[512,128]{1,0:T(8,128)S(1)} %collective-permute-done.1.refs_1_), channel_id=1, source_target_pairs={{0,1},{1,0},{2,3},{3,2},{4,5},{5,4},{6,7},{7,6},{8,9},{9,8},{10,11... | collective-permute-start | bytes 786440 | tf_op jit(solution)/shard_map/ppermute | solution.py:176
  103.7 5.9 %collective-permute-start.8 = (f32[256,128]{1,0:T(8,128)S(1)}, f32[256,128]{1,0:T(8,128)S(1)}, u32[]{:S(2)}, u32[]{:S(2)}) collective-permute-start(f32[256,128]{1,0:T(8,128)S(1)} %slice.22), channel_id=1, source_target_pairs={{0,14},{2,0},{4,2},{6,4},{8,6},{10,8},{12,10},{14,12},{1,15},{3,1}... | collective-permute-start | bytes 393224 | tf_op jit(solution)/shard_map/ppermute | solution.py:174
  106.6 8.6 %collective-permute-start.13 = (f32[512,128]{1,0:T(8,128)}, f32[512,128]{1,0:T(8,128)}, u32[]{:S(2)}, u32[]{:S(2)}) collective-permute-start(f32[512,128]{1,0:T(8,128)} %collective-permute-done.4.refs_4_), channel_id=1, source_target_pairs={{0,1},{1,0},{2,3},{3,2},{4,5},{5,4},{6,7},{7,6},{8,9},{9,8},{10,11... | collective-permute-start | bytes 786440 | tf_op jit(solution)/shard_map/ppermute | solution.py:176
  109.6 5.7 %collective-permute-start.12 = (f32[512,128]{1,0:T(8,128)}, f32[512,128]{1,0:T(8,128)}, u32[]{:S(2)}, u32[]{:S(2)}) collective-permute-start(f32[512,128]{1,0:T(8,128)} %collective-permute-done.3.refs_3_), channel_id=1, source_target_pairs={{0,1},{1,0},{2,3},{3,2},{4,5},{5,4},{6,7},{7,6},{8,9},{9,8},{10,11... | collective-permute-start | bytes 786440 | tf_op jit(solution)/shard_map/ppermute | solution.py:176
  111.1 4.2 %collective-permute-start.15 = (f32[512,128]{1,0:T(8,128)S(1)}, f32[512,128]{1,0:T(8,128)}, u32[]{:S(2)}, u32[]{:S(2)}) collective-permute-start(f32[512,128]{1,0:T(8,128)S(1)} %collective-permute-done.6.refs_6_), channel_id=1, source_target_pairs={{0,1},{1,0},{2,3},{3,2},{4,5},{5,4},{6,7},{7,6},{8,9},{9,8},{10,11... | collective-permute-start | bytes 786440 | tf_op jit(solution)/shard_map/ppermute | solution.py:176
  111.8 3.5 %collective-permute-start.14 = (f32[512,128]{1,0:T(8,128)S(1)}, f32[512,128]{1,0:T(8,128)}, u32[]{:S(2)}, u32[]{:S(2)}) collective-permute-start(f32[512,128]{1,0:T(8,128)S(1)} %collective-permute-done.5.refs_5_), channel_id=1, source_target_pairs={{0,1},{1,0},{2,3},{3,2},{4,5},{5,4},{6,7},{7,6},{8,9},{9,8},{10,11... | collective-permute-start | bytes 786440 | tf_op jit(solution)/shard_map/ppermute | solution.py:176
  113.1 2.3 collective-permute-start.16
  113.1 2.3 copy-start.6
  113.1 2.3 copy-start.8
  113.1 2.3 copy-start.10
  157.9 3.7 %collective-permute-start.17 = (f32[128,512]{1,0:T(8,128)S(1)}, f32[128,512]{1,0:T(8,128)S(1)}, u32[]{:S(2)}, u32[]{:S(2)}) collective-permute-start(f32[128,512]{1,0:T(8,128)S(1)} %bitcast.20), channel_id=1, source_target_pairs={{0,1},{1,0},{2,3},{3,2},{4,5},{5,4},{6,7},{7,6},{8,9},{9,8},{10,11... | collective-permute-start | bytes 786440 | tf_op jit(solution)/shard_map/ppermute | solution.py:324
  161.7 13.4 %collective-permute-start.18 = (f32[256,512]{1,0:T(8,128)S(1)}, f32[256,512]{1,0:T(8,128)S(1)}, u32[]{:S(2)}, u32[]{:S(2)}) collective-permute-start(f32[256,512]{1,0:T(8,128)S(1)} %pad_maximum_fusion.1), channel_id=1, source_target_pairs={{0,16},{16,0},{1,17},{17,1},{2,18},{18,2},{3,19},{19,3},{4,20},{20... | collective-permute-start | bytes 1572872 | tf_op jit(solution)/shard_map/ppermute | solution.py:328
  175.3 71.9 %copy-start.1 = (f32[2048,512]{1,0:T(8,128)S(1)}, f32[2048,512]{1,0:T(8,128)}, u32[]{:S(2)}) copy-start(f32[2048,512]{1,0:T(8,128)} %copy-done) | copy-start | bytes 12582916
  (7 other events, 8.4 us)

commit v2 on v1

--- a/solution.py
+++ b/solution.py
@@ -65,6 +65,13 @@
     )(orbitals, potential)
 
 
+def roll_y(pair, places, lane):
+    shift = 16 * places % 128
+    turned = [pltpu.roll(half, shift, 1) for half in pair]
+    wraps = lane < shift if places > 0 else lane >= shift
+    return [jnp.where(wraps, turned[1], turned[0]), jnp.where(wraps, turned[0], turned[1])]
+
+
 def filter_kernel(in_ref, out_ref, weight, buf_a, buf_b):
     scale = 2.0 / HALF_WIDTH
     centre = (-1.5 * C0 - SHIFT_MID) * scale
@@ -76,64 +83,63 @@
         wide = dot_tn(in_ref[s, 256:272, :], spread) * scale + centre
         for xp in range(4):
             for yh in range(2):
-                weight[4 * s + xp, yh] = wide[xp * 32 : xp * 32 + 32, yh * 128 : yh * 128 + 128]
+                weight[8 * s + 2 * xp + yh] = wide[xp * 32 : xp * 32 + 32, yh * 128 : yh * 128 + 128]
     lane = lax.broadcasted_iota(jnp.int32, (32, 128), 1)
 
-    def plane_of_input(x, yh):
-        return in_ref[x // 4, pl.ds((x % 4) * 64 + yh * 32, 32), :]
-
-    def apply(read, x):
-        near = [read(x, yh) for yh in range(2)]
-        total = [weight[x, yh] * near[yh] for yh in range(2)]
+    def put(ref, plane, value):
+        ref[plane, 8:40, :] = value
+        ref[plane, 4:8, :] = value[28:32, :]
+        ref[plane, 40:44, :] = value[0:4, :]
+
+    def take(plane, _):
+        put(buf_b, plane, in_ref[plane // 8, pl.ds((plane % 8) * 32, 32), :])
+        return 0
+
+    def apply(ref, x):
+        near = [ref[2 * x + yh, 8:40, :] for yh in range(2)]
+        total = [weight[2 * x + yh] * near[yh] for yh in range(2)]
         for m in range(1, 5):
-            up, down = (x + m) & 31, (x + 32 - m) & 31
-            forth = [pltpu.roll(near[yh], 16 * m, 1) for yh in range(2)]
-            back = [pltpu.roll(near[yh], 128 - 16 * m, 1) for yh in range(2)]
-            low, top = lane < 16 * m, lane >= 128 - 16 * m
+            up, down = 2 * ((x + m) & 31), 2 * ((x + 32 - m) & 31)
             for yh in range(2):
-                along_x = read(up, yh) + read(down, yh)
-                along_y = jnp.where(low, forth[1 - yh], forth[yh]) + jnp.where(top, back[1 - yh], back[yh])
-                along_z = pltpu.roll(near[yh], m, 0) + pltpu.roll(near[yh], 32 - m, 0)
-                total[yh] = total[yh] + side[m - 1] * (along_x + along_y + along_z)
-        return total
+                along_x = ref[up + yh, 8:40, :] + ref[down + yh, 8:40, :]
+                along_z = ref[2 * x + yh, 8 - m : 40 - m, :] + ref[2 * x + yh, 8 + m : 40 + m, :]
+                total[yh] = total[yh] + side[m - 1] * (along_x + along_z)
+        forth, back = roll_y(near, 1, lane), roll_y(near, -1, lane)
+        ahead = [side[1] * back[yh] + side[2] * near[yh] + side[3] * forth[yh] for yh in range(2)]
+        behind = [side[1] * forth[yh] + side[2] * near[yh] + side[3] * back[yh] for yh in range(2)]
+        ahead, behind = roll_y(ahead, 3, lane), roll_y(behind, -3, lane)
+        return [total[yh] + (side[0] * (forth[yh] + back[yh]) + (ahead[yh] + behind[yh])) for yh in range(2)]
 
     def first(x, _):
-        total = apply(plane_of_input, x)
-        for yh in range(2):
-            buf_a[x, yh] = 0.5 * total[yh]
+        for yh, total in enumerate(apply(buf_b, x)):
+            put(buf_a, 2 * x + yh, 0.5 * total)
         return 0
 
     def second(x, _):
-        total = apply(lambda p, yh: buf_a[p, yh], x)
-        for yh in range(2):
-            buf_b[x, yh] = total[yh] - plane_of_input(x, yh)
+        for yh, total in enumerate(apply(buf_a, x)):
+            put(buf_b, 2 * x + yh, total - buf_b[2 * x + yh, 8:40, :])
         return 0
 
     def third(x, _):
-        total = apply(lambda p, yh: buf_b[p, yh], x)
-        for yh in range(2):
-            out_ref[x, yh] = total[yh] - buf_a[x, yh]
+        for yh, total in enumerate(apply(buf_b, x)):
+            put(buf_a, 2 * x + yh, total - buf_a[2 * x + yh, 8:40, :])
         return 0
 
     def fourth(x, _):
-        total = apply(lambda p, yh: out_ref[p, yh], x)
-        for yh in range(2):
-            buf_a[x, yh] = total[yh] - buf_b[x, yh]
-        return 0
-
-    def move(x, _):
-        out_ref[x] = buf_a[x]
-        return 0
-
-    for step in (first, second, third, fourth, move):
-        lax.fori_loop(0, 32, step, 0)
+        for yh, total in enumerate(apply(buf_a, x)):
+            out_ref[2 * x + yh] = total - buf_b[2 * x + yh, 8:40, :]
+        return 0
+
+    lax.fori_loop(0, 64, take, 0, unroll=4)
+    for step in (first, second, third, fourth):
+        lax.fori_loop(0, 32, step, 0, unroll=4)
 
 
 def chebyshev(received):
     out = pl.pallas_call(
         filter_kernel,
-        out_shape=jax.ShapeDtypeStruct((32, 2, 32, 128), jnp.float32),
-        scratch_shapes=[pltpu.VMEM((32, 2, 32, 128), jnp.float32)] * 3,
+        out_shape=jax.ShapeDtypeStruct((64, 32, 128), jnp.float32),
+        scratch_shapes=[pltpu.VMEM((64, 32, 128), jnp.float32)] + [pltpu.VMEM((64, 48, 128), jnp.float32)] * 2,
         compiler_params=pltpu.CompilerParams(vmem_limit_bytes=16 * MIB),
     )(received)
     return out.reshape(8, 256, 128)
@@ -220,32 +226,58 @@
     )(place, *blocks, field)
 
 
+def total_of(terms):
+    while len(terms) > 1:
+        terms = [terms[i] + terms[i + 1] for i in range(0, len(terms), 2)]
+    return terms[0]
+
+
 def eliminate(block):
     rows = lax.broadcasted_iota(jnp.int32, (8, 128), 0)
     lanes = lax.broadcasted_iota(jnp.int32, (8, 128), 1)
+
+    def spread_row(tile, i):
+        return jnp.broadcast_to(tile[i : i + 1, :], (8, 128))
+
+    def spread_lane(tile, j):
+        return jnp.broadcast_to(tile[:, j : j + 1], (8, 128))
+
     left = [block[8 * t : 8 * t + 8, :] for t in range(16)]
     right = [jnp.where(lanes == rows + 8 * t, 1.0, 0.0).astype(jnp.float32) for t in range(16)]
-    for j in range(128):
-        t0, i = j // 8, j % 8
-        column = jnp.broadcast_to(left[t0][:, j : j + 1], (8, 128))
-        inverse = 1.0 / jnp.broadcast_to(column[i : i + 1, :], (8, 128))
-        row_l = jnp.broadcast_to(left[t0][i : i + 1, :], (8, 128)) * inverse
-        row_r = jnp.broadcast_to(right[t0][i : i + 1, :], (8, 128)) * inverse
-        for t in range(t0, 16):
-            if t == t0:
-                if i == 7:
-                    continue
-                factor = jnp.where(rows > i, column, 0.0)
-            else:
-                factor = jnp.broadcast_to(left[t][:, j : j + 1], (8, 128))
-            left[t] = left[t] - factor * row_l
-            right[t] = right[t] - factor * row_r
     out = []
-    for t in range(16):
-        pivot = jnp.sum(jnp.where(lanes == rows + 8 * t, left[t], 0.0), axis=1, keepdims=True)
+    for t0 in range(16):
+        columns = [spread_lane(left[t0], 8 * t0 + j) for j in range(8)]
+        corner = [[spread_row(columns[j], i) for j in range(i + 1)] for i in range(8)]
+        row_l = [spread_row(left[t0], i) for i in range(8)]
+        row_r = [spread_row(right[t0], i) for i in range(8)]
+        inverse, factor = [None] * 8, [[None] * 8 for _ in range(8)]
+        for j in range(8):
+            inverse[j] = 1.0 / corner[j][j]
+            for i in range(j + 1, 8):
+                factor[i][j] = corner[i][j] * inverse[j]
+            for i in range(j + 1, 8):
+                for k in range(j + 1, i + 1):
+                    corner[i][k] = corner[i][k] - factor[i][j] * corner[k][j]
+                row_l[i] = row_l[i] - factor[i][j] * row_l[j]
+                row_r[i] = row_r[i] - factor[i][j] * row_r[j]
+        own, pivot = row_r[0], corner[0][0]
+        for i in range(1, 8):
+            own, pivot = jnp.where(rows == i, row_r[i], own), jnp.where(rows == i, corner[i][i], pivot)
         root = lax.rsqrt(pivot)
         root = root * (1.5 - 0.5 * pivot * root * root)
-        out.append(right[t] * root)
+        out.append(own * root)
+        if t0 == 15:
+            break
+        solved_l, solved_r = [None] * 8, [None] * 8
+        for k in range(7, -1, -1):
+            u, v = row_l[k] * inverse[k], row_r[k] * inverse[k]
+            for i in range(7, k, -1):
+                u, v = u - factor[i][k] * solved_l[i], v - factor[i][k] * solved_r[i]
+            solved_l[k], solved_r[k] = u, v
+        for t in range(t0 + 1, 16):
+            weights = [spread_lane(left[t], 8 * t0 + j) for j in range(8)]
+            left[t] = left[t] - total_of([weights[j] * solved_l[j] for j in range(8)])
+            right[t] = right[t] - total_of([weights[j] * solved_r[j] for j in range(8)])
     return jnp.concatenate(out, axis=0)
 
 

time: 255 us -> 197 us (0.77)
  Pallas kernels: 116 us -> 58.2 us
    pallas_call x1, Pallas kernels: 71.8 us -> 21.7 us  [inverse_factor(): pl.pallas_call(inverse_kernel, out_shape=jax.ShapeDtypeStruct((PANEL, PAN...]
    pallas_call x1, Pallas kernels: 18.9 us -> 11.3 us  [chebyshev(): pl.pallas_call(filter_kernel, out_shape=jax.ShapeDtypeStruct((64, 32, 128...]
where the time goes in v2:
time: 197 us; the launch traced here: 196 us
  blocking collectives  68 us (35%)
  Pallas kernels  58.2 us (30%)
  starting transfers between devices  31.6 us (16%)
  waiting for transfers between devices  31.5 us (16%)
  local copies, waits for them, and re-layouts  6.28 us (3%)
    all_to_all x1, blocking collectives, per_device(): lax.all_to_all(pack(orbitals, potential), SPACE, 0, 0, tiled=True)  24 us
    pallas_call x1, Pallas kernels, inverse_factor(): pl.pallas_call(inverse_kernel, out_shape=jax.ShapeDtypeStruct((PANEL, PAN...  21.7 us
    all_to_all x1, blocking collectives, per_device(): back = lax.all_to_all(chebyshev(received), SPACE, 0, 0, tiled=True)  17.8 us
    pallas_call x1, Pallas kernels, products(): pl.pallas_call(products_kernel, in_specs=[pl.BlockSpec(memory_space=pltpu...  14.2 us
    ppermute x3, waiting for transfers between devices, gather_panel(): right = lax.ppermute(right, 'z', ring(8, 1))  14 us
    all_to_all x1, blocking collectives, per_device(): mine = jnp.sum(lax.all_to_all(terms, SPACE, 0, 0, tiled=True), axis=0)  13.3 us
    ppermute x8, starting transfers between devices, gather_panel(): return found + [lax.ppermute(block, 'c', ring(2, 1)) for block in found]  13.1 us
    all_to_all x1, blocking collectives, per_device(): lax.all_to_all(jnp.broadcast_to(mine, (8, 2, 16, PANEL)), SPACE, 0, 0, ti...  12.9 us
  transfers between devices with their start and end apart: 19, of which 7 were waited for; matrix products, arithmetic and copies ran while one was open for 0% of the time, Pallas kernels for 1%

profile of v2, /device:TPU:1, one launch (start us, length us, event | category | flops | bytes accessed | tf_op | source)
XLA Modules:
  0.0 196.2 jit_solution(279351089829184028)
XLA Ops:
  2.0 2.2 %shard_map.28 = f32[8,272,128]{2,1,0:T(8,128)S(1)} custom-call(f32[4,16,32,128]{3,2,1,0:T(8,128)S(1)} %copy-done.2, f32[4,16,32]{2,1,0:T(8,128)S(1)} %copy-done.11), custom_call_target="tpu_custom_call" | custom-call | tf_op jit(solution)/shard_map/pallas_call | solution.py:61
  4.2 24.0 %all_to_all.20.in_ref = f32[8,272,128]{2,1,0:T(8,128)S(1)} all-to-all(f32[8,272,128]{2,1,0:T(8,128)S(1)} %shard_map.28), channel_id=1, replica_groups=mesh['y'=4,'xh'=2,'xl'=2,'z'=8,'c'=2] {'y','xh'}, dimensions={0} | all-to-all | bytes 2228224 | tf_op jit(solution)/shard_map/all_to_all | solution.py:348
  28.2 11.3 %shard_map.29 = f32[64,32,128]{2,1,0:T(8,128)S(1)} custom-call(f32[8,272,128]{2,1,0:T(8,128)S(1)} %all_to_all.20.in_ref), custom_call_target="tpu_custom_call" | custom-call | tf_op jit(solution)/shard_map/pallas_call | solution.py:139
  39.5 17.8 %all_to_all.21.in_ref = f32[8,256,128]{2,1,0:T(8,128)S(1)} all-to-all(f32[8,256,128]{2,1,0:T(8,128)S(1)} %bitcast.16), channel_id=1, replica_groups=mesh['y'=4,'xh'=2,'xl'=2,'z'=8,'c'=2] {'y','xh'}, dimensions={0} | all-to-all | bytes 2097152 | tf_op jit(solution)/shard_map/all_to_all | solution.py:349
  57.7 3.5 %collective-permute-done = f32[256,128]{1,0:T(8,128)S(1)} collective-permute-done((f32[256,128]{1,0:T(8,128)S(1)}, f32[256,128]{1,0:T(8,128)S(1)}, u32[]{:S(2)}, u32[]{:S(2)}) %collective-permute-start) | collective-permute-done | bytes 131104 | tf_op jit(solution)/shard_map/ppermute | solution.py:172
  61.3 1.7 collective-permute-start.1
  63.0 4.0 %collective-permute-start.2 = (f32[512,128]{1,0:T(8,128)S(1)}, f32[512,128]{1,0:T(8,128)S(1)}, u32[]{:S(2)}, u32[]{:S(2)}) collective-permute-start(f32[512,128]{1,0:T(8,128)S(1)} %pad_maximum_fusion.2.refs_0_), channel_id=1, source_target_pairs={{0,14},{2,0},{4,2},{6,4},{8,6},{10,8},{12,10},{14,12},{1,15},{3,1}... | collective-permute-start | bytes 786440 | tf_op jit(solution)/shard_map/ppermute | solution.py:178
  67.0 3.7 %collective-permute-done.1.refs_1_ = f32[512,128]{1,0:T(8,128)S(1)} collective-permute-done((f32[512,128]{1,0:T(8,128)S(1)}, f32[512,128]{1,0:T(8,128)S(1)}, u32[]{:S(2)}, u32[]{:S(2)}) %collective-permute-start.1) | collective-permute-done | bytes 262176 | tf_op jit(solution)/shard_map/ppermute | solution.py:177
  70.7 2.8 %collective-permute-start.4 = (f32[512,128]{1,0:T(8,128)S(1)}, f32[512,128]{1,0:T(8,128)}, u32[]{:S(2)}, u32[]{:S(2)}) collective-permute-start(f32[512,128]{1,0:T(8,128)S(1)} %collective-permute-done.2.refs_2_), channel_id=1, source_target_pairs={{0,14},{2,0},{4,2},{6,4},{8,6},{10,8},{12,10},{14,12},{1,15},{3,1}... | collective-permute-start | bytes 786440 | tf_op jit(solution)/shard_map/ppermute | solution.py:178
  73.4 4.7 %collective-permute-done.3.refs_3_ = f32[512,128]{1,0:T(8,128)} collective-permute-done((f32[512,128]{1,0:T(8,128)S(1)}, f32[512,128]{1,0:T(8,128)}, u32[]{:S(2)}, u32[]{:S(2)}) %collective-permute-start.3) | collective-permute-done | bytes 262176 | tf_op jit(solution)/shard_map/ppermute | solution.py:177
  78.1 3.0 %collective-permute-start.6 = (f32[512,128]{1,0:T(8,128)}, f32[512,128]{1,0:T(8,128)S(1)}, u32[]{:S(2)}, u32[]{:S(2)}) collective-permute-start(f32[512,128]{1,0:T(8,128)} %collective-permute-done.4.refs_4_), channel_id=1, source_target_pairs={{0,14},{2,0},{4,2},{6,4},{8,6},{10,8},{12,10},{14,12},{1,15},{3,1}... | collective-permute-start | bytes 786440 | tf_op jit(solution)/shard_map/ppermute | solution.py:178
  81.1 5.7 %collective-permute-done.5.refs_5_ = f32[512,128]{1,0:T(8,128)S(1)} collective-permute-done((f32[512,128]{1,0:T(8,128)}, f32[512,128]{1,0:T(8,128)S(1)}, u32[]{:S(2)}, u32[]{:S(2)}) %collective-permute-start.5) | collective-permute-done | bytes 262176 | tf_op jit(solution)/shard_map/ppermute | solution.py:177
  86.9 8.7 %collective-permute-start.9 = (f32[512,128]{1,0:T(8,128)S(1)}, f32[512,128]{1,0:T(8,128)S(1)}, u32[]{:S(2)}, u32[]{:S(2)}) collective-permute-start(f32[512,128]{1,0:T(8,128)S(1)} %pad_maximum_fusion.2.refs_0_), channel_id=1, source_target_pairs={{0,1},{1,0},{2,3},{3,2},{4,5},{5,4},{6,7},{7,6},{8,9},{9,8},{10,11... | collective-permute-start | bytes 786440 | tf_op jit(solution)/shard_map/ppermute | solution.py:182
  96.2 2.9 %collective-permute-start.8 = (f32[256,128]{1,0:T(8,128)S(1)}, f32[256,128]{1,0:T(8,128)S(1)}, u32[]{:S(2)}, u32[]{:S(2)}) collective-permute-start(f32[256,128]{1,0:T(8,128)S(1)} %slice.22), channel_id=1, source_target_pairs={{0,14},{2,0},{4,2},{6,4},{8,6},{10,8},{12,10},{14,12},{1,15},{3,1}... | collective-permute-start | bytes 393224 | tf_op jit(solution)/shard_map/ppermute | solution.py:180
  99.1 2.6 %collective-permute-start.13 = (f32[512,128]{1,0:T(8,128)}, f32[512,128]{1,0:T(8,128)}, u32[]{:S(2)}, u32[]{:S(2)}) collective-permute-start(f32[512,128]{1,0:T(8,128)} %collective-permute-done.4.refs_4_), channel_id=1, source_target_pairs={{0,1},{1,0},{2,3},{3,2},{4,5},{5,4},{6,7},{7,6},{8,9},{9,8},{10,11... | collective-permute-start | bytes 786440 | tf_op jit(solution)/shard_map/ppermute | solution.py:182
  105.6 2.1 %shard_map.30.refs_16_.field_ref = f32[2048,128]{1,0:T(8,128)S(1)} custom-call(f32[8,256,128]{2,1,0:T(8,128)S(1)} %all_to_all.21.in_ref), custom_call_target="tpu_custom_call" | custom-call | tf_op jit(solution)/shard_map/pallas_call | solution.py:160
  107.8 14.2 %shard_map.31 = (f32[2048,512]{1,0:T(8,128)S(1)}, f32[256,512]{1,0:T(8,128)S(1)}) custom-call(s32[3]{0:T(128)S(1)} %pad_add_fusion.place_ref, f32[512,128]{1,0:T(8,128)S(1)} %pad_maximum_fusion.2.refs_0_, f32[512,128]{1,0:T(8,128)S(1)} %collective-permute-done.1.refs_1_, f32[512,128]{1,0:T(8,128)S(1)} %copy-done.4, ...), custom_call_target="tpu_custom_call" | custom-call | tf_op jit(solution)/shard_map/pallas_call | solution.py:220
  122.0 2.0 copy-done
  124.0 13.3 %all_to_all.22 = f32[8,2,16,512]{3,2,1,0:T(8,128)S(1)} all-to-all(f32[8,2,16,512]{3,2,1,0:T(8,128)S(1)} %bitcast.19), channel_id=1, replica_groups=mesh['y'=4,'xh'=2,'xl'=2,'z'=8,'c'=2] {'y','xh'}, dimensions={0} | all-to-all | bytes 1048576 | tf_op jit(solution)/shard_map/all_to_all | solution.py:353
  137.5 12.9 %all_to_all.23 = f32[8,2,16,512]{3,2,1,0:T(8,128)S(1)} all-to-all(f32[8,2,16,512]{3,2,1,0:T(8,128)S(1)} %broadcast_in_dim.3), channel_id=1, replica_groups=mesh['y'=4,'xh'=2,'xl'=2,'z'=8,'c'=2] {'y','xh'}, dimensions={0} | all-to-all | bytes 1048576 | tf_op jit(solution)/shard_map/all_to_all | solution.py:354
  150.4 2.5 %collective-permute-start.17 = (f32[128,512]{1,0:T(8,128)S(1)}, f32[128,512]{1,0:T(8,128)S(1)}, u32[]{:S(2)}, u32[]{:S(2)}) collective-permute-start(f32[128,512]{1,0:T(8,128)S(1)} %bitcast.20), channel_id=1, source_target_pairs={{0,1},{1,0},{2,3},{3,2},{4,5},{5,4},{6,7},{7,6},{8,9},{9,8},{10,11... | collective-permute-start | bytes 786440 | tf_op jit(solution)/shard_map/ppermute | solution.py:356
  155.2 12.5 %collective-permute-done.18 = f32[256,512]{1,0:T(8,128)S(1)} collective-permute-done((f32[256,512]{1,0:T(8,128)S(1)}, f32[256,512]{1,0:T(8,128)S(1)}, u32[]{:S(2)}, u32[]{:S(2)}) %collective-permute-start.18) | collective-permute-done | bytes 524320 | tf_op jit(solution)/shard_map/ppermute | solution.py:360
  167.8 21.7 %shard_map.32.inv_ref = f32[512,512]{1,0:T(8,128)S(1)} custom-call(f32[512,512]{1,0:T(8,128)S(1)} %pad_maximum_fusion.gram_ref), custom_call_target="tpu_custom_call" | custom-call | tf_op jit(solution)/shard_map/pallas_call | solution.py:310
  189.5 6.7 %shard_map.33 = f32[2048,128]{1,0:T(8,128)} custom-call(s32[1]{0:T(128)} %bitcast.own_ref, f32[512,512]{1,0:T(8,128)S(1)} %shard_map.32.inv_ref, f32[128,512]{1,0:T(8,128)S(1)} %bitcast.17, f32[2048,512]{1,0:T(8,128)S(1)} %copy-done.1, f32[2048,128]{1,0:T(8,128)S(1)} %shard_map.30.refs_16_.field_ref), custom_call_target="tpu_custom_call" | custom-call | tf_op jit(solution)/shard_map/pallas_call | solution.py:336
  (63 shorter events, 9.5 us)
Async XLA Ops:
  57.3 3.9 %collective-permute-start = (f32[256,128]{1,0:T(8,128)S(1)}, f32[256,128]{1,0:T(8,128)S(1)}, u32[]{:S(2)}, u32[]{:S(2)}) collective-permute-start(f32[256,128]{1,0:T(8,128)S(1)} %slice_bitcast_fusion), channel_id=1, source_target_pairs={{0,16},{16,0},{1,17},{17,1},{2,18},{18,2},{3,19},{19,3},{4,20},{20... | collective-permute-start | bytes 393224 | tf_op jit(solution)/shard_map/ppermute | solution.py:172
  61.3 9.4 %collective-permute-start.1 = (f32[512,128]{1,0:T(8,128)S(1)}, f32[512,128]{1,0:T(8,128)S(1)}, u32[]{:S(2)}, u32[]{:S(2)}) collective-permute-start(f32[512,128]{1,0:T(8,128)S(1)} %pad_maximum_fusion.2.refs_0_), channel_id=1, source_target_pairs={{0,2},{2,4},{4,6},{6,8},{8,10},{10,12},{12,14},{14,0},{1,3},{3,5},... | collective-permute-start | bytes 786440 | tf_op jit(solution)/shard_map/ppermute | solution.py:177
  63.0 7.7 %collective-permute-start.2 = (f32[512,128]{1,0:T(8,128)S(1)}, f32[512,128]{1,0:T(8,128)S(1)}, u32[]{:S(2)}, u32[]{:S(2)}) collective-permute-start(f32[512,128]{1,0:T(8,128)S(1)} %pad_maximum_fusion.2.refs_0_), channel_id=1, source_target_pairs={{0,14},{2,0},{4,2},{6,4},{8,6},{10,8},{12,10},{14,12},{1,15},{3,1}... | collective-permute-start | bytes 786440 | tf_op jit(solution)/shard_map/ppermute | solution.py:178
  70.7 7.4 %collective-permute-start.3 = (f32[512,128]{1,0:T(8,128)S(1)}, f32[512,128]{1,0:T(8,128)}, u32[]{:S(2)}, u32[]{:S(2)}) collective-permute-start(f32[512,128]{1,0:T(8,128)S(1)} %collective-permute-done.1.refs_1_), channel_id=1, source_target_pairs={{0,2},{2,4},{4,6},{6,8},{8,10},{10,12},{12,14},{14,0},{1,3},{3,5},... | collective-permute-start | bytes 786440 | tf_op jit(solution)/shard_map/ppermute | solution.py:177
  70.7 34.1 %copy-start.3 = (f32[512,128]{1,0:T(8,128)}, f32[512,128]{1,0:T(8,128)S(1)}, u32[]{:S(2)}) copy-start(f32[512,128]{1,0:T(8,128)S(1)} %collective-permute-done.2.refs_2_) | copy-start | bytes 786436
  70.7 7.4 %collective-permute-start.4 = (f32[512,128]{1,0:T(8,128)S(1)}, f32[512,128]{1,0:T(8,128)}, u32[]{:S(2)}, u32[]{:S(2)}) collective-permute-start(f32[512,128]{1,0:T(8,128)S(1)} %collective-permute-done.2.refs_2_), channel_id=1, source_target_pairs={{0,14},{2,0},{4,2},{6,4},{8,6},{10,8},{12,10},{14,12},{1,15},{3,1}... | collective-permute-start | bytes 786440 | tf_op jit(solution)/shard_map/ppermute | solution.py:178
  78.1 8.7 %collective-permute-start.5 = (f32[512,128]{1,0:T(8,128)}, f32[512,128]{1,0:T(8,128)S(1)}, u32[]{:S(2)}, u32[]{:S(2)}) collective-permute-start(f32[512,128]{1,0:T(8,128)} %collective-permute-done.3.refs_3_), channel_id=1, source_target_pairs={{0,2},{2,4},{4,6},{6,8},{8,10},{10,12},{12,14},{14,0},{1,3},{3,5},... | collective-permute-start | bytes 786440 | tf_op jit(solution)/shard_map/ppermute | solution.py:177
  78.1 18.0 %collective-permute-start.6 = (f32[512,128]{1,0:T(8,128)}, f32[512,128]{1,0:T(8,128)S(1)}, u32[]{:S(2)}, u32[]{:S(2)}) collective-permute-start(f32[512,128]{1,0:T(8,128)} %collective-permute-done.4.refs_4_), channel_id=1, source_target_pairs={{0,14},{2,0},{4,2},{6,4},{8,6},{10,8},{12,10},{14,12},{1,15},{3,1}... | collective-permute-start | bytes 786440 | tf_op jit(solution)/shard_map/ppermute | solution.py:178
  86.8 12.3 %collective-permute-start.7 = (f32[256,128]{1,0:T(8,128)S(1)}, f32[256,128]{1,0:T(8,128)S(1)}, u32[]{:S(2)}, u32[]{:S(2)}) collective-permute-start(f32[256,128]{1,0:T(8,128)S(1)} %slice.21), channel_id=1, source_target_pairs={{0,2},{2,4},{4,6},{6,8},{8,10},{10,12},{12,14},{14,0},{1,3},{3,5},... | collective-permute-start | bytes 393224 | tf_op jit(solution)/shard_map/ppermute | solution.py:180
  86.9 15.9 %collective-permute-start.9 = (f32[512,128]{1,0:T(8,128)S(1)}, f32[512,128]{1,0:T(8,128)S(1)}, u32[]{:S(2)}, u32[]{:S(2)}) collective-permute-start(f32[512,128]{1,0:T(8,128)S(1)} %pad_maximum_fusion.2.refs_0_), channel_id=1, source_target_pairs={{0,1},{1,0},{2,3},{3,2},{4,5},{5,4},{6,7},{7,6},{8,9},{9,8},{10,11... | collective-permute-start | bytes 786440 | tf_op jit(solution)/shard_map/ppermute | solution.py:182
  95.6 7.9 %collective-permute-start.11 = (f32[512,128]{1,0:T(8,128)S(1)}, f32[512,128]{1,0:T(8,128)S(1)}, u32[]{:S(2)}, u32[]{:S(2)}) collective-permute-start(f32[512,128]{1,0:T(8,128)S(1)} %collective-permute-done.2.refs_2_), channel_id=1, source_target_pairs={{0,1},{1,0},{2,3},{3,2},{4,5},{5,4},{6,7},{7,6},{8,9},{9,8},{10,11... | collective-permute-start | bytes 786440 | tf_op jit(solution)/shard_map/ppermute | solution.py:182
  95.7 9.0 %collective-permute-start.10 = (f32[512,128]{1,0:T(8,128)S(1)}, f32[512,128]{1,0:T(8,128)S(1)}, u32[]{:S(2)}, u32[]{:S(2)}) collective-permute-start(f32[512,128]{1,0:T(8,128)S(1)} %collective-permute-done.1.refs_1_), channel_id=1, source_target_pairs={{0,1},{1,0},{2,3},{3,2},{4,5},{5,4},{6,7},{7,6},{8,9},{9,8},{10,11... | collective-permute-start | bytes 786440 | tf_op jit(solution)/shard_map/ppermute | solution.py:182
  96.2 5.9 %collective-permute-start.8 = (f32[256,128]{1,0:T(8,128)S(1)}, f32[256,128]{1,0:T(8,128)S(1)}, u32[]{:S(2)}, u32[]{:S(2)}) collective-permute-start(f32[256,128]{1,0:T(8,128)S(1)} %slice.22), channel_id=1, source_target_pairs={{0,14},{2,0},{4,2},{6,4},{8,6},{10,8},{12,10},{14,12},{1,15},{3,1}... | collective-permute-start | bytes 393224 | tf_op jit(solution)/shard_map/ppermute | solution.py:180
  99.1 8.6 %collective-permute-start.13 = (f32[512,128]{1,0:T(8,128)}, f32[512,128]{1,0:T(8,128)}, u32[]{:S(2)}, u32[]{:S(2)}) collective-permute-start(f32[512,128]{1,0:T(8,128)} %collective-permute-done.4.refs_4_), channel_id=1, source_target_pairs={{0,1},{1,0},{2,3},{3,2},{4,5},{5,4},{6,7},{7,6},{8,9},{9,8},{10,11... | collective-permute-start | bytes 786440 | tf_op jit(solution)/shard_map/ppermute | solution.py:182
  102.0 5.7 %collective-permute-start.12 = (f32[512,128]{1,0:T(8,128)}, f32[512,128]{1,0:T(8,128)}, u32[]{:S(2)}, u32[]{:S(2)}) collective-permute-start(f32[512,128]{1,0:T(8,128)} %collective-permute-done.3.refs_3_), channel_id=1, source_target_pairs={{0,1},{1,0},{2,3},{3,2},{4,5},{5,4},{6,7},{7,6},{8,9},{9,8},{10,11... | collective-permute-start | bytes 786440 | tf_op jit(solution)/shard_map/ppermute | solution.py:182
  103.5 4.2 %collective-permute-start.15 = (f32[512,128]{1,0:T(8,128)S(1)}, f32[512,128]{1,0:T(8,128)}, u32[]{:S(2)}, u32[]{:S(2)}) collective-permute-start(f32[512,128]{1,0:T(8,128)S(1)} %collective-permute-done.6.refs_6_), channel_id=1, source_target_pairs={{0,1},{1,0},{2,3},{3,2},{4,5},{5,4},{6,7},{7,6},{8,9},{9,8},{10,11... | collective-permute-start | bytes 786440 | tf_op jit(solution)/shard_map/ppermute | solution.py:182
  104.3 3.5 %collective-permute-start.14 = (f32[512,128]{1,0:T(8,128)S(1)}, f32[512,128]{1,0:T(8,128)}, u32[]{:S(2)}, u32[]{:S(2)}) collective-permute-start(f32[512,128]{1,0:T(8,128)S(1)} %collective-permute-done.5.refs_5_), channel_id=1, source_target_pairs={{0,1},{1,0},{2,3},{3,2},{4,5},{5,4},{6,7},{7,6},{8,9},{9,8},{10,11... | collective-permute-start | bytes 786440 | tf_op jit(solution)/shard_map/ppermute | solution.py:182
  105.5 2.3 %collective-permute-start.16 = (f32[512,128]{1,0:T(8,128)S(1)}, f32[512,128]{1,0:T(8,128)}, u32[]{:S(2)}, u32[]{:S(2)}) collective-permute-start(f32[512,128]{1,0:T(8,128)S(1)} %constant_dynamic-update-slice_fusion.refs_7_), channel_id=1, source_target_pairs={{0,1},{1,0},{2,3},{3,2},{4,5},{5,4},{6,7},{7,6},{8,9},{9,8},{10,11... | collective-permute-start | bytes 786440 | tf_op jit(solution)/shard_map/ppermute | solution.py:182
  105.5 2.3 %copy-start.6 = (f32[512,128]{1,0:T(8,128)S(1)}, f32[512,128]{1,0:T(8,128)}, u32[]{:S(2)}) copy-start(f32[512,128]{1,0:T(8,128)} %copy-done.5) | copy-start | bytes 786436
  105.5 2.3 %copy-start.8 = (f32[512,128]{1,0:T(8,128)S(1)}, f32[512,128]{1,0:T(8,128)}, u32[]{:S(2)}) copy-start(f32[512,128]{1,0:T(8,128)} %copy-done.7) | copy-start | bytes 786436
  105.5 2.3 %copy-start.10 = (f32[512,128]{1,0:T(8,128)S(1)}, f32[512,128]{1,0:T(8,128)}, u32[]{:S(2)}) copy-start(f32[512,128]{1,0:T(8,128)} %copy-done.9) | copy-start | bytes 786436
  150.4 3.7 %collective-permute-start.17 = (f32[128,512]{1,0:T(8,128)S(1)}, f32[128,512]{1,0:T(8,128)S(1)}, u32[]{:S(2)}, u32[]{:S(2)}) collective-permute-start(f32[128,512]{1,0:T(8,128)S(1)} %bitcast.20), channel_id=1, source_target_pairs={{0,1},{1,0},{2,3},{3,2},{4,5},{5,4},{6,7},{7,6},{8,9},{9,8},{10,11... | collective-permute-start | bytes 786440 | tf_op jit(solution)/shard_map/ppermute | solution.py:356
  154.2 13.4 %collective-permute-start.18 = (f32[256,512]{1,0:T(8,128)S(1)}, f32[256,512]{1,0:T(8,128)S(1)}, u32[]{:S(2)}, u32[]{:S(2)}) collective-permute-start(f32[256,512]{1,0:T(8,128)S(1)} %pad_maximum_fusion.1), channel_id=1, source_target_pairs={{0,16},{16,0},{1,17},{17,1},{2,18},{18,2},{3,19},{19,3},{4,20},{20... | collective-permute-start | bytes 1572872 | tf_op jit(solution)/shard_map/ppermute | solution.py:360
  167.8 21.8 %copy-start.1 = (f32[2048,512]{1,0:T(8,128)S(1)}, f32[2048,512]{1,0:T(8,128)}, u32[]{:S(2)}) copy-start(f32[2048,512]{1,0:T(8,128)} %copy-done) | copy-start | bytes 12582916
  (7 other events, 8.4 us)

commit v3 on v2

--- a/solution.py
+++ b/solution.py
@@ -51,7 +51,7 @@
             out_ref[g, pl.ds(step * 32, 32), :] = parts[g]
         return 0
 
-    lax.fori_loop(0, 8, body, 0)
+    lax.fori_loop(0, 8, body, 0, unroll=2)
     packed = jnp.concatenate([pot_ref[xp] for xp in range(4)], axis=1)
     for g in range(8):
         out_ref[g, 256:272, :] = packed
@@ -147,13 +147,12 @@
 
 def unpack_kernel(in_ref, out_ref):
     def body(step, _):
-        xp, yh = step // 2, step % 2
         parts = swap_groups([in_ref[g, pl.ds(step * 32, 32), :] for g in range(8)])
         for yl in range(8):
-            out_ref[pl.ds((xp * 16 + yh * 8 + yl) * 32, 32), :] = parts[yl]
-        return 0
-
-    lax.fori_loop(0, 8, body, 0)
+            out_ref[pl.ds(yl * 256 + step * 32, 32), :] = parts[yl]
+        return 0
+
+    lax.fori_loop(0, 8, body, 0, unroll=2)
 
 
 def unpack(back):
@@ -161,6 +160,24 @@
         unpack_kernel,
         out_shape=jax.ShapeDtypeStruct((2048, 128), jnp.float32),
         compiler_params=pltpu.CompilerParams(vmem_limit_bytes=8 * MIB),
+        cost_estimate=pl.CostEstimate(flops=4_000_000, bytes_accessed=4 * MIB, transcendentals=0),
+    )(back)
+
+
+def own_panel_kernel(in_ref, out_ref):
+    turned = in_ref[0].T
+    for yl in range(8):
+        out_ref[:, yl * 256 : yl * 256 + 256] = turned[yl * 16 : yl * 16 + 16, :]
+
+
+def own_panel(back):
+    return pl.pallas_call(
+        own_panel_kernel,
+        grid=(1,),
+        in_specs=[pl.BlockSpec((1, 256, 128), lambda i: (0, 0, 0))],
+        out_specs=pl.BlockSpec((16, 2048), lambda i: (0, 0)),
+        out_shape=jax.ShapeDtypeStruct((16, 2048), jnp.float32),
+        compiler_params=pltpu.CompilerParams(vmem_limit_bytes=4 * MIB),
     )(back)
 
 
@@ -177,7 +194,7 @@
         right = lax.ppermute(right, "z", ring(8, 1))
         left = lax.ppermute(left, "z", ring(8, -1))
         found += [right, left]
-    far = jnp.concatenate([lax.ppermute(right[:256], "z", ring(8, 1)), lax.ppermute(left[256:], "z", ring(8, -1))], axis=0)
+    far = jnp.concatenate([lax.ppermute(right[:16], "z", ring(8, 1)), lax.ppermute(left[16:], "z", ring(8, -1))], axis=0)
     found.append(far)
     return found + [lax.ppermute(block, "c", ring(2, 1)) for block in found]
 
@@ -186,42 +203,38 @@
 
 
 def products_kernel(place_ref, *refs):
-    blocks, (field_ref, panel_ref, out_ref, order) = refs[:16], refs[16:]
+    blocks, (field_ref, panel_ref, out_ref, gram, coupling) = refs[:16], refs[16:]
     xl, z, core = place_ref[0], place_ref[1], place_ref[2]
     for other in range(2):
         for k, offset in enumerate(OFFSETS):
             for xo in range(2):
                 owner = (xl ^ xo) * 16 + ((z + offset) & 7) * 2 + (core ^ other)
-                order[owner] = blocks[other * 8 + k][xo * 256 : xo * 256 + 256, :]
-    for group in range(4):
-
-        def body(step, _, group=group):
-            xp, yh = step // 2, step % 2
-            parts = swap_groups([order[group * 8 + q, pl.ds(step * 32, 32), :] for q in range(8)])
-            for yl in range(8):
-                panel_ref[pl.ds((xp * 16 + yh * 8 + yl) * 32, 32), group * 128 : group * 128 + 128] = parts[yl]
-            return 0
-
-        lax.fori_loop(0, 8, body, 0)
-    column = pl.multiple_of((xl * 2 + core) * 128, 128)
-    out_ref[...] = jnp.zeros_like(out_ref)
+                rows = pl.ds(pl.multiple_of(owner * 16, 16), 16)
+                panel_ref[rows, :] = blocks[other * 8 + k][xo * 16 : xo * 16 + 16, :]
+    mine = pl.ds(pl.multiple_of((xl * 2 + core) * 128, 128), 128)
+    gram[...] = jnp.zeros_like(gram)
+    coupling[...] = jnp.zeros_like(coupling)
 
     def chunk(i, _):
-        rows = pl.ds(i * 512, 512)
-        wide = panel_ref[rows, :]
-        out_ref[0:128, :] += dot_tn(panel_ref[rows, pl.ds(column, 128)], wide)
-        out_ref[128:256, :] += dot_tn(field_ref[rows, :], wide)
+        points = pl.ds(pl.multiple_of(i * 512, 512), 512)
+        wide = panel_ref[:, points]
+        gram[...] += dot_nt(panel_ref[mine, points], wide)
+        coupling[...] += dot_nn(wide, field_ref[points, :])
         return 0
 
     lax.fori_loop(0, 4, chunk, 0)
+    for s in range(8):
+        for j in range(4):
+            out_ref[s, j * 16 : j * 16 + 16, :] = gram[s * 16 : s * 16 + 16, j * 128 : j * 128 + 128]
+        out_ref[s, 64:128, :] = coupling[s * 64 : s * 64 + 64, :]
 
 
 def products(place, blocks, field):
     return pl.pallas_call(
         products_kernel,
         in_specs=[pl.BlockSpec(memory_space=pltpu.SMEM)] + [pl.BlockSpec(memory_space=pltpu.VMEM)] * 17,
-        out_shape=(jax.ShapeDtypeStruct((2048, 512), jnp.float32), jax.ShapeDtypeStruct((256, 512), jnp.float32)),
-        scratch_shapes=[pltpu.VMEM((32, 256, 128), jnp.float32)],
+        out_shape=(jax.ShapeDtypeStruct((512, 2048), jnp.float32), jax.ShapeDtypeStruct((8, 128, 128), jnp.float32)),
+        scratch_shapes=[pltpu.VMEM((128, 512), jnp.float32), pltpu.VMEM((512, 128), jnp.float32)],
         compiler_params=pltpu.CompilerParams(vmem_limit_bytes=28 * MIB),
     )(place, *blocks, field)
 
@@ -281,8 +294,14 @@
     return jnp.concatenate(out, axis=0)
 
 
-def inverse_kernel(gram_ref, inv_ref, work):
-    work[...] = gram_ref[...] * (1.0 / POINTS)
+def inverse_kernel(place_ref, own_ref, by_x_ref, by_core_ref, by_both_ref, inv_ref, work):
+    xl, core = place_ref[0], place_ref[2]
+    for flip, ref in enumerate((own_ref, by_core_ref, by_x_ref, by_both_ref)):
+        piece = (xl ^ (flip // 2)) * 2 + (core ^ (flip % 2))
+        for s in range(8):
+            rows = pl.ds(pl.multiple_of(piece * 128 + s * 16, 16), 16)
+            for j in range(4):
+                work[rows, j * 128 : j * 128 + 128] = ref[s, j * 16 : j * 16 + 16, :] * (1.0 / POINTS)
     inv_ref[...] = jnp.zeros_like(inv_ref)
 
     def diagonal(k, _):
@@ -306,40 +325,46 @@
     lax.fori_loop(0, 4, diagonal, 0)
 
 
-def inverse_factor(gram):
+def inverse_factor(place, pieces):
     return pl.pallas_call(
         inverse_kernel,
+        in_specs=[pl.BlockSpec(memory_space=pltpu.SMEM)] + [pl.BlockSpec(memory_space=pltpu.VMEM)] * 4,
         out_shape=jax.ShapeDtypeStruct((PANEL, PANEL), jnp.float32),
         scratch_shapes=[pltpu.VMEM((PANEL, PANEL), jnp.float32)],
         compiler_params=pltpu.CompilerParams(vmem_limit_bytes=16 * MIB),
-    )(gram)
-
-
-def update_kernel(own_ref, inv_ref, coupling_ref, panel_ref, field_ref, out_ref, mixer):
+    )(place, *pieces)
+
+
+def update_kernel(place_ref, inv_ref, sums_ref, panel_ref, field_ref, out_ref, coupling, mixer):
+    for s in range(8):
+        coupling[s * 64 : s * 64 + 64, :] = sums_ref[s, 64:128, :] * (1.0 / POINTS)
     inverse = inv_ref[...]
-    middle = dot_nt(coupling_ref[...] * (1.0 / POINTS), inverse)
+    middle = dot_nt(coupling[...].T, inverse)
     mixer[...] = -dot_nn(middle, inverse)
-    start = pl.multiple_of(own_ref[0] * 16, 16)
-    mixer[0:16, :] = inv_ref[pl.ds(start, 16), :]
-
-    def chunk(i, _):
-        rows = pl.ds(i * 512, 512)
-        keep = lax.broadcasted_iota(jnp.int32, (512, 128), 1) >= 16
-        base = jnp.where(keep, field_ref[rows, :], 0.0)
-        out_ref[rows, :] = base + dot_nt(panel_ref[rows, :], mixer[...])
-        return 0
-
-    lax.fori_loop(0, 4, chunk, 0)
-
-
-def update(own, inverse, coupling, panel, field):
+    own = place_ref[0] * 16 + place_ref[1] * 2 + place_ref[2]
+    mixer[0:16, :] = inv_ref[pl.ds(pl.multiple_of(own * 16, 16), 16), :]
+    keep = lax.broadcasted_iota(jnp.int32, (256, 128), 1) >= 16
+
+    def chunk(yl, _):
+        points = pl.ds(pl.multiple_of(yl * 256, 256), 256)
+        moved = dot_nn(mixer[...], panel_ref[:, points]).T
+        moved = moved + jnp.where(keep, field_ref[points, :], 0.0)
+        for xp in range(4):
+            for yh in range(2):
+                out_ref[xp, yh * 8 + yl] = moved[xp * 64 + yh * 32 : xp * 64 + yh * 32 + 32, :]
+        return 0
+
+    lax.fori_loop(0, 8, chunk, 0)
+
+
+def update(place, inverse, sums, panel, field):
     return pl.pallas_call(
         update_kernel,
         in_specs=[pl.BlockSpec(memory_space=pltpu.SMEM)] + [pl.BlockSpec(memory_space=pltpu.VMEM)] * 4,
-        out_shape=jax.ShapeDtypeStruct((2048, 128), jnp.float32),
-        scratch_shapes=[pltpu.VMEM((128, PANEL), jnp.float32)],
+        out_shape=jax.ShapeDtypeStruct((4, 16, 32, 128), jnp.float32),
+        scratch_shapes=[pltpu.VMEM((PANEL, 128), jnp.float32), pltpu.VMEM((128, PANEL), jnp.float32)],
         compiler_params=pltpu.CompilerParams(vmem_limit_bytes=28 * MIB),
-    )(own, inverse, coupling, panel, field)
+    )(place, inverse, sums, panel, field)
 
 
 def per_device(orbitals, potential):
@@ -348,20 +373,15 @@
     received = lax.all_to_all(pack(orbitals, potential), SPACE, 0, 0, tiled=True)
     back = lax.all_to_all(chebyshev(received), SPACE, 0, 0, tiled=True)
     field = unpack(back)
-    panel, terms = products(place, gather_panel(back[0]), field)
-    terms = terms.reshape(2, 8, 16, PANEL).swapaxes(0, 1)
+    panel, terms = products(place, gather_panel(own_panel(back)), field)
     mine = jnp.sum(lax.all_to_all(terms, SPACE, 0, 0, tiled=True), axis=0)
-    full = lax.all_to_all(jnp.broadcast_to(mine, (8, 2, 16, PANEL)), SPACE, 0, 0, tiled=True)
-    piece, coupling = full[:, 0].reshape(128, PANEL), full[:, 1].reshape(128, PANEL)
+    sums = lax.all_to_all(jnp.broadcast_to(mine, (8, 128, 128)), SPACE, 0, 0, tiled=True)
+    piece = sums[:, :64]
     by_core = lax.ppermute(piece, "c", ring(2, 1))
-    low = jnp.where(core == 0, piece, by_core)
-    high = jnp.where(core == 0, by_core, piece)
-    half = jnp.concatenate([low, high], axis=0)
-    by_x = lax.ppermute(half, "xl", ring(2, 1))
-    gram = jnp.concatenate([jnp.where(xl == 0, half, by_x), jnp.where(xl == 0, by_x, half)], axis=0)
-    inverse = inverse_factor(gram)
-    own = (xl * 16 + z * 2 + core).astype(jnp.int32).reshape(1)
-    return update(own, inverse, coupling, panel, field).reshape(4, 16, 32, 128)
+    by_x = lax.ppermute(piece, "xl", ring(2, 1))
+    by_both = lax.ppermute(by_x, "c", ring(2, 1))
+    inverse = inverse_factor(place, (piece, by_x, by_core, by_both))
+    return update(place, inverse, sums, panel, field)
 
 
 def solution(mesh):

time: 197 us -> 189 us (0.959)
  waiting for transfers between devices: 31.5 us -> 22.8 us
  starting transfers between devices: 31.6 us -> 37 us
  Pallas kernels: 58.2 us -> 54.4 us
    ppermute x3 -> x4, waiting for transfers between devices: 12.8 us -> 5.29 us  [the longest x1 2.19 us: per_device(): by_x = lax.ppermute(piece, 'xl', ring(2, 1))]
    pallas_call x1, Pallas kernels: 14.2 us -> 10 us  [products(): pl.pallas_call(products_kernel, in_specs=[pl.BlockSpec(memory_space=pltpu...]
    ppermute x3 -> x4, starting transfers between devices: 3.98 us -> 6.9 us  [the longest x1 3.59 us: per_device(): by_both = lax.ppermute(by_x, 'c', ring(2, 1))]
    ppermute x8, starting transfers between devices: 13.1 us -> 15.5 us  [gather_panel(): return found + [lax.ppermute(block, 'c', ring(2, 1)) for block in found]]
    pallas_call x1 -> x2, Pallas kernels: 21.7 us -> 22.4 us  [the longest x1 22.3 us: inverse_factor(): pl.pallas_call(inverse_kernel, in_specs=[pl.BlockSpec(memory_space=pltpu....]
  transfers between devices with their start and end apart: 19 -> 20, of which waited for: 7 -> 7; matrix products, arithmetic and copies ran while one was open for 0% -> 0% of each run, Pallas kernels for 1% -> 1%
where the time goes in v3:
time: 189 us
  blocking collectives  68.3 us (36%)
  Pallas kernels  54.4 us (29%)
  starting transfers between devices  37 us (20%)
  waiting for transfers between devices  22.8 us (12%)
  local copies, waits for them, and re-layouts  6.16 us (3%)
    all_to_all x1, blocking collectives, per_device(): lax.all_to_all(pack(orbitals, potential), SPACE, 0, 0, tiled=True)  24 us
    pallas_call x1, Pallas kernels, inverse_factor(): pl.pallas_call(inverse_kernel, in_specs=[pl.BlockSpec(memory_space=pltpu....  22.3 us
    all_to_all x1, blocking collectives, per_device(): back = lax.all_to_all(chebyshev(received), SPACE, 0, 0, tiled=True)  17.8 us
    ppermute x8, starting transfers between devices, gather_panel(): return found + [lax.ppermute(block, 'c', ring(2, 1)) for block in found]  15.5 us
    ppermute x3, waiting for transfers between devices, gather_panel(): right = lax.ppermute(right, 'z', ring(8, 1))  14 us
    all_to_all x1, blocking collectives, per_device(): mine = jnp.sum(lax.all_to_all(terms, SPACE, 0, 0, tiled=True), axis=0)  13.3 us
    all_to_all x1, blocking collectives, per_device(): lax.all_to_all(jnp.broadcast_to(mine, (8, 128, 128)), SPACE, 0, 0, tiled=...  13.2 us
    pallas_call x1, Pallas kernels, chebyshev(): pl.pallas_call(filter_kernel, out_shape=jax.ShapeDtypeStruct((64, 32, 128...  11.3 us
  transfers between devices with their start and end apart: 20, of which 7 were waited for; matrix products, arithmetic and copies ran while one was open for 0% of the time, Pallas kernels for 1%

profile of v3, /device:TPU:1, one launch (start us, length us, event | category | flops | bytes accessed | tf_op | source)
XLA Modules:
  0.0 189.0 jit_solution(3082573563701971002)
XLA Ops:
  3.6 24.0 %all_to_all.20.in_ref = f32[8,272,128]{2,1,0:T(8,128)S(1)} all-to-all(f32[8,272,128]{2,1,0:T(8,128)S(1)} %shard_map.28), channel_id=1, replica_groups=mesh['y'=4,'xh'=2,'xl'=2,'z'=8,'c'=2] {'y','xh'}, dimensions={0} | all-to-all | bytes 2228224 | tf_op jit(solution)/shard_map/all_to_all | solution.py:373
  27.6 11.3 %shard_map.29 = f32[64,32,128]{2,1,0:T(8,128)S(1)} custom-call(f32[8,272,128]{2,1,0:T(8,128)S(1)} %all_to_all.20.in_ref), custom_call_target="tpu_custom_call" | custom-call | tf_op jit(solution)/shard_map/pallas_call | solution.py:139
  38.9 17.8 %all_to_all.21.in_ref = f32[8,256,128]{2,1,0:T(8,128)S(1)} all-to-all(f32[8,256,128]{2,1,0:T(8,128)S(1)} %bitcast.4), channel_id=1, replica_groups=mesh['y'=4,'xh'=2,'xl'=2,'z'=8,'c'=2] {'y','xh'}, dimensions={0} | all-to-all | bytes 2097152 | tf_op jit(solution)/shard_map/all_to_all | solution.py:374
  57.3 3.5 %collective-permute-done = f32[16,2048]{1,0:T(8,128)S(1)} collective-permute-done((f32[16,2048]{1,0:T(8,128)S(1)}, f32[16,2048]{1,0:T(8,128)S(1)}, u32[]{:S(2)}, u32[]{:S(2)}) %collective-permute-start) | collective-permute-done | bytes 131104 | tf_op jit(solution)/shard_map/ppermute | solution.py:189
  60.8 1.7 collective-permute-start.1
  62.5 4.0 %collective-permute-start.2 = (f32[32,2048]{1,0:T(8,128)S(1)}, f32[32,2048]{1,0:T(8,128)S(1)}, u32[]{:S(2)}, u32[]{:S(2)}) collective-permute-start(f32[32,2048]{1,0:T(8,128)S(1)} %pad_maximum_fusion.refs_0_), channel_id=1, source_target_pairs={{0,14},{2,0},{4,2},{6,4},{8,6},{10,8},{12,10},{14,12},{1,15},{3,1}... | collective-permute-start | bytes 786440 | tf_op jit(solution)/shard_map/ppermute | solution.py:195
  66.6 3.7 %collective-permute-done.1.refs_1_ = f32[32,2048]{1,0:T(8,128)S(1)} collective-permute-done((f32[32,2048]{1,0:T(8,128)S(1)}, f32[32,2048]{1,0:T(8,128)S(1)}, u32[]{:S(2)}, u32[]{:S(2)}) %collective-permute-start.1) | collective-permute-done | bytes 262176 | tf_op jit(solution)/shard_map/ppermute | solution.py:194
  70.2 2.8 %collective-permute-start.4 = (f32[32,2048]{1,0:T(8,128)S(1)}, f32[32,2048]{1,0:T(8,128)}, u32[]{:S(2)}, u32[]{:S(2)}) collective-permute-start(f32[32,2048]{1,0:T(8,128)S(1)} %collective-permute-done.2.refs_2_), channel_id=1, source_target_pairs={{0,14},{2,0},{4,2},{6,4},{8,6},{10,8},{12,10},{14,12},{1,15},{3,1}... | collective-permute-start | bytes 786440 | tf_op jit(solution)/shard_map/ppermute | solution.py:195
  73.0 4.7 %collective-permute-done.3.refs_3_ = f32[32,2048]{1,0:T(8,128)} collective-permute-done((f32[32,2048]{1,0:T(8,128)S(1)}, f32[32,2048]{1,0:T(8,128)}, u32[]{:S(2)}, u32[]{:S(2)}) %collective-permute-start.3) | collective-permute-done | bytes 262176 | tf_op jit(solution)/shard_map/ppermute | solution.py:194
  77.6 3.0 %collective-permute-start.6 = (f32[32,2048]{1,0:T(8,128)}, f32[32,2048]{1,0:T(8,128)S(1)}, u32[]{:S(2)}, u32[]{:S(2)}) collective-permute-start(f32[32,2048]{1,0:T(8,128)} %collective-permute-done.4.refs_4_), channel_id=1, source_target_pairs={{0,14},{2,0},{4,2},{6,4},{8,6},{10,8},{12,10},{14,12},{1,15},{3,1}... | collective-permute-start | bytes 786440 | tf_op jit(solution)/shard_map/ppermute | solution.py:195
  80.7 5.7 %collective-permute-done.5.refs_5_ = f32[32,2048]{1,0:T(8,128)S(1)} collective-permute-done((f32[32,2048]{1,0:T(8,128)}, f32[32,2048]{1,0:T(8,128)S(1)}, u32[]{:S(2)}, u32[]{:S(2)}) %collective-permute-start.5) | collective-permute-done | bytes 262176 | tf_op jit(solution)/shard_map/ppermute | solution.py:194
  86.5 8.7 %collective-permute-start.9 = (f32[32,2048]{1,0:T(8,128)S(1)}, f32[32,2048]{1,0:T(8,128)S(1)}, u32[]{:S(2)}, u32[]{:S(2)}) collective-permute-start(f32[32,2048]{1,0:T(8,128)S(1)} %pad_maximum_fusion.refs_0_), channel_id=1, source_target_pairs={{0,1},{1,0},{2,3},{3,2},{4,5},{5,4},{6,7},{7,6},{8,9},{9,8},{10,11... | collective-permute-start | bytes 786440 | tf_op jit(solution)/shard_map/ppermute | solution.py:199
  95.8 2.8 %collective-permute-start.8 = (f32[16,2048]{1,0:T(8,128)S(1)}, f32[16,2048]{1,0:T(8,128)S(1)}, u32[]{:S(2)}, u32[]{:S(2)}) collective-permute-start(f32[16,2048]{1,0:T(8,128)S(1)} %slice.13), channel_id=1, source_target_pairs={{0,14},{2,0},{4,2},{6,4},{8,6},{10,8},{12,10},{14,12},{1,15},{3,1}... | collective-permute-start | bytes 393224 | tf_op jit(solution)/shard_map/ppermute | solution.py:197
  98.7 1.9 %collective-permute-done.8 = f32[16,2048]{1,0:T(8,128)S(1)} collective-permute-done((f32[16,2048]{1,0:T(8,128)S(1)}, f32[16,2048]{1,0:T(8,128)S(1)}, u32[]{:S(2)}, u32[]{:S(2)}) %collective-permute-start.8) | collective-permute-done | bytes 131104 | tf_op jit(solution)/shard_map/ppermute | solution.py:197
  100.6 5.6 %collective-permute-start.12 = (f32[32,2048]{1,0:T(8,128)}, f32[32,2048]{1,0:T(8,128)}, u32[]{:S(2)}, u32[]{:S(2)}) collective-permute-start(f32[32,2048]{1,0:T(8,128)} %collective-permute-done.3.refs_3_), channel_id=1, source_target_pairs={{0,1},{1,0},{2,3},{3,2},{4,5},{5,4},{6,7},{7,6},{8,9},{9,8},{10,11... | collective-permute-start | bytes 786440 | tf_op jit(solution)/shard_map/ppermute | solution.py:199
  110.7 10.0 %shard_map.32 = (f32[512,2048]{1,0:T(8,128)S(1)}, f32[8,128,128]{2,1,0:T(8,128)S(1)}) custom-call(s32[3]{0:T(128)S(1)} %pad_add_fusion.place_ref, f32[32,2048]{1,0:T(8,128)S(1)} %pad_maximum_fusion.refs_0_, f32[32,2048]{1,0:T(8,128)S(1)} %collective-permute-done.1.refs_1_, f32[32,2048]{1,0:T(8,128)S(1)} %copy-done.4, ...), custom_call_target="tpu_custom_call" | custom-call | tf_op jit(solution)/shard_map/pallas_call | solution.py:233
  120.7 1.9 %copy-done = f32[512,2048]{1,0:T(8,128)} copy-done((f32[512,2048]{1,0:T(8,128)}, f32[512,2048]{1,0:T(8,128)S(1)}, u32[]{:S(2)}) %copy-start) | copy-done | bytes 4194328
  122.7 13.3 %all_to_all.22 = f32[8,128,128]{2,1,0:T(8,128)S(1)} all-to-all(f32[8,128,128]{2,1,0:T(8,128)S(1)} %get-tuple-element.7), channel_id=1, replica_groups=mesh['y'=4,'xh'=2,'xl'=2,'z'=8,'c'=2] {'y','xh'}, dimensions={0} | all-to-all | bytes 1048576 | tf_op jit(solution)/shard_map/all_to_all | solution.py:377
  136.1 13.2 %all_to_all.23.sums_ref = f32[8,128,128]{2,1,0:T(8,128)S(1)} all-to-all(f32[8,128,128]{2,1,0:T(8,128)S(1)} %broadcast_in_dim.3), channel_id=1, replica_groups=mesh['y'=4,'xh'=2,'xl'=2,'z'=8,'c'=2] {'y','xh'}, dimensions={0} | all-to-all | bytes 1048576 | tf_op jit(solution)/shard_map/all_to_all | solution.py:378
  149.7 2.7 %collective-permute-start.18 = (f32[8,64,128]{2,1,0:T(8,128)S(1)}, f32[8,64,128]{2,1,0:T(8,128)S(1)}, u32[]{:S(2)}, u32[]{:S(2)}) collective-permute-start(f32[8,64,128]{2,1,0:T(8,128)S(1)} %slice.14.own_ref), channel_id=1, source_target_pairs={{0,1},{1,0},{2,3},{3,2},{4,5},{5,4},{6,7},{7,6},{8,9},{9,8},{10,11... | collective-permute-start | bytes 786440 | tf_op jit(solution)/shard_map/ppermute | solution.py:380
  152.4 2.2 %collective-permute-done.17.by_x_ref = f32[8,64,128]{2,1,0:T(8,128)S(1)} collective-permute-done((f32[8,64,128]{2,1,0:T(8,128)S(1)}, f32[8,64,128]{2,1,0:T(8,128)S(1)}, u32[]{:S(2)}, u32[]{:S(2)}) %collective-permute-start.17) | collective-permute-done | bytes 262176 | tf_op jit(solution)/shard_map/ppermute | solution.py:381
  154.6 3.6 %collective-permute-start.19 = (f32[8,64,128]{2,1,0:T(8,128)S(1)}, f32[8,64,128]{2,1,0:T(8,128)S(1)}, u32[]{:S(2)}, u32[]{:S(2)}) collective-permute-start(f32[8,64,128]{2,1,0:T(8,128)S(1)} %collective-permute-done.17.by_x_ref), channel_id=1, source_target_pairs={{0,1},{1,0},{2,3},{3,2},{4,5},{5,4},{6,7},{7,6},{8,9},{9,8},{10,11... | collective-permute-start | bytes 786440 | tf_op jit(solution)/shard_map/ppermute | solution.py:382
  159.3 22.3 %shard_map.33.inv_ref = f32[512,512]{1,0:T(8,128)S(1)} custom-call(s32[3]{0:T(128)S(1)} %pad_add_fusion.place_ref, f32[8,64,128]{2,1,0:T(8,128)S(1)} %slice.14.own_ref, f32[8,64,128]{2,1,0:T(8,128)S(1)} %collective-permute-done.17.by_x_ref, f32[8,64,128]{2,1,0:T(8,128)S(1)} %collective-permute-done.18.by_core_ref, ...), custom_call_target="tpu_custom_call" | custom-call | tf_op jit(solution)/shard_map/pallas_call | solution.py:329
  181.6 7.4 %shard_map.34 = f32[4,16,32,128]{3,2,1,0:T(8,128)} custom-call(s32[3]{0:T(128)S(1)} %pad_add_fusion.place_ref, f32[512,512]{1,0:T(8,128)S(1)} %shard_map.33.inv_ref, f32[8,128,128]{2,1,0:T(8,128)S(1)} %all_to_all.23.sums_ref, f32[512,2048]{1,0:T(8,128)S(1)} %copy-done.1, f32[2048,128]{1,0:T(8,128)S(1)} %shard_map.31.refs_16_.field_ref), custom_call_target="tpu_custom_call" | custom-call | tf_op jit(solution)/shard_map/pallas_call | solution.py:361
  (60 shorter events, 10.9 us)
Async XLA Ops:
  56.9 3.9 %collective-permute-start = (f32[16,2048]{1,0:T(8,128)S(1)}, f32[16,2048]{1,0:T(8,128)S(1)}, u32[]{:S(2)}, u32[]{:S(2)}) collective-permute-start(f32[16,2048]{1,0:T(8,128)S(1)} %shard_map.30), channel_id=1, source_target_pairs={{0,16},{16,0},{1,17},{17,1},{2,18},{18,2},{3,19},{19,3},{4,20},{20... | collective-permute-start | bytes 393224 | tf_op jit(solution)/shard_map/ppermute | solution.py:189
  60.8 9.4 %collective-permute-start.1 = (f32[32,2048]{1,0:T(8,128)S(1)}, f32[32,2048]{1,0:T(8,128)S(1)}, u32[]{:S(2)}, u32[]{:S(2)}) collective-permute-start(f32[32,2048]{1,0:T(8,128)S(1)} %pad_maximum_fusion.refs_0_), channel_id=1, source_target_pairs={{0,2},{2,4},{4,6},{6,8},{8,10},{10,12},{12,14},{14,0},{1,3},{3,5},... | collective-permute-start | bytes 786440 | tf_op jit(solution)/shard_map/ppermute | solution.py:194
  62.5 7.7 %collective-permute-start.2 = (f32[32,2048]{1,0:T(8,128)S(1)}, f32[32,2048]{1,0:T(8,128)S(1)}, u32[]{:S(2)}, u32[]{:S(2)}) collective-permute-start(f32[32,2048]{1,0:T(8,128)S(1)} %pad_maximum_fusion.refs_0_), channel_id=1, source_target_pairs={{0,14},{2,0},{4,2},{6,4},{8,6},{10,8},{12,10},{14,12},{1,15},{3,1}... | collective-permute-start | bytes 786440 | tf_op jit(solution)/shard_map/ppermute | solution.py:195
  70.2 7.4 %collective-permute-start.3 = (f32[32,2048]{1,0:T(8,128)S(1)}, f32[32,2048]{1,0:T(8,128)}, u32[]{:S(2)}, u32[]{:S(2)}) collective-permute-start(f32[32,2048]{1,0:T(8,128)S(1)} %collective-permute-done.1.refs_1_), channel_id=1, source_target_pairs={{0,2},{2,4},{4,6},{6,8},{8,10},{10,12},{12,14},{14,0},{1,3},{3,5},... | collective-permute-start | bytes 786440 | tf_op jit(solution)/shard_map/ppermute | solution.py:194
  70.2 38.7 %copy-start.3 = (f32[32,2048]{1,0:T(8,128)}, f32[32,2048]{1,0:T(8,128)S(1)}, u32[]{:S(2)}) copy-start(f32[32,2048]{1,0:T(8,128)S(1)} %collective-permute-done.2.refs_2_) | copy-start | bytes 786436
  70.2 7.4 %collective-permute-start.4 = (f32[32,2048]{1,0:T(8,128)S(1)}, f32[32,2048]{1,0:T(8,128)}, u32[]{:S(2)}, u32[]{:S(2)}) collective-permute-start(f32[32,2048]{1,0:T(8,128)S(1)} %collective-permute-done.2.refs_2_), channel_id=1, source_target_pairs={{0,14},{2,0},{4,2},{6,4},{8,6},{10,8},{12,10},{14,12},{1,15},{3,1}... | collective-permute-start | bytes 786440 | tf_op jit(solution)/shard_map/ppermute | solution.py:195
  77.6 8.7 %collective-permute-start.5 = (f32[32,2048]{1,0:T(8,128)}, f32[32,2048]{1,0:T(8,128)S(1)}, u32[]{:S(2)}, u32[]{:S(2)}) collective-permute-start(f32[32,2048]{1,0:T(8,128)} %collective-permute-done.3.refs_3_), channel_id=1, source_target_pairs={{0,2},{2,4},{4,6},{6,8},{8,10},{10,12},{12,14},{14,0},{1,3},{3,5},... | collective-permute-start | bytes 786440 | tf_op jit(solution)/shard_map/ppermute | solution.py:194
  77.6 18.0 %collective-permute-start.6 = (f32[32,2048]{1,0:T(8,128)}, f32[32,2048]{1,0:T(8,128)S(1)}, u32[]{:S(2)}, u32[]{:S(2)}) collective-permute-start(f32[32,2048]{1,0:T(8,128)} %collective-permute-done.4.refs_4_), channel_id=1, source_target_pairs={{0,14},{2,0},{4,2},{6,4},{8,6},{10,8},{12,10},{14,12},{1,15},{3,1}... | collective-permute-start | bytes 786440 | tf_op jit(solution)/shard_map/ppermute | solution.py:195
  86.4 9.4 %collective-permute-start.7 = (f32[16,2048]{1,0:T(8,128)S(1)}, f32[16,2048]{1,0:T(8,128)S(1)}, u32[]{:S(2)}, u32[]{:S(2)}) collective-permute-start(f32[16,2048]{1,0:T(8,128)S(1)} %slice.12), channel_id=1, source_target_pairs={{0,2},{2,4},{4,6},{6,8},{8,10},{10,12},{12,14},{14,0},{1,3},{3,5},... | collective-permute-start | bytes 393224 | tf_op jit(solution)/shard_map/ppermute | solution.py:197
  86.5 19.8 %collective-permute-start.9 = (f32[32,2048]{1,0:T(8,128)S(1)}, f32[32,2048]{1,0:T(8,128)S(1)}, u32[]{:S(2)}, u32[]{:S(2)}) collective-permute-start(f32[32,2048]{1,0:T(8,128)S(1)} %pad_maximum_fusion.refs_0_), channel_id=1, source_target_pairs={{0,1},{1,0},{2,3},{3,2},{4,5},{5,4},{6,7},{7,6},{8,9},{9,8},{10,11... | collective-permute-start | bytes 786440 | tf_op jit(solution)/shard_map/ppermute | solution.py:199
  95.2 11.8 %collective-permute-start.11 = (f32[32,2048]{1,0:T(8,128)S(1)}, f32[32,2048]{1,0:T(8,128)S(1)}, u32[]{:S(2)}, u32[]{:S(2)}) collective-permute-start(f32[32,2048]{1,0:T(8,128)S(1)} %collective-permute-done.2.refs_2_), channel_id=1, source_target_pairs={{0,1},{1,0},{2,3},{3,2},{4,5},{5,4},{6,7},{7,6},{8,9},{9,8},{10,11... | collective-permute-start | bytes 786440 | tf_op jit(solution)/shard_map/ppermute | solution.py:199
  95.3 12.9 %collective-permute-start.10 = (f32[32,2048]{1,0:T(8,128)S(1)}, f32[32,2048]{1,0:T(8,128)S(1)}, u32[]{:S(2)}, u32[]{:S(2)}) collective-permute-start(f32[32,2048]{1,0:T(8,128)S(1)} %collective-permute-done.1.refs_1_), channel_id=1, source_target_pairs={{0,1},{1,0},{2,3},{3,2},{4,5},{5,4},{6,7},{7,6},{8,9},{9,8},{10,11... | collective-permute-start | bytes 786440 | tf_op jit(solution)/shard_map/ppermute | solution.py:199
  95.7 14.9 %collective-permute-start.13 = (f32[32,2048]{1,0:T(8,128)}, f32[32,2048]{1,0:T(8,128)}, u32[]{:S(2)}, u32[]{:S(2)}) collective-permute-start(f32[32,2048]{1,0:T(8,128)} %collective-permute-done.4.refs_4_), channel_id=1, source_target_pairs={{0,1},{1,0},{2,3},{3,2},{4,5},{5,4},{6,7},{7,6},{8,9},{9,8},{10,11... | collective-permute-start | bytes 786440 | tf_op jit(solution)/shard_map/ppermute | solution.py:199
  95.8 4.8 %collective-permute-start.8 = (f32[16,2048]{1,0:T(8,128)S(1)}, f32[16,2048]{1,0:T(8,128)S(1)}, u32[]{:S(2)}, u32[]{:S(2)}) collective-permute-start(f32[16,2048]{1,0:T(8,128)S(1)} %slice.13), channel_id=1, source_target_pairs={{0,14},{2,0},{4,2},{6,4},{8,6},{10,8},{12,10},{14,12},{1,15},{3,1}... | collective-permute-start | bytes 393224 | tf_op jit(solution)/shard_map/ppermute | solution.py:197
  100.6 10.0 %collective-permute-start.12 = (f32[32,2048]{1,0:T(8,128)}, f32[32,2048]{1,0:T(8,128)}, u32[]{:S(2)}, u32[]{:S(2)}) collective-permute-start(f32[32,2048]{1,0:T(8,128)} %collective-permute-done.3.refs_3_), channel_id=1, source_target_pairs={{0,1},{1,0},{2,3},{3,2},{4,5},{5,4},{6,7},{7,6},{8,9},{9,8},{10,11... | collective-permute-start | bytes 786440 | tf_op jit(solution)/shard_map/ppermute | solution.py:199
  106.9 3.7 %collective-permute-start.15 = (f32[32,2048]{1,0:T(8,128)S(1)}, f32[32,2048]{1,0:T(8,128)}, u32[]{:S(2)}, u32[]{:S(2)}) collective-permute-start(f32[32,2048]{1,0:T(8,128)S(1)} %collective-permute-done.6.refs_6_), channel_id=1, source_target_pairs={{0,1},{1,0},{2,3},{3,2},{4,5},{5,4},{6,7},{7,6},{8,9},{9,8},{10,11... | collective-permute-start | bytes 786440 | tf_op jit(solution)/shard_map/ppermute | solution.py:199
  107.7 3.0 %collective-permute-start.14 = (f32[32,2048]{1,0:T(8,128)S(1)}, f32[32,2048]{1,0:T(8,128)}, u32[]{:S(2)}, u32[]{:S(2)}) collective-permute-start(f32[32,2048]{1,0:T(8,128)S(1)} %collective-permute-done.5.refs_5_), channel_id=1, source_target_pairs={{0,1},{1,0},{2,3},{3,2},{4,5},{5,4},{6,7},{7,6},{8,9},{9,8},{10,11... | collective-permute-start | bytes 786440 | tf_op jit(solution)/shard_map/ppermute | solution.py:199
  108.9 1.8 collective-permute-start.16
  108.9 1.8 copy-start.10
  120.7 2.0 %copy-start = (f32[512,2048]{1,0:T(8,128)}, f32[512,2048]{1,0:T(8,128)S(1)}, u32[]{:S(2)}) copy-start(f32[512,2048]{1,0:T(8,128)S(1)} %get-tuple-element.8.panel_ref) | copy-start | bytes 12582916
  136.0 45.6 %copy-start.1 = (f32[512,2048]{1,0:T(8,128)S(1)}, f32[512,2048]{1,0:T(8,128)}, u32[]{:S(2)}) copy-start(f32[512,2048]{1,0:T(8,128)} %copy-done) | copy-start | bytes 12582916
  149.3 5.3 %collective-permute-start.17 = (f32[8,64,128]{2,1,0:T(8,128)S(1)}, f32[8,64,128]{2,1,0:T(8,128)S(1)}, u32[]{:S(2)}, u32[]{:S(2)}) collective-permute-start(f32[8,64,128]{2,1,0:T(8,128)S(1)} %slice.14.own_ref), channel_id=1, source_target_pairs={{0,16},{16,0},{1,17},{17,1},{2,18},{18,2},{3,19},{19,3},{4,20},{20... | collective-permute-start | bytes 786440 | tf_op jit(solution)/shard_map/ppermute | solution.py:381
  149.7 8.5 %collective-permute-start.18 = (f32[8,64,128]{2,1,0:T(8,128)S(1)}, f32[8,64,128]{2,1,0:T(8,128)S(1)}, u32[]{:S(2)}, u32[]{:S(2)}) collective-permute-start(f32[8,64,128]{2,1,0:T(8,128)S(1)} %slice.14.own_ref), channel_id=1, source_target_pairs={{0,1},{1,0},{2,3},{3,2},{4,5},{5,4},{6,7},{7,6},{8,9},{9,8},{10,11... | collective-permute-start | bytes 786440 | tf_op jit(solution)/shard_map/ppermute | solution.py:380
  154.6 4.8 %collective-permute-start.19 = (f32[8,64,128]{2,1,0:T(8,128)S(1)}, f32[8,64,128]{2,1,0:T(8,128)S(1)}, u32[]{:S(2)}, u32[]{:S(2)}) collective-permute-start(f32[8,64,128]{2,1,0:T(8,128)S(1)} %collective-permute-done.17.by_x_ref), channel_id=1, source_target_pairs={{0,1},{1,0},{2,3},{3,2},{4,5},{5,4},{6,7},{7,6},{8,9},{9,8},{10,11... | collective-permute-start | bytes 786440 | tf_op jit(solution)/shard_map/ppermute | solution.py:382
  (8 other events, 9.3 us)

commit v4 on v3

--- a/solution.py
+++ b/solution.py
@@ -15,6 +15,7 @@
 SPACE = ("y", "xh")
 HI = lax.Precision.HIGHEST
 MIB = 1024 * 1024
+BIG = 56
 
 
 def dot_nn(a, b):
@@ -44,24 +45,27 @@
 
 
 def pack_kernel(orb_ref, pot_ref, out_ref):
-    def body(step, _):
-        xp, yh = step // 2, step % 2
-        parts = swap_groups([orb_ref[xp, yh * 8 + yl] for yl in range(8)])
+    xp = pl.program_id(0)
+    for yh in range(2):
+        parts = swap_groups([orb_ref[0, yh * 8 + yl] for yl in range(8)])
         for g in range(8):
-            out_ref[g, pl.ds(step * 32, 32), :] = parts[g]
-        return 0
-
-    lax.fori_loop(0, 8, body, 0, unroll=2)
-    packed = jnp.concatenate([pot_ref[xp] for xp in range(4)], axis=1)
-    for g in range(8):
-        out_ref[g, 256:272, :] = packed
+            out_ref[g, pl.ds(pl.multiple_of(xp * 64 + yh * 32, 32), 32), :] = parts[g]
+
+    @pl.when(xp == 3)
+    def _():
+        packed = jnp.concatenate([pot_ref[p] for p in range(4)], axis=1)
+        for g in range(8):
+            out_ref[g, 256:272, :] = packed
 
 
 def pack(orbitals, potential):
     return pl.pallas_call(
         pack_kernel,
+        grid=(4,),
+        in_specs=[pl.BlockSpec((1, 16, 32, 128), lambda i: (i, 0, 0, 0)), pl.BlockSpec((4, 16, 32), lambda i: (0, 0, 0))],
+        out_specs=pl.BlockSpec((8, 272, 128), lambda i: (0, 0, 0)),
         out_shape=jax.ShapeDtypeStruct((8, 272, 128), jnp.float32),
-        compiler_params=pltpu.CompilerParams(vmem_limit_bytes=8 * MIB),
+        compiler_params=pltpu.CompilerParams(vmem_limit_bytes=BIG * MIB),
     )(orbitals, potential)
 
 
@@ -145,39 +149,21 @@
     return out.reshape(8, 256, 128)
 
 
-def unpack_kernel(in_ref, out_ref):
-    def body(step, _):
-        parts = swap_groups([in_ref[g, pl.ds(step * 32, 32), :] for g in range(8)])
-        for yl in range(8):
-            out_ref[pl.ds(yl * 256 + step * 32, 32), :] = parts[yl]
-        return 0
-
-    lax.fori_loop(0, 8, body, 0, unroll=2)
-
-
-def unpack(back):
-    return pl.pallas_call(
-        unpack_kernel,
-        out_shape=jax.ShapeDtypeStruct((2048, 128), jnp.float32),
-        compiler_params=pltpu.CompilerParams(vmem_limit_bytes=8 * MIB),
-        cost_estimate=pl.CostEstimate(flops=4_000_000, bytes_accessed=4 * MIB, transcendentals=0),
-    )(back)
-
-
-def own_panel_kernel(in_ref, out_ref):
+def turn_kernel(in_ref, out_ref):
     turned = in_ref[0].T
     for yl in range(8):
         out_ref[:, yl * 256 : yl * 256 + 256] = turned[yl * 16 : yl * 16 + 16, :]
 
 
-def own_panel(back):
+def turn(back, groups):
     return pl.pallas_call(
-        own_panel_kernel,
-        grid=(1,),
-        in_specs=[pl.BlockSpec((1, 256, 128), lambda i: (0, 0, 0))],
-        out_specs=pl.BlockSpec((16, 2048), lambda i: (0, 0)),
-        out_shape=jax.ShapeDtypeStruct((16, 2048), jnp.float32),
+        turn_kernel,
+        grid=(groups,),
+        in_specs=[pl.BlockSpec((1, 256, 128), lambda i: (i, 0, 0))],
+        out_specs=pl.BlockSpec((16, 2048), lambda i: (i, 0)),
+        out_shape=jax.ShapeDtypeStruct((16 * groups, 2048), jnp.float32),
         compiler_params=pltpu.CompilerParams(vmem_limit_bytes=4 * MIB),
+        cost_estimate=pl.CostEstimate(flops=groups * 500_000, bytes_accessed=groups * MIB // 4, transcendentals=0),
     )(back)
 
 
@@ -185,57 +171,75 @@
     return [(i, (i + step) % count) for i in range(count)]
 
 
-def gather_panel(own):
+def gather_panel(own, field):
     other = lax.ppermute(own, "xl", ring(2, 1))
-    pair = jnp.concatenate([own, other], axis=0)
-    found = [pair]
-    right = left = pair
-    for _ in range(3):
-        right = lax.ppermute(right, "z", ring(8, 1))
-        left = lax.ppermute(left, "z", ring(8, -1))
-        found += [right, left]
-    far = jnp.concatenate([lax.ppermute(right[:16], "z", ring(8, 1)), lax.ppermute(left[16:], "z", ring(8, -1))], axis=0)
-    found.append(far)
-    return found + [lax.ppermute(block, "c", ring(2, 1)) for block in found]
+    right = left = pair = jnp.concatenate([own, other], axis=0)
+    found, swapped, waiting = [pair], [], [pair]
+    for step in range(4):
+        swaps = [lax.ppermute(block, "c", ring(2, 1)) for block in waiting]
+        if step < 3:
+            right = lax.ppermute(right, "z", ring(8, 1))
+            left = lax.ppermute(left, "z", ring(8, -1))
+            waiting = [right, left]
+            found += waiting
+        else:
+            far_r = lax.ppermute(right[:16], "z", ring(8, 1))
+            far_l = lax.ppermute(left[16:], "z", ring(8, -1))
+            found.append(jnp.concatenate([far_r, far_l], axis=0))
+        right, left, swaps, field = lax.optimization_barrier((right, left, swaps, field))
+        swapped += swaps
+    return found + swapped + [lax.ppermute(found[-1], "c", ring(2, 1))], field
 
 
 OFFSETS = (0, -1, 1, -2, 2, -3, 3, 4)
 
 
 def products_kernel(place_ref, *refs):
-    blocks, (field_ref, panel_ref, out_ref, gram, coupling) = refs[:16], refs[16:]
+    blocks, (field_ref, home_ref, out_ref, panel_ref, acc, sems) = refs[:16], refs[16:]
     xl, z, core = place_ref[0], place_ref[1], place_ref[2]
+    copies = []
     for other in range(2):
         for k, offset in enumerate(OFFSETS):
             for xo in range(2):
                 owner = (xl ^ xo) * 16 + ((z + offset) & 7) * 2 + (core ^ other)
                 rows = pl.ds(pl.multiple_of(owner * 16, 16), 16)
-                panel_ref[rows, :] = blocks[other * 8 + k][xo * 16 : xo * 16 + 16, :]
+                source = blocks[other * 8 + k].at[pl.ds(xo * 16, 16), :]
+                copies.append(pltpu.make_async_copy(source, panel_ref.at[rows, :], sems.at[len(copies)]))
+                copies[-1].start()
     mine = pl.ds(pl.multiple_of((xl * 2 + core) * 128, 128), 128)
-    gram[...] = jnp.zeros_like(gram)
-    coupling[...] = jnp.zeros_like(coupling)
+    acc[...] = jnp.zeros_like(acc)
+    for copy in copies:
+        copy.wait()
+    home = pltpu.make_async_copy(panel_ref, home_ref, sems.at[32])
+    home.start()
 
     def chunk(i, _):
         points = pl.ds(pl.multiple_of(i * 512, 512), 512)
-        wide = panel_ref[:, points]
-        gram[...] += dot_nt(panel_ref[mine, points], wide)
-        coupling[...] += dot_nn(wide, field_ref[points, :])
+        rows = jnp.concatenate([panel_ref[mine, points], field_ref[:, points]], axis=0)
+        acc[...] += dot_nt(rows, panel_ref[:, points])
         return 0
 
     lax.fori_loop(0, 4, chunk, 0)
     for s in range(8):
-        for j in range(4):
-            out_ref[s, j * 16 : j * 16 + 16, :] = gram[s * 16 : s * 16 + 16, j * 128 : j * 128 + 128]
-        out_ref[s, 64:128, :] = coupling[s * 64 : s * 64 + 64, :]
+        out_ref[s, 0:16, :] = acc[s * 16 : s * 16 + 16, :]
+        out_ref[s, 16:32, :] = acc[128 + s * 16 : 128 + s * 16 + 16, :]
+    home.wait()
 
 
 def products(place, blocks, field):
     return pl.pallas_call(
         products_kernel,
-        in_specs=[pl.BlockSpec(memory_space=pltpu.SMEM)] + [pl.BlockSpec(memory_space=pltpu.VMEM)] * 17,
-        out_shape=(jax.ShapeDtypeStruct((512, 2048), jnp.float32), jax.ShapeDtypeStruct((8, 128, 128), jnp.float32)),
-        scratch_shapes=[pltpu.VMEM((128, 512), jnp.float32), pltpu.VMEM((512, 128), jnp.float32)],
-        compiler_params=pltpu.CompilerParams(vmem_limit_bytes=28 * MIB),
+        in_specs=[pl.BlockSpec(memory_space=pltpu.SMEM)]
+        + [pl.BlockSpec(memory_space=pl.ANY)] * 16
+        + [pl.BlockSpec(memory_space=pltpu.VMEM)],
+        out_shape=(jax.ShapeDtypeStruct((512, 2048), jnp.float32), jax.ShapeDtypeStruct((8, 32, 512), jnp.float32)),
+        out_specs=(pl.BlockSpec(memory_space=pl.ANY), pl.BlockSpec(memory_space=pltpu.VMEM)),
+        scratch_shapes=[
+            pltpu.VMEM((512, 2048), jnp.float32),
+            pltpu.VMEM((256, 512), jnp.float32),
+            pltpu.SemaphoreType.DMA((33,)),
+        ],
+        compiler_params=pltpu.CompilerParams(vmem_limit_bytes=BIG * MIB),
     )(place, *blocks, field)
 
 
@@ -300,8 +304,7 @@
         piece = (xl ^ (flip // 2)) * 2 + (core ^ (flip % 2))
         for s in range(8):
             rows = pl.ds(pl.multiple_of(piece * 128 + s * 16, 16), 16)
-            for j in range(4):
-                work[rows, j * 128 : j * 128 + 128] = ref[s, j * 16 : j * 16 + 16, :] * (1.0 / POINTS)
+            work[rows, :] = ref[s] * (1.0 / POINTS)
     inv_ref[...] = jnp.zeros_like(inv_ref)
 
     def diagonal(k, _):
@@ -336,35 +339,39 @@
 
 
 def update_kernel(place_ref, inv_ref, sums_ref, panel_ref, field_ref, out_ref, coupling, mixer):
-    for s in range(8):
-        coupling[s * 64 : s * 64 + 64, :] = sums_ref[s, 64:128, :] * (1.0 / POINTS)
-    inverse = inv_ref[...]
-    middle = dot_nt(coupling[...].T, inverse)
-    mixer[...] = -dot_nn(middle, inverse)
-    own = place_ref[0] * 16 + place_ref[1] * 2 + place_ref[2]
-    mixer[0:16, :] = inv_ref[pl.ds(pl.multiple_of(own * 16, 16), 16), :]
-    keep = lax.broadcasted_iota(jnp.int32, (256, 128), 1) >= 16
-
-    def chunk(yl, _):
-        points = pl.ds(pl.multiple_of(yl * 256, 256), 256)
-        moved = dot_nn(mixer[...], panel_ref[:, points]).T
-        moved = moved + jnp.where(keep, field_ref[points, :], 0.0)
-        for xp in range(4):
-            for yh in range(2):
-                out_ref[xp, yh * 8 + yl] = moved[xp * 64 + yh * 32 : xp * 64 + yh * 32 + 32, :]
-        return 0
-
-    lax.fori_loop(0, 8, chunk, 0)
+    @pl.when(pl.program_id(0) == 0)
+    def _():
+        for s in range(8):
+            coupling[s * 16 : s * 16 + 16, :] = sums_ref[s, 16:32, :] * (1.0 / POINTS)
+        inverse = inv_ref[...]
+        mixer[...] = -dot_nn(dot_nt(coupling[...], inverse), inverse)
+        own = place_ref[0] * 16 + place_ref[1] * 2 + place_ref[2]
+        mixer[0:16, :] = inv_ref[pl.ds(pl.multiple_of(own * 16, 16), 16), :]
+
+    keep = lax.broadcasted_iota(jnp.int32, (128, 256), 0) >= 16
+    moved = (dot_nn(mixer[...], panel_ref[...]) + jnp.where(keep, field_ref[...], 0.0)).T
+    for xp in range(4):
+        for yh in range(2):
+            out_ref[xp, yh, 0] = moved[xp * 64 + yh * 32 : xp * 64 + yh * 32 + 32, :]
 
 
 def update(place, inverse, sums, panel, field):
-    return pl.pallas_call(
+    out = pl.pallas_call(
         update_kernel,
-        in_specs=[pl.BlockSpec(memory_space=pltpu.SMEM)] + [pl.BlockSpec(memory_space=pltpu.VMEM)] * 4,
-        out_shape=jax.ShapeDtypeStruct((4, 16, 32, 128), jnp.float32),
-        scratch_shapes=[pltpu.VMEM((PANEL, 128), jnp.float32), pltpu.VMEM((128, PANEL), jnp.float32)],
-        compiler_params=pltpu.CompilerParams(vmem_limit_bytes=28 * MIB),
+        grid=(8,),
+        in_specs=[
+            pl.BlockSpec(memory_space=pltpu.SMEM),
+            pl.BlockSpec((PANEL, PANEL), lambda i: (0, 0)),
+            pl.BlockSpec((8, 32, PANEL), lambda i: (0, 0, 0)),
+            pl.BlockSpec((PANEL, 256), lambda i: (0, i)),
+            pl.BlockSpec((128, 256), lambda i: (0, i)),
+        ],
+        out_specs=pl.BlockSpec((4, 2, 1, 32, 128), lambda i: (0, 0, i, 0, 0)),
+        out_shape=jax.ShapeDtypeStruct((4, 2, 8, 32, 128), jnp.float32),
+        scratch_shapes=[pltpu.VMEM((128, PANEL), jnp.float32)] * 2,
+        compiler_params=pltpu.CompilerParams(vmem_limit_bytes=16 * MIB),
     )(place, inverse, sums, panel, field)
+    return out.reshape(4, 16, 32, 128)
 
 
 def per_device(orbitals, potential):
@@ -372,11 +379,11 @@
     place = jnp.stack([xl, z, core]).astype(jnp.int32)
     received = lax.all_to_all(pack(orbitals, potential), SPACE, 0, 0, tiled=True)
     back = lax.all_to_all(chebyshev(received), SPACE, 0, 0, tiled=True)
-    field = unpack(back)
-    panel, terms = products(place, gather_panel(own_panel(back)), field)
+    blocks, field = gather_panel(turn(back, 1), turn(back, 8))
+    panel, terms = products(place, blocks, field)
     mine = jnp.sum(lax.all_to_all(terms, SPACE, 0, 0, tiled=True), axis=0)
-    sums = lax.all_to_all(jnp.broadcast_to(mine, (8, 128, 128)), SPACE, 0, 0, tiled=True)
-    piece = sums[:, :64]
+    sums = lax.all_to_all(jnp.broadcast_to(mine, (8, 32, PANEL)), SPACE, 0, 0, tiled=True)
+    piece = sums[:, :16]
     by_core = lax.ppermute(piece, "c", ring(2, 1))
     by_x = lax.ppermute(piece, "xl", ring(2, 1))
     by_both = lax.ppermute(by_x, "c", ring(2, 1))

time: 189 us -> 188 us (level)
  starting transfers between devices: 37 us -> 33.4 us
  waiting for transfers between devices: 22.8 us -> 25.9 us
  local copies, waits for them, and re-layouts: 6.16 us -> 3.32 us
    ppermute x3, waiting for transfers between devices: 0.01 us -> 6.23 us  [gather_panel(): left = lax.ppermute(left, 'z', ring(8, -1))]
    ppermute x10, starting transfers between devices: 18.4 us -> 14.2 us  [the longest x7 8.38 us: gather_panel(): swaps = [lax.ppermute(block, 'c', ring(2, 1)) for block in waiting]]
    unnamed x25 -> x37, local copies, waits for them, and re-layouts: 6.07 us -> 3.22 us
    ppermute x3, waiting for transfers between devices: 14 us -> 11.4 us  [gather_panel(): right = lax.ppermute(right, 'z', ring(8, 1))]
    ppermute x3, starting transfers between devices: 9.81 us -> 12 us  [gather_panel(): left = lax.ppermute(left, 'z', ring(8, -1))]
    pallas_call x4, Pallas kernels: 10.7 us -> 12.9 us  [the longest x1 7.71 us: update(): pl.pallas_call(update_kernel, grid=(8,), in_specs=[pl.BlockSpec(memory_sp...]
  transfers between devices with their start and end apart: 20 -> 20, of which waited for: 7 -> 11; matrix products, arithmetic and copies ran while one was open for 0% -> 0% of each run, Pallas kernels for 1% -> 0%
where the time goes in v4:
time: 188 us
  blocking collectives  69.2 us (37%)
  Pallas kernels  55.2 us (29%)
  starting transfers between devices  33.4 us (18%)
  waiting for transfers between devices  25.9 us (14%)
  local copies, waits for them, and re-layouts  3.32 us (2%)
    all_to_all x1, blocking collectives, per_device(): lax.all_to_all(pack(orbitals, potential), SPACE, 0, 0, tiled=True)  24.2 us
    pallas_call x1, Pallas kernels, inverse_factor(): pl.pallas_call(inverse_kernel, in_specs=[pl.BlockSpec(memory_space=pltpu....  22.3 us
    all_to_all x1, blocking collectives, per_device(): back = lax.all_to_all(chebyshev(received), SPACE, 0, 0, tiled=True)  17.8 us
    all_to_all x1, blocking collectives, per_device(): mine = jnp.sum(lax.all_to_all(terms, SPACE, 0, 0, tiled=True), axis=0)  14.7 us
    all_to_all x1, blocking collectives, per_device(): lax.all_to_all(jnp.broadcast_to(mine, (8, 32, PANEL)), SPACE, 0, 0, tiled...  12.5 us
    ppermute x3, starting transfers between devices, gather_panel(): left = lax.ppermute(left, 'z', ring(8, -1))  12 us
    ppermute x3, waiting for transfers between devices, gather_panel(): right = lax.ppermute(right, 'z', ring(8, 1))  11.4 us
    pallas_call x1, Pallas kernels, chebyshev(): pl.pallas_call(filter_kernel, out_shape=jax.ShapeDtypeStruct((64, 32, 128...  11.3 us
  transfers between devices with their start and end apart: 20, of which 11 were waited for; matrix products, arithmetic and copies ran while one was open for 0% of the time, Pallas kernels for 0%

profile of v4, /device:TPU:1, one launch (start us, length us, event | category | flops | bytes accessed | tf_op | source)
XLA Modules:
  0.0 187.9 jit_solution(13776736649900194781)
XLA Ops:
  0.0 4.2 %shard_map.28 = f32[8,272,128]{2,1,0:T(8,128)} custom-call(f32[4,16,32,128]{3,2,1,0:T(8,128)} %orb_ref.1, f32[4,16,32]{2,1,0:T(8,128)} %pot_ref.1), custom_call_target="tpu_custom_call" | custom-call | tf_op jit(solution)/shard_map/pallas_call | solution.py:62
  4.2 24.2 %all_to_all.20.in_ref = f32[8,272,128]{2,1,0:T(8,128)S(1)} all-to-all(f32[8,272,128]{2,1,0:T(8,128)} %shard_map.28), channel_id=1, replica_groups=mesh['y'=4,'xh'=2,'xl'=2,'z'=8,'c'=2] {'y','xh'}, dimensions={0} | all-to-all | bytes 2228224 | tf_op jit(solution)/shard_map/all_to_all | solution.py:380
  28.4 11.3 %shard_map.29 = f32[64,32,128]{2,1,0:T(8,128)S(1)} custom-call(f32[8,272,128]{2,1,0:T(8,128)S(1)} %all_to_all.20.in_ref), custom_call_target="tpu_custom_call" | custom-call | tf_op jit(solution)/shard_map/pallas_call | solution.py:143
  39.7 17.8 %all_to_all.21.in_ref = f32[8,256,128]{2,1,0:T(8,128)S(1)} all-to-all(f32[8,256,128]{2,1,0:T(8,128)S(1)} %bitcast.5), channel_id=1, replica_groups=mesh['y'=4,'xh'=2,'xl'=2,'z'=8,'c'=2] {'y','xh'}, dimensions={0} | all-to-all | bytes 2097152 | tf_op jit(solution)/shard_map/all_to_all | solution.py:381
  58.0 3.5 %collective-permute-done = f32[16,2048]{1,0:T(8,128)S(1)} collective-permute-done((f32[16,2048]{1,0:T(8,128)S(1)}, f32[16,2048]{1,0:T(8,128)S(1)}, u32[]{:S(2)}, u32[]{:S(2)}) %collective-permute-start) | collective-permute-done | bytes 131104 | tf_op jit(solution)/shard_map/ppermute | solution.py:175
  61.6 4.4 %collective-permute-start.3 = (f32[32,2048]{1,0:T(8,128)S(1)}, f32[32,2048]{1,0:T(8,128)S(1)}, u32[]{:S(2)}, u32[]{:S(2)}) collective-permute-start(f32[32,2048]{1,0:T(8,128)S(1)} %pad_maximum_fusion.refs_0_), channel_id=1, source_target_pairs={{0,1},{1,0},{2,3},{3,2},{4,5},{5,4},{6,7},{7,6},{8,9},{9,8},{10,11... | collective-permute-start | bytes 786440 | tf_op jit(solution)/shard_map/ppermute | solution.py:179
  66.0 5.6 %collective-permute-start.2 = (f32[32,2048]{1,0:T(8,128)S(1)}, f32[32,2048]{1,0:T(8,128)S(1)}, u32[]{:S(2)}, u32[]{:S(2)}) collective-permute-start(f32[32,2048]{1,0:T(8,128)S(1)} %pad_maximum_fusion.refs_0_), channel_id=1, source_target_pairs={{0,14},{2,0},{4,2},{6,4},{8,6},{10,8},{12,10},{14,12},{1,15},{3,1}... | collective-permute-start | bytes 786440 | tf_op jit(solution)/shard_map/ppermute | solution.py:182
  73.4 3.8 %collective-permute-done.2.refs_2_ = f32[32,2048]{1,0:T(8,128)S(1)} collective-permute-done((f32[32,2048]{1,0:T(8,128)S(1)}, f32[32,2048]{1,0:T(8,128)S(1)}, u32[]{:S(2)}, u32[]{:S(2)}) %collective-permute-start.2) | collective-permute-done | bytes 262176 | tf_op jit(solution)/shard_map/ppermute | solution.py:182
  77.2 3.1 %collective-permute-done.1.refs_1_ = f32[32,2048]{1,0:T(8,128)S(1)} collective-permute-done((f32[32,2048]{1,0:T(8,128)S(1)}, f32[32,2048]{1,0:T(8,128)S(1)}, u32[]{:S(2)}, u32[]{:S(2)}) %collective-permute-start.1) | collective-permute-done | bytes 262176 | tf_op jit(solution)/shard_map/ppermute | solution.py:181
  81.5 3.0 %collective-permute-start.5 = (f32[32,2048]{1,0:T(8,128)S(1)}, f32[32,2048]{1,0:T(8,128)S(1)}, u32[]{:S(2)}, u32[]{:S(2)}) collective-permute-start(f32[32,2048]{1,0:T(8,128)S(1)} %collective-permute-done.2.refs_2_), channel_id=1, source_target_pairs={{0,14},{2,0},{4,2},{6,4},{8,6},{10,8},{12,10},{14,12},{1,15},{3,1}... | collective-permute-start | bytes 786440 | tf_op jit(solution)/shard_map/ppermute | solution.py:182
  84.8 3.4 %collective-permute-done.4.refs_3_ = f32[32,2048]{1,0:T(8,128)S(1)} collective-permute-done((f32[32,2048]{1,0:T(8,128)S(1)}, f32[32,2048]{1,0:T(8,128)S(1)}, u32[]{:S(2)}, u32[]{:S(2)}) %collective-permute-start.4) | collective-permute-done | bytes 262176 | tf_op jit(solution)/shard_map/ppermute | solution.py:181
  91.2 3.5 %collective-permute-start.9 = (f32[32,2048]{1,0:T(8,128)S(1)}, f32[32,2048]{1,0:T(8,128)S(1)}, u32[]{:S(2)}, u32[]{:S(2)}) collective-permute-start(f32[32,2048]{1,0:T(8,128)S(1)} %collective-permute-done.5.refs_4_), channel_id=1, source_target_pairs={{0,14},{2,0},{4,2},{6,4},{8,6},{10,8},{12,10},{14,12},{1,15},{3,1}... | collective-permute-start | bytes 786440 | tf_op jit(solution)/shard_map/ppermute | solution.py:182
  94.7 4.9 %collective-permute-done.8.refs_5_ = f32[32,2048]{1,0:T(8,128)S(1)} collective-permute-done((f32[32,2048]{1,0:T(8,128)S(1)}, f32[32,2048]{1,0:T(8,128)S(1)}, u32[]{:S(2)}, u32[]{:S(2)}) %collective-permute-start.8) | collective-permute-done | bytes 262176 | tf_op jit(solution)/shard_map/ppermute | solution.py:181
  100.6 3.0 %collective-permute-start.13 = (f32[16,2048]{1,0:T(8,128)S(1)}, f32[16,2048]{1,0:T(8,128)S(1)}, u32[]{:S(2)}, u32[]{:S(2)}) collective-permute-start(f32[16,2048]{1,0:T(8,128)S(1)} %slice.10), channel_id=1, source_target_pairs={{0,14},{2,0},{4,2},{6,4},{8,6},{10,8},{12,10},{14,12},{1,15},{3,1}... | collective-permute-start | bytes 393224 | tf_op jit(solution)/shard_map/ppermute | solution.py:187
  105.9 2.2 %collective-permute-start.16 = (f32[32,2048]{1,0:T(8,128)S(1)}, f32[32,2048]{1,0:T(8,128)}, u32[]{:S(2)}, u32[]{:S(2)}) collective-permute-start(f32[32,2048]{1,0:T(8,128)S(1)} %constant_dynamic-update-slice_fusion.refs_7_), channel_id=1, source_target_pairs={{0,1},{1,0},{2,3},{3,2},{4,5},{5,4},{6,7},{7,6},{8,9},{9,8},{10,11... | collective-permute-start | bytes 786440 | tf_op jit(solution)/shard_map/ppermute | solution.py:191
  109.5 8.8 %shard_map.32 = (f32[512,2048]{1,0:T(8,128)}, f32[8,32,512]{2,1,0:T(8,128)}) custom-call(s32[3]{0:T(128)} %pad_add_fusion.place_ref, f32[32,2048]{1,0:T(8,128)} %copy-done.4, f32[32,2048]{1,0:T(8,128)} %copy-done.10, f32[32,2048]{1,0:T(8,128)} %copy-done.9, f32[32,2048]{1,0:T(8,128)} %copy-done.11, f32[32,2048]{1,0:T(8,128)} %copy-done.13, ...), custom_call_target="tpu_custom_call" | custom-call | tf_op jit(solution)/shard_map/pallas_call | solution.py:230
  118.3 14.7 %all_to_all.22 = f32[8,32,512]{2,1,0:T(8,128)S(1)} all-to-all(f32[8,32,512]{2,1,0:T(8,128)} %get-tuple-element.41), channel_id=1, replica_groups=mesh['y'=4,'xh'=2,'xl'=2,'z'=8,'c'=2] {'y','xh'}, dimensions={0} | all-to-all | bytes 1048576 | tf_op jit(solution)/shard_map/all_to_all | solution.py:384
  133.1 12.5 %all_to_all.23.sums_ref = f32[8,32,512]{2,1,0:T(8,128)S(1)} all-to-all(f32[8,32,512]{2,1,0:T(8,128)S(1)} %broadcast_in_dim.3), channel_id=1, replica_groups=mesh['y'=4,'xh'=2,'xl'=2,'z'=8,'c'=2] {'y','xh'}, dimensions={0} | all-to-all | bytes 1048576 | tf_op jit(solution)/shard_map/all_to_all | solution.py:385
  146.0 2.8 %collective-permute-start.18 = (f32[8,16,512]{2,1,0:T(8,128)S(1)}, f32[8,16,512]{2,1,0:T(8,128)S(1)}, u32[]{:S(2)}, u32[]{:S(2)}) collective-permute-start(f32[8,16,512]{2,1,0:T(8,128)S(1)} %slice.12.own_ref), channel_id=1, source_target_pairs={{0,1},{1,0},{2,3},{3,2},{4,5},{5,4},{6,7},{7,6},{8,9},{9,8},{10,11... | collective-permute-start | bytes 786440 | tf_op jit(solution)/shard_map/ppermute | solution.py:387
  148.8 2.2 %collective-permute-done.17.by_x_ref = f32[8,16,512]{2,1,0:T(8,128)S(1)} collective-permute-done((f32[8,16,512]{2,1,0:T(8,128)S(1)}, f32[8,16,512]{2,1,0:T(8,128)S(1)}, u32[]{:S(2)}, u32[]{:S(2)}) %collective-permute-start.17) | collective-permute-done | bytes 262176 | tf_op jit(solution)/shard_map/ppermute | solution.py:388
  150.9 3.6 %collective-permute-start.19 = (f32[8,16,512]{2,1,0:T(8,128)S(1)}, f32[8,16,512]{2,1,0:T(8,128)S(1)}, u32[]{:S(2)}, u32[]{:S(2)}) collective-permute-start(f32[8,16,512]{2,1,0:T(8,128)S(1)} %collective-permute-done.17.by_x_ref), channel_id=1, source_target_pairs={{0,1},{1,0},{2,3},{3,2},{4,5},{5,4},{6,7},{7,6},{8,9},{9,8},{10,11... | collective-permute-start | bytes 786440 | tf_op jit(solution)/shard_map/ppermute | solution.py:389
  155.7 22.3 %shard_map.33.inv_ref = f32[512,512]{1,0:T(8,128)S(1)} custom-call(s32[3]{0:T(128)S(1)} %copy-done.3, f32[8,16,512]{2,1,0:T(8,128)S(1)} %slice.12.own_ref, f32[8,16,512]{2,1,0:T(8,128)S(1)} %collective-permute-done.17.by_x_ref, f32[8,16,512]{2,1,0:T(8,128)S(1)} %collective-permute-done.18.by_core_ref, f32[8,16,512]{2,1,0:T(8,128)S(1)} %collective-permute-done.19.by_both_ref), custom_call_target="tpu_custom_call" | custom-call | tf_op jit(solution)/shard_map/pallas_call | solution.py:332
  178.0 2.2 %copy-done.2 = f32[512,2048]{1,0:T(8,128)S(1)} copy-done((f32[512,2048]{1,0:T(8,128)S(1)}, f32[512,2048]{1,0:T(8,128)}, u32[]{:S(2)}) %copy-start.2) | copy-done | bytes 4194328
  180.2 7.7 %shard_map.34 = f32[4,2,8,32,128]{4,3,2,1,0:T(8,128)} custom-call(s32[3]{0:T(128)S(1)} %copy-done.3, f32[512,512]{1,0:T(8,128)S(1)} %shard_map.33.inv_ref, f32[8,32,512]{2,1,0:T(8,128)S(1)} %all_to_all.23.sums_ref, f32[512,2048]{1,0:T(8,128)S(1)} %copy-done.2, f32[128,2048]{1,0:T(8,128)S(1)} %copy-done.1), custom_call_target="tpu_custom_call" | custom-call | tf_op jit(solution)/shard_map/pallas_call | solution.py:359
  (72 shorter events, 13.1 us)
Async XLA Ops:
  57.6 3.9 %collective-permute-start = (f32[16,2048]{1,0:T(8,128)S(1)}, f32[16,2048]{1,0:T(8,128)S(1)}, u32[]{:S(2)}, u32[]{:S(2)}) collective-permute-start(f32[16,2048]{1,0:T(8,128)S(1)} %shard_map.30), channel_id=1, source_target_pairs={{0,16},{16,0},{1,17},{17,1},{2,18},{18,2},{3,19},{19,3},{4,20},{20... | collective-permute-start | bytes 393224 | tf_op jit(solution)/shard_map/ppermute | solution.py:175
  61.6 38.4 %copy-start.4 = (f32[32,2048]{1,0:T(8,128)}, f32[32,2048]{1,0:T(8,128)S(1)}, u32[]{:S(2)}) copy-start(f32[32,2048]{1,0:T(8,128)S(1)} %pad_maximum_fusion.refs_0_) | copy-start | bytes 786436
  61.6 11.8 %collective-permute-start.3 = (f32[32,2048]{1,0:T(8,128)S(1)}, f32[32,2048]{1,0:T(8,128)S(1)}, u32[]{:S(2)}, u32[]{:S(2)}) collective-permute-start(f32[32,2048]{1,0:T(8,128)S(1)} %pad_maximum_fusion.refs_0_), channel_id=1, source_target_pairs={{0,1},{1,0},{2,3},{3,2},{4,5},{5,4},{6,7},{7,6},{8,9},{9,8},{10,11... | collective-permute-start | bytes 786440 | tf_op jit(solution)/shard_map/ppermute | solution.py:179
  66.0 11.2 %collective-permute-start.2 = (f32[32,2048]{1,0:T(8,128)S(1)}, f32[32,2048]{1,0:T(8,128)S(1)}, u32[]{:S(2)}, u32[]{:S(2)}) collective-permute-start(f32[32,2048]{1,0:T(8,128)S(1)} %pad_maximum_fusion.refs_0_), channel_id=1, source_target_pairs={{0,14},{2,0},{4,2},{6,4},{8,6},{10,8},{12,10},{14,12},{1,15},{3,1}... | collective-permute-start | bytes 786440 | tf_op jit(solution)/shard_map/ppermute | solution.py:182
  71.6 8.7 %collective-permute-start.1 = (f32[32,2048]{1,0:T(8,128)S(1)}, f32[32,2048]{1,0:T(8,128)S(1)}, u32[]{:S(2)}, u32[]{:S(2)}) collective-permute-start(f32[32,2048]{1,0:T(8,128)S(1)} %pad_maximum_fusion.refs_0_), channel_id=1, source_target_pairs={{0,2},{2,4},{4,6},{6,8},{8,10},{10,12},{12,14},{14,0},{1,3},{3,5},... | collective-permute-start | bytes 786440 | tf_op jit(solution)/shard_map/ppermute | solution.py:181
  73.4 36.0 %copy-start.8 = (f32[32,2048]{1,0:T(8,128)}, f32[32,2048]{1,0:T(8,128)S(1)}, u32[]{:S(2)}) copy-start(f32[32,2048]{1,0:T(8,128)S(1)} %collective-permute-done.3.refs_8_) | copy-start | bytes 786436
  77.2 32.1 %copy-start.9 = (f32[32,2048]{1,0:T(8,128)}, f32[32,2048]{1,0:T(8,128)S(1)}, u32[]{:S(2)}) copy-start(f32[32,2048]{1,0:T(8,128)S(1)} %collective-permute-done.2.refs_2_) | copy-start | bytes 786436
  80.3 7.8 %collective-permute-start.4 = (f32[32,2048]{1,0:T(8,128)S(1)}, f32[32,2048]{1,0:T(8,128)S(1)}, u32[]{:S(2)}, u32[]{:S(2)}) collective-permute-start(f32[32,2048]{1,0:T(8,128)S(1)} %collective-permute-done.1.refs_1_), channel_id=1, source_target_pairs={{0,2},{2,4},{4,6},{6,8},{8,10},{10,12},{12,14},{14,0},{1,3},{3,5},... | collective-permute-start | bytes 786440 | tf_op jit(solution)/shard_map/ppermute | solution.py:181
  80.3 4.4 %collective-permute-start.7 = (f32[32,2048]{1,0:T(8,128)S(1)}, f32[32,2048]{1,0:T(8,128)S(1)}, u32[]{:S(2)}, u32[]{:S(2)}) collective-permute-start(f32[32,2048]{1,0:T(8,128)S(1)} %collective-permute-done.2.refs_2_), channel_id=1, source_target_pairs={{0,1},{1,0},{2,3},{3,2},{4,5},{5,4},{6,7},{7,6},{8,9},{9,8},{10,11... | collective-permute-start | bytes 786440 | tf_op jit(solution)/shard_map/ppermute | solution.py:179
  81.5 8.7 %collective-permute-start.5 = (f32[32,2048]{1,0:T(8,128)S(1)}, f32[32,2048]{1,0:T(8,128)S(1)}, u32[]{:S(2)}, u32[]{:S(2)}) collective-permute-start(f32[32,2048]{1,0:T(8,128)S(1)} %collective-permute-done.2.refs_2_), channel_id=1, source_target_pairs={{0,14},{2,0},{4,2},{6,4},{8,6},{10,8},{12,10},{14,12},{1,15},{3,1}... | collective-permute-start | bytes 786440 | tf_op jit(solution)/shard_map/ppermute | solution.py:182
  84.5 5.7 %collective-permute-start.6 = (f32[32,2048]{1,0:T(8,128)S(1)}, f32[32,2048]{1,0:T(8,128)S(1)}, u32[]{:S(2)}, u32[]{:S(2)}) collective-permute-start(f32[32,2048]{1,0:T(8,128)S(1)} %collective-permute-done.1.refs_1_), channel_id=1, source_target_pairs={{0,1},{1,0},{2,3},{3,2},{4,5},{5,4},{6,7},{7,6},{8,9},{9,8},{10,11... | collective-permute-start | bytes 786440 | tf_op jit(solution)/shard_map/ppermute | solution.py:179
  90.2 9.4 %collective-permute-start.8 = (f32[32,2048]{1,0:T(8,128)S(1)}, f32[32,2048]{1,0:T(8,128)S(1)}, u32[]{:S(2)}, u32[]{:S(2)}) collective-permute-start(f32[32,2048]{1,0:T(8,128)S(1)} %collective-permute-done.4.refs_3_), channel_id=1, source_target_pairs={{0,2},{2,4},{4,6},{6,8},{8,10},{10,12},{12,14},{14,0},{1,3},{3,5},... | collective-permute-start | bytes 786440 | tf_op jit(solution)/shard_map/ppermute | solution.py:181
  90.2 4.5 %collective-permute-start.10 = (f32[32,2048]{1,0:T(8,128)S(1)}, f32[32,2048]{1,0:T(8,128)S(1)}, u32[]{:S(2)}, u32[]{:S(2)}) collective-permute-start(f32[32,2048]{1,0:T(8,128)S(1)} %collective-permute-done.4.refs_3_), channel_id=1, source_target_pairs={{0,1},{1,0},{2,3},{3,2},{4,5},{5,4},{6,7},{7,6},{8,9},{9,8},{10,11... | collective-permute-start | bytes 786440 | tf_op jit(solution)/shard_map/ppermute | solution.py:179
  91.1 3.6 %collective-permute-start.11 = (f32[32,2048]{1,0:T(8,128)S(1)}, f32[32,2048]{1,0:T(8,128)S(1)}, u32[]{:S(2)}, u32[]{:S(2)}) collective-permute-start(f32[32,2048]{1,0:T(8,128)S(1)} %collective-permute-done.5.refs_4_), channel_id=1, source_target_pairs={{0,1},{1,0},{2,3},{3,2},{4,5},{5,4},{6,7},{7,6},{8,9},{9,8},{10,11... | collective-permute-start | bytes 786440 | tf_op jit(solution)/shard_map/ppermute | solution.py:179
  91.2 8.8 %collective-permute-start.9 = (f32[32,2048]{1,0:T(8,128)S(1)}, f32[32,2048]{1,0:T(8,128)S(1)}, u32[]{:S(2)}, u32[]{:S(2)}) collective-permute-start(f32[32,2048]{1,0:T(8,128)S(1)} %collective-permute-done.5.refs_4_), channel_id=1, source_target_pairs={{0,14},{2,0},{4,2},{6,4},{8,6},{10,8},{12,10},{14,12},{1,15},{3,1}... | collective-permute-start | bytes 786440 | tf_op jit(solution)/shard_map/ppermute | solution.py:182
  100.0 5.8 %collective-permute-start.12 = (f32[16,2048]{1,0:T(8,128)S(1)}, f32[16,2048]{1,0:T(8,128)S(1)}, u32[]{:S(2)}, u32[]{:S(2)}) collective-permute-start(f32[16,2048]{1,0:T(8,128)S(1)} %slice.9), channel_id=1, source_target_pairs={{0,2},{2,4},{4,6},{6,8},{8,10},{10,12},{12,14},{14,0},{1,3},{3,5},... | collective-permute-start | bytes 393224 | tf_op jit(solution)/shard_map/ppermute | solution.py:186
  100.6 5.2 %collective-permute-start.13 = (f32[16,2048]{1,0:T(8,128)S(1)}, f32[16,2048]{1,0:T(8,128)S(1)}, u32[]{:S(2)}, u32[]{:S(2)}) collective-permute-start(f32[16,2048]{1,0:T(8,128)S(1)} %slice.10), channel_id=1, source_target_pairs={{0,14},{2,0},{4,2},{6,4},{8,6},{10,8},{12,10},{14,12},{1,15},{3,1}... | collective-permute-start | bytes 393224 | tf_op jit(solution)/shard_map/ppermute | solution.py:187
  103.6 5.1 %collective-permute-start.14 = (f32[32,2048]{1,0:T(8,128)S(1)}, f32[32,2048]{1,0:T(8,128)S(1)}, u32[]{:S(2)}, u32[]{:S(2)}) collective-permute-start(f32[32,2048]{1,0:T(8,128)S(1)} %collective-permute-done.8.refs_5_), channel_id=1, source_target_pairs={{0,1},{1,0},{2,3},{3,2},{4,5},{5,4},{6,7},{7,6},{8,9},{9,8},{10,11... | collective-permute-start | bytes 786440 | tf_op jit(solution)/shard_map/ppermute | solution.py:179
  105.1 3.6 %collective-permute-start.15 = (f32[32,2048]{1,0:T(8,128)S(1)}, f32[32,2048]{1,0:T(8,128)}, u32[]{:S(2)}, u32[]{:S(2)}) collective-permute-start(f32[32,2048]{1,0:T(8,128)S(1)} %collective-permute-done.9.refs_6_), channel_id=1, source_target_pairs={{0,1},{1,0},{2,3},{3,2},{4,5},{5,4},{6,7},{7,6},{8,9},{9,8},{10,11... | collective-permute-start | bytes 786440 | tf_op jit(solution)/shard_map/ppermute | solution.py:179
  105.9 3.5 %collective-permute-start.16 = (f32[32,2048]{1,0:T(8,128)S(1)}, f32[32,2048]{1,0:T(8,128)}, u32[]{:S(2)}, u32[]{:S(2)}) collective-permute-start(f32[32,2048]{1,0:T(8,128)S(1)} %constant_dynamic-update-slice_fusion.refs_7_), channel_id=1, source_target_pairs={{0,1},{1,0},{2,3},{3,2},{4,5},{5,4},{6,7},{7,6},{8,9},{9,8},{10,11... | collective-permute-start | bytes 786440 | tf_op jit(solution)/shard_map/ppermute | solution.py:191
  145.6 32.4 %copy-start.1 = (f32[128,2048]{1,0:T(8,128)S(1)}, f32[128,2048]{1,0:T(8,128)}, u32[]{:S(2)}) copy-start(f32[128,2048]{1,0:T(8,128)} %copy-done) | copy-start | bytes 3145732
  145.6 5.3 %collective-permute-start.17 = (f32[8,16,512]{2,1,0:T(8,128)S(1)}, f32[8,16,512]{2,1,0:T(8,128)S(1)}, u32[]{:S(2)}, u32[]{:S(2)}) collective-permute-start(f32[8,16,512]{2,1,0:T(8,128)S(1)} %slice.12.own_ref), channel_id=1, source_target_pairs={{0,16},{16,0},{1,17},{17,1},{2,18},{18,2},{3,19},{19,3},{4,20},{20... | collective-permute-start | bytes 786440 | tf_op jit(solution)/shard_map/ppermute | solution.py:388
  146.0 8.5 %collective-permute-start.18 = (f32[8,16,512]{2,1,0:T(8,128)S(1)}, f32[8,16,512]{2,1,0:T(8,128)S(1)}, u32[]{:S(2)}, u32[]{:S(2)}) collective-permute-start(f32[8,16,512]{2,1,0:T(8,128)S(1)} %slice.12.own_ref), channel_id=1, source_target_pairs={{0,1},{1,0},{2,3},{3,2},{4,5},{5,4},{6,7},{7,6},{8,9},{9,8},{10,11... | collective-permute-start | bytes 786440 | tf_op jit(solution)/shard_map/ppermute | solution.py:387
  150.9 4.8 %collective-permute-start.19 = (f32[8,16,512]{2,1,0:T(8,128)S(1)}, f32[8,16,512]{2,1,0:T(8,128)S(1)}, u32[]{:S(2)}, u32[]{:S(2)}) collective-permute-start(f32[8,16,512]{2,1,0:T(8,128)S(1)} %collective-permute-done.17.by_x_ref), channel_id=1, source_target_pairs={{0,1},{1,0},{2,3},{3,2},{4,5},{5,4},{6,7},{7,6},{8,9},{9,8},{10,11... | collective-permute-start | bytes 786440 | tf_op jit(solution)/shard_map/ppermute | solution.py:389
  (14 other events, 192.4 us)

commit v5 on v4

--- a/solution.py
+++ b/solution.py
@@ -172,45 +172,62 @@
 
 
 def gather_panel(own, field):
-    other = lax.ppermute(own, "xl", ring(2, 1))
-    right = left = pair = jnp.concatenate([own, other], axis=0)
-    found, swapped, waiting = [pair], [], [pair]
-    for step in range(4):
-        swaps = [lax.ppermute(block, "c", ring(2, 1)) for block in waiting]
-        if step < 3:
-            right = lax.ppermute(right, "z", ring(8, 1))
-            left = lax.ppermute(left, "z", ring(8, -1))
-            waiting = [right, left]
-            found += waiting
-        else:
-            far_r = lax.ppermute(right[:16], "z", ring(8, 1))
-            far_l = lax.ppermute(left[16:], "z", ring(8, -1))
-            found.append(jnp.concatenate([far_r, far_l], axis=0))
-        right, left, swaps, field = lax.optimization_barrier((right, left, swaps, field))
-        swapped += swaps
-    return found + swapped + [lax.ppermute(found[-1], "c", ring(2, 1))], field
-
-
-OFFSETS = (0, -1, 1, -2, 2, -3, 3, 4)
+    def step(right, left, swaps, more=()):
+        moved = (
+            lax.ppermute(right, "z", ring(8, 1)),
+            lax.ppermute(left, "z", ring(8, -1)),
+            [lax.ppermute(block, "c", ring(2, 1)) for block in swaps],
+            *(lax.ppermute(block, "xl", ring(2, 1)) for block in more),
+        )
+        return lax.optimization_barrier(moved)
+
+    right1, left1, swap0, other = step(own, own, [own], [own])
+    both_r = jnp.concatenate([right1, other], axis=0)
+    both_l = jnp.concatenate([other, left1], axis=0)
+    right2, left2, swap1 = step(both_r, both_l, [both_r, left1])
+    right2, left2, field = lax.optimization_barrier((right2, left2, field))
+    right3, left3, swap2 = step(right2, left2, [right2, left2])
+    right4, left4, swap3 = step(right3[8:], left3[:24], [right3, left3])
+    right5, left5, swap4 = step(right4[16:], left4[:8], [right4, left4])
+    last = jnp.concatenate([right5, left5], axis=0)
+    swap5 = [lax.ppermute(last, "c", ring(2, 1))]
+    here = [own, both_r, left1, right2, left2, right3, left3, right4, left4, last]
+    return here + swap0 + swap1 + swap2 + swap3 + swap4 + swap5, field
+
+
+PARTS = (
+    ((0, 16, 0, 0, 0),),
+    ((0, 16, 0, -1, 0), (16, 16, 1, 0, 0)),
+    ((0, 16, 0, 1, 0),),
+    ((0, 16, 0, -2, 0), (16, 16, 1, -1, 0)),
+    ((0, 16, 1, 1, 0), (16, 16, 0, 2, 0)),
+    ((0, 16, 0, -3, 0), (16, 16, 1, -2, 0)),
+    ((0, 16, 1, 2, 0), (16, 16, 0, 3, 0)),
+    ((0, 8, 0, 4, 8), (8, 16, 1, -3, 0)),
+    ((0, 16, 1, 3, 0), (16, 8, 0, 4, 0)),
+    ((0, 8, 1, 4, 8), (8, 8, 1, 4, 0)),
+)
+BLOCKS = 2 * len(PARTS)
+COPIES = 2 * sum(len(parts) for parts in PARTS)
 
 
 def products_kernel(place_ref, *refs):
-    blocks, (field_ref, home_ref, out_ref, panel_ref, acc, sems) = refs[:16], refs[16:]
+    blocks, (field_ref, home_ref, out_ref, panel_ref, acc, sems) = refs[:BLOCKS], refs[BLOCKS:]
     xl, z, core = place_ref[0], place_ref[1], place_ref[2]
     copies = []
-    for other in range(2):
-        for k, offset in enumerate(OFFSETS):
-            for xo in range(2):
-                owner = (xl ^ xo) * 16 + ((z + offset) & 7) * 2 + (core ^ other)
-                rows = pl.ds(pl.multiple_of(owner * 16, 16), 16)
-                source = blocks[other * 8 + k].at[pl.ds(xo * 16, 16), :]
+    for flip in range(2):
+        for k, parts in enumerate(PARTS):
+            for first, count, xo, offset, into in parts:
+                owner = (xl ^ xo) * 16 + ((z + offset) & 7) * 2 + (core ^ flip)
+                rows = pl.ds(pl.multiple_of(owner * 16 + into, 8), count)
+                source = blocks[flip * len(PARTS) + k].at[pl.ds(first, count), :]
                 copies.append(pltpu.make_async_copy(source, panel_ref.at[rows, :], sems.at[len(copies)]))
                 copies[-1].start()
     mine = pl.ds(pl.multiple_of((xl * 2 + core) * 128, 128), 128)
     acc[...] = jnp.zeros_like(acc)
     for copy in copies:
         copy.wait()
-    home = pltpu.make_async_copy(panel_ref, home_ref, sems.at[32])
+    home = pltpu.make_async_copy(panel_ref, home_ref, sems.at[COPIES])
     home.start()
 
     def chunk(i, _):
@@ -230,14 +247,14 @@
     return pl.pallas_call(
         products_kernel,
         in_specs=[pl.BlockSpec(memory_space=pltpu.SMEM)]
-        + [pl.BlockSpec(memory_space=pl.ANY)] * 16
+        + [pl.BlockSpec(memory_space=pl.ANY)] * BLOCKS
         + [pl.BlockSpec(memory_space=pltpu.VMEM)],
         out_shape=(jax.ShapeDtypeStruct((512, 2048), jnp.float32), jax.ShapeDtypeStruct((8, 32, 512), jnp.float32)),
         out_specs=(pl.BlockSpec(memory_space=pl.ANY), pl.BlockSpec(memory_space=pltpu.VMEM)),
         scratch_shapes=[
             pltpu.VMEM((512, 2048), jnp.float32),
             pltpu.VMEM((256, 512), jnp.float32),
-            pltpu.SemaphoreType.DMA((33,)),
+            pltpu.SemaphoreType.DMA((COPIES + 1,)),
         ],
         compiler_params=pltpu.CompilerParams(vmem_limit_bytes=BIG * MIB),
     )(place, *blocks, field)
@@ -298,9 +315,8 @@
     return jnp.concatenate(out, axis=0)
 
 
-def inverse_kernel(place_ref, own_ref, by_x_ref, by_core_ref, by_both_ref, inv_ref, work):
-    xl, core = place_ref[0], place_ref[2]
-    for flip, ref in enumerate((own_ref, by_core_ref, by_x_ref, by_both_ref)):
+def invert(pieces, xl, core, work, inv_ref):
+    for flip, ref in enumerate(pieces):
         piece = (xl ^ (flip // 2)) * 2 + (core ^ (flip % 2))
         for s in range(8):
             rows = pl.ds(pl.multiple_of(piece * 128 + s * 16, 16), 16)
@@ -328,25 +344,19 @@
     lax.fori_loop(0, 4, diagonal, 0)
 
 
-def inverse_factor(place, pieces):
-    return pl.pallas_call(
-        inverse_kernel,
-        in_specs=[pl.BlockSpec(memory_space=pltpu.SMEM)] + [pl.BlockSpec(memory_space=pltpu.VMEM)] * 4,
-        out_shape=jax.ShapeDtypeStruct((PANEL, PANEL), jnp.float32),
-        scratch_shapes=[pltpu.VMEM((PANEL, PANEL), jnp.float32)],
-        compiler_params=pltpu.CompilerParams(vmem_limit_bytes=16 * MIB),
-    )(place, *pieces)
-
-
-def update_kernel(place_ref, inv_ref, sums_ref, panel_ref, field_ref, out_ref, coupling, mixer):
+def update_kernel(place_ref, own_ref, by_core_ref, by_x_ref, by_both_ref, sums_ref, panel_ref, field_ref, out_ref, *scratch):
+    work, inverse, coupling, mixer = scratch
+    xl, z, core = place_ref[0], place_ref[1], place_ref[2]
+
     @pl.when(pl.program_id(0) == 0)
     def _():
+        invert((own_ref, by_core_ref, by_x_ref, by_both_ref), xl, core, work, inverse)
         for s in range(8):
             coupling[s * 16 : s * 16 + 16, :] = sums_ref[s, 16:32, :] * (1.0 / POINTS)
-        inverse = inv_ref[...]
-        mixer[...] = -dot_nn(dot_nt(coupling[...], inverse), inverse)
-        own = place_ref[0] * 16 + place_ref[1] * 2 + place_ref[2]
-        mixer[0:16, :] = inv_ref[pl.ds(pl.multiple_of(own * 16, 16), 16), :]
+        factor = inverse[...]
+        mixer[...] = -dot_nn(dot_nt(coupling[...], factor), factor)
+        own = xl * 16 + z * 2 + core
+        mixer[0:16, :] = inverse[pl.ds(pl.multiple_of(own * 16, 16), 16), :]
 
     keep = lax.broadcasted_iota(jnp.int32, (128, 256), 0) >= 16
     moved = (dot_nn(mixer[...], panel_ref[...]) + jnp.where(keep, field_ref[...], 0.0)).T
@@ -355,22 +365,23 @@
             out_ref[xp, yh, 0] = moved[xp * 64 + yh * 32 : xp * 64 + yh * 32 + 32, :]
 
 
-def update(place, inverse, sums, panel, field):
+def update(place, pieces, sums, panel, field):
+    whole = pl.BlockSpec((8, 16, PANEL), lambda i: (0, 0, 0))
     out = pl.pallas_call(
         update_kernel,
         grid=(8,),
         in_specs=[
             pl.BlockSpec(memory_space=pltpu.SMEM),
-            pl.BlockSpec((PANEL, PANEL), lambda i: (0, 0)),
+            *[whole] * 4,
             pl.BlockSpec((8, 32, PANEL), lambda i: (0, 0, 0)),
             pl.BlockSpec((PANEL, 256), lambda i: (0, i)),
             pl.BlockSpec((128, 256), lambda i: (0, i)),
         ],
         out_specs=pl.BlockSpec((4, 2, 1, 32, 128), lambda i: (0, 0, i, 0, 0)),
         out_shape=jax.ShapeDtypeStruct((4, 2, 8, 32, 128), jnp.float32),
-        scratch_shapes=[pltpu.VMEM((128, PANEL), jnp.float32)] * 2,
-        compiler_params=pltpu.CompilerParams(vmem_limit_bytes=16 * MIB),
-    )(place, inverse, sums, panel, field)
+        scratch_shapes=[pltpu.VMEM((PANEL, PANEL), jnp.float32)] * 2 + [pltpu.VMEM((128, PANEL), jnp.float32)] * 2,
+        compiler_params=pltpu.CompilerParams(vmem_limit_bytes=52 * MIB),
+    )(place, *pieces, sums, panel, field)
     return out.reshape(4, 16, 32, 128)
 
 
@@ -387,8 +398,7 @@
     by_core = lax.ppermute(piece, "c", ring(2, 1))
     by_x = lax.ppermute(piece, "xl", ring(2, 1))
     by_both = lax.ppermute(by_x, "c", ring(2, 1))
-    inverse = inverse_factor(place, (piece, by_x, by_core, by_both))
-    return update(place, inverse, sums, panel, field)
+    return update(place, (piece, by_core, by_x, by_both), sums, panel, field)
 
 
 def solution(mesh):

time: 188 us -> 193 us (1.027)
  waiting for transfers between devices: 25.9 us -> 30.3 us
    pallas_call x1, Pallas kernels: 7.71 us -> 31.4 us  [update(): pl.pallas_call(update_kernel, grid=(8,), in_specs=[pl.BlockSpec(memory_sp...]
    pallas_call x1 -> x0, Pallas kernels: 22.3 us -> none  [inverse_factor(): pl.pallas_call(inverse_kernel, in_specs=[pl.BlockSpec(memory_space=pltpu....]
    ppermute x17 -> x21, waiting for transfers between devices: 22.5 us -> 27.8 us  [the longest x5 17.5 us: step(): lax.ppermute(right, 'z', ring(8, 1))]
    ppermute x17 -> x21, starting transfers between devices: 26.6 us -> 25.6 us  [the longest x5 11.5 us: step(): lax.ppermute(left, 'z', ring(8, -1))]
  transfers between devices with their start and end apart: 20 -> 24, of which waited for: 11 -> 12; matrix products, arithmetic and copies ran while one was open for 0% -> 0% of each run, Pallas kernels for 0% -> 0%
where the time goes in v5:
time: 193 us; the launch traced here: 192 us
  blocking collectives  69.2 us (36%)
  Pallas kernels  56.6 us (29%)
  starting transfers between devices  33.3 us (17%)
  waiting for transfers between devices  30.3 us (16%)
    pallas_call x1, Pallas kernels, update(): pl.pallas_call(update_kernel, grid=(8,), in_specs=[pl.BlockSpec(memory_sp...  31.4 us
    all_to_all x1, blocking collectives, per_device(): lax.all_to_all(pack(orbitals, potential), SPACE, 0, 0, tiled=True)  24.2 us
    all_to_all x1, blocking collectives, per_device(): back = lax.all_to_all(chebyshev(received), SPACE, 0, 0, tiled=True)  17.8 us
    ppermute x5, waiting for transfers between devices, step(): lax.ppermute(right, 'z', ring(8, 1))  17.5 us
    all_to_all x1, blocking collectives, per_device(): mine = jnp.sum(lax.all_to_all(terms, SPACE, 0, 0, tiled=True), axis=0)  14.8 us
    all_to_all x1, blocking collectives, per_device(): lax.all_to_all(jnp.broadcast_to(mine, (8, 32, PANEL)), SPACE, 0, 0, tiled...  12.5 us
    ppermute x5, starting transfers between devices, step(): lax.ppermute(left, 'z', ring(8, -1))  11.5 us
    pallas_call x1, Pallas kernels, chebyshev(): pl.pallas_call(filter_kernel, out_shape=jax.ShapeDtypeStruct((64, 32, 128...  11.3 us
  transfers between devices with their start and end apart: 24, of which 12 were waited for; matrix products, arithmetic and copies ran while one was open for 0% of the time, Pallas kernels for 0%

profile of v5, /device:TPU:1, one launch (start us, length us, event | category | flops | bytes accessed | tf_op | source)
XLA Modules:
  0.0 192.3 jit_solution(9736443489628185964)
XLA Ops:
  0.0 4.2 %shard_map.28 = f32[8,272,128]{2,1,0:T(8,128)} custom-call(f32[4,16,32,128]{3,2,1,0:T(8,128)} %orb_ref.1, f32[4,16,32]{2,1,0:T(8,128)} %pot_ref.1), custom_call_target="tpu_custom_call" | custom-call | tf_op jit(solution)/shard_map/pallas_call | solution.py:62
  4.2 24.2 %all_to_all.20.in_ref = f32[8,272,128]{2,1,0:T(8,128)S(1)} all-to-all(f32[8,272,128]{2,1,0:T(8,128)} %shard_map.28), channel_id=1, replica_groups=mesh['y'=4,'xh'=2,'xl'=2,'z'=8,'c'=2] {'y','xh'}, dimensions={0} | all-to-all | bytes 2228224 | tf_op jit(solution)/shard_map/all_to_all | solution.py:391
  28.4 11.3 %shard_map.29 = f32[64,32,128]{2,1,0:T(8,128)S(1)} custom-call(f32[8,272,128]{2,1,0:T(8,128)S(1)} %all_to_all.20.in_ref), custom_call_target="tpu_custom_call" | custom-call | tf_op jit(solution)/shard_map/pallas_call | solution.py:143
  39.7 17.8 %all_to_all.21.in_ref = f32[8,256,128]{2,1,0:T(8,128)S(1)} all-to-all(f32[8,256,128]{2,1,0:T(8,128)S(1)} %bitcast.5), channel_id=1, replica_groups=mesh['y'=4,'xh'=2,'xl'=2,'z'=8,'c'=2] {'y','xh'}, dimensions={0} | all-to-all | bytes 2097152 | tf_op jit(solution)/shard_map/all_to_all | solution.py:392
  58.1 3.5 %collective-permute-start.2 = (f32[16,2048]{1,0:T(8,128)S(1)}, f32[16,2048]{1,0:T(8,128)S(1)}, u32[]{:S(2)}, u32[]{:S(2)}) collective-permute-start(f32[16,2048]{1,0:T(8,128)S(1)} %shard_map.30.refs_0_), channel_id=1, source_target_pairs={{0,1},{1,0},{2,3},{3,2},{4,5},{5,4},{6,7},{7,6},{8,9},{9,8},{10,11... | collective-permute-start | bytes 393224 | tf_op jit(solution)/shard_map/ppermute | solution.py:179
  61.5 5.6 %collective-permute-start.1 = (f32[16,2048]{1,0:T(8,128)S(1)}, f32[16,2048]{1,0:T(8,128)S(1)}, u32[]{:S(2)}, u32[]{:S(2)}) collective-permute-start(f32[16,2048]{1,0:T(8,128)S(1)} %shard_map.30.refs_0_), channel_id=1, source_target_pairs={{0,14},{2,0},{4,2},{6,4},{8,6},{10,8},{12,10},{14,12},{1,15},{3,1}... | collective-permute-start | bytes 393224 | tf_op jit(solution)/shard_map/ppermute | solution.py:178
  67.1 2.9 %collective-permute-done.1.refs_2_ = f32[16,2048]{1,0:T(8,128)S(1)} collective-permute-done((f32[16,2048]{1,0:T(8,128)S(1)}, f32[16,2048]{1,0:T(8,128)S(1)}, u32[]{:S(2)}, u32[]{:S(2)}) %collective-permute-start.1) | collective-permute-done | bytes 131104 | tf_op jit(solution)/shard_map/ppermute | solution.py:178
  70.0 3.1 %collective-permute-done = f32[16,2048]{1,0:T(8,128)S(1)} collective-permute-done((f32[16,2048]{1,0:T(8,128)S(1)}, f32[16,2048]{1,0:T(8,128)S(1)}, u32[]{:S(2)}, u32[]{:S(2)}) %collective-permute-start) | collective-permute-done | bytes 131104 | tf_op jit(solution)/shard_map/ppermute | solution.py:177
  78.3 1.7 collective-permute-done.5.refs_4_
  80.0 3.8 %collective-permute-done.4.refs_3_ = f32[32,2048]{1,0:T(8,128)S(1)} collective-permute-done((f32[32,2048]{1,0:T(8,128)S(1)}, f32[32,2048]{1,0:T(8,128)S(1)}, u32[]{:S(2)}, u32[]{:S(2)}) %collective-permute-start.4) | collective-permute-done | bytes 262176 | tf_op jit(solution)/shard_map/ppermute | solution.py:177
  85.1 2.4 %collective-permute-start.9 = (f32[32,2048]{1,0:T(8,128)S(1)}, f32[32,2048]{1,0:T(8,128)S(1)}, u32[]{:S(2)}, u32[]{:S(2)}) collective-permute-start(f32[32,2048]{1,0:T(8,128)S(1)} %collective-permute-done.5.refs_4_), channel_id=1, source_target_pairs={{0,14},{2,0},{4,2},{6,4},{8,6},{10,8},{12,10},{14,12},{1,15},{3,1}... | collective-permute-start | bytes 786440 | tf_op jit(solution)/shard_map/ppermute | solution.py:178
  87.6 6.2 %collective-permute-done.8.refs_5_ = f32[32,2048]{1,0:T(8,128)S(1)} collective-permute-done((f32[32,2048]{1,0:T(8,128)S(1)}, f32[32,2048]{1,0:T(8,128)S(1)}, u32[]{:S(2)}, u32[]{:S(2)}) %collective-permute-start.8) | collective-permute-done | bytes 262176 | tf_op jit(solution)/shard_map/ppermute | solution.py:177
  94.8 3.0 %collective-permute-start.13 = (f32[24,2048]{1,0:T(8,128)S(1)}, f32[24,2048]{1,0:T(8,128)S(1)}, u32[]{:S(2)}, u32[]{:S(2)}) collective-permute-start(f32[24,2048]{1,0:T(8,128)S(1)} %slice.16), channel_id=1, source_target_pairs={{0,14},{2,0},{4,2},{6,4},{8,6},{10,8},{12,10},{14,12},{1,15},{3,1}... | collective-permute-start | bytes 589832 | tf_op jit(solution)/shard_map/ppermute | solution.py:178
  97.8 3.8 %collective-permute-done.13.refs_8_ = f32[24,2048]{1,0:T(8,128)S(1)} collective-permute-done((f32[24,2048]{1,0:T(8,128)S(1)}, f32[24,2048]{1,0:T(8,128)S(1)}, u32[]{:S(2)}, u32[]{:S(2)}) %collective-permute-start.13) | collective-permute-done | bytes 196640 | tf_op jit(solution)/shard_map/ppermute | solution.py:178
  101.5 3.1 %collective-permute-done.12.refs_7_ = f32[24,2048]{1,0:T(8,128)S(1)} collective-permute-done((f32[24,2048]{1,0:T(8,128)S(1)}, f32[24,2048]{1,0:T(8,128)S(1)}, u32[]{:S(2)}, u32[]{:S(2)}) %collective-permute-start.12) | collective-permute-done | bytes 196640 | tf_op jit(solution)/shard_map/ppermute | solution.py:177
  104.7 1.8 collective-permute-start.18
  108.1 1.6 collective-permute-done.17
  111.1 1.9 collective-permute-start.20
  114.7 8.7 %shard_map.32 = (f32[512,2048]{1,0:T(8,128)}, f32[8,32,512]{2,1,0:T(8,128)}) custom-call(s32[3]{0:T(128)} %pad_add_fusion.place_ref, f32[16,2048]{1,0:T(8,128)} %copy-done.1, f32[32,2048]{1,0:T(8,128)} %copy-done.5, f32[16,2048]{1,0:T(8,128)} %copy-done.6, f32[32,2048]{1,0:T(8,128)} %copy-done.12, f32[32,2048]{1,0:T(8,128)} %copy-done.10, ...), custom_call_target="tpu_custom_call" | custom-call | tf_op jit(solution)/shard_map/pallas_call | solution.py:247
  123.5 14.8 %all_to_all.22 = f32[8,32,512]{2,1,0:T(8,128)S(1)} all-to-all(f32[8,32,512]{2,1,0:T(8,128)} %get-tuple-element.53), channel_id=1, replica_groups=mesh['y'=4,'xh'=2,'xl'=2,'z'=8,'c'=2] {'y','xh'}, dimensions={0} | all-to-all | bytes 1048576 | tf_op jit(solution)/shard_map/all_to_all | solution.py:395
  138.3 12.5 %all_to_all.23.sums_ref = f32[8,32,512]{2,1,0:T(8,128)S(1)} all-to-all(f32[8,32,512]{2,1,0:T(8,128)S(1)} %broadcast_in_dim.3), channel_id=1, replica_groups=mesh['y'=4,'xh'=2,'xl'=2,'z'=8,'c'=2] {'y','xh'}, dimensions={0} | all-to-all | bytes 1048576 | tf_op jit(solution)/shard_map/all_to_all | solution.py:396
  152.1 2.8 %collective-permute-start.21 = (f32[8,16,512]{2,1,0:T(8,128)S(1)}, f32[8,16,512]{2,1,0:T(8,128)S(1)}, u32[]{:S(2)}, u32[]{:S(2)}) collective-permute-start(f32[8,16,512]{2,1,0:T(8,128)S(1)} %slice.20.own_ref), channel_id=1, source_target_pairs={{0,1},{1,0},{2,3},{3,2},{4,5},{5,4},{6,7},{7,6},{8,9},{9,8},{10,11... | collective-permute-start | bytes 786440 | tf_op jit(solution)/shard_map/ppermute | solution.py:398
  156.1 3.6 %collective-permute-start.23 = (f32[8,16,512]{2,1,0:T(8,128)S(1)}, f32[8,16,512]{2,1,0:T(8,128)S(1)}, u32[]{:S(2)}, u32[]{:S(2)}) collective-permute-start(f32[8,16,512]{2,1,0:T(8,128)S(1)} %collective-permute-done.22.by_x_ref), channel_id=1, source_target_pairs={{0,1},{1,0},{2,3},{3,2},{4,5},{5,4},{6,7},{7,6},{8,9},{9,8},{10,11... | collective-permute-start | bytes 786440 | tf_op jit(solution)/shard_map/ppermute | solution.py:400
  160.9 31.4 %shard_map.33 = f32[4,2,8,32,128]{4,3,2,1,0:T(8,128)} custom-call(s32[3]{0:T(128)S(1)} %copy-done.2, f32[8,16,512]{2,1,0:T(8,128)S(1)} %slice.20.own_ref, f32[8,16,512]{2,1,0:T(8,128)S(1)} %collective-permute-done.21.by_core_ref, f32[8,16,512]{2,1,0:T(8,128)S(1)} %collective-permute-done.22.by_x_ref, f32[8,16,512]{2,1,0:T(8,128)S(1)} %collective-permute-done.23.by_both_ref, ...), custom_call_target="tpu_custom_call" | custom-call | tf_op jit(solution)/shard_map/pallas_call | solution.py:370
  (91 shorter events, 16.4 us)
Async XLA Ops:
  57.7 9.4 %collective-permute-start.3 = (f32[16,2048]{1,0:T(8,128)S(1)}, f32[16,2048]{1,0:T(8,128)S(1)}, u32[]{:S(2)}, u32[]{:S(2)}) collective-permute-start(f32[16,2048]{1,0:T(8,128)S(1)} %shard_map.30.refs_0_), channel_id=1, source_target_pairs={{0,16},{16,0},{1,17},{17,1},{2,18},{18,2},{3,19},{19,3},{4,20},{20... | collective-permute-start | bytes 393224 | tf_op jit(solution)/shard_map/ppermute | solution.py:180
  58.1 9.0 %collective-permute-start.2 = (f32[16,2048]{1,0:T(8,128)S(1)}, f32[16,2048]{1,0:T(8,128)S(1)}, u32[]{:S(2)}, u32[]{:S(2)}) collective-permute-start(f32[16,2048]{1,0:T(8,128)S(1)} %shard_map.30.refs_0_), channel_id=1, source_target_pairs={{0,1},{1,0},{2,3},{3,2},{4,5},{5,4},{6,7},{7,6},{8,9},{9,8},{10,11... | collective-permute-start | bytes 393224 | tf_op jit(solution)/shard_map/ppermute | solution.py:179
  61.5 8.5 %collective-permute-start.1 = (f32[16,2048]{1,0:T(8,128)S(1)}, f32[16,2048]{1,0:T(8,128)S(1)}, u32[]{:S(2)}, u32[]{:S(2)}) collective-permute-start(f32[16,2048]{1,0:T(8,128)S(1)} %shard_map.30.refs_0_), channel_id=1, source_target_pairs={{0,14},{2,0},{4,2},{6,4},{8,6},{10,8},{12,10},{14,12},{1,15},{3,1}... | collective-permute-start | bytes 393224 | tf_op jit(solution)/shard_map/ppermute | solution.py:178
  67.1 6.0 %collective-permute-start = (f32[16,2048]{1,0:T(8,128)S(1)}, f32[16,2048]{1,0:T(8,128)S(1)}, u32[]{:S(2)}, u32[]{:S(2)}) collective-permute-start(f32[16,2048]{1,0:T(8,128)S(1)} %shard_map.30.refs_0_), channel_id=1, source_target_pairs={{0,2},{2,4},{4,6},{6,8},{8,10},{10,12},{12,14},{14,0},{1,3},{3,5},... | collective-permute-start | bytes 393224 | tf_op jit(solution)/shard_map/ppermute | solution.py:177
  73.2 6.8 %collective-permute-start.5 = (f32[32,2048]{1,0:T(8,128)S(1)}, f32[32,2048]{1,0:T(8,128)S(1)}, u32[]{:S(2)}, u32[]{:S(2)}) collective-permute-start(f32[32,2048]{1,0:T(8,128)S(1)} %pad_maximum_fusion), channel_id=1, source_target_pairs={{0,14},{2,0},{4,2},{6,4},{8,6},{10,8},{12,10},{14,12},{1,15},{3,1}... | collective-permute-start | bytes 786440 | tf_op jit(solution)/shard_map/ppermute | solution.py:178
  73.6 6.4 %collective-permute-start.6 = (f32[32,2048]{1,0:T(8,128)S(1)}, f32[32,2048]{1,0:T(8,128)S(1)}, u32[]{:S(2)}, u32[]{:S(2)}) collective-permute-start(f32[32,2048]{1,0:T(8,128)S(1)} %constant_dynamic-update-slice_fusion.refs_1_), channel_id=1, source_target_pairs={{0,1},{1,0},{2,3},{3,2},{4,5},{5,4},{6,7},{7,6},{8,9},{9,8},{10,11... | collective-permute-start | bytes 786440 | tf_op jit(solution)/shard_map/ppermute | solution.py:179
  74.7 9.1 %collective-permute-start.4 = (f32[32,2048]{1,0:T(8,128)S(1)}, f32[32,2048]{1,0:T(8,128)S(1)}, u32[]{:S(2)}, u32[]{:S(2)}) collective-permute-start(f32[32,2048]{1,0:T(8,128)S(1)} %constant_dynamic-update-slice_fusion.refs_1_), channel_id=1, source_target_pairs={{0,2},{2,4},{4,6},{6,8},{8,10},{10,12},{12,14},{14,0},{1,3},{3,5},... | collective-permute-start | bytes 786440 | tf_op jit(solution)/shard_map/ppermute | solution.py:177
  76.1 2.2 %collective-permute-start.7 = (f32[16,2048]{1,0:T(8,128)S(1)}, f32[16,2048]{1,0:T(8,128)S(1)}, u32[]{:S(2)}, u32[]{:S(2)}) collective-permute-start(f32[16,2048]{1,0:T(8,128)S(1)} %collective-permute-done.1.refs_2_), channel_id=1, source_target_pairs={{0,1},{1,0},{2,3},{3,2},{4,5},{5,4},{6,7},{7,6},{8,9},{9,8},{10,11... | collective-permute-start | bytes 393224 | tf_op jit(solution)/shard_map/ppermute | solution.py:179
  83.8 3.7 %collective-permute-start.10 = (f32[32,2048]{1,0:T(8,128)S(1)}, f32[32,2048]{1,0:T(8,128)S(1)}, u32[]{:S(2)}, u32[]{:S(2)}) collective-permute-start(f32[32,2048]{1,0:T(8,128)S(1)} %collective-permute-done.4.refs_3_), channel_id=1, source_target_pairs={{0,1},{1,0},{2,3},{3,2},{4,5},{5,4},{6,7},{7,6},{8,9},{9,8},{10,11... | collective-permute-start | bytes 786440 | tf_op jit(solution)/shard_map/ppermute | solution.py:179
  84.6 9.1 %collective-permute-start.8 = (f32[32,2048]{1,0:T(8,128)S(1)}, f32[32,2048]{1,0:T(8,128)S(1)}, u32[]{:S(2)}, u32[]{:S(2)}) collective-permute-start(f32[32,2048]{1,0:T(8,128)S(1)} %collective-permute-done.4.refs_3_), channel_id=1, source_target_pairs={{0,2},{2,4},{4,6},{6,8},{8,10},{10,12},{12,14},{14,0},{1,3},{3,5},... | collective-permute-start | bytes 786440 | tf_op jit(solution)/shard_map/ppermute | solution.py:177
  84.8 8.9 %collective-permute-start.11 = (f32[32,2048]{1,0:T(8,128)S(1)}, f32[32,2048]{1,0:T(8,128)S(1)}, u32[]{:S(2)}, u32[]{:S(2)}) collective-permute-start(f32[32,2048]{1,0:T(8,128)S(1)} %collective-permute-done.5.refs_4_), channel_id=1, source_target_pairs={{0,1},{1,0},{2,3},{3,2},{4,5},{5,4},{6,7},{7,6},{8,9},{9,8},{10,11... | collective-permute-start | bytes 786440 | tf_op jit(solution)/shard_map/ppermute | solution.py:179
  85.1 8.6 %collective-permute-start.9 = (f32[32,2048]{1,0:T(8,128)S(1)}, f32[32,2048]{1,0:T(8,128)S(1)}, u32[]{:S(2)}, u32[]{:S(2)}) collective-permute-start(f32[32,2048]{1,0:T(8,128)S(1)} %collective-permute-done.5.refs_4_), channel_id=1, source_target_pairs={{0,14},{2,0},{4,2},{6,4},{8,6},{10,8},{12,10},{14,12},{1,15},{3,1}... | collective-permute-start | bytes 786440 | tf_op jit(solution)/shard_map/ppermute | solution.py:178
  93.8 10.9 %collective-permute-start.14 = (f32[32,2048]{1,0:T(8,128)S(1)}, f32[32,2048]{1,0:T(8,128)S(1)}, u32[]{:S(2)}, u32[]{:S(2)}) collective-permute-start(f32[32,2048]{1,0:T(8,128)S(1)} %collective-permute-done.8.refs_5_), channel_id=1, source_target_pairs={{0,1},{1,0},{2,3},{3,2},{4,5},{5,4},{6,7},{7,6},{8,9},{9,8},{10,11... | collective-permute-start | bytes 786440 | tf_op jit(solution)/shard_map/ppermute | solution.py:179
  94.6 10.0 %collective-permute-start.15 = (f32[32,2048]{1,0:T(8,128)S(1)}, f32[32,2048]{1,0:T(8,128)S(1)}, u32[]{:S(2)}, u32[]{:S(2)}) collective-permute-start(f32[32,2048]{1,0:T(8,128)S(1)} %collective-permute-done.9.refs_6_), channel_id=1, source_target_pairs={{0,1},{1,0},{2,3},{3,2},{4,5},{5,4},{6,7},{7,6},{8,9},{9,8},{10,11... | collective-permute-start | bytes 786440 | tf_op jit(solution)/shard_map/ppermute | solution.py:179
  94.8 6.8 %collective-permute-start.13 = (f32[24,2048]{1,0:T(8,128)S(1)}, f32[24,2048]{1,0:T(8,128)S(1)}, u32[]{:S(2)}, u32[]{:S(2)}) collective-permute-start(f32[24,2048]{1,0:T(8,128)S(1)} %slice.16), channel_id=1, source_target_pairs={{0,14},{2,0},{4,2},{6,4},{8,6},{10,8},{12,10},{14,12},{1,15},{3,1}... | collective-permute-start | bytes 589832 | tf_op jit(solution)/shard_map/ppermute | solution.py:178
  97.8 6.8 %collective-permute-start.12 = (f32[24,2048]{1,0:T(8,128)S(1)}, f32[24,2048]{1,0:T(8,128)S(1)}, u32[]{:S(2)}, u32[]{:S(2)}) collective-permute-start(f32[24,2048]{1,0:T(8,128)S(1)} %slice.15), channel_id=1, source_target_pairs={{0,2},{2,4},{4,6},{6,8},{8,10},{10,12},{12,14},{14,0},{1,3},{3,5},... | collective-permute-start | bytes 589832 | tf_op jit(solution)/shard_map/ppermute | solution.py:177
  104.7 6.4 %collective-permute-start.18 = (f32[24,2048]{1,0:T(8,128)S(1)}, f32[24,2048]{1,0:T(8,128)S(1)}, u32[]{:S(2)}, u32[]{:S(2)}) collective-permute-start(f32[24,2048]{1,0:T(8,128)S(1)} %collective-permute-done.12.refs_7_), channel_id=1, source_target_pairs={{0,1},{1,0},{2,3},{3,2},{4,5},{5,4},{6,7},{7,6},{8,9},{9,8},{10,11... | collective-permute-start | bytes 589832 | tf_op jit(solution)/shard_map/ppermute | solution.py:179
  106.4 4.6 %collective-permute-start.19 = (f32[24,2048]{1,0:T(8,128)S(1)}, f32[24,2048]{1,0:T(8,128)S(1)}, u32[]{:S(2)}, u32[]{:S(2)}) collective-permute-start(f32[24,2048]{1,0:T(8,128)S(1)} %collective-permute-done.13.refs_8_), channel_id=1, source_target_pairs={{0,1},{1,0},{2,3},{3,2},{4,5},{5,4},{6,7},{7,6},{8,9},{9,8},{10,11... | collective-permute-start | bytes 589832 | tf_op jit(solution)/shard_map/ppermute | solution.py:179
  106.5 3.2 %collective-permute-start.17 = (f32[8,2048]{1,0:T(8,128)S(1)}, f32[8,2048]{1,0:T(8,128)S(1)}, u32[]{:S(2)}, u32[]{:S(2)}) collective-permute-start(f32[8,2048]{1,0:T(8,128)S(1)} %slice.18), channel_id=1, source_target_pairs={{0,14},{2,0},{4,2},{6,4},{8,6},{10,8},{12,10},{14,12},{1,15},{3,1}... | collective-permute-start | bytes 196616 | tf_op jit(solution)/shard_map/ppermute | solution.py:178
  106.6 4.4 %collective-permute-start.16 = (f32[8,2048]{1,0:T(8,128)S(1)}, f32[8,2048]{1,0:T(8,128)S(1)}, u32[]{:S(2)}, u32[]{:S(2)}) collective-permute-start(f32[8,2048]{1,0:T(8,128)S(1)} %slice.17), channel_id=1, source_target_pairs={{0,2},{2,4},{4,6},{6,8},{8,10},{10,12},{12,14},{14,0},{1,3},{3,5},... | collective-permute-start | bytes 196616 | tf_op jit(solution)/shard_map/ppermute | solution.py:177
  111.1 2.8 %collective-permute-start.20 = (f32[16,2048]{1,0:T(8,128)S(1)}, f32[16,2048]{1,0:T(8,128)S(1)}, u32[]{:S(2)}, u32[]{:S(2)}) collective-permute-start(f32[16,2048]{1,0:T(8,128)S(1)} %constant_dynamic-update-slice_fusion.2.refs_9_), channel_id=1, source_target_pairs={{0,1},{1,0},{2,3},{3,2},{4,5},{5,4},{6,7},{7,6},{8,9},{9,8},{10,11... | collective-permute-start | bytes 393224 | tf_op jit(solution)/shard_map/ppermute | solution.py:193
  150.8 5.3 %collective-permute-start.22 = (f32[8,16,512]{2,1,0:T(8,128)S(1)}, f32[8,16,512]{2,1,0:T(8,128)S(1)}, u32[]{:S(2)}, u32[]{:S(2)}) collective-permute-start(f32[8,16,512]{2,1,0:T(8,128)S(1)} %slice.20.own_ref), channel_id=1, source_target_pairs={{0,16},{16,0},{1,17},{17,1},{2,18},{18,2},{3,19},{19,3},{4,20},{20... | collective-permute-start | bytes 786440 | tf_op jit(solution)/shard_map/ppermute | solution.py:399
  152.1 7.7 %collective-permute-start.21 = (f32[8,16,512]{2,1,0:T(8,128)S(1)}, f32[8,16,512]{2,1,0:T(8,128)S(1)}, u32[]{:S(2)}, u32[]{:S(2)}) collective-permute-start(f32[8,16,512]{2,1,0:T(8,128)S(1)} %slice.20.own_ref), channel_id=1, source_target_pairs={{0,1},{1,0},{2,3},{3,2},{4,5},{5,4},{6,7},{7,6},{8,9},{9,8},{10,11... | collective-permute-start | bytes 786440 | tf_op jit(solution)/shard_map/ppermute | solution.py:398
  156.1 4.8 %collective-permute-start.23 = (f32[8,16,512]{2,1,0:T(8,128)S(1)}, f32[8,16,512]{2,1,0:T(8,128)S(1)}, u32[]{:S(2)}, u32[]{:S(2)}) collective-permute-start(f32[8,16,512]{2,1,0:T(8,128)S(1)} %collective-permute-done.22.by_x_ref), channel_id=1, source_target_pairs={{0,1},{1,0},{2,3},{3,2},{4,5},{5,4},{6,7},{7,6},{8,9},{9,8},{10,11... | collective-permute-start | bytes 786440 | tf_op jit(solution)/shard_map/ppermute | solution.py:400
  (22 other events, 335.8 us)

commit v6 on v4

--- a/solution.py
+++ b/solution.py
@@ -172,21 +172,21 @@
 
 
 def gather_panel(own, field):
-    other = lax.ppermute(own, "xl", ring(2, 1))
+    other, field = lax.optimization_barrier((lax.ppermute(own, "xl", ring(2, 1)), field))
     right = left = pair = jnp.concatenate([own, other], axis=0)
-    found, swapped, waiting = [pair], [], [pair]
+    found, swapped, waiting = [pair], [], []
     for step in range(4):
         swaps = [lax.ppermute(block, "c", ring(2, 1)) for block in waiting]
         if step < 3:
             right = lax.ppermute(right, "z", ring(8, 1))
             left = lax.ppermute(left, "z", ring(8, -1))
-            waiting = [right, left]
-            found += waiting
+            waiting = [right, left] if step else [pair, right, left]
+            found += [right, left]
         else:
             far_r = lax.ppermute(right[:16], "z", ring(8, 1))
             far_l = lax.ppermute(left[16:], "z", ring(8, -1))
             found.append(jnp.concatenate([far_r, far_l], axis=0))
-        right, left, swaps, field = lax.optimization_barrier((right, left, swaps, field))
+        right, left, swaps = lax.optimization_barrier((right, left, swaps))
         swapped += swaps
     return found + swapped + [lax.ppermute(found[-1], "c", ring(2, 1))], field
 
@@ -198,31 +198,40 @@
     blocks, (field_ref, home_ref, out_ref, panel_ref, acc, sems) = refs[:16], refs[16:]
     xl, z, core = place_ref[0], place_ref[1], place_ref[2]
     copies = []
-    for other in range(2):
-        for k, offset in enumerate(OFFSETS):
-            for xo in range(2):
-                owner = (xl ^ xo) * 16 + ((z + offset) & 7) * 2 + (core ^ other)
-                rows = pl.ds(pl.multiple_of(owner * 16, 16), 16)
-                source = blocks[other * 8 + k].at[pl.ds(xo * 16, 16), :]
-                copies.append(pltpu.make_async_copy(source, panel_ref.at[rows, :], sems.at[len(copies)]))
-                copies[-1].start()
-    mine = pl.ds(pl.multiple_of((xl * 2 + core) * 128, 128), 128)
+    for half in range(2):
+        points = pl.ds(half * 1024, 1024)
+        for flip in range(2):
+            for k, offset in enumerate(OFFSETS):
+                for xo in range(2):
+                    owner = (xl ^ xo) * 16 + ((z + offset) & 7) * 2 + (core ^ flip)
+                    rows = pl.ds(pl.multiple_of(owner * 16, 16), 16)
+                    source = blocks[flip * 8 + k].at[pl.ds(xo * 16, 16), points]
+                    copies.append(pltpu.make_async_copy(source, panel_ref.at[rows, points], sems.at[len(copies)]))
+                    copies[-1].start()
+    long = pl.ds(pl.multiple_of((3 - core) * 128, 128), 128)
+    short = pl.ds(pl.multiple_of(core * 128, 128), 128)
     acc[...] = jnp.zeros_like(acc)
-    for copy in copies:
-        copy.wait()
-    home = pltpu.make_async_copy(panel_ref, home_ref, sems.at[32])
-    home.start()
 
     def chunk(i, _):
         points = pl.ds(pl.multiple_of(i * 512, 512), 512)
-        rows = jnp.concatenate([panel_ref[mine, points], field_ref[:, points]], axis=0)
+        rows = jnp.concatenate([panel_ref[long, points], panel_ref[short, points], field_ref[:, points]], axis=0)
         acc[...] += dot_nt(rows, panel_ref[:, points])
         return 0
 
-    lax.fori_loop(0, 4, chunk, 0)
+    for half in range(2):
+        for copy in copies[half * 32 : half * 32 + 32]:
+            copy.wait()
+        if half:
+            home = pltpu.make_async_copy(panel_ref, home_ref, sems.at[64])
+            home.start()
+        lax.fori_loop(half * 2, half * 2 + 2, chunk, 0)
     for s in range(8):
-        out_ref[s, 0:16, :] = acc[s * 16 : s * 16 + 16, :]
-        out_ref[s, 16:32, :] = acc[128 + s * 16 : 128 + s * 16 + 16, :]
+        rows = slice(s * 16, s * 16 + 16)
+        lower = slice(128 + s * 16, 128 + s * 16 + 16)
+        out_ref[s, :, 0:384] = acc[rows, 0:384]
+        out_ref[s, :, 384:512] = jnp.where(core == 0, acc[rows, 384:512], acc[lower, 128:256])
+        out_ref[s, :, 512:640] = acc[lower, 0:128]
+        out_ref[s, :, 640:1152] = acc[256 + s * 16 : 256 + s * 16 + 16, :]
     home.wait()
 
 
@@ -232,12 +241,12 @@
         in_specs=[pl.BlockSpec(memory_space=pltpu.SMEM)]
         + [pl.BlockSpec(memory_space=pl.ANY)] * 16
         + [pl.BlockSpec(memory_space=pltpu.VMEM)],
-        out_shape=(jax.ShapeDtypeStruct((512, 2048), jnp.float32), jax.ShapeDtypeStruct((8, 32, 512), jnp.float32)),
+        out_shape=(jax.ShapeDtypeStruct((512, 2048), jnp.float32), jax.ShapeDtypeStruct((8, 16, 1152), jnp.float32)),
         out_specs=(pl.BlockSpec(memory_space=pl.ANY), pl.BlockSpec(memory_space=pltpu.VMEM)),
         scratch_shapes=[
             pltpu.VMEM((512, 2048), jnp.float32),
-            pltpu.VMEM((256, 512), jnp.float32),
-            pltpu.SemaphoreType.DMA((33,)),
+            pltpu.VMEM((384, 512), jnp.float32),
+            pltpu.SemaphoreType.DMA((65,)),
         ],
         compiler_params=pltpu.CompilerParams(vmem_limit_bytes=BIG * MIB),
     )(place, *blocks, field)
@@ -298,13 +307,15 @@
     return jnp.concatenate(out, axis=0)
 
 
-def inverse_kernel(place_ref, own_ref, by_x_ref, by_core_ref, by_both_ref, inv_ref, work):
-    xl, core = place_ref[0], place_ref[2]
-    for flip, ref in enumerate((own_ref, by_core_ref, by_x_ref, by_both_ref)):
-        piece = (xl ^ (flip // 2)) * 2 + (core ^ (flip % 2))
+def invert(pieces, core, work, inv_ref):
+    for flip, ref in enumerate(pieces):
+        owner = core ^ flip
         for s in range(8):
-            rows = pl.ds(pl.multiple_of(piece * 128 + s * 16, 16), 16)
-            work[rows, :] = ref[s] * (1.0 / POINTS)
+            tile = ref[s] * (1.0 / POINTS)
+            work[pl.ds(pl.multiple_of((3 - owner) * 128 + s * 16, 16), 16), 0:384] = tile[:, 0:384]
+            square = pl.multiple_of((3 - 2 * owner) * 128, 128)
+            work[pl.ds(pl.multiple_of(square + s * 16, 16), 16), pl.ds(square, 128)] = tile[:, 384:512]
+            work[pl.ds(pl.multiple_of(owner * 128 + s * 16, 16), 16), 0:128] = tile[:, 512:640]
     inv_ref[...] = jnp.zeros_like(inv_ref)
 
     def diagonal(k, _):
@@ -328,25 +339,19 @@
     lax.fori_loop(0, 4, diagonal, 0)
 
 
-def inverse_factor(place, pieces):
-    return pl.pallas_call(
-        inverse_kernel,
-        in_specs=[pl.BlockSpec(memory_space=pltpu.SMEM)] + [pl.BlockSpec(memory_space=pltpu.VMEM)] * 4,
-        out_shape=jax.ShapeDtypeStruct((PANEL, PANEL), jnp.float32),
-        scratch_shapes=[pltpu.VMEM((PANEL, PANEL), jnp.float32)],
-        compiler_params=pltpu.CompilerParams(vmem_limit_bytes=16 * MIB),
-    )(place, *pieces)
-
-
-def update_kernel(place_ref, inv_ref, sums_ref, panel_ref, field_ref, out_ref, coupling, mixer):
+def update_kernel(place_ref, sums_ref, by_core_ref, panel_ref, field_ref, out_ref, *scratch):
+    work, inverse, coupling, mixer = scratch
+    xl, z, core = place_ref[0], place_ref[1], place_ref[2]
+
     @pl.when(pl.program_id(0) == 0)
     def _():
+        invert((sums_ref, by_core_ref), core, work, inverse)
         for s in range(8):
-            coupling[s * 16 : s * 16 + 16, :] = sums_ref[s, 16:32, :] * (1.0 / POINTS)
-        inverse = inv_ref[...]
-        mixer[...] = -dot_nn(dot_nt(coupling[...], inverse), inverse)
-        own = place_ref[0] * 16 + place_ref[1] * 2 + place_ref[2]
-        mixer[0:16, :] = inv_ref[pl.ds(pl.multiple_of(own * 16, 16), 16), :]
+            coupling[s * 16 : s * 16 + 16, :] = sums_ref[s, :, 640:1152] * (1.0 / POINTS)
+        factor = inverse[...]
+        mixer[...] = -dot_nn(dot_nt(coupling[...], factor), factor)
+        own = xl * 16 + z * 2 + core
+        mixer[0:16, :] = inverse[pl.ds(pl.multiple_of(own * 16, 16), 16), :]
 
     keep = lax.broadcasted_iota(jnp.int32, (128, 256), 0) >= 16
     moved = (dot_nn(mixer[...], panel_ref[...]) + jnp.where(keep, field_ref[...], 0.0)).T
@@ -355,22 +360,22 @@
             out_ref[xp, yh, 0] = moved[xp * 64 + yh * 32 : xp * 64 + yh * 32 + 32, :]
 
 
-def update(place, inverse, sums, panel, field):
+def update(place, sums, by_core, panel, field):
     out = pl.pallas_call(
         update_kernel,
         grid=(8,),
         in_specs=[
             pl.BlockSpec(memory_space=pltpu.SMEM),
-            pl.BlockSpec((PANEL, PANEL), lambda i: (0, 0)),
-            pl.BlockSpec((8, 32, PANEL), lambda i: (0, 0, 0)),
+            pl.BlockSpec((8, 16, 1152), lambda i: (0, 0, 0)),
+            pl.BlockSpec((8, 16, 640), lambda i: (0, 0, 0)),
             pl.BlockSpec((PANEL, 256), lambda i: (0, i)),
             pl.BlockSpec((128, 256), lambda i: (0, i)),
         ],
         out_specs=pl.BlockSpec((4, 2, 1, 32, 128), lambda i: (0, 0, i, 0, 0)),
         out_shape=jax.ShapeDtypeStruct((4, 2, 8, 32, 128), jnp.float32),
-        scratch_shapes=[pltpu.VMEM((128, PANEL), jnp.float32)] * 2,
-        compiler_params=pltpu.CompilerParams(vmem_limit_bytes=16 * MIB),
-    )(place, inverse, sums, panel, field)
+        scratch_shapes=[pltpu.VMEM((PANEL, PANEL), jnp.float32)] * 2 + [pltpu.VMEM((128, PANEL), jnp.float32)] * 2,
+        compiler_params=pltpu.CompilerParams(vmem_limit_bytes=52 * MIB),
+    )(place, sums, by_core, panel, field)
     return out.reshape(4, 16, 32, 128)
 
 
@@ -382,13 +387,9 @@
     blocks, field = gather_panel(turn(back, 1), turn(back, 8))
     panel, terms = products(place, blocks, field)
     mine = jnp.sum(lax.all_to_all(terms, SPACE, 0, 0, tiled=True), axis=0)
-    sums = lax.all_to_all(jnp.broadcast_to(mine, (8, 32, PANEL)), SPACE, 0, 0, tiled=True)
-    piece = sums[:, :16]
-    by_core = lax.ppermute(piece, "c", ring(2, 1))
-    by_x = lax.ppermute(piece, "xl", ring(2, 1))
-    by_both = lax.ppermute(by_x, "c", ring(2, 1))
-    inverse = inverse_factor(place, (piece, by_x, by_core, by_both))
-    return update(place, inverse, sums, panel, field)
+    sums = lax.all_to_all(jnp.broadcast_to(mine, (8, 16, 1152)), SPACE, 0, 0, tiled=True)
+    by_core = lax.ppermute(sums[:, :, :640], "c", ring(2, 1))
+    return update(place, sums, by_core, panel, field)
 
 
 def solution(mesh):

time: 188 us -> 184 us (0.979)
  waiting for transfers between devices: 25.9 us -> 16.9 us
  Pallas kernels: 55.2 us -> 57.7 us
  local copies, waits for them, and re-layouts: 3.32 us -> 1.13 us
  blocking collectives: 69.2 us -> 71.2 us
  starting transfers between devices: 33.4 us -> 35.4 us
    pallas_call x1, Pallas kernels: 7.71 us -> 31.2 us  [update(): pl.pallas_call(update_kernel, grid=(8,), in_specs=[pl.BlockSpec(memory_sp...]
    pallas_call x1 -> x0, Pallas kernels: 22.3 us -> none  [inverse_factor(): pl.pallas_call(inverse_kernel, in_specs=[pl.BlockSpec(memory_space=pltpu....]
    ppermute x7, starting transfers between devices: 8.38 us -> 14.5 us  [gather_panel(): swaps = [lax.ppermute(block, 'c', ring(2, 1)) for block in waiting]]
    ppermute x3, waiting for transfers between devices: 11.4 us -> 6.72 us  [gather_panel(): right = lax.ppermute(right, 'z', ring(8, 1))]
    ppermute x4 -> x2, starting transfers between devices: 7.19 us -> 3.02 us  [the longest x1 2.63 us: per_device(): by_core = lax.ppermute(sums[:, :, :640], 'c', ring(2, 1))]
    ppermute x4 -> x2, waiting for transfers between devices: 6.81 us -> 2.95 us  [the longest x1 1.69 us: gather_panel(): lax.ppermute(own, 'xl', ring(2, 1))]
    unnamed x37 -> x33, local copies, waits for them, and re-layouts: 3.22 us -> 1.04 us
  transfers between devices with their start and end apart: 20 -> 18, of which waited for: 11 -> 8; matrix products, arithmetic and copies ran while one was open for 0% -> 0% of each run, Pallas kernels for 0% -> 0%
where the time goes in v6:
time: 184 us; the launch traced here: 183 us
  blocking collectives  71.2 us (39%)
  Pallas kernels  57.7 us (31%)
  starting transfers between devices  35.4 us (19%)
  waiting for transfers between devices  16.9 us (9%)
    pallas_call x1, Pallas kernels, update(): pl.pallas_call(update_kernel, grid=(8,), in_specs=[pl.BlockSpec(memory_sp...  31.2 us
    all_to_all x1, blocking collectives, per_device(): lax.all_to_all(pack(orbitals, potential), SPACE, 0, 0, tiled=True)  24.2 us
    all_to_all x1, blocking collectives, per_device(): back = lax.all_to_all(chebyshev(received), SPACE, 0, 0, tiled=True)  17.8 us
    all_to_all x1, blocking collectives, per_device(): mine = jnp.sum(lax.all_to_all(terms, SPACE, 0, 0, tiled=True), axis=0)  15.3 us
    ppermute x7, starting transfers between devices, gather_panel(): swaps = [lax.ppermute(block, 'c', ring(2, 1)) for block in waiting]  14.5 us
    all_to_all x1, blocking collectives, per_device(): lax.all_to_all(jnp.broadcast_to(mine, (8, 16, 1152)), SPACE, 0, 0, tiled=...  13.9 us
    ppermute x3, starting transfers between devices, gather_panel(): left = lax.ppermute(left, 'z', ring(8, -1))  12.1 us
    pallas_call x1, Pallas kernels, chebyshev(): pl.pallas_call(filter_kernel, out_shape=jax.ShapeDtypeStruct((64, 32, 128...  11.3 us
  transfers between devices with their start and end apart: 18, of which 8 were waited for; matrix products, arithmetic and copies ran while one was open for 0% of the time, Pallas kernels for 0%

profile of v6, /device:TPU:1, one launch (start us, length us, event | category | flops | bytes accessed | tf_op | source)
XLA Modules:
  0.0 183.3 jit_solution(12437542355122105299)
XLA Ops:
  0.0 4.2 %shard_map.28 = f32[8,272,128]{2,1,0:T(8,128)} custom-call(f32[4,16,32,128]{3,2,1,0:T(8,128)} %orb_ref.1, f32[4,16,32]{2,1,0:T(8,128)} %pot_ref.1), custom_call_target="tpu_custom_call" | custom-call | tf_op jit(solution)/shard_map/pallas_call | solution.py:62
  4.2 24.2 %all_to_all.20.in_ref = f32[8,272,128]{2,1,0:T(8,128)S(1)} all-to-all(f32[8,272,128]{2,1,0:T(8,128)} %shard_map.28), channel_id=1, replica_groups=mesh['y'=4,'xh'=2,'xl'=2,'z'=8,'c'=2] {'y','xh'}, dimensions={0} | all-to-all | bytes 2228224 | tf_op jit(solution)/shard_map/all_to_all | solution.py:385
  28.4 11.3 %shard_map.29 = f32[64,32,128]{2,1,0:T(8,128)S(1)} custom-call(f32[8,272,128]{2,1,0:T(8,128)S(1)} %all_to_all.20.in_ref), custom_call_target="tpu_custom_call" | custom-call | tf_op jit(solution)/shard_map/pallas_call | solution.py:143
  39.7 17.8 %all_to_all.21.in_ref = f32[8,256,128]{2,1,0:T(8,128)S(1)} all-to-all(f32[8,256,128]{2,1,0:T(8,128)S(1)} %bitcast.5), channel_id=1, replica_groups=mesh['y'=4,'xh'=2,'xl'=2,'z'=8,'c'=2] {'y','xh'}, dimensions={0} | all-to-all | bytes 2097152 | tf_op jit(solution)/shard_map/all_to_all | solution.py:386
  58.9 1.0 copy-done
  59.9 1.7 collective-permute-done
  61.6 5.6 %collective-permute-start.2 = (f32[32,2048]{1,0:T(8,128)S(1)}, f32[32,2048]{1,0:T(8,128)S(1)}, u32[]{:S(2)}, u32[]{:S(2)}) collective-permute-start(f32[32,2048]{1,0:T(8,128)S(1)} %pad_maximum_fusion.refs_0_), channel_id=1, source_target_pairs={{0,14},{2,0},{4,2},{6,4},{8,6},{10,8},{12,10},{14,12},{1,15},{3,1}... | collective-permute-start | bytes 786440 | tf_op jit(solution)/shard_map/ppermute | solution.py:182
  67.2 4.6 %collective-permute-start.5 = (f32[32,2048]{1,0:T(8,128)S(1)}, f32[32,2048]{1,0:T(8,128)S(1)}, u32[]{:S(2)}, u32[]{:S(2)}) collective-permute-start(f32[32,2048]{1,0:T(8,128)S(1)} %pad_maximum_fusion.refs_0_), channel_id=1, source_target_pairs={{0,1},{1,0},{2,3},{3,2},{4,5},{5,4},{6,7},{7,6},{8,9},{9,8},{10,11... | collective-permute-start | bytes 786440 | tf_op jit(solution)/shard_map/ppermute | solution.py:179
  71.9 1.8 collective-permute-done.1.refs_1_
  73.7 7.2 %collective-permute-start.7 = (f32[32,2048]{1,0:T(8,128)S(1)}, f32[32,2048]{1,0:T(8,128)S(1)}, u32[]{:S(2)}, u32[]{:S(2)}) collective-permute-start(f32[32,2048]{1,0:T(8,128)S(1)} %collective-permute-done.2.refs_2_), channel_id=1, source_target_pairs={{0,1},{1,0},{2,3},{3,2},{4,5},{5,4},{6,7},{7,6},{8,9},{9,8},{10,11... | collective-permute-start | bytes 786440 | tf_op jit(solution)/shard_map/ppermute | solution.py:179
  80.8 3.0 %collective-permute-start.4 = (f32[32,2048]{1,0:T(8,128)S(1)}, f32[32,2048]{1,0:T(8,128)S(1)}, u32[]{:S(2)}, u32[]{:S(2)}) collective-permute-start(f32[32,2048]{1,0:T(8,128)S(1)} %collective-permute-done.2.refs_2_), channel_id=1, source_target_pairs={{0,14},{2,0},{4,2},{6,4},{8,6},{10,8},{12,10},{14,12},{1,15},{3,1}... | collective-permute-start | bytes 786440 | tf_op jit(solution)/shard_map/ppermute | solution.py:182
  84.1 5.4 %collective-permute-done.4.refs_4_ = f32[32,2048]{1,0:T(8,128)S(1)} collective-permute-done((f32[32,2048]{1,0:T(8,128)S(1)}, f32[32,2048]{1,0:T(8,128)S(1)}, u32[]{:S(2)}, u32[]{:S(2)}) %collective-permute-start.4) | collective-permute-done | bytes 262176 | tf_op jit(solution)/shard_map/ppermute | solution.py:182
  89.5 0.9 collective-permute-start.10
  90.5 3.5 %collective-permute-start.9 = (f32[32,2048]{1,0:T(8,128)S(1)}, f32[32,2048]{1,0:T(8,128)S(1)}, u32[]{:S(2)}, u32[]{:S(2)}) collective-permute-start(f32[32,2048]{1,0:T(8,128)S(1)} %collective-permute-done.4.refs_4_), channel_id=1, source_target_pairs={{0,14},{2,0},{4,2},{6,4},{8,6},{10,8},{12,10},{14,12},{1,15},{3,1}... | collective-permute-start | bytes 786440 | tf_op jit(solution)/shard_map/ppermute | solution.py:182
  94.0 4.9 %collective-permute-done.8.refs_5_ = f32[32,2048]{1,0:T(8,128)S(1)} collective-permute-done((f32[32,2048]{1,0:T(8,128)S(1)}, f32[32,2048]{1,0:T(8,128)S(1)}, u32[]{:S(2)}, u32[]{:S(2)}) %collective-permute-start.8) | collective-permute-done | bytes 262176 | tf_op jit(solution)/shard_map/ppermute | solution.py:181
  99.4 3.4 %collective-permute-start.13 = (f32[16,2048]{1,0:T(8,128)S(1)}, f32[16,2048]{1,0:T(8,128)S(1)}, u32[]{:S(2)}, u32[]{:S(2)}) collective-permute-start(f32[16,2048]{1,0:T(8,128)S(1)} %slice.10), channel_id=1, source_target_pairs={{0,14},{2,0},{4,2},{6,4},{8,6},{10,8},{12,10},{14,12},{1,15},{3,1}... | collective-permute-start | bytes 393224 | tf_op jit(solution)/shard_map/ppermute | solution.py:187
  102.9 1.5 collective-permute-start.14
  105.2 2.2 %collective-permute-start.16 = (f32[32,2048]{1,0:T(8,128)S(1)}, f32[32,2048]{1,0:T(8,128)}, u32[]{:S(2)}, u32[]{:S(2)}) collective-permute-start(f32[32,2048]{1,0:T(8,128)S(1)} %constant_dynamic-update-slice_fusion.refs_7_), channel_id=1, source_target_pairs={{0,1},{1,0},{2,3},{3,2},{4,5},{5,4},{6,7},{7,6},{8,9},{9,8},{10,11... | collective-permute-start | bytes 786440 | tf_op jit(solution)/shard_map/ppermute | solution.py:191
  108.8 10.0 %shard_map.32 = (f32[512,2048]{1,0:T(8,128)}, f32[8,16,1152]{2,1,0:T(8,128)}) custom-call(s32[3]{0:T(128)} %pad_add_fusion.place_ref, f32[32,2048]{1,0:T(8,128)} %copy-done.3, f32[32,2048]{1,0:T(8,128)} %copy-done.8, f32[32,2048]{1,0:T(8,128)} %copy-done.7, f32[32,2048]{1,0:T(8,128)} %copy-done.10, f32[32,2048]{1,0:T(8,128)} %copy-done.12, ...), custom_call_target="tpu_custom_call" | custom-call | tf_op jit(solution)/shard_map/pallas_call | solution.py:239
  118.8 15.3 %all_to_all.22 = f32[8,16,1152]{2,1,0:T(8,128)S(1)} all-to-all(f32[8,16,1152]{2,1,0:T(8,128)} %get-tuple-element.37), channel_id=1, replica_groups=mesh['y'=4,'xh'=2,'xl'=2,'z'=8,'c'=2] {'y','xh'}, dimensions={0} | all-to-all | bytes 1179648 | tf_op jit(solution)/shard_map/all_to_all | solution.py:389
  134.2 13.9 %all_to_all.23.sums_ref = f32[8,16,1152]{2,1,0:T(8,128)S(1)} all-to-all(f32[8,16,1152]{2,1,0:T(8,128)S(1)} %broadcast_in_dim.3), channel_id=1, replica_groups=mesh['y'=4,'xh'=2,'xl'=2,'z'=8,'c'=2] {'y','xh'}, dimensions={0} | all-to-all | bytes 1179648 | tf_op jit(solution)/shard_map/all_to_all | solution.py:390
  148.2 2.6 %collective-permute-start.17 = (f32[8,16,640]{2,1,0:T(8,128)S(1)}, f32[8,16,640]{2,1,0:T(8,128)S(1)}, u32[]{:S(2)}, u32[]{:S(2)}) collective-permute-start(f32[8,16,640]{2,1,0:T(8,128)S(1)} %slice.12), channel_id=1, source_target_pairs={{0,1},{1,0},{2,3},{3,2},{4,5},{5,4},{6,7},{7,6},{8,9},{9,8},{10,11... | collective-permute-start | bytes 983048 | tf_op jit(solution)/shard_map/ppermute | solution.py:391
  150.8 1.3 collective-permute-done.17.by_core_ref
  152.1 31.2 %shard_map.33 = f32[4,2,8,32,128]{4,3,2,1,0:T(8,128)} custom-call(s32[3]{0:T(128)S(1)} %copy-done.2, f32[8,16,1152]{2,1,0:T(8,128)S(1)} %all_to_all.23.sums_ref, f32[8,16,640]{2,1,0:T(8,128)S(1)} %collective-permute-done.17.by_core_ref, f32[512,2048]{1,0:T(8,128)} %get-tuple-element.38.panel_ref, f32[128,2048]{1,0:T(8,128)S(1)} %copy-done.1), custom_call_target="tpu_custom_call" | custom-call | tf_op jit(solution)/shard_map/pallas_call | solution.py:364
  (63 shorter events, 4.5 us)
Async XLA Ops:
  57.6 3.9 %collective-permute-start = (f32[16,2048]{1,0:T(8,128)S(1)}, f32[16,2048]{1,0:T(8,128)S(1)}, u32[]{:S(2)}, u32[]{:S(2)}) collective-permute-start(f32[16,2048]{1,0:T(8,128)S(1)} %shard_map.30), channel_id=1, source_target_pairs={{0,16},{16,0},{1,17},{17,1},{2,18},{18,2},{3,19},{19,3},{4,20},{20... | collective-permute-start | bytes 393224 | tf_op jit(solution)/shard_map/ppermute | solution.py:175
  61.6 47.1 %copy-start.3 = (f32[32,2048]{1,0:T(8,128)}, f32[32,2048]{1,0:T(8,128)S(1)}, u32[]{:S(2)}) copy-start(f32[32,2048]{1,0:T(8,128)S(1)} %pad_maximum_fusion.refs_0_) | copy-start | bytes 786436
  61.6 10.3 %collective-permute-start.2 = (f32[32,2048]{1,0:T(8,128)S(1)}, f32[32,2048]{1,0:T(8,128)S(1)}, u32[]{:S(2)}, u32[]{:S(2)}) collective-permute-start(f32[32,2048]{1,0:T(8,128)S(1)} %pad_maximum_fusion.refs_0_), channel_id=1, source_target_pairs={{0,14},{2,0},{4,2},{6,4},{8,6},{10,8},{12,10},{14,12},{1,15},{3,1}... | collective-permute-start | bytes 786440 | tf_op jit(solution)/shard_map/ppermute | solution.py:182
  67.2 6.4 %collective-permute-start.1 = (f32[32,2048]{1,0:T(8,128)S(1)}, f32[32,2048]{1,0:T(8,128)S(1)}, u32[]{:S(2)}, u32[]{:S(2)}) collective-permute-start(f32[32,2048]{1,0:T(8,128)S(1)} %pad_maximum_fusion.refs_0_), channel_id=1, source_target_pairs={{0,2},{2,4},{4,6},{6,8},{8,10},{10,12},{12,14},{14,0},{1,3},{3,5},... | collective-permute-start | bytes 786440 | tf_op jit(solution)/shard_map/ppermute | solution.py:181
  67.2 16.8 %collective-permute-start.5 = (f32[32,2048]{1,0:T(8,128)S(1)}, f32[32,2048]{1,0:T(8,128)S(1)}, u32[]{:S(2)}, u32[]{:S(2)}) collective-permute-start(f32[32,2048]{1,0:T(8,128)S(1)} %pad_maximum_fusion.refs_0_), channel_id=1, source_target_pairs={{0,1},{1,0},{2,3},{3,2},{4,5},{5,4},{6,7},{7,6},{8,9},{9,8},{10,11... | collective-permute-start | bytes 786440 | tf_op jit(solution)/shard_map/ppermute | solution.py:179
  71.9 36.8 %copy-start.7 = (f32[32,2048]{1,0:T(8,128)}, f32[32,2048]{1,0:T(8,128)S(1)}, u32[]{:S(2)}) copy-start(f32[32,2048]{1,0:T(8,128)S(1)} %collective-permute-done.2.refs_2_) | copy-start | bytes 786436
  73.7 35.0 %copy-start.8 = (f32[32,2048]{1,0:T(8,128)}, f32[32,2048]{1,0:T(8,128)S(1)}, u32[]{:S(2)}) copy-start(f32[32,2048]{1,0:T(8,128)S(1)} %collective-permute-done.1.refs_1_) | copy-start | bytes 786436
  73.7 10.4 %collective-permute-start.3 = (f32[32,2048]{1,0:T(8,128)S(1)}, f32[32,2048]{1,0:T(8,128)S(1)}, u32[]{:S(2)}, u32[]{:S(2)}) collective-permute-start(f32[32,2048]{1,0:T(8,128)S(1)} %collective-permute-done.1.refs_1_), channel_id=1, source_target_pairs={{0,2},{2,4},{4,6},{6,8},{8,10},{10,12},{12,14},{14,0},{1,3},{3,5},... | collective-permute-start | bytes 786440 | tf_op jit(solution)/shard_map/ppermute | solution.py:181
  73.7 10.4 %collective-permute-start.7 = (f32[32,2048]{1,0:T(8,128)S(1)}, f32[32,2048]{1,0:T(8,128)S(1)}, u32[]{:S(2)}, u32[]{:S(2)}) collective-permute-start(f32[32,2048]{1,0:T(8,128)S(1)} %collective-permute-done.2.refs_2_), channel_id=1, source_target_pairs={{0,1},{1,0},{2,3},{3,2},{4,5},{5,4},{6,7},{7,6},{8,9},{9,8},{10,11... | collective-permute-start | bytes 786440 | tf_op jit(solution)/shard_map/ppermute | solution.py:179
  80.8 8.7 %collective-permute-start.4 = (f32[32,2048]{1,0:T(8,128)S(1)}, f32[32,2048]{1,0:T(8,128)S(1)}, u32[]{:S(2)}, u32[]{:S(2)}) collective-permute-start(f32[32,2048]{1,0:T(8,128)S(1)} %collective-permute-done.2.refs_2_), channel_id=1, source_target_pairs={{0,14},{2,0},{4,2},{6,4},{8,6},{10,8},{12,10},{14,12},{1,15},{3,1}... | collective-permute-start | bytes 786440 | tf_op jit(solution)/shard_map/ppermute | solution.py:182
  83.8 5.7 %collective-permute-start.6 = (f32[32,2048]{1,0:T(8,128)S(1)}, f32[32,2048]{1,0:T(8,128)S(1)}, u32[]{:S(2)}, u32[]{:S(2)}) collective-permute-start(f32[32,2048]{1,0:T(8,128)S(1)} %collective-permute-done.1.refs_1_), channel_id=1, source_target_pairs={{0,1},{1,0},{2,3},{3,2},{4,5},{5,4},{6,7},{7,6},{8,9},{9,8},{10,11... | collective-permute-start | bytes 786440 | tf_op jit(solution)/shard_map/ppermute | solution.py:179
  84.1 24.6 %copy-start.9 = (f32[32,2048]{1,0:T(8,128)}, f32[32,2048]{1,0:T(8,128)S(1)}, u32[]{:S(2)}) copy-start(f32[32,2048]{1,0:T(8,128)S(1)} %collective-permute-done.5.refs_8_) | copy-start | bytes 786436
  84.1 24.6 %copy-start.11 = (f32[32,2048]{1,0:T(8,128)}, f32[32,2048]{1,0:T(8,128)S(1)}, u32[]{:S(2)}) copy-start(f32[32,2048]{1,0:T(8,128)S(1)} %collective-permute-done.7.refs_10_) | copy-start | bytes 786436
  84.1 24.6 %copy-start.10 = (f32[32,2048]{1,0:T(8,128)}, f32[32,2048]{1,0:T(8,128)S(1)}, u32[]{:S(2)}) copy-start(f32[32,2048]{1,0:T(8,128)S(1)} %collective-permute-done.3.refs_3_) | copy-start | bytes 786436
  89.5 9.4 %collective-permute-start.8 = (f32[32,2048]{1,0:T(8,128)S(1)}, f32[32,2048]{1,0:T(8,128)S(1)}, u32[]{:S(2)}, u32[]{:S(2)}) collective-permute-start(f32[32,2048]{1,0:T(8,128)S(1)} %collective-permute-done.3.refs_3_), channel_id=1, source_target_pairs={{0,2},{2,4},{4,6},{6,8},{8,10},{10,12},{12,14},{14,0},{1,3},{3,5},... | collective-permute-start | bytes 786440 | tf_op jit(solution)/shard_map/ppermute | solution.py:181
  89.5 4.5 %collective-permute-start.10 = (f32[32,2048]{1,0:T(8,128)S(1)}, f32[32,2048]{1,0:T(8,128)S(1)}, u32[]{:S(2)}, u32[]{:S(2)}) collective-permute-start(f32[32,2048]{1,0:T(8,128)S(1)} %collective-permute-done.3.refs_3_), channel_id=1, source_target_pairs={{0,1},{1,0},{2,3},{3,2},{4,5},{5,4},{6,7},{7,6},{8,9},{9,8},{10,11... | collective-permute-start | bytes 786440 | tf_op jit(solution)/shard_map/ppermute | solution.py:179
  90.4 3.6 %collective-permute-start.11 = (f32[32,2048]{1,0:T(8,128)S(1)}, f32[32,2048]{1,0:T(8,128)S(1)}, u32[]{:S(2)}, u32[]{:S(2)}) collective-permute-start(f32[32,2048]{1,0:T(8,128)S(1)} %collective-permute-done.4.refs_4_), channel_id=1, source_target_pairs={{0,1},{1,0},{2,3},{3,2},{4,5},{5,4},{6,7},{7,6},{8,9},{9,8},{10,11... | collective-permute-start | bytes 786440 | tf_op jit(solution)/shard_map/ppermute | solution.py:179
  90.5 8.8 %collective-permute-start.9 = (f32[32,2048]{1,0:T(8,128)S(1)}, f32[32,2048]{1,0:T(8,128)S(1)}, u32[]{:S(2)}, u32[]{:S(2)}) collective-permute-start(f32[32,2048]{1,0:T(8,128)S(1)} %collective-permute-done.4.refs_4_), channel_id=1, source_target_pairs={{0,14},{2,0},{4,2},{6,4},{8,6},{10,8},{12,10},{14,12},{1,15},{3,1}... | collective-permute-start | bytes 786440 | tf_op jit(solution)/shard_map/ppermute | solution.py:182
  99.3 5.8 %collective-permute-start.12 = (f32[16,2048]{1,0:T(8,128)S(1)}, f32[16,2048]{1,0:T(8,128)S(1)}, u32[]{:S(2)}, u32[]{:S(2)}) collective-permute-start(f32[16,2048]{1,0:T(8,128)S(1)} %slice.9), channel_id=1, source_target_pairs={{0,2},{2,4},{4,6},{6,8},{8,10},{10,12},{12,14},{14,0},{1,3},{3,5},... | collective-permute-start | bytes 393224 | tf_op jit(solution)/shard_map/ppermute | solution.py:186
  99.4 5.7 %collective-permute-start.13 = (f32[16,2048]{1,0:T(8,128)S(1)}, f32[16,2048]{1,0:T(8,128)S(1)}, u32[]{:S(2)}, u32[]{:S(2)}) collective-permute-start(f32[16,2048]{1,0:T(8,128)S(1)} %slice.10), channel_id=1, source_target_pairs={{0,14},{2,0},{4,2},{6,4},{8,6},{10,8},{12,10},{14,12},{1,15},{3,1}... | collective-permute-start | bytes 393224 | tf_op jit(solution)/shard_map/ppermute | solution.py:187
  102.9 5.1 %collective-permute-start.14 = (f32[32,2048]{1,0:T(8,128)S(1)}, f32[32,2048]{1,0:T(8,128)}, u32[]{:S(2)}, u32[]{:S(2)}) collective-permute-start(f32[32,2048]{1,0:T(8,128)S(1)} %collective-permute-done.8.refs_5_), channel_id=1, source_target_pairs={{0,1},{1,0},{2,3},{3,2},{4,5},{5,4},{6,7},{7,6},{8,9},{9,8},{10,11... | collective-permute-start | bytes 786440 | tf_op jit(solution)/shard_map/ppermute | solution.py:179
  104.4 3.6 %collective-permute-start.15 = (f32[32,2048]{1,0:T(8,128)S(1)}, f32[32,2048]{1,0:T(8,128)}, u32[]{:S(2)}, u32[]{:S(2)}) collective-permute-start(f32[32,2048]{1,0:T(8,128)S(1)} %collective-permute-done.9.refs_6_), channel_id=1, source_target_pairs={{0,1},{1,0},{2,3},{3,2},{4,5},{5,4},{6,7},{7,6},{8,9},{9,8},{10,11... | collective-permute-start | bytes 786440 | tf_op jit(solution)/shard_map/ppermute | solution.py:179
  105.2 3.5 %collective-permute-start.16 = (f32[32,2048]{1,0:T(8,128)S(1)}, f32[32,2048]{1,0:T(8,128)}, u32[]{:S(2)}, u32[]{:S(2)}) collective-permute-start(f32[32,2048]{1,0:T(8,128)S(1)} %constant_dynamic-update-slice_fusion.refs_7_), channel_id=1, source_target_pairs={{0,1},{1,0},{2,3},{3,2},{4,5},{5,4},{6,7},{7,6},{8,9},{9,8},{10,11... | collective-permute-start | bytes 786440 | tf_op jit(solution)/shard_map/ppermute | solution.py:191
  148.2 3.9 %collective-permute-start.17 = (f32[8,16,640]{2,1,0:T(8,128)S(1)}, f32[8,16,640]{2,1,0:T(8,128)S(1)}, u32[]{:S(2)}, u32[]{:S(2)}) collective-permute-start(f32[8,16,640]{2,1,0:T(8,128)S(1)} %slice.12), channel_id=1, source_target_pairs={{0,1},{1,0},{2,3},{3,2},{4,5},{5,4},{6,7},{7,6},{8,9},{9,8},{10,11... | collective-permute-start | bytes 983048 | tf_op jit(solution)/shard_map/ppermute | solution.py:391
  (10 other events, 127.5 us)

commit v7 on v6

--- a/solution.py
+++ b/solution.py
@@ -171,24 +171,30 @@
     return [(i, (i + step) % count) for i in range(count)]
 
 
-def gather_panel(own, field):
-    other, field = lax.optimization_barrier((lax.ppermute(own, "xl", ring(2, 1)), field))
-    right = left = pair = jnp.concatenate([own, other], axis=0)
-    found, swapped, waiting = [pair], [], []
-    for step in range(4):
-        swaps = [lax.ppermute(block, "c", ring(2, 1)) for block in waiting]
-        if step < 3:
-            right = lax.ppermute(right, "z", ring(8, 1))
-            left = lax.ppermute(left, "z", ring(8, -1))
-            waiting = [right, left] if step else [pair, right, left]
-            found += [right, left]
-        else:
-            far_r = lax.ppermute(right[:16], "z", ring(8, 1))
-            far_l = lax.ppermute(left[16:], "z", ring(8, -1))
-            found.append(jnp.concatenate([far_r, far_l], axis=0))
-        right, left, swaps = lax.optimization_barrier((right, left, swaps))
-        swapped += swaps
-    return found + swapped + [lax.ppermute(found[-1], "c", ring(2, 1))], field
+def gather_panel(own, field, xl):
+    def right(block):
+        return lax.ppermute(block, "z", ring(8, 1))
+
+    def left(block):
+        return lax.ppermute(block, "z", ring(8, -1))
+
+    def swap(block):
+        return lax.ppermute(block, "c", ring(2, 1))
+
+    then = lax.optimization_barrier
+    other, field = then((lax.ppermute(own, "xl", ring(2, 1)), field))
+    pair = jnp.concatenate([jnp.where(xl == 0, own, other), jnp.where(xl == 0, other, own)], axis=0)
+    right1, left1 = right(pair), left(pair)
+    next_r, pair_s = then((right1, swap(pair)))
+    right2, left2 = right(next_r), left(left1)
+    next_r, right1_s = then((right2, swap(right1)))
+    next_l, left1_s = then((left2, swap(left1)))
+    right3, left3 = right(next_r), left(next_l)
+    next_r, right2_s = then((right3, swap(right2)))
+    next_l, left2_s = then((left3, swap(left2)))
+    far = jnp.concatenate([right(next_r[:16]), left(next_l[16:])], axis=0)
+    here = [pair, right1, left1, right2, left2, right3, left3, far]
+    return here + [pair_s, right1_s, left1_s, right2_s, left2_s, swap(right3), swap(left3), swap(far)], field
 
 
 OFFSETS = (0, -1, 1, -2, 2, -3, 3, 4)
@@ -196,33 +202,31 @@
 
 def products_kernel(place_ref, *refs):
     blocks, (field_ref, home_ref, out_ref, panel_ref, acc, sems) = refs[:16], refs[16:]
-    xl, z, core = place_ref[0], place_ref[1], place_ref[2]
+    z, core = place_ref[1], place_ref[2]
     copies = []
     for half in range(2):
         points = pl.ds(half * 1024, 1024)
         for flip in range(2):
             for k, offset in enumerate(OFFSETS):
-                for xo in range(2):
-                    owner = (xl ^ xo) * 16 + ((z + offset) & 7) * 2 + (core ^ flip)
-                    rows = pl.ds(pl.multiple_of(owner * 16, 16), 16)
-                    source = blocks[flip * 8 + k].at[pl.ds(xo * 16, 16), points]
-                    copies.append(pltpu.make_async_copy(source, panel_ref.at[rows, points], sems.at[len(copies)]))
-                    copies[-1].start()
-    long = pl.ds(pl.multiple_of((3 - core) * 128, 128), 128)
+                first = (((z + offset) & 7) * 2 + (core ^ flip)) * 16
+                target = panel_ref.at[:, pl.ds(pl.multiple_of(first, 16), 16), points]
+                copies.append(pltpu.make_async_copy(blocks[flip * 8 + k].at[:, :, points], target, sems.at[len(copies)]))
+                copies[-1].start()
+    long = pl.ds(pl.multiple_of((1 - core) * 128, 128), 128)
     short = pl.ds(pl.multiple_of(core * 128, 128), 128)
     acc[...] = jnp.zeros_like(acc)
 
     def chunk(i, _):
         points = pl.ds(pl.multiple_of(i * 512, 512), 512)
-        rows = jnp.concatenate([panel_ref[long, points], panel_ref[short, points], field_ref[:, points]], axis=0)
-        acc[...] += dot_nt(rows, panel_ref[:, points])
+        rows = jnp.concatenate([panel_ref[1, long, points], panel_ref[0, short, points], field_ref[:, points]], axis=0)
+        acc[...] += dot_nt(rows, panel_ref[:, :, points].reshape(PANEL, 512))
         return 0
 
     for half in range(2):
-        for copy in copies[half * 32 : half * 32 + 32]:
+        for copy in copies[half * 16 : half * 16 + 16]:
             copy.wait()
         if half:
-            home = pltpu.make_async_copy(panel_ref, home_ref, sems.at[64])
+            home = pltpu.make_async_copy(panel_ref, home_ref, sems.at[32])
             home.start()
         lax.fori_loop(half * 2, half * 2 + 2, chunk, 0)
     for s in range(8):
@@ -236,20 +240,21 @@
 
 
 def products(place, blocks, field):
-    return pl.pallas_call(
+    panel, terms = pl.pallas_call(
         products_kernel,
         in_specs=[pl.BlockSpec(memory_space=pltpu.SMEM)]
         + [pl.BlockSpec(memory_space=pl.ANY)] * 16
         + [pl.BlockSpec(memory_space=pltpu.VMEM)],
-        out_shape=(jax.ShapeDtypeStruct((512, 2048), jnp.float32), jax.ShapeDtypeStruct((8, 16, 1152), jnp.float32)),
+        out_shape=(jax.ShapeDtypeStruct((2, 256, 2048), jnp.float32), jax.ShapeDtypeStruct((8, 16, 1152), jnp.float32)),
         out_specs=(pl.BlockSpec(memory_space=pl.ANY), pl.BlockSpec(memory_space=pltpu.VMEM)),
         scratch_shapes=[
-            pltpu.VMEM((512, 2048), jnp.float32),
+            pltpu.VMEM((2, 256, 2048), jnp.float32),
             pltpu.VMEM((384, 512), jnp.float32),
-            pltpu.SemaphoreType.DMA((65,)),
+            pltpu.SemaphoreType.DMA((33,)),
         ],
         compiler_params=pltpu.CompilerParams(vmem_limit_bytes=BIG * MIB),
-    )(place, *blocks, field)
+    )(place, *(block.reshape(2, 16, 2048) for block in blocks), field)
+    return panel.reshape(PANEL, 2048), terms
 
 
 def total_of(terms):
@@ -384,7 +389,7 @@
     place = jnp.stack([xl, z, core]).astype(jnp.int32)
     received = lax.all_to_all(pack(orbitals, potential), SPACE, 0, 0, tiled=True)
     back = lax.all_to_all(chebyshev(received), SPACE, 0, 0, tiled=True)
-    blocks, field = gather_panel(turn(back, 1), turn(back, 8))
+    blocks, field = gather_panel(turn(back, 1), turn(back, 8), xl)
     panel, terms = products(place, blocks, field)
     mine = jnp.sum(lax.all_to_all(terms, SPACE, 0, 0, tiled=True), axis=0)
     sums = lax.all_to_all(jnp.broadcast_to(mine, (8, 16, 1152)), SPACE, 0, 0, tiled=True)

time: 184 us -> 181 us (0.984)
  starting transfers between devices: 35.4 us -> 28.3 us
  waiting for transfers between devices: 16.9 us -> 21.2 us
    ppermute x17, starting transfers between devices: 32.8 us -> 25.7 us  [the longest x4 12.3 us: left(): return lax.ppermute(block, 'z', ring(8, -1))]
    ppermute x17, waiting for transfers between devices: 15.6 us -> 20 us  [the longest x4 17.5 us: right(): return lax.ppermute(block, 'z', ring(8, 1))]
  transfers between devices with their start and end apart: 18 -> 18, of which waited for: 8 -> 7; matrix products, arithmetic and copies ran while one was open for 0% -> 0% of each run, Pallas kernels for 0% -> 0%
where the time goes in v7:
time: 181 us; the launch traced here: 180 us
  blocking collectives  71.2 us (39%)
  Pallas kernels  57.4 us (32%)
  starting transfers between devices  28.3 us (16%)
  waiting for transfers between devices  21.2 us (12%)
    pallas_call x1, Pallas kernels, update(): pl.pallas_call(update_kernel, grid=(8,), in_specs=[pl.BlockSpec(memory_sp...  31.2 us
    all_to_all x1, blocking collectives, per_device(): lax.all_to_all(pack(orbitals, potential), SPACE, 0, 0, tiled=True)  24.2 us
    all_to_all x1, blocking collectives, per_device(): back = lax.all_to_all(chebyshev(received), SPACE, 0, 0, tiled=True)  17.8 us
    ppermute x4, waiting for transfers between devices, right(): return lax.ppermute(block, 'z', ring(8, 1))  17.5 us
    all_to_all x1, blocking collectives, per_device(): mine = jnp.sum(lax.all_to_all(terms, SPACE, 0, 0, tiled=True), axis=0)  15.3 us
    all_to_all x1, blocking collectives, per_device(): lax.all_to_all(jnp.broadcast_to(mine, (8, 16, 1152)), SPACE, 0, 0, tiled=...  13.9 us
    ppermute x4, starting transfers between devices, left(): return lax.ppermute(block, 'z', ring(8, -1))  12.3 us
    pallas_call x1, Pallas kernels, chebyshev(): pl.pallas_call(filter_kernel, out_shape=jax.ShapeDtypeStruct((64, 32, 128...  11.3 us
  transfers between devices with their start and end apart: 18, of which 7 were waited for; matrix products, arithmetic and copies ran while one was open for 0% of the time, Pallas kernels for 0%

profile of v7, /device:TPU:1, one launch (start us, length us, event | category | flops | bytes accessed | tf_op | source)
XLA Modules:
  0.0 180.3 jit_solution(2962669501707692637)
XLA Ops:
  0.0 4.2 %shard_map.28 = f32[8,272,128]{2,1,0:T(8,128)} custom-call(f32[4,16,32,128]{3,2,1,0:T(8,128)} %orb_ref.1, f32[4,16,32]{2,1,0:T(8,128)} %pot_ref.1), custom_call_target="tpu_custom_call" | custom-call | tf_op jit(solution)/shard_map/pallas_call | solution.py:62
  4.2 24.2 %all_to_all.20.in_ref = f32[8,272,128]{2,1,0:T(8,128)S(1)} all-to-all(f32[8,272,128]{2,1,0:T(8,128)} %shard_map.28), channel_id=1, replica_groups=mesh['y'=4,'xh'=2,'xl'=2,'z'=8,'c'=2] {'y','xh'}, dimensions={0} | all-to-all | bytes 2228224 | tf_op jit(solution)/shard_map/all_to_all | solution.py:390
  28.4 11.3 %shard_map.29 = f32[64,32,128]{2,1,0:T(8,128)S(1)} custom-call(f32[8,272,128]{2,1,0:T(8,128)S(1)} %all_to_all.20.in_ref), custom_call_target="tpu_custom_call" | custom-call | tf_op jit(solution)/shard_map/pallas_call | solution.py:143
  39.7 17.8 %all_to_all.21.in_ref = f32[8,256,128]{2,1,0:T(8,128)S(1)} all-to-all(f32[8,256,128]{2,1,0:T(8,128)S(1)} %bitcast.22), channel_id=1, replica_groups=mesh['y'=4,'xh'=2,'xl'=2,'z'=8,'c'=2] {'y','xh'}, dimensions={0} | all-to-all | bytes 2097152 | tf_op jit(solution)/shard_map/all_to_all | solution.py:391
  59.8 1.7 collective-permute-done
  61.6 4.4 %collective-permute-start.3 = (f32[32,2048]{1,0:T(8,128)S(1)}, f32[32,2048]{1,0:T(8,128)S(1)}, u32[]{:S(2)}, u32[]{:S(2)}) collective-permute-start(f32[32,2048]{1,0:T(8,128)S(1)} %pad_maximum_fusion), channel_id=1, source_target_pairs={{0,1},{1,0},{2,3},{3,2},{4,5},{5,4},{6,7},{7,6},{8,9},{9,8},{10,11... | collective-permute-start | bytes 786440 | tf_op jit(solution)/shard_map/ppermute | solution.py:182
  66.0 1.7 collective-permute-start.1
  67.7 3.9 %collective-permute-start.2 = (f32[32,2048]{1,0:T(8,128)S(1)}, f32[32,2048]{1,0:T(8,128)S(1)}, u32[]{:S(2)}, u32[]{:S(2)}) collective-permute-start(f32[32,2048]{1,0:T(8,128)S(1)} %pad_maximum_fusion), channel_id=1, source_target_pairs={{0,14},{2,0},{4,2},{6,4},{8,6},{10,8},{12,10},{14,12},{1,15},{3,1}... | collective-permute-start | bytes 786440 | tf_op jit(solution)/shard_map/ppermute | solution.py:179
  71.6 6.6 %collective-permute-done.1 = f32[32,2048]{1,0:T(8,128)S(1)} collective-permute-done((f32[32,2048]{1,0:T(8,128)S(1)}, f32[32,2048]{1,0:T(8,128)S(1)}, u32[]{:S(2)}, u32[]{:S(2)}) %collective-permute-start.1) | collective-permute-done | bytes 262176 | tf_op jit(solution)/shard_map/ppermute | solution.py:176
  79.0 2.9 %collective-permute-start.5 = (f32[32,2048]{1,0:T(8,128)S(1)}, f32[32,2048]{1,0:T(8,128)S(1)}, u32[]{:S(2)}, u32[]{:S(2)}) collective-permute-start(f32[32,2048]{1,0:T(8,128)S(1)} %collective-permute-done.2), channel_id=1, source_target_pairs={{0,14},{2,0},{4,2},{6,4},{8,6},{10,8},{12,10},{14,12},{1,15},{3,1}... | collective-permute-start | bytes 786440 | tf_op jit(solution)/shard_map/ppermute | solution.py:179
  81.9 4.7 %collective-permute-done.4 = f32[32,2048]{1,0:T(8,128)S(1)} collective-permute-done((f32[32,2048]{1,0:T(8,128)S(1)}, f32[32,2048]{1,0:T(8,128)S(1)}, u32[]{:S(2)}, u32[]{:S(2)}) %collective-permute-start.4) | collective-permute-done | bytes 262176 | tf_op jit(solution)/shard_map/ppermute | solution.py:176
  86.6 1.6 collective-permute-start.10
  88.2 2.8 %collective-permute-start.9 = (f32[32,2048]{1,0:T(8,128)S(1)}, f32[32,2048]{1,0:T(8,128)S(1)}, u32[]{:S(2)}, u32[]{:S(2)}) collective-permute-start(f32[32,2048]{1,0:T(8,128)S(1)} %collective-permute-done.5), channel_id=1, source_target_pairs={{0,14},{2,0},{4,2},{6,4},{8,6},{10,8},{12,10},{14,12},{1,15},{3,1}... | collective-permute-start | bytes 786440 | tf_op jit(solution)/shard_map/ppermute | solution.py:179
  92.1 5.2 %collective-permute-done.7 = f32[32,2048]{1,0:T(8,128)S(1)} collective-permute-done((f32[32,2048]{1,0:T(8,128)S(1)}, f32[32,2048]{1,0:T(8,128)S(1)}, u32[]{:S(2)}, u32[]{:S(2)}) %collective-permute-start.7) | collective-permute-done | bytes 262176 | tf_op jit(solution)/shard_map/ppermute | solution.py:176
  97.4 2.7 %collective-permute-start.13 = (f32[16,2048]{1,0:T(8,128)S(1)}, f32[16,2048]{1,0:T(8,128)S(1)}, u32[]{:S(2)}, u32[]{:S(2)}) collective-permute-start(f32[16,2048]{1,0:T(8,128)S(1)} %slice.10), channel_id=1, source_target_pairs={{0,14},{2,0},{4,2},{6,4},{8,6},{10,8},{12,10},{14,12},{1,15},{3,1}... | collective-permute-start | bytes 393224 | tf_op jit(solution)/shard_map/ppermute | solution.py:179
  100.2 1.4 collective-permute-start.15
  101.6 1.1 collective-permute-done.11
  102.8 1.9 %collective-permute-start.16 = (f32[32,2048]{1,0:T(8,128)S(1)}, f32[32,2048]{1,0:T(8,128)}, u32[]{:S(2)}, u32[]{:S(2)}) collective-permute-start(f32[32,2048]{1,0:T(8,128)S(1)} %constant_dynamic-update-slice_fusion), channel_id=1, source_target_pairs={{0,1},{1,0},{2,3},{3,2},{4,5},{5,4},{6,7},{7,6},{8,9},{9,8},{10,11... | collective-permute-start | bytes 786440 | tf_op jit(solution)/shard_map/ppermute | solution.py:182
  106.0 9.8 %shard_map.32 = (f32[2,256,2048]{2,1,0:T(8,128)}, f32[8,16,1152]{2,1,0:T(8,128)}) custom-call(s32[3]{0:T(128)} %pad_add_fusion.place_ref, f32[2,16,2048]{2,1,0:T(8,128)} %bitcast.24, f32[2,16,2048]{2,1,0:T(8,128)} %bitcast.29, f32[2,16,2048]{2,1,0:T(8,128)} %bitcast.30, f32[2,16,2048]{2,1,0:T(8,128)} %bitcast.31, f32[2,16,2048]{2,1,0:T(8,128)} %bitcast.34, ...), custom_call_target="tpu_custom_call" | custom-call | tf_op jit(solution)/shard_map/pallas_call | solution.py:243
  115.8 15.3 %all_to_all.22 = f32[8,16,1152]{2,1,0:T(8,128)S(1)} all-to-all(f32[8,16,1152]{2,1,0:T(8,128)} %get-tuple-element.31), channel_id=1, replica_groups=mesh['y'=4,'xh'=2,'xl'=2,'z'=8,'c'=2] {'y','xh'}, dimensions={0} | all-to-all | bytes 1179648 | tf_op jit(solution)/shard_map/all_to_all | solution.py:394
  131.2 13.9 %all_to_all.23.sums_ref = f32[8,16,1152]{2,1,0:T(8,128)S(1)} all-to-all(f32[8,16,1152]{2,1,0:T(8,128)S(1)} %broadcast_in_dim.3), channel_id=1, replica_groups=mesh['y'=4,'xh'=2,'xl'=2,'z'=8,'c'=2] {'y','xh'}, dimensions={0} | all-to-all | bytes 1179648 | tf_op jit(solution)/shard_map/all_to_all | solution.py:395
  145.2 2.6 %collective-permute-start.17 = (f32[8,16,640]{2,1,0:T(8,128)S(1)}, f32[8,16,640]{2,1,0:T(8,128)S(1)}, u32[]{:S(2)}, u32[]{:S(2)}) collective-permute-start(f32[8,16,640]{2,1,0:T(8,128)S(1)} %slice.12), channel_id=1, source_target_pairs={{0,1},{1,0},{2,3},{3,2},{4,5},{5,4},{6,7},{7,6},{8,9},{9,8},{10,11... | collective-permute-start | bytes 983048 | tf_op jit(solution)/shard_map/ppermute | solution.py:396
  147.8 1.3 collective-permute-done.17.by_core_ref
  149.1 31.2 %shard_map.33 = f32[4,2,8,32,128]{4,3,2,1,0:T(8,128)} custom-call(s32[3]{0:T(128)S(1)} %copy-done.2, f32[8,16,1152]{2,1,0:T(8,128)S(1)} %all_to_all.23.sums_ref, f32[8,16,640]{2,1,0:T(8,128)S(1)} %collective-permute-done.17.by_core_ref, f32[512,2048]{1,0:T(8,128)} %bitcast.23, f32[128,2048]{1,0:T(8,128)S(1)} %copy-done.1), custom_call_target="tpu_custom_call" | custom-call | tf_op jit(solution)/shard_map/pallas_call | solution.py:369
  (64 shorter events, 5.8 us)
Async XLA Ops:
  57.6 3.9 %collective-permute-start = (f32[16,2048]{1,0:T(8,128)S(1)}, f32[16,2048]{1,0:T(8,128)S(1)}, u32[]{:S(2)}, u32[]{:S(2)}) collective-permute-start(f32[16,2048]{1,0:T(8,128)S(1)} %shard_map.30), channel_id=1, source_target_pairs={{0,16},{16,0},{1,17},{17,1},{2,18},{18,2},{3,19},{19,3},{4,20},{20... | collective-permute-start | bytes 393224 | tf_op jit(solution)/shard_map/ppermute | solution.py:185
  61.6 44.3 %copy-start.3 = (f32[32,2048]{1,0:T(8,128)}, f32[32,2048]{1,0:T(8,128)S(1)}, u32[]{:S(2)}) copy-start(f32[32,2048]{1,0:T(8,128)S(1)} %pad_maximum_fusion) | copy-start | bytes 786436
  61.6 10.0 %collective-permute-start.3 = (f32[32,2048]{1,0:T(8,128)S(1)}, f32[32,2048]{1,0:T(8,128)S(1)}, u32[]{:S(2)}, u32[]{:S(2)}) collective-permute-start(f32[32,2048]{1,0:T(8,128)S(1)} %pad_maximum_fusion), channel_id=1, source_target_pairs={{0,1},{1,0},{2,3},{3,2},{4,5},{5,4},{6,7},{7,6},{8,9},{9,8},{10,11... | collective-permute-start | bytes 786440 | tf_op jit(solution)/shard_map/ppermute | solution.py:182
  66.0 12.2 %collective-permute-start.1 = (f32[32,2048]{1,0:T(8,128)S(1)}, f32[32,2048]{1,0:T(8,128)S(1)}, u32[]{:S(2)}, u32[]{:S(2)}) collective-permute-start(f32[32,2048]{1,0:T(8,128)S(1)} %pad_maximum_fusion), channel_id=1, source_target_pairs={{0,2},{2,4},{4,6},{6,8},{8,10},{10,12},{12,14},{14,0},{1,3},{3,5},... | collective-permute-start | bytes 786440 | tf_op jit(solution)/shard_map/ppermute | solution.py:176
  67.7 11.2 %collective-permute-start.2 = (f32[32,2048]{1,0:T(8,128)S(1)}, f32[32,2048]{1,0:T(8,128)S(1)}, u32[]{:S(2)}, u32[]{:S(2)}) collective-permute-start(f32[32,2048]{1,0:T(8,128)S(1)} %pad_maximum_fusion), channel_id=1, source_target_pairs={{0,14},{2,0},{4,2},{6,4},{8,6},{10,8},{12,10},{14,12},{1,15},{3,1}... | collective-permute-start | bytes 786440 | tf_op jit(solution)/shard_map/ppermute | solution.py:179
  71.6 34.3 %copy-start.7 = (f32[32,2048]{1,0:T(8,128)}, f32[32,2048]{1,0:T(8,128)S(1)}, u32[]{:S(2)}) copy-start(f32[32,2048]{1,0:T(8,128)S(1)} %collective-permute-done.3) | copy-start | bytes 786436
  78.2 27.8 %copy-start.8 = (f32[32,2048]{1,0:T(8,128)}, f32[32,2048]{1,0:T(8,128)S(1)}, u32[]{:S(2)}) copy-start(f32[32,2048]{1,0:T(8,128)S(1)} %collective-permute-done.1) | copy-start | bytes 786436
  78.2 8.4 %collective-permute-start.4 = (f32[32,2048]{1,0:T(8,128)S(1)}, f32[32,2048]{1,0:T(8,128)S(1)}, u32[]{:S(2)}, u32[]{:S(2)}) collective-permute-start(f32[32,2048]{1,0:T(8,128)S(1)} %collective-permute-done.1), channel_id=1, source_target_pairs={{0,2},{2,4},{4,6},{6,8},{8,10},{10,12},{12,14},{14,0},{1,3},{3,5},... | collective-permute-start | bytes 786440 | tf_op jit(solution)/shard_map/ppermute | solution.py:176
  78.2 8.4 %collective-permute-start.6 = (f32[32,2048]{1,0:T(8,128)S(1)}, f32[32,2048]{1,0:T(8,128)S(1)}, u32[]{:S(2)}, u32[]{:S(2)}) collective-permute-start(f32[32,2048]{1,0:T(8,128)S(1)} %collective-permute-done.1), channel_id=1, source_target_pairs={{0,1},{1,0},{2,3},{3,2},{4,5},{5,4},{6,7},{7,6},{8,9},{9,8},{10,11... | collective-permute-start | bytes 786440 | tf_op jit(solution)/shard_map/ppermute | solution.py:182
  78.9 27.1 %copy-start.9 = (f32[32,2048]{1,0:T(8,128)}, f32[32,2048]{1,0:T(8,128)S(1)}, u32[]{:S(2)}) copy-start(f32[32,2048]{1,0:T(8,128)S(1)} %collective-permute-done.2) | copy-start | bytes 786436
  78.9 9.3 %collective-permute-start.8 = (f32[32,2048]{1,0:T(8,128)S(1)}, f32[32,2048]{1,0:T(8,128)S(1)}, u32[]{:S(2)}, u32[]{:S(2)}) collective-permute-start(f32[32,2048]{1,0:T(8,128)S(1)} %collective-permute-done.2), channel_id=1, source_target_pairs={{0,1},{1,0},{2,3},{3,2},{4,5},{5,4},{6,7},{7,6},{8,9},{9,8},{10,11... | collective-permute-start | bytes 786440 | tf_op jit(solution)/shard_map/ppermute | solution.py:182
  79.0 9.2 %collective-permute-start.5 = (f32[32,2048]{1,0:T(8,128)S(1)}, f32[32,2048]{1,0:T(8,128)S(1)}, u32[]{:S(2)}, u32[]{:S(2)}) collective-permute-start(f32[32,2048]{1,0:T(8,128)S(1)} %collective-permute-done.2), channel_id=1, source_target_pairs={{0,14},{2,0},{4,2},{6,4},{8,6},{10,8},{12,10},{14,12},{1,15},{3,1}... | collective-permute-start | bytes 786440 | tf_op jit(solution)/shard_map/ppermute | solution.py:179
  86.6 19.4 %copy-start.10 = (f32[32,2048]{1,0:T(8,128)}, f32[32,2048]{1,0:T(8,128)S(1)}, u32[]{:S(2)}) copy-start(f32[32,2048]{1,0:T(8,128)S(1)} %collective-permute-done.4) | copy-start | bytes 786436
  86.6 19.4 %copy-start.11 = (f32[32,2048]{1,0:T(8,128)}, f32[32,2048]{1,0:T(8,128)S(1)}, u32[]{:S(2)}) copy-start(f32[32,2048]{1,0:T(8,128)S(1)} %collective-permute-done.6) | copy-start | bytes 786436
  86.6 5.5 %collective-permute-start.10 = (f32[32,2048]{1,0:T(8,128)S(1)}, f32[32,2048]{1,0:T(8,128)S(1)}, u32[]{:S(2)}, u32[]{:S(2)}) collective-permute-start(f32[32,2048]{1,0:T(8,128)S(1)} %collective-permute-done.4), channel_id=1, source_target_pairs={{0,1},{1,0},{2,3},{3,2},{4,5},{5,4},{6,7},{7,6},{8,9},{9,8},{10,11... | collective-permute-start | bytes 786440 | tf_op jit(solution)/shard_map/ppermute | solution.py:182
  88.2 9.1 %collective-permute-start.7 = (f32[32,2048]{1,0:T(8,128)S(1)}, f32[32,2048]{1,0:T(8,128)S(1)}, u32[]{:S(2)}, u32[]{:S(2)}) collective-permute-start(f32[32,2048]{1,0:T(8,128)S(1)} %collective-permute-done.4), channel_id=1, source_target_pairs={{0,2},{2,4},{4,6},{6,8},{8,10},{10,12},{12,14},{14,0},{1,3},{3,5},... | collective-permute-start | bytes 786440 | tf_op jit(solution)/shard_map/ppermute | solution.py:176
  88.2 9.2 %collective-permute-start.9 = (f32[32,2048]{1,0:T(8,128)S(1)}, f32[32,2048]{1,0:T(8,128)S(1)}, u32[]{:S(2)}, u32[]{:S(2)}) collective-permute-start(f32[32,2048]{1,0:T(8,128)S(1)} %collective-permute-done.5), channel_id=1, source_target_pairs={{0,14},{2,0},{4,2},{6,4},{8,6},{10,8},{12,10},{14,12},{1,15},{3,1}... | collective-permute-start | bytes 786440 | tf_op jit(solution)/shard_map/ppermute | solution.py:179
  91.0 6.4 %collective-permute-start.12 = (f32[32,2048]{1,0:T(8,128)S(1)}, f32[32,2048]{1,0:T(8,128)S(1)}, u32[]{:S(2)}, u32[]{:S(2)}) collective-permute-start(f32[32,2048]{1,0:T(8,128)S(1)} %collective-permute-done.5), channel_id=1, source_target_pairs={{0,1},{1,0},{2,3},{3,2},{4,5},{5,4},{6,7},{7,6},{8,9},{9,8},{10,11... | collective-permute-start | bytes 786440 | tf_op jit(solution)/shard_map/ppermute | solution.py:182
  97.3 5.4 %collective-permute-start.11 = (f32[16,2048]{1,0:T(8,128)S(1)}, f32[16,2048]{1,0:T(8,128)S(1)}, u32[]{:S(2)}, u32[]{:S(2)}) collective-permute-start(f32[16,2048]{1,0:T(8,128)S(1)} %slice.9), channel_id=1, source_target_pairs={{0,2},{2,4},{4,6},{6,8},{8,10},{10,12},{12,14},{14,0},{1,3},{3,5},... | collective-permute-start | bytes 393224 | tf_op jit(solution)/shard_map/ppermute | solution.py:176
  97.4 5.3 %collective-permute-start.13 = (f32[16,2048]{1,0:T(8,128)S(1)}, f32[16,2048]{1,0:T(8,128)S(1)}, u32[]{:S(2)}, u32[]{:S(2)}) collective-permute-start(f32[16,2048]{1,0:T(8,128)S(1)} %slice.10), channel_id=1, source_target_pairs={{0,14},{2,0},{4,2},{6,4},{8,6},{10,8},{12,10},{14,12},{1,15},{3,1}... | collective-permute-start | bytes 393224 | tf_op jit(solution)/shard_map/ppermute | solution.py:179
  100.2 5.1 %collective-permute-start.15 = (f32[32,2048]{1,0:T(8,128)S(1)}, f32[32,2048]{1,0:T(8,128)}, u32[]{:S(2)}, u32[]{:S(2)}) collective-permute-start(f32[32,2048]{1,0:T(8,128)S(1)} %collective-permute-done.9), channel_id=1, source_target_pairs={{0,1},{1,0},{2,3},{3,2},{4,5},{5,4},{6,7},{7,6},{8,9},{9,8},{10,11... | collective-permute-start | bytes 786440 | tf_op jit(solution)/shard_map/ppermute | solution.py:182
  101.6 3.6 %collective-permute-start.14 = (f32[32,2048]{1,0:T(8,128)S(1)}, f32[32,2048]{1,0:T(8,128)}, u32[]{:S(2)}, u32[]{:S(2)}) collective-permute-start(f32[32,2048]{1,0:T(8,128)S(1)} %collective-permute-done.7), channel_id=1, source_target_pairs={{0,1},{1,0},{2,3},{3,2},{4,5},{5,4},{6,7},{7,6},{8,9},{9,8},{10,11... | collective-permute-start | bytes 786440 | tf_op jit(solution)/shard_map/ppermute | solution.py:182
  102.8 3.1 %collective-permute-start.16 = (f32[32,2048]{1,0:T(8,128)S(1)}, f32[32,2048]{1,0:T(8,128)}, u32[]{:S(2)}, u32[]{:S(2)}) collective-permute-start(f32[32,2048]{1,0:T(8,128)S(1)} %constant_dynamic-update-slice_fusion), channel_id=1, source_target_pairs={{0,1},{1,0},{2,3},{3,2},{4,5},{5,4},{6,7},{7,6},{8,9},{9,8},{10,11... | collective-permute-start | bytes 786440 | tf_op jit(solution)/shard_map/ppermute | solution.py:182
  145.2 3.9 %collective-permute-start.17 = (f32[8,16,640]{2,1,0:T(8,128)S(1)}, f32[8,16,640]{2,1,0:T(8,128)S(1)}, u32[]{:S(2)}, u32[]{:S(2)}) collective-permute-start(f32[8,16,640]{2,1,0:T(8,128)S(1)} %slice.12), channel_id=1, source_target_pairs={{0,1},{1,0},{2,3},{3,2},{4,5},{5,4},{6,7},{7,6},{8,9},{9,8},{10,11... | collective-permute-start | bytes 983048 | tf_op jit(solution)/shard_map/ppermute | solution.py:396
  (10 other events, 115.3 us)

commit v8 on v7

--- a/solution.py
+++ b/solution.py
@@ -44,27 +44,34 @@
     return arrays
 
 
-def pack_kernel(orb_ref, pot_ref, out_ref):
-    xp = pl.program_id(0)
-    for yh in range(2):
-        parts = swap_groups([orb_ref[0, yh * 8 + yl] for yl in range(8)])
-        for g in range(8):
-            out_ref[g, pl.ds(pl.multiple_of(xp * 64 + yh * 32, 32), 32), :] = parts[g]
-
-    @pl.when(xp == 3)
-    def _():
-        packed = jnp.concatenate([pot_ref[p] for p in range(4)], axis=1)
-        for g in range(8):
-            out_ref[g, 256:272, :] = packed
+def pack_kernel(orb_ref, pot_ref, out_ref, orb, pot, sems):
+    copies = [pltpu.make_async_copy(orb_ref.at[xp], orb.at[xp], sems.at[xp]) for xp in range(4)]
+    copies.append(pltpu.make_async_copy(pot_ref, pot, sems.at[4]))
+    for copy in copies:
+        copy.start()
+    for xp in range(4):
+        copies[xp].wait()
+        for yh in range(2):
+            parts = swap_groups([orb[xp, yh * 8 + yl] for yl in range(8)])
+            for g in range(8):
+                out_ref[g, xp * 64 + yh * 32 : xp * 64 + yh * 32 + 32, :] = parts[g]
+    copies[4].wait()
+    packed = jnp.concatenate([pot[p] for p in range(4)], axis=1)
+    for g in range(8):
+        out_ref[g, 256:272, :] = packed
 
 
 def pack(orbitals, potential):
     return pl.pallas_call(
         pack_kernel,
-        grid=(4,),
-        in_specs=[pl.BlockSpec((1, 16, 32, 128), lambda i: (i, 0, 0, 0)), pl.BlockSpec((4, 16, 32), lambda i: (0, 0, 0))],
-        out_specs=pl.BlockSpec((8, 272, 128), lambda i: (0, 0, 0)),
+        in_specs=[pl.BlockSpec(memory_space=pl.ANY)] * 2,
+        out_specs=pl.BlockSpec(memory_space=pltpu.VMEM),
         out_shape=jax.ShapeDtypeStruct((8, 272, 128), jnp.float32),
+        scratch_shapes=[
+            pltpu.VMEM((4, 16, 32, 128), jnp.float32),
+            pltpu.VMEM((4, 16, 32), jnp.float32),
+            pltpu.SemaphoreType.DMA((5,)),
+        ],
         compiler_params=pltpu.CompilerParams(vmem_limit_bytes=BIG * MIB),
     )(orbitals, potential)
 
@@ -201,7 +208,7 @@
 
 
 def products_kernel(place_ref, *refs):
-    blocks, (field_ref, home_ref, out_ref, panel_ref, acc, sems) = refs[:16], refs[16:]
+    blocks, (field_ref, home_ref, out_ref, panel_ref, acc, corner, sems) = refs[:16], refs[16:]
     z, core = place_ref[1], place_ref[2]
     copies = []
     for half in range(2):
@@ -215,11 +222,13 @@
     long = pl.ds(pl.multiple_of((1 - core) * 128, 128), 128)
     short = pl.ds(pl.multiple_of(core * 128, 128), 128)
     acc[...] = jnp.zeros_like(acc)
+    corner[...] = jnp.zeros_like(corner)
 
     def chunk(i, _):
         points = pl.ds(pl.multiple_of(i * 512, 512), 512)
-        rows = jnp.concatenate([panel_ref[1, long, points], panel_ref[0, short, points], field_ref[:, points]], axis=0)
+        rows = jnp.concatenate([panel_ref[1, long, points], field_ref[:, points]], axis=0)
         acc[...] += dot_nt(rows, panel_ref[:, :, points].reshape(PANEL, 512))
+        corner[...] += dot_nt(panel_ref[0, short, points], panel_ref[0, :, points])
         return 0
 
     for half in range(2):
@@ -231,11 +240,10 @@
         lax.fori_loop(half * 2, half * 2 + 2, chunk, 0)
     for s in range(8):
         rows = slice(s * 16, s * 16 + 16)
-        lower = slice(128 + s * 16, 128 + s * 16 + 16)
         out_ref[s, :, 0:384] = acc[rows, 0:384]
-        out_ref[s, :, 384:512] = jnp.where(core == 0, acc[rows, 384:512], acc[lower, 128:256])
-        out_ref[s, :, 512:640] = acc[lower, 0:128]
-        out_ref[s, :, 640:1152] = acc[256 + s * 16 : 256 + s * 16 + 16, :]
+        out_ref[s, :, 384:512] = jnp.where(core == 0, acc[rows, 384:512], corner[rows, 128:256])
+        out_ref[s, :, 512:640] = corner[rows, 0:128]
+        out_ref[s, :, 640:1152] = acc[128 + s * 16 : 128 + s * 16 + 16, :]
     home.wait()
 
 
@@ -249,7 +257,8 @@
         out_specs=(pl.BlockSpec(memory_space=pl.ANY), pl.BlockSpec(memory_space=pltpu.VMEM)),
         scratch_shapes=[
             pltpu.VMEM((2, 256, 2048), jnp.float32),
-            pltpu.VMEM((384, 512), jnp.float32),
+            pltpu.VMEM((256, 512), jnp.float32),
+            pltpu.VMEM((128, 256), jnp.float32),
             pltpu.SemaphoreType.DMA((33,)),
         ],
         compiler_params=pltpu.CompilerParams(vmem_limit_bytes=BIG * MIB),
@@ -358,25 +367,27 @@
         own = xl * 16 + z * 2 + core
         mixer[0:16, :] = inverse[pl.ds(pl.multiple_of(own * 16, 16), 16), :]
 
-    keep = lax.broadcasted_iota(jnp.int32, (128, 256), 0) >= 16
+    keep = lax.broadcasted_iota(jnp.int32, (128, 512), 0) >= 16
     moved = (dot_nn(mixer[...], panel_ref[...]) + jnp.where(keep, field_ref[...], 0.0)).T
-    for xp in range(4):
-        for yh in range(2):
-            out_ref[xp, yh, 0] = moved[xp * 64 + yh * 32 : xp * 64 + yh * 32 + 32, :]
+    for low in range(2):
+        for xp in range(4):
+            for yh in range(2):
+                first = low * 256 + xp * 64 + yh * 32
+                out_ref[xp, yh, low] = moved[first : first + 32, :]
 
 
 def update(place, sums, by_core, panel, field):
     out = pl.pallas_call(
         update_kernel,
-        grid=(8,),
+        grid=(4,),
         in_specs=[
             pl.BlockSpec(memory_space=pltpu.SMEM),
             pl.BlockSpec((8, 16, 1152), lambda i: (0, 0, 0)),
             pl.BlockSpec((8, 16, 640), lambda i: (0, 0, 0)),
-            pl.BlockSpec((PANEL, 256), lambda i: (0, i)),
-            pl.BlockSpec((128, 256), lambda i: (0, i)),
+            pl.BlockSpec((PANEL, 512), lambda i: (0, i)),
+            pl.BlockSpec((128, 512), lambda i: (0, i)),
         ],
-        out_specs=pl.BlockSpec((4, 2, 1, 32, 128), lambda i: (0, 0, i, 0, 0)),
+        out_specs=pl.BlockSpec((4, 2, 2, 32, 128), lambda i: (0, 0, i, 0, 0)),
         out_shape=jax.ShapeDtypeStruct((4, 2, 8, 32, 128), jnp.float32),
         scratch_shapes=[pltpu.VMEM((PANEL, PANEL), jnp.float32)] * 2 + [pltpu.VMEM((128, PANEL), jnp.float32)] * 2,
         compiler_params=pltpu.CompilerParams(vmem_limit_bytes=52 * MIB),

time: 181 us -> 178 us (0.983)
  Pallas kernels: 57.4 us -> 54.7 us
    pallas_call x2, Pallas kernels: 35.4 us -> 32.7 us  [the longest x1 29.1 us: update(): pl.pallas_call(update_kernel, grid=(4,), in_specs=[pl.BlockSpec(memory_sp...]
where the time goes in v8:
time: 178 us
  blocking collectives  71.2 us (40%)
  Pallas kernels  54.7 us (31%)
  starting transfers between devices  28.5 us (16%)
  waiting for transfers between devices  21 us (12%)
    pallas_call x1, Pallas kernels, update(): pl.pallas_call(update_kernel, grid=(4,), in_specs=[pl.BlockSpec(memory_sp...  29.1 us
    all_to_all x1, blocking collectives, per_device(): lax.all_to_all(pack(orbitals, potential), SPACE, 0, 0, tiled=True)  24.2 us
    all_to_all x1, blocking collectives, per_device(): back = lax.all_to_all(chebyshev(received), SPACE, 0, 0, tiled=True)  17.8 us
    ppermute x4, waiting for transfers between devices, right(): return lax.ppermute(block, 'z', ring(8, 1))  17.4 us
    all_to_all x1, blocking collectives, per_device(): mine = jnp.sum(lax.all_to_all(terms, SPACE, 0, 0, tiled=True), axis=0)  15.3 us
    all_to_all x1, blocking collectives, per_device(): lax.all_to_all(jnp.broadcast_to(mine, (8, 16, 1152)), SPACE, 0, 0, tiled=...  13.9 us
    ppermute x4, starting transfers between devices, left(): return lax.ppermute(block, 'z', ring(8, -1))  12.5 us
    pallas_call x1, Pallas kernels, chebyshev(): pl.pallas_call(filter_kernel, out_shape=jax.ShapeDtypeStruct((64, 32, 128...  11.3 us
  transfers between devices with their start and end apart: 18, of which 7 were waited for; matrix products, arithmetic and copies ran while one was open for 0% of the time, Pallas kernels for 0%

profile of v8, /device:TPU:1, one launch (start us, length us, event | category | flops | bytes accessed | tf_op | source)
XLA Modules:
  0.0 177.6 jit_solution(8193548678104556233)
XLA Ops:
  0.0 3.7 %shard_map.28 = f32[8,272,128]{2,1,0:T(8,128)} custom-call(f32[4,16,32,128]{3,2,1,0:T(8,128)} %orb_ref.1, f32[4,16,32]{2,1,0:T(8,128)} %pot_ref.1), custom_call_target="tpu_custom_call" | custom-call | tf_op jit(solution)/shard_map/pallas_call | solution.py:65
  3.7 24.2 %all_to_all.20.in_ref = f32[8,272,128]{2,1,0:T(8,128)S(1)} all-to-all(f32[8,272,128]{2,1,0:T(8,128)} %shard_map.28), channel_id=1, replica_groups=mesh['y'=4,'xh'=2,'xl'=2,'z'=8,'c'=2] {'y','xh'}, dimensions={0} | all-to-all | bytes 2228224 | tf_op jit(solution)/shard_map/all_to_all | solution.py:401
  27.8 11.3 %shard_map.29 = f32[64,32,128]{2,1,0:T(8,128)S(1)} custom-call(f32[8,272,128]{2,1,0:T(8,128)S(1)} %all_to_all.20.in_ref), custom_call_target="tpu_custom_call" | custom-call | tf_op jit(solution)/shard_map/pallas_call | solution.py:150
  39.2 17.8 %all_to_all.21.in_ref = f32[8,256,128]{2,1,0:T(8,128)S(1)} all-to-all(f32[8,256,128]{2,1,0:T(8,128)S(1)} %bitcast.22), channel_id=1, replica_groups=mesh['y'=4,'xh'=2,'xl'=2,'z'=8,'c'=2] {'y','xh'}, dimensions={0} | all-to-all | bytes 2097152 | tf_op jit(solution)/shard_map/all_to_all | solution.py:402
  59.3 1.7 collective-permute-done
  61.1 4.4 %collective-permute-start.3 = (f32[32,2048]{1,0:T(8,128)S(1)}, f32[32,2048]{1,0:T(8,128)S(1)}, u32[]{:S(2)}, u32[]{:S(2)}) collective-permute-start(f32[32,2048]{1,0:T(8,128)S(1)} %pad_maximum_fusion), channel_id=1, source_target_pairs={{0,1},{1,0},{2,3},{3,2},{4,5},{5,4},{6,7},{7,6},{8,9},{9,8},{10,11... | collective-permute-start | bytes 786440 | tf_op jit(solution)/shard_map/ppermute | solution.py:189
  65.5 1.7 collective-permute-start.1
  67.1 3.9 %collective-permute-start.2 = (f32[32,2048]{1,0:T(8,128)S(1)}, f32[32,2048]{1,0:T(8,128)S(1)}, u32[]{:S(2)}, u32[]{:S(2)}) collective-permute-start(f32[32,2048]{1,0:T(8,128)S(1)} %pad_maximum_fusion), channel_id=1, source_target_pairs={{0,14},{2,0},{4,2},{6,4},{8,6},{10,8},{12,10},{14,12},{1,15},{3,1}... | collective-permute-start | bytes 786440 | tf_op jit(solution)/shard_map/ppermute | solution.py:186
  71.1 6.6 %collective-permute-done.1 = f32[32,2048]{1,0:T(8,128)S(1)} collective-permute-done((f32[32,2048]{1,0:T(8,128)S(1)}, f32[32,2048]{1,0:T(8,128)S(1)}, u32[]{:S(2)}, u32[]{:S(2)}) %collective-permute-start.1) | collective-permute-done | bytes 262176 | tf_op jit(solution)/shard_map/ppermute | solution.py:183
  78.4 2.9 %collective-permute-start.5 = (f32[32,2048]{1,0:T(8,128)S(1)}, f32[32,2048]{1,0:T(8,128)S(1)}, u32[]{:S(2)}, u32[]{:S(2)}) collective-permute-start(f32[32,2048]{1,0:T(8,128)S(1)} %collective-permute-done.2), channel_id=1, source_target_pairs={{0,14},{2,0},{4,2},{6,4},{8,6},{10,8},{12,10},{14,12},{1,15},{3,1}... | collective-permute-start | bytes 786440 | tf_op jit(solution)/shard_map/ppermute | solution.py:186
  81.4 4.7 %collective-permute-done.4 = f32[32,2048]{1,0:T(8,128)S(1)} collective-permute-done((f32[32,2048]{1,0:T(8,128)S(1)}, f32[32,2048]{1,0:T(8,128)S(1)}, u32[]{:S(2)}, u32[]{:S(2)}) %collective-permute-start.4) | collective-permute-done | bytes 262176 | tf_op jit(solution)/shard_map/ppermute | solution.py:183
  86.1 1.6 collective-permute-start.10
  87.7 2.8 %collective-permute-start.9 = (f32[32,2048]{1,0:T(8,128)S(1)}, f32[32,2048]{1,0:T(8,128)S(1)}, u32[]{:S(2)}, u32[]{:S(2)}) collective-permute-start(f32[32,2048]{1,0:T(8,128)S(1)} %collective-permute-done.5), channel_id=1, source_target_pairs={{0,14},{2,0},{4,2},{6,4},{8,6},{10,8},{12,10},{14,12},{1,15},{3,1}... | collective-permute-start | bytes 786440 | tf_op jit(solution)/shard_map/ppermute | solution.py:186
  90.5 1.1 collective-permute-start.12
  91.6 5.2 %collective-permute-done.7 = f32[32,2048]{1,0:T(8,128)S(1)} collective-permute-done((f32[32,2048]{1,0:T(8,128)S(1)}, f32[32,2048]{1,0:T(8,128)S(1)}, u32[]{:S(2)}, u32[]{:S(2)}) %collective-permute-start.7) | collective-permute-done | bytes 262176 | tf_op jit(solution)/shard_map/ppermute | solution.py:183
  96.9 2.9 %collective-permute-start.13 = (f32[16,2048]{1,0:T(8,128)S(1)}, f32[16,2048]{1,0:T(8,128)S(1)}, u32[]{:S(2)}, u32[]{:S(2)}) collective-permute-start(f32[16,2048]{1,0:T(8,128)S(1)} %slice.10), channel_id=1, source_target_pairs={{0,14},{2,0},{4,2},{6,4},{8,6},{10,8},{12,10},{14,12},{1,15},{3,1}... | collective-permute-start | bytes 393224 | tf_op jit(solution)/shard_map/ppermute | solution.py:186
  99.8 1.4 collective-permute-start.15
  102.3 1.9 %collective-permute-start.16 = (f32[32,2048]{1,0:T(8,128)S(1)}, f32[32,2048]{1,0:T(8,128)}, u32[]{:S(2)}, u32[]{:S(2)}) collective-permute-start(f32[32,2048]{1,0:T(8,128)S(1)} %constant_dynamic-update-slice_fusion), channel_id=1, source_target_pairs={{0,1},{1,0},{2,3},{3,2},{4,5},{5,4},{6,7},{7,6},{8,9},{9,8},{10,11... | collective-permute-start | bytes 786440 | tf_op jit(solution)/shard_map/ppermute | solution.py:189
  105.5 9.7 %shard_map.32 = (f32[2,256,2048]{2,1,0:T(8,128)}, f32[8,16,1152]{2,1,0:T(8,128)}) custom-call(s32[3]{0:T(128)} %pad_add_fusion.place_ref, f32[2,16,2048]{2,1,0:T(8,128)} %bitcast.24, f32[2,16,2048]{2,1,0:T(8,128)} %bitcast.29, f32[2,16,2048]{2,1,0:T(8,128)} %bitcast.30, f32[2,16,2048]{2,1,0:T(8,128)} %bitcast.31, f32[2,16,2048]{2,1,0:T(8,128)} %bitcast.34, ...), custom_call_target="tpu_custom_call" | custom-call | tf_op jit(solution)/shard_map/pallas_call | solution.py:251
  115.3 15.3 %all_to_all.22 = f32[8,16,1152]{2,1,0:T(8,128)S(1)} all-to-all(f32[8,16,1152]{2,1,0:T(8,128)} %get-tuple-element.31), channel_id=1, replica_groups=mesh['y'=4,'xh'=2,'xl'=2,'z'=8,'c'=2] {'y','xh'}, dimensions={0} | all-to-all | bytes 1179648 | tf_op jit(solution)/shard_map/all_to_all | solution.py:405
  130.7 13.9 %all_to_all.23.sums_ref = f32[8,16,1152]{2,1,0:T(8,128)S(1)} all-to-all(f32[8,16,1152]{2,1,0:T(8,128)S(1)} %broadcast_in_dim.3), channel_id=1, replica_groups=mesh['y'=4,'xh'=2,'xl'=2,'z'=8,'c'=2] {'y','xh'}, dimensions={0} | all-to-all | bytes 1179648 | tf_op jit(solution)/shard_map/all_to_all | solution.py:406
  144.6 2.6 %collective-permute-start.17 = (f32[8,16,640]{2,1,0:T(8,128)S(1)}, f32[8,16,640]{2,1,0:T(8,128)S(1)}, u32[]{:S(2)}, u32[]{:S(2)}) collective-permute-start(f32[8,16,640]{2,1,0:T(8,128)S(1)} %slice.12), channel_id=1, source_target_pairs={{0,1},{1,0},{2,3},{3,2},{4,5},{5,4},{6,7},{7,6},{8,9},{9,8},{10,11... | collective-permute-start | bytes 983048 | tf_op jit(solution)/shard_map/ppermute | solution.py:407
  147.2 1.3 collective-permute-done.17.by_core_ref
  148.5 29.1 %shard_map.33 = f32[4,2,8,32,128]{4,3,2,1,0:T(8,128)} custom-call(s32[3]{0:T(128)S(1)} %copy-done.2, f32[8,16,1152]{2,1,0:T(8,128)S(1)} %all_to_all.23.sums_ref, f32[8,16,640]{2,1,0:T(8,128)S(1)} %collective-permute-done.17.by_core_ref, f32[512,2048]{1,0:T(8,128)} %bitcast.23, f32[128,2048]{1,0:T(8,128)S(1)} %copy-done.1), custom_call_target="tpu_custom_call" | custom-call | tf_op jit(solution)/shard_map/pallas_call | solution.py:380
  (64 shorter events, 5.7 us)
Async XLA Ops:
  57.1 3.9 %collective-permute-start = (f32[16,2048]{1,0:T(8,128)S(1)}, f32[16,2048]{1,0:T(8,128)S(1)}, u32[]{:S(2)}, u32[]{:S(2)}) collective-permute-start(f32[16,2048]{1,0:T(8,128)S(1)} %shard_map.30), channel_id=1, source_target_pairs={{0,16},{16,0},{1,17},{17,1},{2,18},{18,2},{3,19},{19,3},{4,20},{20... | collective-permute-start | bytes 393224 | tf_op jit(solution)/shard_map/ppermute | solution.py:192
  61.1 44.4 %copy-start.3 = (f32[32,2048]{1,0:T(8,128)}, f32[32,2048]{1,0:T(8,128)S(1)}, u32[]{:S(2)}) copy-start(f32[32,2048]{1,0:T(8,128)S(1)} %pad_maximum_fusion) | copy-start | bytes 786436
  61.1 10.0 %collective-permute-start.3 = (f32[32,2048]{1,0:T(8,128)S(1)}, f32[32,2048]{1,0:T(8,128)S(1)}, u32[]{:S(2)}, u32[]{:S(2)}) collective-permute-start(f32[32,2048]{1,0:T(8,128)S(1)} %pad_maximum_fusion), channel_id=1, source_target_pairs={{0,1},{1,0},{2,3},{3,2},{4,5},{5,4},{6,7},{7,6},{8,9},{9,8},{10,11... | collective-permute-start | bytes 786440 | tf_op jit(solution)/shard_map/ppermute | solution.py:189
  65.5 12.2 %collective-permute-start.1 = (f32[32,2048]{1,0:T(8,128)S(1)}, f32[32,2048]{1,0:T(8,128)S(1)}, u32[]{:S(2)}, u32[]{:S(2)}) collective-permute-start(f32[32,2048]{1,0:T(8,128)S(1)} %pad_maximum_fusion), channel_id=1, source_target_pairs={{0,2},{2,4},{4,6},{6,8},{8,10},{10,12},{12,14},{14,0},{1,3},{3,5},... | collective-permute-start | bytes 786440 | tf_op jit(solution)/shard_map/ppermute | solution.py:183
  67.1 11.2 %collective-permute-start.2 = (f32[32,2048]{1,0:T(8,128)S(1)}, f32[32,2048]{1,0:T(8,128)S(1)}, u32[]{:S(2)}, u32[]{:S(2)}) collective-permute-start(f32[32,2048]{1,0:T(8,128)S(1)} %pad_maximum_fusion), channel_id=1, source_target_pairs={{0,14},{2,0},{4,2},{6,4},{8,6},{10,8},{12,10},{14,12},{1,15},{3,1}... | collective-permute-start | bytes 786440 | tf_op jit(solution)/shard_map/ppermute | solution.py:186
  71.1 34.3 %copy-start.7 = (f32[32,2048]{1,0:T(8,128)}, f32[32,2048]{1,0:T(8,128)S(1)}, u32[]{:S(2)}) copy-start(f32[32,2048]{1,0:T(8,128)S(1)} %collective-permute-done.3) | copy-start | bytes 786436
  77.7 27.8 %copy-start.8 = (f32[32,2048]{1,0:T(8,128)}, f32[32,2048]{1,0:T(8,128)S(1)}, u32[]{:S(2)}) copy-start(f32[32,2048]{1,0:T(8,128)S(1)} %collective-permute-done.1) | copy-start | bytes 786436
  77.7 8.4 %collective-permute-start.4 = (f32[32,2048]{1,0:T(8,128)S(1)}, f32[32,2048]{1,0:T(8,128)S(1)}, u32[]{:S(2)}, u32[]{:S(2)}) collective-permute-start(f32[32,2048]{1,0:T(8,128)S(1)} %collective-permute-done.1), channel_id=1, source_target_pairs={{0,2},{2,4},{4,6},{6,8},{8,10},{10,12},{12,14},{14,0},{1,3},{3,5},... | collective-permute-start | bytes 786440 | tf_op jit(solution)/shard_map/ppermute | solution.py:183
  77.7 8.4 %collective-permute-start.6 = (f32[32,2048]{1,0:T(8,128)S(1)}, f32[32,2048]{1,0:T(8,128)S(1)}, u32[]{:S(2)}, u32[]{:S(2)}) collective-permute-start(f32[32,2048]{1,0:T(8,128)S(1)} %collective-permute-done.1), channel_id=1, source_target_pairs={{0,1},{1,0},{2,3},{3,2},{4,5},{5,4},{6,7},{7,6},{8,9},{9,8},{10,11... | collective-permute-start | bytes 786440 | tf_op jit(solution)/shard_map/ppermute | solution.py:189
  78.3 27.1 %copy-start.9 = (f32[32,2048]{1,0:T(8,128)}, f32[32,2048]{1,0:T(8,128)S(1)}, u32[]{:S(2)}) copy-start(f32[32,2048]{1,0:T(8,128)S(1)} %collective-permute-done.2) | copy-start | bytes 786436
  78.3 9.3 %collective-permute-start.8 = (f32[32,2048]{1,0:T(8,128)S(1)}, f32[32,2048]{1,0:T(8,128)S(1)}, u32[]{:S(2)}, u32[]{:S(2)}) collective-permute-start(f32[32,2048]{1,0:T(8,128)S(1)} %collective-permute-done.2), channel_id=1, source_target_pairs={{0,1},{1,0},{2,3},{3,2},{4,5},{5,4},{6,7},{7,6},{8,9},{9,8},{10,11... | collective-permute-start | bytes 786440 | tf_op jit(solution)/shard_map/ppermute | solution.py:189
  78.4 9.2 %collective-permute-start.5 = (f32[32,2048]{1,0:T(8,128)S(1)}, f32[32,2048]{1,0:T(8,128)S(1)}, u32[]{:S(2)}, u32[]{:S(2)}) collective-permute-start(f32[32,2048]{1,0:T(8,128)S(1)} %collective-permute-done.2), channel_id=1, source_target_pairs={{0,14},{2,0},{4,2},{6,4},{8,6},{10,8},{12,10},{14,12},{1,15},{3,1}... | collective-permute-start | bytes 786440 | tf_op jit(solution)/shard_map/ppermute | solution.py:186
  86.0 19.4 %copy-start.10 = (f32[32,2048]{1,0:T(8,128)}, f32[32,2048]{1,0:T(8,128)S(1)}, u32[]{:S(2)}) copy-start(f32[32,2048]{1,0:T(8,128)S(1)} %collective-permute-done.4) | copy-start | bytes 786436
  86.0 19.4 %copy-start.11 = (f32[32,2048]{1,0:T(8,128)}, f32[32,2048]{1,0:T(8,128)S(1)}, u32[]{:S(2)}) copy-start(f32[32,2048]{1,0:T(8,128)S(1)} %collective-permute-done.6) | copy-start | bytes 786436
  86.1 5.5 %collective-permute-start.10 = (f32[32,2048]{1,0:T(8,128)S(1)}, f32[32,2048]{1,0:T(8,128)S(1)}, u32[]{:S(2)}, u32[]{:S(2)}) collective-permute-start(f32[32,2048]{1,0:T(8,128)S(1)} %collective-permute-done.4), channel_id=1, source_target_pairs={{0,1},{1,0},{2,3},{3,2},{4,5},{5,4},{6,7},{7,6},{8,9},{9,8},{10,11... | collective-permute-start | bytes 786440 | tf_op jit(solution)/shard_map/ppermute | solution.py:189
  87.7 9.1 %collective-permute-start.7 = (f32[32,2048]{1,0:T(8,128)S(1)}, f32[32,2048]{1,0:T(8,128)S(1)}, u32[]{:S(2)}, u32[]{:S(2)}) collective-permute-start(f32[32,2048]{1,0:T(8,128)S(1)} %collective-permute-done.4), channel_id=1, source_target_pairs={{0,2},{2,4},{4,6},{6,8},{8,10},{10,12},{12,14},{14,0},{1,3},{3,5},... | collective-permute-start | bytes 786440 | tf_op jit(solution)/shard_map/ppermute | solution.py:183
  87.7 9.2 %collective-permute-start.9 = (f32[32,2048]{1,0:T(8,128)S(1)}, f32[32,2048]{1,0:T(8,128)S(1)}, u32[]{:S(2)}, u32[]{:S(2)}) collective-permute-start(f32[32,2048]{1,0:T(8,128)S(1)} %collective-permute-done.5), channel_id=1, source_target_pairs={{0,14},{2,0},{4,2},{6,4},{8,6},{10,8},{12,10},{14,12},{1,15},{3,1}... | collective-permute-start | bytes 786440 | tf_op jit(solution)/shard_map/ppermute | solution.py:186
  90.5 6.4 %collective-permute-start.12 = (f32[32,2048]{1,0:T(8,128)S(1)}, f32[32,2048]{1,0:T(8,128)S(1)}, u32[]{:S(2)}, u32[]{:S(2)}) collective-permute-start(f32[32,2048]{1,0:T(8,128)S(1)} %collective-permute-done.5), channel_id=1, source_target_pairs={{0,1},{1,0},{2,3},{3,2},{4,5},{5,4},{6,7},{7,6},{8,9},{9,8},{10,11... | collective-permute-start | bytes 786440 | tf_op jit(solution)/shard_map/ppermute | solution.py:189
  96.8 5.4 %collective-permute-start.11 = (f32[16,2048]{1,0:T(8,128)S(1)}, f32[16,2048]{1,0:T(8,128)S(1)}, u32[]{:S(2)}, u32[]{:S(2)}) collective-permute-start(f32[16,2048]{1,0:T(8,128)S(1)} %slice.9), channel_id=1, source_target_pairs={{0,2},{2,4},{4,6},{6,8},{8,10},{10,12},{12,14},{14,0},{1,3},{3,5},... | collective-permute-start | bytes 393224 | tf_op jit(solution)/shard_map/ppermute | solution.py:183
  96.9 5.3 %collective-permute-start.13 = (f32[16,2048]{1,0:T(8,128)S(1)}, f32[16,2048]{1,0:T(8,128)S(1)}, u32[]{:S(2)}, u32[]{:S(2)}) collective-permute-start(f32[16,2048]{1,0:T(8,128)S(1)} %slice.10), channel_id=1, source_target_pairs={{0,14},{2,0},{4,2},{6,4},{8,6},{10,8},{12,10},{14,12},{1,15},{3,1}... | collective-permute-start | bytes 393224 | tf_op jit(solution)/shard_map/ppermute | solution.py:186
  99.8 4.9 %collective-permute-start.15 = (f32[32,2048]{1,0:T(8,128)S(1)}, f32[32,2048]{1,0:T(8,128)}, u32[]{:S(2)}, u32[]{:S(2)}) collective-permute-start(f32[32,2048]{1,0:T(8,128)S(1)} %collective-permute-done.9), channel_id=1, source_target_pairs={{0,1},{1,0},{2,3},{3,2},{4,5},{5,4},{6,7},{7,6},{8,9},{9,8},{10,11... | collective-permute-start | bytes 786440 | tf_op jit(solution)/shard_map/ppermute | solution.py:189
  101.2 3.5 %collective-permute-start.14 = (f32[32,2048]{1,0:T(8,128)S(1)}, f32[32,2048]{1,0:T(8,128)}, u32[]{:S(2)}, u32[]{:S(2)}) collective-permute-start(f32[32,2048]{1,0:T(8,128)S(1)} %collective-permute-done.7), channel_id=1, source_target_pairs={{0,1},{1,0},{2,3},{3,2},{4,5},{5,4},{6,7},{7,6},{8,9},{9,8},{10,11... | collective-permute-start | bytes 786440 | tf_op jit(solution)/shard_map/ppermute | solution.py:189
  102.3 3.1 %collective-permute-start.16 = (f32[32,2048]{1,0:T(8,128)S(1)}, f32[32,2048]{1,0:T(8,128)}, u32[]{:S(2)}, u32[]{:S(2)}) collective-permute-start(f32[32,2048]{1,0:T(8,128)S(1)} %constant_dynamic-update-slice_fusion), channel_id=1, source_target_pairs={{0,1},{1,0},{2,3},{3,2},{4,5},{5,4},{6,7},{7,6},{8,9},{9,8},{10,11... | collective-permute-start | bytes 786440 | tf_op jit(solution)/shard_map/ppermute | solution.py:189
  144.6 3.9 %collective-permute-start.17 = (f32[8,16,640]{2,1,0:T(8,128)S(1)}, f32[8,16,640]{2,1,0:T(8,128)S(1)}, u32[]{:S(2)}, u32[]{:S(2)}) collective-permute-start(f32[8,16,640]{2,1,0:T(8,128)S(1)} %slice.12), channel_id=1, source_target_pairs={{0,1},{1,0},{2,3},{3,2},{4,5},{5,4},{6,7},{7,6},{8,9},{9,8},{10,11... | collective-permute-start | bytes 983048 | tf_op jit(solution)/shard_map/ppermute | solution.py:407
  (10 other events, 115.3 us)

commit v9 on v8

--- a/solution.py
+++ b/solution.py
@@ -44,33 +44,44 @@
     return arrays
 
 
-def pack_kernel(orb_ref, pot_ref, out_ref, orb, pot, sems):
+def pack_kernel(orb_ref, pot_ref, sent_ref, orb, pot, out_ref, sems):
     copies = [pltpu.make_async_copy(orb_ref.at[xp], orb.at[xp], sems.at[xp]) for xp in range(4)]
     copies.append(pltpu.make_async_copy(pot_ref, pot, sems.at[4]))
     for copy in copies:
         copy.start()
+
+    def send(first, count):
+        rows = pl.ds(first, count)
+        copies.append(pltpu.make_async_copy(out_ref.at[:, rows, :], sent_ref.at[:, rows, :], sems.at[len(copies)]))
+        copies[-1].start()
+
+    copies[4].wait()
+    packed = jnp.concatenate([pot[p] for p in range(4)], axis=1)
+    for g in range(8):
+        out_ref[g, 256:272, :] = packed
+    send(256, 16)
     for xp in range(4):
         copies[xp].wait()
         for yh in range(2):
             parts = swap_groups([orb[xp, yh * 8 + yl] for yl in range(8)])
             for g in range(8):
                 out_ref[g, xp * 64 + yh * 32 : xp * 64 + yh * 32 + 32, :] = parts[g]
-    copies[4].wait()
-    packed = jnp.concatenate([pot[p] for p in range(4)], axis=1)
-    for g in range(8):
-        out_ref[g, 256:272, :] = packed
+        send(xp * 64, 64)
+    for copy in copies[5:]:
+        copy.wait()
 
 
 def pack(orbitals, potential):
     return pl.pallas_call(
         pack_kernel,
         in_specs=[pl.BlockSpec(memory_space=pl.ANY)] * 2,
-        out_specs=pl.BlockSpec(memory_space=pltpu.VMEM),
+        out_specs=pl.BlockSpec(memory_space=pl.ANY),
         out_shape=jax.ShapeDtypeStruct((8, 272, 128), jnp.float32),
         scratch_shapes=[
             pltpu.VMEM((4, 16, 32, 128), jnp.float32),
             pltpu.VMEM((4, 16, 32), jnp.float32),
-            pltpu.SemaphoreType.DMA((5,)),
+            pltpu.VMEM((8, 272, 128), jnp.float32),
+            pltpu.SemaphoreType.DMA((10,)),
         ],
         compiler_params=pltpu.CompilerParams(vmem_limit_bytes=BIG * MIB),
     )(orbitals, potential)
@@ -231,12 +242,14 @@
         corner[...] += dot_nt(panel_ref[0, short, points], panel_ref[0, :, points])
         return 0
 
+    homes = []
     for half in range(2):
         for copy in copies[half * 16 : half * 16 + 16]:
             copy.wait()
-        if half:
-            home = pltpu.make_async_copy(panel_ref, home_ref, sems.at[32])
-            home.start()
+        for part in range(8):
+            place = (slice(None), pl.ds(part * 32, 32), pl.ds(half * 1024, 1024))
+            homes.append(pltpu.make_async_copy(panel_ref.at[place], home_ref.at[place], sems.at[32 + len(homes)]))
+            homes[-1].start()
         lax.fori_loop(half * 2, half * 2 + 2, chunk, 0)
     for s in range(8):
         rows = slice(s * 16, s * 16 + 16)
@@ -244,7 +257,8 @@
         out_ref[s, :, 384:512] = jnp.where(core == 0, acc[rows, 384:512], corner[rows, 128:256])
         out_ref[s, :, 512:640] = corner[rows, 0:128]
         out_ref[s, :, 640:1152] = acc[128 + s * 16 : 128 + s * 16 + 16, :]
-    home.wait()
+    for copy in homes:
+        copy.wait()
 
 
 def products(place, blocks, field):
@@ -259,7 +273,7 @@
             pltpu.VMEM((2, 256, 2048), jnp.float32),
             pltpu.VMEM((256, 512), jnp.float32),
             pltpu.VMEM((128, 256), jnp.float32),
-            pltpu.SemaphoreType.DMA((33,)),
+            pltpu.SemaphoreType.DMA((48,)),
         ],
         compiler_params=pltpu.CompilerParams(vmem_limit_bytes=BIG * MIB),
     )(place, *(block.reshape(2, 16, 2048) for block in blocks), field)
@@ -354,11 +368,16 @@
 
 
 def update_kernel(place_ref, sums_ref, by_core_ref, panel_ref, field_ref, out_ref, *scratch):
-    work, inverse, coupling, mixer = scratch
+    work, inverse, coupling, mixer, held, sems = scratch
     xl, z, core = place_ref[0], place_ref[1], place_ref[2]
 
     @pl.when(pl.program_id(0) == 0)
     def _():
+        copies = []
+        for part in range(8):
+            rows = pl.ds(part * 64, 64)
+            copies.append(pltpu.make_async_copy(panel_ref.at[rows, :], held.at[rows, :], sems.at[part]))
+            copies[-1].start()
         invert((sums_ref, by_core_ref), core, work, inverse)
         for s in range(8):
             coupling[s * 16 : s * 16 + 16, :] = sums_ref[s, :, 640:1152] * (1.0 / POINTS)
@@ -366,9 +385,12 @@
         mixer[...] = -dot_nn(dot_nt(coupling[...], factor), factor)
         own = xl * 16 + z * 2 + core
         mixer[0:16, :] = inverse[pl.ds(pl.multiple_of(own * 16, 16), 16), :]
+        for copy in copies:
+            copy.wait()
 
     keep = lax.broadcasted_iota(jnp.int32, (128, 512), 0) >= 16
-    moved = (dot_nn(mixer[...], panel_ref[...]) + jnp.where(keep, field_ref[...], 0.0)).T
+    points = pl.ds(pl.multiple_of(pl.program_id(0) * 512, 512), 512)
+    moved = (dot_nn(mixer[...], held[:, points]) + jnp.where(keep, field_ref[...], 0.0)).T
     for low in range(2):
         for xp in range(4):
             for yh in range(2):
@@ -384,12 +406,14 @@
             pl.BlockSpec(memory_space=pltpu.SMEM),
             pl.BlockSpec((8, 16, 1152), lambda i: (0, 0, 0)),
             pl.BlockSpec((8, 16, 640), lambda i: (0, 0, 0)),
-            pl.BlockSpec((PANEL, 512), lambda i: (0, i)),
+            pl.BlockSpec(memory_space=pl.ANY),
             pl.BlockSpec((128, 512), lambda i: (0, i)),
         ],
         out_specs=pl.BlockSpec((4, 2, 2, 32, 128), lambda i: (0, 0, i, 0, 0)),
         out_shape=jax.ShapeDtypeStruct((4, 2, 8, 32, 128), jnp.float32),
-        scratch_shapes=[pltpu.VMEM((PANEL, PANEL), jnp.float32)] * 2 + [pltpu.VMEM((128, PANEL), jnp.float32)] * 2,
+        scratch_shapes=[pltpu.VMEM((PANEL, PANEL), jnp.float32)] * 2
+        + [pltpu.VMEM((128, PANEL), jnp.float32)] * 2
+        + [pltpu.VMEM((PANEL, 2048), jnp.float32), pltpu.SemaphoreType.DMA((8,))],
         compiler_params=pltpu.CompilerParams(vmem_limit_bytes=52 * MIB),
     )(place, sums, by_core, panel, field)
     return out.reshape(4, 16, 32, 128)

time: 178 us -> 177 us (level)
  no operation moved by 1% of the time
where the time goes in v9:
time: 177 us
  blocking collectives  71.2 us (40%)
  Pallas kernels  53.7 us (30%)
  starting transfers between devices  28.5 us (16%)
  waiting for transfers between devices  21 us (12%)
    pallas_call x1, Pallas kernels, update(): pl.pallas_call(update_kernel, grid=(4,), in_specs=[pl.BlockSpec(memory_sp...  28 us
    all_to_all x1, blocking collectives, per_device(): lax.all_to_all(pack(orbitals, potential), SPACE, 0, 0, tiled=True)  24.2 us
    all_to_all x1, blocking collectives, per_device(): back = lax.all_to_all(chebyshev(received), SPACE, 0, 0, tiled=True)  17.8 us
    ppermute x4, waiting for transfers between devices, right(): return lax.ppermute(block, 'z', ring(8, 1))  17.4 us
    all_to_all x1, blocking collectives, per_device(): mine = jnp.sum(lax.all_to_all(terms, SPACE, 0, 0, tiled=True), axis=0)  15.3 us
    all_to_all x1, blocking collectives, per_device(): lax.all_to_all(jnp.broadcast_to(mine, (8, 16, 1152)), SPACE, 0, 0, tiled=...  13.9 us
    ppermute x4, starting transfers between devices, left(): return lax.ppermute(block, 'z', ring(8, -1))  12.5 us
    pallas_call x1, Pallas kernels, chebyshev(): pl.pallas_call(filter_kernel, out_shape=jax.ShapeDtypeStruct((64, 32, 128...  11.3 us
  transfers between devices with their start and end apart: 18, of which 7 were waited for; matrix products, arithmetic and copies ran while one was open for 0% of the time, Pallas kernels for 0%

profile of v9, /device:TPU:1, one launch (start us, length us, event | category | flops | bytes accessed | tf_op | source)
XLA Modules:
  0.0 176.7 jit_solution(9198598658941499558)
XLA Ops:
  0.0 3.6 %shard_map.28 = f32[8,272,128]{2,1,0:T(8,128)} custom-call(f32[4,16,32,128]{3,2,1,0:T(8,128)} %orb_ref.1, f32[4,16,32]{2,1,0:T(8,128)} %pot_ref.1), custom_call_target="tpu_custom_call" | custom-call | tf_op jit(solution)/shard_map/pallas_call | solution.py:75
  3.6 24.2 %all_to_all.20.in_ref = f32[8,272,128]{2,1,0:T(8,128)S(1)} all-to-all(f32[8,272,128]{2,1,0:T(8,128)} %shard_map.28), channel_id=1, replica_groups=mesh['y'=4,'xh'=2,'xl'=2,'z'=8,'c'=2] {'y','xh'}, dimensions={0} | all-to-all | bytes 2228224 | tf_op jit(solution)/shard_map/all_to_all | solution.py:425
  27.8 11.3 %shard_map.29 = f32[64,32,128]{2,1,0:T(8,128)S(1)} custom-call(f32[8,272,128]{2,1,0:T(8,128)S(1)} %all_to_all.20.in_ref), custom_call_target="tpu_custom_call" | custom-call | tf_op jit(solution)/shard_map/pallas_call | solution.py:161
  39.1 17.8 %all_to_all.21.in_ref = f32[8,256,128]{2,1,0:T(8,128)S(1)} all-to-all(f32[8,256,128]{2,1,0:T(8,128)S(1)} %bitcast.22), channel_id=1, replica_groups=mesh['y'=4,'xh'=2,'xl'=2,'z'=8,'c'=2] {'y','xh'}, dimensions={0} | all-to-all | bytes 2097152 | tf_op jit(solution)/shard_map/all_to_all | solution.py:426
  59.2 1.7 collective-permute-done
  61.0 4.4 %collective-permute-start.3 = (f32[32,2048]{1,0:T(8,128)S(1)}, f32[32,2048]{1,0:T(8,128)S(1)}, u32[]{:S(2)}, u32[]{:S(2)}) collective-permute-start(f32[32,2048]{1,0:T(8,128)S(1)} %pad_maximum_fusion), channel_id=1, source_target_pairs={{0,1},{1,0},{2,3},{3,2},{4,5},{5,4},{6,7},{7,6},{8,9},{9,8},{10,11... | collective-permute-start | bytes 786440 | tf_op jit(solution)/shard_map/ppermute | solution.py:200
  65.4 1.7 collective-permute-start.1
  67.0 3.9 %collective-permute-start.2 = (f32[32,2048]{1,0:T(8,128)S(1)}, f32[32,2048]{1,0:T(8,128)S(1)}, u32[]{:S(2)}, u32[]{:S(2)}) collective-permute-start(f32[32,2048]{1,0:T(8,128)S(1)} %pad_maximum_fusion), channel_id=1, source_target_pairs={{0,14},{2,0},{4,2},{6,4},{8,6},{10,8},{12,10},{14,12},{1,15},{3,1}... | collective-permute-start | bytes 786440 | tf_op jit(solution)/shard_map/ppermute | solution.py:197
  71.0 6.6 %collective-permute-done.1 = f32[32,2048]{1,0:T(8,128)S(1)} collective-permute-done((f32[32,2048]{1,0:T(8,128)S(1)}, f32[32,2048]{1,0:T(8,128)S(1)}, u32[]{:S(2)}, u32[]{:S(2)}) %collective-permute-start.1) | collective-permute-done | bytes 262176 | tf_op jit(solution)/shard_map/ppermute | solution.py:194
  78.3 2.9 %collective-permute-start.5 = (f32[32,2048]{1,0:T(8,128)S(1)}, f32[32,2048]{1,0:T(8,128)S(1)}, u32[]{:S(2)}, u32[]{:S(2)}) collective-permute-start(f32[32,2048]{1,0:T(8,128)S(1)} %collective-permute-done.2), channel_id=1, source_target_pairs={{0,14},{2,0},{4,2},{6,4},{8,6},{10,8},{12,10},{14,12},{1,15},{3,1}... | collective-permute-start | bytes 786440 | tf_op jit(solution)/shard_map/ppermute | solution.py:197
  81.3 4.7 %collective-permute-done.4 = f32[32,2048]{1,0:T(8,128)S(1)} collective-permute-done((f32[32,2048]{1,0:T(8,128)S(1)}, f32[32,2048]{1,0:T(8,128)S(1)}, u32[]{:S(2)}, u32[]{:S(2)}) %collective-permute-start.4) | collective-permute-done | bytes 262176 | tf_op jit(solution)/shard_map/ppermute | solution.py:194
  86.0 1.6 collective-permute-start.10
  87.6 2.8 %collective-permute-start.9 = (f32[32,2048]{1,0:T(8,128)S(1)}, f32[32,2048]{1,0:T(8,128)S(1)}, u32[]{:S(2)}, u32[]{:S(2)}) collective-permute-start(f32[32,2048]{1,0:T(8,128)S(1)} %collective-permute-done.5), channel_id=1, source_target_pairs={{0,14},{2,0},{4,2},{6,4},{8,6},{10,8},{12,10},{14,12},{1,15},{3,1}... | collective-permute-start | bytes 786440 | tf_op jit(solution)/shard_map/ppermute | solution.py:197
  90.4 1.1 collective-permute-start.12
  91.5 5.2 %collective-permute-done.7 = f32[32,2048]{1,0:T(8,128)S(1)} collective-permute-done((f32[32,2048]{1,0:T(8,128)S(1)}, f32[32,2048]{1,0:T(8,128)S(1)}, u32[]{:S(2)}, u32[]{:S(2)}) %collective-permute-start.7) | collective-permute-done | bytes 262176 | tf_op jit(solution)/shard_map/ppermute | solution.py:194
  96.8 2.9 %collective-permute-start.13 = (f32[16,2048]{1,0:T(8,128)S(1)}, f32[16,2048]{1,0:T(8,128)S(1)}, u32[]{:S(2)}, u32[]{:S(2)}) collective-permute-start(f32[16,2048]{1,0:T(8,128)S(1)} %slice.10), channel_id=1, source_target_pairs={{0,14},{2,0},{4,2},{6,4},{8,6},{10,8},{12,10},{14,12},{1,15},{3,1}... | collective-permute-start | bytes 393224 | tf_op jit(solution)/shard_map/ppermute | solution.py:197
  99.7 1.4 collective-permute-start.15
  102.2 1.9 %collective-permute-start.16 = (f32[32,2048]{1,0:T(8,128)S(1)}, f32[32,2048]{1,0:T(8,128)}, u32[]{:S(2)}, u32[]{:S(2)}) collective-permute-start(f32[32,2048]{1,0:T(8,128)S(1)} %constant_dynamic-update-slice_fusion), channel_id=1, source_target_pairs={{0,1},{1,0},{2,3},{3,2},{4,5},{5,4},{6,7},{7,6},{8,9},{9,8},{10,11... | collective-permute-start | bytes 786440 | tf_op jit(solution)/shard_map/ppermute | solution.py:200
  105.4 9.9 %shard_map.32 = (f32[2,256,2048]{2,1,0:T(8,128)}, f32[8,16,1152]{2,1,0:T(8,128)}) custom-call(s32[3]{0:T(128)} %pad_add_fusion.place_ref, f32[2,16,2048]{2,1,0:T(8,128)} %bitcast.24, f32[2,16,2048]{2,1,0:T(8,128)} %bitcast.29, f32[2,16,2048]{2,1,0:T(8,128)} %bitcast.30, f32[2,16,2048]{2,1,0:T(8,128)} %bitcast.31, f32[2,16,2048]{2,1,0:T(8,128)} %bitcast.34, ...), custom_call_target="tpu_custom_call" | custom-call | tf_op jit(solution)/shard_map/pallas_call | solution.py:265
  115.4 15.3 %all_to_all.22 = f32[8,16,1152]{2,1,0:T(8,128)S(1)} all-to-all(f32[8,16,1152]{2,1,0:T(8,128)} %get-tuple-element.31), channel_id=1, replica_groups=mesh['y'=4,'xh'=2,'xl'=2,'z'=8,'c'=2] {'y','xh'}, dimensions={0} | all-to-all | bytes 1179648 | tf_op jit(solution)/shard_map/all_to_all | solution.py:429
  130.8 13.9 %all_to_all.23.sums_ref = f32[8,16,1152]{2,1,0:T(8,128)S(1)} all-to-all(f32[8,16,1152]{2,1,0:T(8,128)S(1)} %broadcast_in_dim.3), channel_id=1, replica_groups=mesh['y'=4,'xh'=2,'xl'=2,'z'=8,'c'=2] {'y','xh'}, dimensions={0} | all-to-all | bytes 1179648 | tf_op jit(solution)/shard_map/all_to_all | solution.py:430
  144.7 2.6 %collective-permute-start.17 = (f32[8,16,640]{2,1,0:T(8,128)S(1)}, f32[8,16,640]{2,1,0:T(8,128)S(1)}, u32[]{:S(2)}, u32[]{:S(2)}) collective-permute-start(f32[8,16,640]{2,1,0:T(8,128)S(1)} %slice.12), channel_id=1, source_target_pairs={{0,1},{1,0},{2,3},{3,2},{4,5},{5,4},{6,7},{7,6},{8,9},{9,8},{10,11... | collective-permute-start | bytes 983048 | tf_op jit(solution)/shard_map/ppermute | solution.py:431
  147.3 1.3 collective-permute-done.17.by_core_ref
  148.6 28.0 %shard_map.33 = f32[4,2,8,32,128]{4,3,2,1,0:T(8,128)} custom-call(s32[3]{0:T(128)S(1)} %copy-done.2, f32[8,16,1152]{2,1,0:T(8,128)S(1)} %all_to_all.23.sums_ref, f32[8,16,640]{2,1,0:T(8,128)S(1)} %collective-permute-done.17.by_core_ref, f32[512,2048]{1,0:T(8,128)} %bitcast.23, f32[128,2048]{1,0:T(8,128)S(1)} %copy-done.1), custom_call_target="tpu_custom_call" | custom-call | tf_op jit(solution)/shard_map/pallas_call | solution.py:402
  (64 shorter events, 5.7 us)
Async XLA Ops:
  57.0 3.9 %collective-permute-start = (f32[16,2048]{1,0:T(8,128)S(1)}, f32[16,2048]{1,0:T(8,128)S(1)}, u32[]{:S(2)}, u32[]{:S(2)}) collective-permute-start(f32[16,2048]{1,0:T(8,128)S(1)} %shard_map.30), channel_id=1, source_target_pairs={{0,16},{16,0},{1,17},{17,1},{2,18},{18,2},{3,19},{19,3},{4,20},{20... | collective-permute-start | bytes 393224 | tf_op jit(solution)/shard_map/ppermute | solution.py:203
  61.0 44.3 %copy-start.3 = (f32[32,2048]{1,0:T(8,128)}, f32[32,2048]{1,0:T(8,128)S(1)}, u32[]{:S(2)}) copy-start(f32[32,2048]{1,0:T(8,128)S(1)} %pad_maximum_fusion) | copy-start | bytes 786436
  61.0 10.0 %collective-permute-start.3 = (f32[32,2048]{1,0:T(8,128)S(1)}, f32[32,2048]{1,0:T(8,128)S(1)}, u32[]{:S(2)}, u32[]{:S(2)}) collective-permute-start(f32[32,2048]{1,0:T(8,128)S(1)} %pad_maximum_fusion), channel_id=1, source_target_pairs={{0,1},{1,0},{2,3},{3,2},{4,5},{5,4},{6,7},{7,6},{8,9},{9,8},{10,11... | collective-permute-start | bytes 786440 | tf_op jit(solution)/shard_map/ppermute | solution.py:200
  65.4 12.2 %collective-permute-start.1 = (f32[32,2048]{1,0:T(8,128)S(1)}, f32[32,2048]{1,0:T(8,128)S(1)}, u32[]{:S(2)}, u32[]{:S(2)}) collective-permute-start(f32[32,2048]{1,0:T(8,128)S(1)} %pad_maximum_fusion), channel_id=1, source_target_pairs={{0,2},{2,4},{4,6},{6,8},{8,10},{10,12},{12,14},{14,0},{1,3},{3,5},... | collective-permute-start | bytes 786440 | tf_op jit(solution)/shard_map/ppermute | solution.py:194
  67.0 11.2 %collective-permute-start.2 = (f32[32,2048]{1,0:T(8,128)S(1)}, f32[32,2048]{1,0:T(8,128)S(1)}, u32[]{:S(2)}, u32[]{:S(2)}) collective-permute-start(f32[32,2048]{1,0:T(8,128)S(1)} %pad_maximum_fusion), channel_id=1, source_target_pairs={{0,14},{2,0},{4,2},{6,4},{8,6},{10,8},{12,10},{14,12},{1,15},{3,1}... | collective-permute-start | bytes 786440 | tf_op jit(solution)/shard_map/ppermute | solution.py:197
  71.0 34.3 %copy-start.7 = (f32[32,2048]{1,0:T(8,128)}, f32[32,2048]{1,0:T(8,128)S(1)}, u32[]{:S(2)}) copy-start(f32[32,2048]{1,0:T(8,128)S(1)} %collective-permute-done.3) | copy-start | bytes 786436
  77.6 27.8 %copy-start.8 = (f32[32,2048]{1,0:T(8,128)}, f32[32,2048]{1,0:T(8,128)S(1)}, u32[]{:S(2)}) copy-start(f32[32,2048]{1,0:T(8,128)S(1)} %collective-permute-done.1) | copy-start | bytes 786436
  77.6 8.4 %collective-permute-start.4 = (f32[32,2048]{1,0:T(8,128)S(1)}, f32[32,2048]{1,0:T(8,128)S(1)}, u32[]{:S(2)}, u32[]{:S(2)}) collective-permute-start(f32[32,2048]{1,0:T(8,128)S(1)} %collective-permute-done.1), channel_id=1, source_target_pairs={{0,2},{2,4},{4,6},{6,8},{8,10},{10,12},{12,14},{14,0},{1,3},{3,5},... | collective-permute-start | bytes 786440 | tf_op jit(solution)/shard_map/ppermute | solution.py:194
  77.6 8.4 %collective-permute-start.6 = (f32[32,2048]{1,0:T(8,128)S(1)}, f32[32,2048]{1,0:T(8,128)S(1)}, u32[]{:S(2)}, u32[]{:S(2)}) collective-permute-start(f32[32,2048]{1,0:T(8,128)S(1)} %collective-permute-done.1), channel_id=1, source_target_pairs={{0,1},{1,0},{2,3},{3,2},{4,5},{5,4},{6,7},{7,6},{8,9},{9,8},{10,11... | collective-permute-start | bytes 786440 | tf_op jit(solution)/shard_map/ppermute | solution.py:200
  78.2 27.1 %copy-start.9 = (f32[32,2048]{1,0:T(8,128)}, f32[32,2048]{1,0:T(8,128)S(1)}, u32[]{:S(2)}) copy-start(f32[32,2048]{1,0:T(8,128)S(1)} %collective-permute-done.2) | copy-start | bytes 786436
  78.2 9.3 %collective-permute-start.8 = (f32[32,2048]{1,0:T(8,128)S(1)}, f32[32,2048]{1,0:T(8,128)S(1)}, u32[]{:S(2)}, u32[]{:S(2)}) collective-permute-start(f32[32,2048]{1,0:T(8,128)S(1)} %collective-permute-done.2), channel_id=1, source_target_pairs={{0,1},{1,0},{2,3},{3,2},{4,5},{5,4},{6,7},{7,6},{8,9},{9,8},{10,11... | collective-permute-start | bytes 786440 | tf_op jit(solution)/shard_map/ppermute | solution.py:200
  78.3 9.2 %collective-permute-start.5 = (f32[32,2048]{1,0:T(8,128)S(1)}, f32[32,2048]{1,0:T(8,128)S(1)}, u32[]{:S(2)}, u32[]{:S(2)}) collective-permute-start(f32[32,2048]{1,0:T(8,128)S(1)} %collective-permute-done.2), channel_id=1, source_target_pairs={{0,14},{2,0},{4,2},{6,4},{8,6},{10,8},{12,10},{14,12},{1,15},{3,1}... | collective-permute-start | bytes 786440 | tf_op jit(solution)/shard_map/ppermute | solution.py:197
  86.0 19.4 %copy-start.10 = (f32[32,2048]{1,0:T(8,128)}, f32[32,2048]{1,0:T(8,128)S(1)}, u32[]{:S(2)}) copy-start(f32[32,2048]{1,0:T(8,128)S(1)} %collective-permute-done.4) | copy-start | bytes 786436
  86.0 19.4 %copy-start.11 = (f32[32,2048]{1,0:T(8,128)}, f32[32,2048]{1,0:T(8,128)S(1)}, u32[]{:S(2)}) copy-start(f32[32,2048]{1,0:T(8,128)S(1)} %collective-permute-done.6) | copy-start | bytes 786436
  86.0 5.5 %collective-permute-start.10 = (f32[32,2048]{1,0:T(8,128)S(1)}, f32[32,2048]{1,0:T(8,128)S(1)}, u32[]{:S(2)}, u32[]{:S(2)}) collective-permute-start(f32[32,2048]{1,0:T(8,128)S(1)} %collective-permute-done.4), channel_id=1, source_target_pairs={{0,1},{1,0},{2,3},{3,2},{4,5},{5,4},{6,7},{7,6},{8,9},{9,8},{10,11... | collective-permute-start | bytes 786440 | tf_op jit(solution)/shard_map/ppermute | solution.py:200
  87.6 9.1 %collective-permute-start.7 = (f32[32,2048]{1,0:T(8,128)S(1)}, f32[32,2048]{1,0:T(8,128)S(1)}, u32[]{:S(2)}, u32[]{:S(2)}) collective-permute-start(f32[32,2048]{1,0:T(8,128)S(1)} %collective-permute-done.4), channel_id=1, source_target_pairs={{0,2},{2,4},{4,6},{6,8},{8,10},{10,12},{12,14},{14,0},{1,3},{3,5},... | collective-permute-start | bytes 786440 | tf_op jit(solution)/shard_map/ppermute | solution.py:194
  87.6 9.2 %collective-permute-start.9 = (f32[32,2048]{1,0:T(8,128)S(1)}, f32[32,2048]{1,0:T(8,128)S(1)}, u32[]{:S(2)}, u32[]{:S(2)}) collective-permute-start(f32[32,2048]{1,0:T(8,128)S(1)} %collective-permute-done.5), channel_id=1, source_target_pairs={{0,14},{2,0},{4,2},{6,4},{8,6},{10,8},{12,10},{14,12},{1,15},{3,1}... | collective-permute-start | bytes 786440 | tf_op jit(solution)/shard_map/ppermute | solution.py:197
  90.4 6.4 %collective-permute-start.12 = (f32[32,2048]{1,0:T(8,128)S(1)}, f32[32,2048]{1,0:T(8,128)S(1)}, u32[]{:S(2)}, u32[]{:S(2)}) collective-permute-start(f32[32,2048]{1,0:T(8,128)S(1)} %collective-permute-done.5), channel_id=1, source_target_pairs={{0,1},{1,0},{2,3},{3,2},{4,5},{5,4},{6,7},{7,6},{8,9},{9,8},{10,11... | collective-permute-start | bytes 786440 | tf_op jit(solution)/shard_map/ppermute | solution.py:200
  96.7 5.4 %collective-permute-start.11 = (f32[16,2048]{1,0:T(8,128)S(1)}, f32[16,2048]{1,0:T(8,128)S(1)}, u32[]{:S(2)}, u32[]{:S(2)}) collective-permute-start(f32[16,2048]{1,0:T(8,128)S(1)} %slice.9), channel_id=1, source_target_pairs={{0,2},{2,4},{4,6},{6,8},{8,10},{10,12},{12,14},{14,0},{1,3},{3,5},... | collective-permute-start | bytes 393224 | tf_op jit(solution)/shard_map/ppermute | solution.py:194
  96.8 5.3 %collective-permute-start.13 = (f32[16,2048]{1,0:T(8,128)S(1)}, f32[16,2048]{1,0:T(8,128)S(1)}, u32[]{:S(2)}, u32[]{:S(2)}) collective-permute-start(f32[16,2048]{1,0:T(8,128)S(1)} %slice.10), channel_id=1, source_target_pairs={{0,14},{2,0},{4,2},{6,4},{8,6},{10,8},{12,10},{14,12},{1,15},{3,1}... | collective-permute-start | bytes 393224 | tf_op jit(solution)/shard_map/ppermute | solution.py:197
  99.7 4.9 %collective-permute-start.15 = (f32[32,2048]{1,0:T(8,128)S(1)}, f32[32,2048]{1,0:T(8,128)}, u32[]{:S(2)}, u32[]{:S(2)}) collective-permute-start(f32[32,2048]{1,0:T(8,128)S(1)} %collective-permute-done.9), channel_id=1, source_target_pairs={{0,1},{1,0},{2,3},{3,2},{4,5},{5,4},{6,7},{7,6},{8,9},{9,8},{10,11... | collective-permute-start | bytes 786440 | tf_op jit(solution)/shard_map/ppermute | solution.py:200
  101.2 3.5 %collective-permute-start.14 = (f32[32,2048]{1,0:T(8,128)S(1)}, f32[32,2048]{1,0:T(8,128)}, u32[]{:S(2)}, u32[]{:S(2)}) collective-permute-start(f32[32,2048]{1,0:T(8,128)S(1)} %collective-permute-done.7), channel_id=1, source_target_pairs={{0,1},{1,0},{2,3},{3,2},{4,5},{5,4},{6,7},{7,6},{8,9},{9,8},{10,11... | collective-permute-start | bytes 786440 | tf_op jit(solution)/shard_map/ppermute | solution.py:200
  102.2 3.1 %collective-permute-start.16 = (f32[32,2048]{1,0:T(8,128)S(1)}, f32[32,2048]{1,0:T(8,128)}, u32[]{:S(2)}, u32[]{:S(2)}) collective-permute-start(f32[32,2048]{1,0:T(8,128)S(1)} %constant_dynamic-update-slice_fusion), channel_id=1, source_target_pairs={{0,1},{1,0},{2,3},{3,2},{4,5},{5,4},{6,7},{7,6},{8,9},{9,8},{10,11... | collective-permute-start | bytes 786440 | tf_op jit(solution)/shard_map/ppermute | solution.py:200
  144.7 3.9 %collective-permute-start.17 = (f32[8,16,640]{2,1,0:T(8,128)S(1)}, f32[8,16,640]{2,1,0:T(8,128)S(1)}, u32[]{:S(2)}, u32[]{:S(2)}) collective-permute-start(f32[8,16,640]{2,1,0:T(8,128)S(1)} %slice.12), channel_id=1, source_target_pairs={{0,1},{1,0},{2,3},{3,2},{4,5},{5,4},{6,7},{7,6},{8,9},{9,8},{10,11... | collective-permute-start | bytes 983048 | tf_op jit(solution)/shard_map/ppermute | solution.py:431
  (10 other events, 115.3 us)

commit v10 on v9

--- a/solution.py
+++ b/solution.py
@@ -218,66 +218,57 @@
 OFFSETS = (0, -1, 1, -2, 2, -3, 3, 4)
 
 
+def collect(blocks, z, core, panel_ref, sems, cut, points):
+    copies = []
+    for flip in range(2):
+        for k, offset in enumerate(OFFSETS):
+            first = (((z + offset) & 7) * 2 + (core ^ flip)) * 16
+            target = panel_ref.at[:, pl.ds(pl.multiple_of(first, 16), 16), points]
+            source = blocks[flip * 8 + k].at[:, :, points]
+            copies.append(pltpu.make_async_copy(source, target, sems.at[cut * 16 + len(copies)]))
+            copies[-1].start()
+    return copies
+
+
 def products_kernel(place_ref, *refs):
-    blocks, (field_ref, home_ref, out_ref, panel_ref, acc, corner, sems) = refs[:16], refs[16:]
+    blocks, (field_ref, out_ref, panel_ref, acc, corner, sems) = refs[:16], refs[16:]
     z, core = place_ref[1], place_ref[2]
-    copies = []
-    for half in range(2):
-        points = pl.ds(half * 1024, 1024)
-        for flip in range(2):
-            for k, offset in enumerate(OFFSETS):
-                first = (((z + offset) & 7) * 2 + (core ^ flip)) * 16
-                target = panel_ref.at[:, pl.ds(pl.multiple_of(first, 16), 16), points]
-                copies.append(pltpu.make_async_copy(blocks[flip * 8 + k].at[:, :, points], target, sems.at[len(copies)]))
-                copies[-1].start()
+    copies = [collect(blocks, z, core, panel_ref, sems, cut, pl.ds(cut * 512, 512)) for cut in range(4)]
     long = pl.ds(pl.multiple_of((1 - core) * 128, 128), 128)
     short = pl.ds(pl.multiple_of(core * 128, 128), 128)
     acc[...] = jnp.zeros_like(acc)
     corner[...] = jnp.zeros_like(corner)
 
-    def chunk(i, _):
-        points = pl.ds(pl.multiple_of(i * 512, 512), 512)
+    for cut in range(4):
+        for copy in copies[cut]:
+            copy.wait()
+        points = pl.ds(cut * 512, 512)
         rows = jnp.concatenate([panel_ref[1, long, points], field_ref[:, points]], axis=0)
         acc[...] += dot_nt(rows, panel_ref[:, :, points].reshape(PANEL, 512))
         corner[...] += dot_nt(panel_ref[0, short, points], panel_ref[0, :, points])
-        return 0
-
-    homes = []
-    for half in range(2):
-        for copy in copies[half * 16 : half * 16 + 16]:
-            copy.wait()
-        for part in range(8):
-            place = (slice(None), pl.ds(part * 32, 32), pl.ds(half * 1024, 1024))
-            homes.append(pltpu.make_async_copy(panel_ref.at[place], home_ref.at[place], sems.at[32 + len(homes)]))
-            homes[-1].start()
-        lax.fori_loop(half * 2, half * 2 + 2, chunk, 0)
     for s in range(8):
         rows = slice(s * 16, s * 16 + 16)
         out_ref[s, :, 0:384] = acc[rows, 0:384]
         out_ref[s, :, 384:512] = jnp.where(core == 0, acc[rows, 384:512], corner[rows, 128:256])
         out_ref[s, :, 512:640] = corner[rows, 0:128]
         out_ref[s, :, 640:1152] = acc[128 + s * 16 : 128 + s * 16 + 16, :]
-    for copy in homes:
-        copy.wait()
 
 
 def products(place, blocks, field):
-    panel, terms = pl.pallas_call(
+    return pl.pallas_call(
         products_kernel,
         in_specs=[pl.BlockSpec(memory_space=pltpu.SMEM)]
         + [pl.BlockSpec(memory_space=pl.ANY)] * 16
         + [pl.BlockSpec(memory_space=pltpu.VMEM)],
-        out_shape=(jax.ShapeDtypeStruct((2, 256, 2048), jnp.float32), jax.ShapeDtypeStruct((8, 16, 1152), jnp.float32)),
-        out_specs=(pl.BlockSpec(memory_space=pl.ANY), pl.BlockSpec(memory_space=pltpu.VMEM)),
+        out_shape=jax.ShapeDtypeStruct((8, 16, 1152), jnp.float32),
         scratch_shapes=[
             pltpu.VMEM((2, 256, 2048), jnp.float32),
             pltpu.VMEM((256, 512), jnp.float32),
             pltpu.VMEM((128, 256), jnp.float32),
-            pltpu.SemaphoreType.DMA((48,)),
+            pltpu.SemaphoreType.DMA((64,)),
         ],
         compiler_params=pltpu.CompilerParams(vmem_limit_bytes=BIG * MIB),
-    )(place, *(block.reshape(2, 16, 2048) for block in blocks), field)
-    return panel.reshape(PANEL, 2048), terms
+    )(place, *blocks, field)
 
 
 def total_of(terms):
@@ -367,17 +358,13 @@
     lax.fori_loop(0, 4, diagonal, 0)
 
 
-def update_kernel(place_ref, sums_ref, by_core_ref, panel_ref, field_ref, out_ref, *scratch):
-    work, inverse, coupling, mixer, held, sems = scratch
+def update_kernel(place_ref, sums_ref, by_core_ref, field_ref, *refs):
+    blocks, (out_ref, work, inverse, coupling, mixer, held, sems) = refs[:16], refs[16:]
     xl, z, core = place_ref[0], place_ref[1], place_ref[2]
 
     @pl.when(pl.program_id(0) == 0)
     def _():
-        copies = []
-        for part in range(8):
-            rows = pl.ds(part * 64, 64)
-            copies.append(pltpu.make_async_copy(panel_ref.at[rows, :], held.at[rows, :], sems.at[part]))
-            copies[-1].start()
+        copies = collect(blocks, z, core, held, sems, 0, pl.ds(0, 2048))
         invert((sums_ref, by_core_ref), core, work, inverse)
         for s in range(8):
             coupling[s * 16 : s * 16 + 16, :] = sums_ref[s, :, 640:1152] * (1.0 / POINTS)
@@ -390,7 +377,7 @@
 
     keep = lax.broadcasted_iota(jnp.int32, (128, 512), 0) >= 16
     points = pl.ds(pl.multiple_of(pl.program_id(0) * 512, 512), 512)
-    moved = (dot_nn(mixer[...], held[:, points]) + jnp.where(keep, field_ref[...], 0.0)).T
+    moved = (dot_nn(mixer[...], held[:, :, points].reshape(PANEL, 512)) + jnp.where(keep, field_ref[...], 0.0)).T
     for low in range(2):
         for xp in range(4):
             for yh in range(2):
@@ -398,7 +385,7 @@
                 out_ref[xp, yh, low] = moved[first : first + 32, :]
 
 
-def update(place, sums, by_core, panel, field):
+def update(place, sums, by_core, field, blocks):
     out = pl.pallas_call(
         update_kernel,
         grid=(4,),
@@ -406,16 +393,16 @@
             pl.BlockSpec(memory_space=pltpu.SMEM),
             pl.BlockSpec((8, 16, 1152), lambda i: (0, 0, 0)),
             pl.BlockSpec((8, 16, 640), lambda i: (0, 0, 0)),
-            pl.BlockSpec(memory_space=pl.ANY),
             pl.BlockSpec((128, 512), lambda i: (0, i)),
+            *[pl.BlockSpec(memory_space=pl.ANY)] * 16,
         ],
         out_specs=pl.BlockSpec((4, 2, 2, 32, 128), lambda i: (0, 0, i, 0, 0)),
         out_shape=jax.ShapeDtypeStruct((4, 2, 8, 32, 128), jnp.float32),
         scratch_shapes=[pltpu.VMEM((PANEL, PANEL), jnp.float32)] * 2
         + [pltpu.VMEM((128, PANEL), jnp.float32)] * 2
-        + [pltpu.VMEM((PANEL, 2048), jnp.float32), pltpu.SemaphoreType.DMA((8,))],
-        compiler_params=pltpu.CompilerParams(vmem_limit_bytes=52 * MIB),
-    )(place, sums, by_core, panel, field)
+        + [pltpu.VMEM((2, 256, 2048), jnp.float32), pltpu.SemaphoreType.DMA((16,))],
+        compiler_params=pltpu.CompilerParams(vmem_limit_bytes=48 * MIB),
+    )(place, sums, by_core, field, *blocks)
     return out.reshape(4, 16, 32, 128)
 
 
@@ -425,11 +412,12 @@
     received = lax.all_to_all(pack(orbitals, potential), SPACE, 0, 0, tiled=True)
     back = lax.all_to_all(chebyshev(received), SPACE, 0, 0, tiled=True)
     blocks, field = gather_panel(turn(back, 1), turn(back, 8), xl)
-    panel, terms = products(place, blocks, field)
+    blocks = [block.reshape(2, 16, 2048) for block in blocks]
+    terms = products(place, blocks, field)
     mine = jnp.sum(lax.all_to_all(terms, SPACE, 0, 0, tiled=True), axis=0)
     sums = lax.all_to_all(jnp.broadcast_to(mine, (8, 16, 1152)), SPACE, 0, 0, tiled=True)
     by_core = lax.ppermute(sums[:, :, :640], "c", ring(2, 1))
-    return update(place, sums, by_core, panel, field)
+    return update(place, sums, by_core, field, blocks)
 
 
 def solution(mesh):

time: 177 us -> 181 us (1.023)
  Pallas kernels: 53.7 us -> 55.9 us
    pallas_call x1, Pallas kernels: 9.93 us -> 11.7 us  [products(): pl.pallas_call(products_kernel, in_specs=[pl.BlockSpec(memory_space=pltpu...]
where the time goes in v10:
time: 181 us; the launch traced here: 180 us
  blocking collectives  71.5 us (40%)
  Pallas kernels  55.9 us (31%)
  starting transfers between devices  28.5 us (16%)
  waiting for transfers between devices  21 us (12%)
  local copies, waits for them, and re-layouts  2.12 us (1%)
    pallas_call x1, Pallas kernels, update(): pl.pallas_call(update_kernel, grid=(4,), in_specs=[pl.BlockSpec(memory_sp...  28.3 us
    all_to_all x1, blocking collectives, per_device(): lax.all_to_all(pack(orbitals, potential), SPACE, 0, 0, tiled=True)  24.2 us
    all_to_all x1, blocking collectives, per_device(): back = lax.all_to_all(chebyshev(received), SPACE, 0, 0, tiled=True)  17.8 us
    ppermute x4, waiting for transfers between devices, right(): return lax.ppermute(block, 'z', ring(8, 1))  17.4 us
    all_to_all x1, blocking collectives, per_device(): mine = jnp.sum(lax.all_to_all(terms, SPACE, 0, 0, tiled=True), axis=0)  15.4 us
    all_to_all x1, blocking collectives, per_device(): lax.all_to_all(jnp.broadcast_to(mine, (8, 16, 1152)), SPACE, 0, 0, tiled=...  14 us
    ppermute x4, starting transfers between devices, left(): return lax.ppermute(block, 'z', ring(8, -1))  12.5 us
    pallas_call x1, Pallas kernels, products(): pl.pallas_call(products_kernel, in_specs=[pl.BlockSpec(memory_space=pltpu...  11.7 us
  transfers between devices with their start and end apart: 18, of which 7 were waited for; matrix products, arithmetic and copies ran while one was open for 0% of the time, Pallas kernels for 0%

profile of v10, /device:TPU:1, one launch (start us, length us, event | category | flops | bytes accessed | tf_op | source)
XLA Modules:
  0.0 180.3 jit_solution(2972782375526624683)
XLA Ops:
  0.0 3.6 %shard_map.28 = f32[8,272,128]{2,1,0:T(8,128)} custom-call(f32[4,16,32,128]{3,2,1,0:T(8,128)} %orb_ref.1, f32[4,16,32]{2,1,0:T(8,128)} %pot_ref.1), custom_call_target="tpu_custom_call" | custom-call | tf_op jit(solution)/shard_map/pallas_call | solution.py:75
  3.6 24.2 %all_to_all.20.in_ref = f32[8,272,128]{2,1,0:T(8,128)S(1)} all-to-all(f32[8,272,128]{2,1,0:T(8,128)} %shard_map.28), channel_id=1, replica_groups=mesh['y'=4,'xh'=2,'xl'=2,'z'=8,'c'=2] {'y','xh'}, dimensions={0} | all-to-all | bytes 2228224 | tf_op jit(solution)/shard_map/all_to_all | solution.py:412
  27.7 11.3 %shard_map.29 = f32[64,32,128]{2,1,0:T(8,128)S(1)} custom-call(f32[8,272,128]{2,1,0:T(8,128)S(1)} %all_to_all.20.in_ref), custom_call_target="tpu_custom_call" | custom-call | tf_op jit(solution)/shard_map/pallas_call | solution.py:161
  39.1 17.8 %all_to_all.21.in_ref = f32[8,256,128]{2,1,0:T(8,128)S(1)} all-to-all(f32[8,256,128]{2,1,0:T(8,128)S(1)} %bitcast.21), channel_id=1, replica_groups=mesh['y'=4,'xh'=2,'xl'=2,'z'=8,'c'=2] {'y','xh'}, dimensions={0} | all-to-all | bytes 2097152 | tf_op jit(solution)/shard_map/all_to_all | solution.py:413
  59.2 1.7 collective-permute-done
  61.0 4.4 %collective-permute-start.3 = (f32[32,2048]{1,0:T(8,128)S(1)}, f32[32,2048]{1,0:T(8,128)S(1)}, u32[]{:S(2)}, u32[]{:S(2)}) collective-permute-start(f32[32,2048]{1,0:T(8,128)S(1)} %pad_maximum_fusion), channel_id=1, source_target_pairs={{0,1},{1,0},{2,3},{3,2},{4,5},{5,4},{6,7},{7,6},{8,9},{9,8},{10,11... | collective-permute-start | bytes 786440 | tf_op jit(solution)/shard_map/ppermute | solution.py:200
  65.4 1.7 collective-permute-start.1
  67.0 3.9 %collective-permute-start.2 = (f32[32,2048]{1,0:T(8,128)S(1)}, f32[32,2048]{1,0:T(8,128)S(1)}, u32[]{:S(2)}, u32[]{:S(2)}) collective-permute-start(f32[32,2048]{1,0:T(8,128)S(1)} %pad_maximum_fusion), channel_id=1, source_target_pairs={{0,14},{2,0},{4,2},{6,4},{8,6},{10,8},{12,10},{14,12},{1,15},{3,1}... | collective-permute-start | bytes 786440 | tf_op jit(solution)/shard_map/ppermute | solution.py:197
  71.0 6.6 %collective-permute-done.1 = f32[32,2048]{1,0:T(8,128)S(1)} collective-permute-done((f32[32,2048]{1,0:T(8,128)S(1)}, f32[32,2048]{1,0:T(8,128)S(1)}, u32[]{:S(2)}, u32[]{:S(2)}) %collective-permute-start.1) | collective-permute-done | bytes 262176 | tf_op jit(solution)/shard_map/ppermute | solution.py:194
  78.3 2.9 %collective-permute-start.5 = (f32[32,2048]{1,0:T(8,128)S(1)}, f32[32,2048]{1,0:T(8,128)S(1)}, u32[]{:S(2)}, u32[]{:S(2)}) collective-permute-start(f32[32,2048]{1,0:T(8,128)S(1)} %collective-permute-done.2), channel_id=1, source_target_pairs={{0,14},{2,0},{4,2},{6,4},{8,6},{10,8},{12,10},{14,12},{1,15},{3,1}... | collective-permute-start | bytes 786440 | tf_op jit(solution)/shard_map/ppermute | solution.py:197
  81.3 4.7 %collective-permute-done.4 = f32[32,2048]{1,0:T(8,128)S(1)} collective-permute-done((f32[32,2048]{1,0:T(8,128)S(1)}, f32[32,2048]{1,0:T(8,128)S(1)}, u32[]{:S(2)}, u32[]{:S(2)}) %collective-permute-start.4) | collective-permute-done | bytes 262176 | tf_op jit(solution)/shard_map/ppermute | solution.py:194
  86.0 1.6 collective-permute-start.10
  87.6 2.8 %collective-permute-start.9 = (f32[32,2048]{1,0:T(8,128)S(1)}, f32[32,2048]{1,0:T(8,128)S(1)}, u32[]{:S(2)}, u32[]{:S(2)}) collective-permute-start(f32[32,2048]{1,0:T(8,128)S(1)} %collective-permute-done.5), channel_id=1, source_target_pairs={{0,14},{2,0},{4,2},{6,4},{8,6},{10,8},{12,10},{14,12},{1,15},{3,1}... | collective-permute-start | bytes 786440 | tf_op jit(solution)/shard_map/ppermute | solution.py:197
  90.4 1.1 collective-permute-start.12
  91.5 5.2 %collective-permute-done.7 = f32[32,2048]{1,0:T(8,128)S(1)} collective-permute-done((f32[32,2048]{1,0:T(8,128)S(1)}, f32[32,2048]{1,0:T(8,128)S(1)}, u32[]{:S(2)}, u32[]{:S(2)}) %collective-permute-start.7) | collective-permute-done | bytes 262176 | tf_op jit(solution)/shard_map/ppermute | solution.py:194
  96.8 2.9 %collective-permute-start.13 = (f32[16,2048]{1,0:T(8,128)S(1)}, f32[16,2048]{1,0:T(8,128)S(1)}, u32[]{:S(2)}, u32[]{:S(2)}) collective-permute-start(f32[16,2048]{1,0:T(8,128)S(1)} %slice.10), channel_id=1, source_target_pairs={{0,14},{2,0},{4,2},{6,4},{8,6},{10,8},{12,10},{14,12},{1,15},{3,1}... | collective-permute-start | bytes 393224 | tf_op jit(solution)/shard_map/ppermute | solution.py:197
  99.7 1.4 collective-permute-start.15
  102.2 1.9 %collective-permute-start.16 = (f32[32,2048]{1,0:T(8,128)S(1)}, f32[32,2048]{1,0:T(8,128)}, u32[]{:S(2)}, u32[]{:S(2)}) collective-permute-start(f32[32,2048]{1,0:T(8,128)S(1)} %constant_dynamic-update-slice_fusion), channel_id=1, source_target_pairs={{0,1},{1,0},{2,3},{3,2},{4,5},{5,4},{6,7},{7,6},{8,9},{9,8},{10,11... | collective-permute-start | bytes 786440 | tf_op jit(solution)/shard_map/ppermute | solution.py:200
  105.4 11.7 %shard_map.32 = f32[8,16,1152]{2,1,0:T(8,128)} custom-call(s32[3]{0:T(128)} %pad_add_fusion.place_ref, f32[2,16,2048]{2,1,0:T(8,128)} %bitcast.22, f32[2,16,2048]{2,1,0:T(8,128)} %bitcast.32, f32[2,16,2048]{2,1,0:T(8,128)} %bitcast.34, f32[2,16,2048]{2,1,0:T(8,128)} %bitcast.36, f32[2,16,2048]{2,1,0:T(8,128)} %bitcast.42, f32[2,16,2048]{2,1,0:T(8,128)} %bitcast.24, ...), custom_call_target="tpu_custom_call" | custom-call | tf_op jit(solution)/shard_map/pallas_call | solution.py:258
  117.2 15.4 %all_to_all.22 = f32[8,16,1152]{2,1,0:T(8,128)S(1)} all-to-all(f32[8,16,1152]{2,1,0:T(8,128)} %shard_map.32), channel_id=1, replica_groups=mesh['y'=4,'xh'=2,'xl'=2,'z'=8,'c'=2] {'y','xh'}, dimensions={0} | all-to-all | bytes 1179648 | tf_op jit(solution)/shard_map/all_to_all | solution.py:417
  132.8 14.0 %all_to_all.23.sums_ref = f32[8,16,1152]{2,1,0:T(8,128)S(1)} all-to-all(f32[8,16,1152]{2,1,0:T(8,128)S(1)} %broadcast_in_dim.3), channel_id=1, replica_groups=mesh['y'=4,'xh'=2,'xl'=2,'z'=8,'c'=2] {'y','xh'}, dimensions={0} | all-to-all | bytes 1179648 | tf_op jit(solution)/shard_map/all_to_all | solution.py:418
  146.9 2.6 %collective-permute-start.17 = (f32[8,16,640]{2,1,0:T(8,128)S(1)}, f32[8,16,640]{2,1,0:T(8,128)S(1)}, u32[]{:S(2)}, u32[]{:S(2)}) collective-permute-start(f32[8,16,640]{2,1,0:T(8,128)S(1)} %slice.12), channel_id=1, source_target_pairs={{0,1},{1,0},{2,3},{3,2},{4,5},{5,4},{6,7},{7,6},{8,9},{9,8},{10,11... | collective-permute-start | bytes 983048 | tf_op jit(solution)/shard_map/ppermute | solution.py:419
  149.5 1.3 collective-permute-done.17.by_core_ref
  151.8 28.3 %shard_map.33 = f32[4,2,8,32,128]{4,3,2,1,0:T(8,128)} custom-call(s32[3]{0:T(128)S(1)} %copy-done.28, f32[8,16,1152]{2,1,0:T(8,128)S(1)} %all_to_all.23.sums_ref, f32[8,16,640]{2,1,0:T(8,128)S(1)} %collective-permute-done.17.by_core_ref, f32[128,2048]{1,0:T(8,128)S(1)} %copy-done.1, f32[2,16,2048]{2,1,0:T(8,128)S(1)} %bitcast.23, ...), custom_call_target="tpu_custom_call" | custom-call | tf_op jit(solution)/shard_map/pallas_call | solution.py:389
  (90 shorter events, 6.7 us)
Async XLA Ops:
  57.0 3.9 %collective-permute-start = (f32[16,2048]{1,0:T(8,128)S(1)}, f32[16,2048]{1,0:T(8,128)S(1)}, u32[]{:S(2)}, u32[]{:S(2)}) collective-permute-start(f32[16,2048]{1,0:T(8,128)S(1)} %shard_map.30), channel_id=1, source_target_pairs={{0,16},{16,0},{1,17},{17,1},{2,18},{18,2},{3,19},{19,3},{4,20},{20... | collective-permute-start | bytes 393224 | tf_op jit(solution)/shard_map/ppermute | solution.py:203
  61.0 44.4 %copy-start.2 = (f32[32,2048]{1,0:T(8,128)}, f32[32,2048]{1,0:T(8,128)S(1)}, u32[]{:S(2)}) copy-start(f32[32,2048]{1,0:T(8,128)S(1)} %pad_maximum_fusion) | copy-start | bytes 786436
  61.0 10.0 %collective-permute-start.3 = (f32[32,2048]{1,0:T(8,128)S(1)}, f32[32,2048]{1,0:T(8,128)S(1)}, u32[]{:S(2)}, u32[]{:S(2)}) collective-permute-start(f32[32,2048]{1,0:T(8,128)S(1)} %pad_maximum_fusion), channel_id=1, source_target_pairs={{0,1},{1,0},{2,3},{3,2},{4,5},{5,4},{6,7},{7,6},{8,9},{9,8},{10,11... | collective-permute-start | bytes 786440 | tf_op jit(solution)/shard_map/ppermute | solution.py:200
  65.4 12.2 %collective-permute-start.1 = (f32[32,2048]{1,0:T(8,128)S(1)}, f32[32,2048]{1,0:T(8,128)S(1)}, u32[]{:S(2)}, u32[]{:S(2)}) collective-permute-start(f32[32,2048]{1,0:T(8,128)S(1)} %pad_maximum_fusion), channel_id=1, source_target_pairs={{0,2},{2,4},{4,6},{6,8},{8,10},{10,12},{12,14},{14,0},{1,3},{3,5},... | collective-permute-start | bytes 786440 | tf_op jit(solution)/shard_map/ppermute | solution.py:194
  67.0 11.2 %collective-permute-start.2 = (f32[32,2048]{1,0:T(8,128)S(1)}, f32[32,2048]{1,0:T(8,128)S(1)}, u32[]{:S(2)}, u32[]{:S(2)}) collective-permute-start(f32[32,2048]{1,0:T(8,128)S(1)} %pad_maximum_fusion), channel_id=1, source_target_pairs={{0,14},{2,0},{4,2},{6,4},{8,6},{10,8},{12,10},{14,12},{1,15},{3,1}... | collective-permute-start | bytes 786440 | tf_op jit(solution)/shard_map/ppermute | solution.py:197
  71.0 34.3 %copy-start.10 = (f32[32,2048]{1,0:T(8,128)}, f32[32,2048]{1,0:T(8,128)S(1)}, u32[]{:S(2)}) copy-start(f32[32,2048]{1,0:T(8,128)S(1)} %collective-permute-done.3) | copy-start | bytes 786436
  77.6 8.4 %collective-permute-start.4 = (f32[32,2048]{1,0:T(8,128)S(1)}, f32[32,2048]{1,0:T(8,128)S(1)}, u32[]{:S(2)}, u32[]{:S(2)}) collective-permute-start(f32[32,2048]{1,0:T(8,128)S(1)} %collective-permute-done.1), channel_id=1, source_target_pairs={{0,2},{2,4},{4,6},{6,8},{8,10},{10,12},{12,14},{14,0},{1,3},{3,5},... | collective-permute-start | bytes 786440 | tf_op jit(solution)/shard_map/ppermute | solution.py:194
  77.6 8.4 %collective-permute-start.6 = (f32[32,2048]{1,0:T(8,128)S(1)}, f32[32,2048]{1,0:T(8,128)S(1)}, u32[]{:S(2)}, u32[]{:S(2)}) collective-permute-start(f32[32,2048]{1,0:T(8,128)S(1)} %collective-permute-done.1), channel_id=1, source_target_pairs={{0,1},{1,0},{2,3},{3,2},{4,5},{5,4},{6,7},{7,6},{8,9},{9,8},{10,11... | collective-permute-start | bytes 786440 | tf_op jit(solution)/shard_map/ppermute | solution.py:200
  78.2 9.3 %collective-permute-start.8 = (f32[32,2048]{1,0:T(8,128)S(1)}, f32[32,2048]{1,0:T(8,128)S(1)}, u32[]{:S(2)}, u32[]{:S(2)}) collective-permute-start(f32[32,2048]{1,0:T(8,128)S(1)} %collective-permute-done.2), channel_id=1, source_target_pairs={{0,1},{1,0},{2,3},{3,2},{4,5},{5,4},{6,7},{7,6},{8,9},{9,8},{10,11... | collective-permute-start | bytes 786440 | tf_op jit(solution)/shard_map/ppermute | solution.py:200
  78.3 9.2 %collective-permute-start.5 = (f32[32,2048]{1,0:T(8,128)S(1)}, f32[32,2048]{1,0:T(8,128)S(1)}, u32[]{:S(2)}, u32[]{:S(2)}) collective-permute-start(f32[32,2048]{1,0:T(8,128)S(1)} %collective-permute-done.2), channel_id=1, source_target_pairs={{0,14},{2,0},{4,2},{6,4},{8,6},{10,8},{12,10},{14,12},{1,15},{3,1}... | collective-permute-start | bytes 786440 | tf_op jit(solution)/shard_map/ppermute | solution.py:197
  86.0 5.5 %collective-permute-start.10 = (f32[32,2048]{1,0:T(8,128)S(1)}, f32[32,2048]{1,0:T(8,128)S(1)}, u32[]{:S(2)}, u32[]{:S(2)}) collective-permute-start(f32[32,2048]{1,0:T(8,128)S(1)} %collective-permute-done.4), channel_id=1, source_target_pairs={{0,1},{1,0},{2,3},{3,2},{4,5},{5,4},{6,7},{7,6},{8,9},{9,8},{10,11... | collective-permute-start | bytes 786440 | tf_op jit(solution)/shard_map/ppermute | solution.py:200
  87.6 9.1 %collective-permute-start.7 = (f32[32,2048]{1,0:T(8,128)S(1)}, f32[32,2048]{1,0:T(8,128)S(1)}, u32[]{:S(2)}, u32[]{:S(2)}) collective-permute-start(f32[32,2048]{1,0:T(8,128)S(1)} %collective-permute-done.4), channel_id=1, source_target_pairs={{0,2},{2,4},{4,6},{6,8},{8,10},{10,12},{12,14},{14,0},{1,3},{3,5},... | collective-permute-start | bytes 786440 | tf_op jit(solution)/shard_map/ppermute | solution.py:194
  87.6 9.2 %collective-permute-start.9 = (f32[32,2048]{1,0:T(8,128)S(1)}, f32[32,2048]{1,0:T(8,128)S(1)}, u32[]{:S(2)}, u32[]{:S(2)}) collective-permute-start(f32[32,2048]{1,0:T(8,128)S(1)} %collective-permute-done.5), channel_id=1, source_target_pairs={{0,14},{2,0},{4,2},{6,4},{8,6},{10,8},{12,10},{14,12},{1,15},{3,1}... | collective-permute-start | bytes 786440 | tf_op jit(solution)/shard_map/ppermute | solution.py:197
  90.4 6.4 %collective-permute-start.12 = (f32[32,2048]{1,0:T(8,128)S(1)}, f32[32,2048]{1,0:T(8,128)S(1)}, u32[]{:S(2)}, u32[]{:S(2)}) collective-permute-start(f32[32,2048]{1,0:T(8,128)S(1)} %collective-permute-done.5), channel_id=1, source_target_pairs={{0,1},{1,0},{2,3},{3,2},{4,5},{5,4},{6,7},{7,6},{8,9},{9,8},{10,11... | collective-permute-start | bytes 786440 | tf_op jit(solution)/shard_map/ppermute | solution.py:200
  96.7 5.4 %collective-permute-start.11 = (f32[16,2048]{1,0:T(8,128)S(1)}, f32[16,2048]{1,0:T(8,128)S(1)}, u32[]{:S(2)}, u32[]{:S(2)}) collective-permute-start(f32[16,2048]{1,0:T(8,128)S(1)} %slice.9), channel_id=1, source_target_pairs={{0,2},{2,4},{4,6},{6,8},{8,10},{10,12},{12,14},{14,0},{1,3},{3,5},... | collective-permute-start | bytes 393224 | tf_op jit(solution)/shard_map/ppermute | solution.py:194
  96.8 5.3 %collective-permute-start.13 = (f32[16,2048]{1,0:T(8,128)S(1)}, f32[16,2048]{1,0:T(8,128)S(1)}, u32[]{:S(2)}, u32[]{:S(2)}) collective-permute-start(f32[16,2048]{1,0:T(8,128)S(1)} %slice.10), channel_id=1, source_target_pairs={{0,14},{2,0},{4,2},{6,4},{8,6},{10,8},{12,10},{14,12},{1,15},{3,1}... | collective-permute-start | bytes 393224 | tf_op jit(solution)/shard_map/ppermute | solution.py:197
  99.7 4.9 %collective-permute-start.15 = (f32[32,2048]{1,0:T(8,128)S(1)}, f32[32,2048]{1,0:T(8,128)}, u32[]{:S(2)}, u32[]{:S(2)}) collective-permute-start(f32[32,2048]{1,0:T(8,128)S(1)} %collective-permute-done.9), channel_id=1, source_target_pairs={{0,1},{1,0},{2,3},{3,2},{4,5},{5,4},{6,7},{7,6},{8,9},{9,8},{10,11... | collective-permute-start | bytes 786440 | tf_op jit(solution)/shard_map/ppermute | solution.py:200
  101.1 3.5 %collective-permute-start.14 = (f32[32,2048]{1,0:T(8,128)S(1)}, f32[32,2048]{1,0:T(8,128)}, u32[]{:S(2)}, u32[]{:S(2)}) collective-permute-start(f32[32,2048]{1,0:T(8,128)S(1)} %collective-permute-done.7), channel_id=1, source_target_pairs={{0,1},{1,0},{2,3},{3,2},{4,5},{5,4},{6,7},{7,6},{8,9},{9,8},{10,11... | collective-permute-start | bytes 786440 | tf_op jit(solution)/shard_map/ppermute | solution.py:200
  102.2 3.1 %collective-permute-start.16 = (f32[32,2048]{1,0:T(8,128)S(1)}, f32[32,2048]{1,0:T(8,128)}, u32[]{:S(2)}, u32[]{:S(2)}) collective-permute-start(f32[32,2048]{1,0:T(8,128)S(1)} %constant_dynamic-update-slice_fusion), channel_id=1, source_target_pairs={{0,1},{1,0},{2,3},{3,2},{4,5},{5,4},{6,7},{7,6},{8,9},{9,8},{10,11... | collective-permute-start | bytes 786440 | tf_op jit(solution)/shard_map/ppermute | solution.py:200
  117.2 33.6 %copy-start.19 = (f32[32,2048]{1,0:T(8,128)S(1)}, f32[32,2048]{1,0:T(8,128)}, u32[]{:S(2)}) copy-start(f32[32,2048]{1,0:T(8,128)} %copy-done.18) | copy-start | bytes 786436
  117.2 33.6 %copy-start.21 = (f32[32,2048]{1,0:T(8,128)S(1)}, f32[32,2048]{1,0:T(8,128)}, u32[]{:S(2)}) copy-start(f32[32,2048]{1,0:T(8,128)} %copy-done.20) | copy-start | bytes 786436
  117.2 33.6 %copy-start.23 = (f32[32,2048]{1,0:T(8,128)S(1)}, f32[32,2048]{1,0:T(8,128)}, u32[]{:S(2)}) copy-start(f32[32,2048]{1,0:T(8,128)} %copy-done.22) | copy-start | bytes 786436
  117.2 33.6 %copy-start.25 = (f32[32,2048]{1,0:T(8,128)S(1)}, f32[32,2048]{1,0:T(8,128)}, u32[]{:S(2)}) copy-start(f32[32,2048]{1,0:T(8,128)} %copy-done.24) | copy-start | bytes 786436
  146.9 3.9 %collective-permute-start.17 = (f32[8,16,640]{2,1,0:T(8,128)S(1)}, f32[8,16,640]{2,1,0:T(8,128)S(1)}, u32[]{:S(2)}, u32[]{:S(2)}) collective-permute-start(f32[8,16,640]{2,1,0:T(8,128)S(1)} %slice.12), channel_id=1, source_target_pairs={{0,1},{1,0},{2,3},{3,2},{4,5},{5,4},{6,7},{7,6},{8,9},{9,8},{10,11... | collective-permute-start | bytes 983048 | tf_op jit(solution)/shard_map/ppermute | solution.py:419
  (23 other events, 355.3 us)

commit v11 on v9

--- a/solution.py
+++ b/solution.py
@@ -238,8 +238,10 @@
     def chunk(i, _):
         points = pl.ds(pl.multiple_of(i * 512, 512), 512)
         rows = jnp.concatenate([panel_ref[1, long, points], field_ref[:, points]], axis=0)
-        acc[...] += dot_nt(rows, panel_ref[:, :, points].reshape(PANEL, 512))
-        corner[...] += dot_nt(panel_ref[0, short, points], panel_ref[0, :, points])
+        acc[:, 256:512] += dot_nt(rows, panel_ref[1, :, points])
+        low = dot_nt(jnp.concatenate([rows, panel_ref[0, short, points]], axis=0), panel_ref[0, :, points])
+        acc[:, 0:256] += low[0:256]
+        corner[...] += low[256:384]
         return 0
 
     homes = []

time: 177 us -> 176 us (level)
  no operation moved by 1% of the time
where the time goes in v11:
time: 176 us
  blocking collectives  71.2 us (40%)
  Pallas kernels  52.9 us (30%)
  starting transfers between devices  28.5 us (16%)
  waiting for transfers between devices  21 us (12%)
    pallas_call x1, Pallas kernels, update(): pl.pallas_call(update_kernel, grid=(4,), in_specs=[pl.BlockSpec(memory_sp...  28 us
    all_to_all x1, blocking collectives, per_device(): lax.all_to_all(pack(orbitals, potential), SPACE, 0, 0, tiled=True)  24.2 us
    all_to_all x1, blocking collectives, per_device(): back = lax.all_to_all(chebyshev(received), SPACE, 0, 0, tiled=True)  17.8 us
    ppermute x4, waiting for transfers between devices, right(): return lax.ppermute(block, 'z', ring(8, 1))  17.4 us
    all_to_all x1, blocking collectives, per_device(): mine = jnp.sum(lax.all_to_all(terms, SPACE, 0, 0, tiled=True), axis=0)  15.3 us
    all_to_all x1, blocking collectives, per_device(): lax.all_to_all(jnp.broadcast_to(mine, (8, 16, 1152)), SPACE, 0, 0, tiled=...  13.9 us
    ppermute x4, starting transfers between devices, left(): return lax.ppermute(block, 'z', ring(8, -1))  12.5 us
    pallas_call x1, Pallas kernels, chebyshev(): pl.pallas_call(filter_kernel, out_shape=jax.ShapeDtypeStruct((64, 32, 128...  11.3 us
  transfers between devices with their start and end apart: 18, of which 7 were waited for; matrix products, arithmetic and copies ran while one was open for 0% of the time, Pallas kernels for 0%

profile of v11, /device:TPU:1, one launch (start us, length us, event | category | flops | bytes accessed | tf_op | source)
XLA Modules:
  0.0 176.0 jit_solution(14364150925637132981)
XLA Ops:
  0.0 3.6 %shard_map.28 = f32[8,272,128]{2,1,0:T(8,128)} custom-call(f32[4,16,32,128]{3,2,1,0:T(8,128)} %orb_ref.1, f32[4,16,32]{2,1,0:T(8,128)} %pot_ref.1), custom_call_target="tpu_custom_call" | custom-call | tf_op jit(solution)/shard_map/pallas_call | solution.py:75
  3.6 24.2 %all_to_all.20.in_ref = f32[8,272,128]{2,1,0:T(8,128)S(1)} all-to-all(f32[8,272,128]{2,1,0:T(8,128)} %shard_map.28), channel_id=1, replica_groups=mesh['y'=4,'xh'=2,'xl'=2,'z'=8,'c'=2] {'y','xh'}, dimensions={0} | all-to-all | bytes 2228224 | tf_op jit(solution)/shard_map/all_to_all | solution.py:427
  27.8 11.3 %shard_map.29 = f32[64,32,128]{2,1,0:T(8,128)S(1)} custom-call(f32[8,272,128]{2,1,0:T(8,128)S(1)} %all_to_all.20.in_ref), custom_call_target="tpu_custom_call" | custom-call | tf_op jit(solution)/shard_map/pallas_call | solution.py:161
  39.1 17.8 %all_to_all.21.in_ref = f32[8,256,128]{2,1,0:T(8,128)S(1)} all-to-all(f32[8,256,128]{2,1,0:T(8,128)S(1)} %bitcast.22), channel_id=1, replica_groups=mesh['y'=4,'xh'=2,'xl'=2,'z'=8,'c'=2] {'y','xh'}, dimensions={0} | all-to-all | bytes 2097152 | tf_op jit(solution)/shard_map/all_to_all | solution.py:428
  59.2 1.7 collective-permute-done
  61.0 4.4 %collective-permute-start.3 = (f32[32,2048]{1,0:T(8,128)S(1)}, f32[32,2048]{1,0:T(8,128)S(1)}, u32[]{:S(2)}, u32[]{:S(2)}) collective-permute-start(f32[32,2048]{1,0:T(8,128)S(1)} %pad_maximum_fusion), channel_id=1, source_target_pairs={{0,1},{1,0},{2,3},{3,2},{4,5},{5,4},{6,7},{7,6},{8,9},{9,8},{10,11... | collective-permute-start | bytes 786440 | tf_op jit(solution)/shard_map/ppermute | solution.py:200
  65.4 1.7 collective-permute-start.1
  67.0 3.9 %collective-permute-start.2 = (f32[32,2048]{1,0:T(8,128)S(1)}, f32[32,2048]{1,0:T(8,128)S(1)}, u32[]{:S(2)}, u32[]{:S(2)}) collective-permute-start(f32[32,2048]{1,0:T(8,128)S(1)} %pad_maximum_fusion), channel_id=1, source_target_pairs={{0,14},{2,0},{4,2},{6,4},{8,6},{10,8},{12,10},{14,12},{1,15},{3,1}... | collective-permute-start | bytes 786440 | tf_op jit(solution)/shard_map/ppermute | solution.py:197
  71.0 6.6 %collective-permute-done.1 = f32[32,2048]{1,0:T(8,128)S(1)} collective-permute-done((f32[32,2048]{1,0:T(8,128)S(1)}, f32[32,2048]{1,0:T(8,128)S(1)}, u32[]{:S(2)}, u32[]{:S(2)}) %collective-permute-start.1) | collective-permute-done | bytes 262176 | tf_op jit(solution)/shard_map/ppermute | solution.py:194
  78.3 2.9 %collective-permute-start.5 = (f32[32,2048]{1,0:T(8,128)S(1)}, f32[32,2048]{1,0:T(8,128)S(1)}, u32[]{:S(2)}, u32[]{:S(2)}) collective-permute-start(f32[32,2048]{1,0:T(8,128)S(1)} %collective-permute-done.2), channel_id=1, source_target_pairs={{0,14},{2,0},{4,2},{6,4},{8,6},{10,8},{12,10},{14,12},{1,15},{3,1}... | collective-permute-start | bytes 786440 | tf_op jit(solution)/shard_map/ppermute | solution.py:197
  81.3 4.7 %collective-permute-done.4 = f32[32,2048]{1,0:T(8,128)S(1)} collective-permute-done((f32[32,2048]{1,0:T(8,128)S(1)}, f32[32,2048]{1,0:T(8,128)S(1)}, u32[]{:S(2)}, u32[]{:S(2)}) %collective-permute-start.4) | collective-permute-done | bytes 262176 | tf_op jit(solution)/shard_map/ppermute | solution.py:194
  86.0 1.6 collective-permute-start.10
  87.6 2.8 %collective-permute-start.9 = (f32[32,2048]{1,0:T(8,128)S(1)}, f32[32,2048]{1,0:T(8,128)S(1)}, u32[]{:S(2)}, u32[]{:S(2)}) collective-permute-start(f32[32,2048]{1,0:T(8,128)S(1)} %collective-permute-done.5), channel_id=1, source_target_pairs={{0,14},{2,0},{4,2},{6,4},{8,6},{10,8},{12,10},{14,12},{1,15},{3,1}... | collective-permute-start | bytes 786440 | tf_op jit(solution)/shard_map/ppermute | solution.py:197
  90.4 1.1 collective-permute-start.12
  91.5 5.2 %collective-permute-done.7 = f32[32,2048]{1,0:T(8,128)S(1)} collective-permute-done((f32[32,2048]{1,0:T(8,128)S(1)}, f32[32,2048]{1,0:T(8,128)S(1)}, u32[]{:S(2)}, u32[]{:S(2)}) %collective-permute-start.7) | collective-permute-done | bytes 262176 | tf_op jit(solution)/shard_map/ppermute | solution.py:194
  96.8 2.9 %collective-permute-start.13 = (f32[16,2048]{1,0:T(8,128)S(1)}, f32[16,2048]{1,0:T(8,128)S(1)}, u32[]{:S(2)}, u32[]{:S(2)}) collective-permute-start(f32[16,2048]{1,0:T(8,128)S(1)} %slice.10), channel_id=1, source_target_pairs={{0,14},{2,0},{4,2},{6,4},{8,6},{10,8},{12,10},{14,12},{1,15},{3,1}... | collective-permute-start | bytes 393224 | tf_op jit(solution)/shard_map/ppermute | solution.py:197
  99.7 1.4 collective-permute-start.15
  102.2 1.9 %collective-permute-start.16 = (f32[32,2048]{1,0:T(8,128)S(1)}, f32[32,2048]{1,0:T(8,128)}, u32[]{:S(2)}, u32[]{:S(2)}) collective-permute-start(f32[32,2048]{1,0:T(8,128)S(1)} %constant_dynamic-update-slice_fusion), channel_id=1, source_target_pairs={{0,1},{1,0},{2,3},{3,2},{4,5},{5,4},{6,7},{7,6},{8,9},{9,8},{10,11... | collective-permute-start | bytes 786440 | tf_op jit(solution)/shard_map/ppermute | solution.py:200
  105.4 9.2 %shard_map.32 = (f32[2,256,2048]{2,1,0:T(8,128)}, f32[8,16,1152]{2,1,0:T(8,128)}) custom-call(s32[3]{0:T(128)} %pad_add_fusion.place_ref, f32[2,16,2048]{2,1,0:T(8,128)} %bitcast.24, f32[2,16,2048]{2,1,0:T(8,128)} %bitcast.29, f32[2,16,2048]{2,1,0:T(8,128)} %bitcast.30, f32[2,16,2048]{2,1,0:T(8,128)} %bitcast.31, f32[2,16,2048]{2,1,0:T(8,128)} %bitcast.34, ...), custom_call_target="tpu_custom_call" | custom-call | tf_op jit(solution)/shard_map/pallas_call | solution.py:267
  114.6 15.3 %all_to_all.22 = f32[8,16,1152]{2,1,0:T(8,128)S(1)} all-to-all(f32[8,16,1152]{2,1,0:T(8,128)} %get-tuple-element.31), channel_id=1, replica_groups=mesh['y'=4,'xh'=2,'xl'=2,'z'=8,'c'=2] {'y','xh'}, dimensions={0} | all-to-all | bytes 1179648 | tf_op jit(solution)/shard_map/all_to_all | solution.py:431
  130.0 13.9 %all_to_all.23.sums_ref = f32[8,16,1152]{2,1,0:T(8,128)S(1)} all-to-all(f32[8,16,1152]{2,1,0:T(8,128)S(1)} %broadcast_in_dim.3), channel_id=1, replica_groups=mesh['y'=4,'xh'=2,'xl'=2,'z'=8,'c'=2] {'y','xh'}, dimensions={0} | all-to-all | bytes 1179648 | tf_op jit(solution)/shard_map/all_to_all | solution.py:432
  143.9 2.6 %collective-permute-start.17 = (f32[8,16,640]{2,1,0:T(8,128)S(1)}, f32[8,16,640]{2,1,0:T(8,128)S(1)}, u32[]{:S(2)}, u32[]{:S(2)}) collective-permute-start(f32[8,16,640]{2,1,0:T(8,128)S(1)} %slice.12), channel_id=1, source_target_pairs={{0,1},{1,0},{2,3},{3,2},{4,5},{5,4},{6,7},{7,6},{8,9},{9,8},{10,11... | collective-permute-start | bytes 983048 | tf_op jit(solution)/shard_map/ppermute | solution.py:433
  146.6 1.3 collective-permute-done.17.by_core_ref
  147.8 28.0 %shard_map.33 = f32[4,2,8,32,128]{4,3,2,1,0:T(8,128)} custom-call(s32[3]{0:T(128)S(1)} %copy-done.2, f32[8,16,1152]{2,1,0:T(8,128)S(1)} %all_to_all.23.sums_ref, f32[8,16,640]{2,1,0:T(8,128)S(1)} %collective-permute-done.17.by_core_ref, f32[512,2048]{1,0:T(8,128)} %bitcast.23, f32[128,2048]{1,0:T(8,128)S(1)} %copy-done.1), custom_call_target="tpu_custom_call" | custom-call | tf_op jit(solution)/shard_map/pallas_call | solution.py:404
  (64 shorter events, 5.7 us)
Async XLA Ops:
  57.0 3.9 %collective-permute-start = (f32[16,2048]{1,0:T(8,128)S(1)}, f32[16,2048]{1,0:T(8,128)S(1)}, u32[]{:S(2)}, u32[]{:S(2)}) collective-permute-start(f32[16,2048]{1,0:T(8,128)S(1)} %shard_map.30), channel_id=1, source_target_pairs={{0,16},{16,0},{1,17},{17,1},{2,18},{18,2},{3,19},{19,3},{4,20},{20... | collective-permute-start | bytes 393224 | tf_op jit(solution)/shard_map/ppermute | solution.py:203
  61.0 44.3 %copy-start.3 = (f32[32,2048]{1,0:T(8,128)}, f32[32,2048]{1,0:T(8,128)S(1)}, u32[]{:S(2)}) copy-start(f32[32,2048]{1,0:T(8,128)S(1)} %pad_maximum_fusion) | copy-start | bytes 786436
  61.0 10.0 %collective-permute-start.3 = (f32[32,2048]{1,0:T(8,128)S(1)}, f32[32,2048]{1,0:T(8,128)S(1)}, u32[]{:S(2)}, u32[]{:S(2)}) collective-permute-start(f32[32,2048]{1,0:T(8,128)S(1)} %pad_maximum_fusion), channel_id=1, source_target_pairs={{0,1},{1,0},{2,3},{3,2},{4,5},{5,4},{6,7},{7,6},{8,9},{9,8},{10,11... | collective-permute-start | bytes 786440 | tf_op jit(solution)/shard_map/ppermute | solution.py:200
  65.4 12.2 %collective-permute-start.1 = (f32[32,2048]{1,0:T(8,128)S(1)}, f32[32,2048]{1,0:T(8,128)S(1)}, u32[]{:S(2)}, u32[]{:S(2)}) collective-permute-start(f32[32,2048]{1,0:T(8,128)S(1)} %pad_maximum_fusion), channel_id=1, source_target_pairs={{0,2},{2,4},{4,6},{6,8},{8,10},{10,12},{12,14},{14,0},{1,3},{3,5},... | collective-permute-start | bytes 786440 | tf_op jit(solution)/shard_map/ppermute | solution.py:194
  67.0 11.2 %collective-permute-start.2 = (f32[32,2048]{1,0:T(8,128)S(1)}, f32[32,2048]{1,0:T(8,128)S(1)}, u32[]{:S(2)}, u32[]{:S(2)}) collective-permute-start(f32[32,2048]{1,0:T(8,128)S(1)} %pad_maximum_fusion), channel_id=1, source_target_pairs={{0,14},{2,0},{4,2},{6,4},{8,6},{10,8},{12,10},{14,12},{1,15},{3,1}... | collective-permute-start | bytes 786440 | tf_op jit(solution)/shard_map/ppermute | solution.py:197
  71.0 34.3 %copy-start.7 = (f32[32,2048]{1,0:T(8,128)}, f32[32,2048]{1,0:T(8,128)S(1)}, u32[]{:S(2)}) copy-start(f32[32,2048]{1,0:T(8,128)S(1)} %collective-permute-done.3) | copy-start | bytes 786436
  77.6 27.8 %copy-start.8 = (f32[32,2048]{1,0:T(8,128)}, f32[32,2048]{1,0:T(8,128)S(1)}, u32[]{:S(2)}) copy-start(f32[32,2048]{1,0:T(8,128)S(1)} %collective-permute-done.1) | copy-start | bytes 786436
  77.6 8.4 %collective-permute-start.4 = (f32[32,2048]{1,0:T(8,128)S(1)}, f32[32,2048]{1,0:T(8,128)S(1)}, u32[]{:S(2)}, u32[]{:S(2)}) collective-permute-start(f32[32,2048]{1,0:T(8,128)S(1)} %collective-permute-done.1), channel_id=1, source_target_pairs={{0,2},{2,4},{4,6},{6,8},{8,10},{10,12},{12,14},{14,0},{1,3},{3,5},... | collective-permute-start | bytes 786440 | tf_op jit(solution)/shard_map/ppermute | solution.py:194
  77.6 8.4 %collective-permute-start.6 = (f32[32,2048]{1,0:T(8,128)S(1)}, f32[32,2048]{1,0:T(8,128)S(1)}, u32[]{:S(2)}, u32[]{:S(2)}) collective-permute-start(f32[32,2048]{1,0:T(8,128)S(1)} %collective-permute-done.1), channel_id=1, source_target_pairs={{0,1},{1,0},{2,3},{3,2},{4,5},{5,4},{6,7},{7,6},{8,9},{9,8},{10,11... | collective-permute-start | bytes 786440 | tf_op jit(solution)/shard_map/ppermute | solution.py:200
  78.2 27.1 %copy-start.9 = (f32[32,2048]{1,0:T(8,128)}, f32[32,2048]{1,0:T(8,128)S(1)}, u32[]{:S(2)}) copy-start(f32[32,2048]{1,0:T(8,128)S(1)} %collective-permute-done.2) | copy-start | bytes 786436
  78.2 9.3 %collective-permute-start.8 = (f32[32,2048]{1,0:T(8,128)S(1)}, f32[32,2048]{1,0:T(8,128)S(1)}, u32[]{:S(2)}, u32[]{:S(2)}) collective-permute-start(f32[32,2048]{1,0:T(8,128)S(1)} %collective-permute-done.2), channel_id=1, source_target_pairs={{0,1},{1,0},{2,3},{3,2},{4,5},{5,4},{6,7},{7,6},{8,9},{9,8},{10,11... | collective-permute-start | bytes 786440 | tf_op jit(solution)/shard_map/ppermute | solution.py:200
  78.3 9.2 %collective-permute-start.5 = (f32[32,2048]{1,0:T(8,128)S(1)}, f32[32,2048]{1,0:T(8,128)S(1)}, u32[]{:S(2)}, u32[]{:S(2)}) collective-permute-start(f32[32,2048]{1,0:T(8,128)S(1)} %collective-permute-done.2), channel_id=1, source_target_pairs={{0,14},{2,0},{4,2},{6,4},{8,6},{10,8},{12,10},{14,12},{1,15},{3,1}... | collective-permute-start | bytes 786440 | tf_op jit(solution)/shard_map/ppermute | solution.py:197
  86.0 19.4 %copy-start.10 = (f32[32,2048]{1,0:T(8,128)}, f32[32,2048]{1,0:T(8,128)S(1)}, u32[]{:S(2)}) copy-start(f32[32,2048]{1,0:T(8,128)S(1)} %collective-permute-done.4) | copy-start | bytes 786436
  86.0 19.4 %copy-start.11 = (f32[32,2048]{1,0:T(8,128)}, f32[32,2048]{1,0:T(8,128)S(1)}, u32[]{:S(2)}) copy-start(f32[32,2048]{1,0:T(8,128)S(1)} %collective-permute-done.6) | copy-start | bytes 786436
  86.0 5.5 %collective-permute-start.10 = (f32[32,2048]{1,0:T(8,128)S(1)}, f32[32,2048]{1,0:T(8,128)S(1)}, u32[]{:S(2)}, u32[]{:S(2)}) collective-permute-start(f32[32,2048]{1,0:T(8,128)S(1)} %collective-permute-done.4), channel_id=1, source_target_pairs={{0,1},{1,0},{2,3},{3,2},{4,5},{5,4},{6,7},{7,6},{8,9},{9,8},{10,11... | collective-permute-start | bytes 786440 | tf_op jit(solution)/shard_map/ppermute | solution.py:200
  87.6 9.1 %collective-permute-start.7 = (f32[32,2048]{1,0:T(8,128)S(1)}, f32[32,2048]{1,0:T(8,128)S(1)}, u32[]{:S(2)}, u32[]{:S(2)}) collective-permute-start(f32[32,2048]{1,0:T(8,128)S(1)} %collective-permute-done.4), channel_id=1, source_target_pairs={{0,2},{2,4},{4,6},{6,8},{8,10},{10,12},{12,14},{14,0},{1,3},{3,5},... | collective-permute-start | bytes 786440 | tf_op jit(solution)/shard_map/ppermute | solution.py:194
  87.6 9.2 %collective-permute-start.9 = (f32[32,2048]{1,0:T(8,128)S(1)}, f32[32,2048]{1,0:T(8,128)S(1)}, u32[]{:S(2)}, u32[]{:S(2)}) collective-permute-start(f32[32,2048]{1,0:T(8,128)S(1)} %collective-permute-done.5), channel_id=1, source_target_pairs={{0,14},{2,0},{4,2},{6,4},{8,6},{10,8},{12,10},{14,12},{1,15},{3,1}... | collective-permute-start | bytes 786440 | tf_op jit(solution)/shard_map/ppermute | solution.py:197
  90.4 6.4 %collective-permute-start.12 = (f32[32,2048]{1,0:T(8,128)S(1)}, f32[32,2048]{1,0:T(8,128)S(1)}, u32[]{:S(2)}, u32[]{:S(2)}) collective-permute-start(f32[32,2048]{1,0:T(8,128)S(1)} %collective-permute-done.5), channel_id=1, source_target_pairs={{0,1},{1,0},{2,3},{3,2},{4,5},{5,4},{6,7},{7,6},{8,9},{9,8},{10,11... | collective-permute-start | bytes 786440 | tf_op jit(solution)/shard_map/ppermute | solution.py:200
  96.7 5.4 %collective-permute-start.11 = (f32[16,2048]{1,0:T(8,128)S(1)}, f32[16,2048]{1,0:T(8,128)S(1)}, u32[]{:S(2)}, u32[]{:S(2)}) collective-permute-start(f32[16,2048]{1,0:T(8,128)S(1)} %slice.9), channel_id=1, source_target_pairs={{0,2},{2,4},{4,6},{6,8},{8,10},{10,12},{12,14},{14,0},{1,3},{3,5},... | collective-permute-start | bytes 393224 | tf_op jit(solution)/shard_map/ppermute | solution.py:194
  96.8 5.3 %collective-permute-start.13 = (f32[16,2048]{1,0:T(8,128)S(1)}, f32[16,2048]{1,0:T(8,128)S(1)}, u32[]{:S(2)}, u32[]{:S(2)}) collective-permute-start(f32[16,2048]{1,0:T(8,128)S(1)} %slice.10), channel_id=1, source_target_pairs={{0,14},{2,0},{4,2},{6,4},{8,6},{10,8},{12,10},{14,12},{1,15},{3,1}... | collective-permute-start | bytes 393224 | tf_op jit(solution)/shard_map/ppermute | solution.py:197
  99.7 4.9 %collective-permute-start.15 = (f32[32,2048]{1,0:T(8,128)S(1)}, f32[32,2048]{1,0:T(8,128)}, u32[]{:S(2)}, u32[]{:S(2)}) collective-permute-start(f32[32,2048]{1,0:T(8,128)S(1)} %collective-permute-done.9), channel_id=1, source_target_pairs={{0,1},{1,0},{2,3},{3,2},{4,5},{5,4},{6,7},{7,6},{8,9},{9,8},{10,11... | collective-permute-start | bytes 786440 | tf_op jit(solution)/shard_map/ppermute | solution.py:200
  101.2 3.5 %collective-permute-start.14 = (f32[32,2048]{1,0:T(8,128)S(1)}, f32[32,2048]{1,0:T(8,128)}, u32[]{:S(2)}, u32[]{:S(2)}) collective-permute-start(f32[32,2048]{1,0:T(8,128)S(1)} %collective-permute-done.7), channel_id=1, source_target_pairs={{0,1},{1,0},{2,3},{3,2},{4,5},{5,4},{6,7},{7,6},{8,9},{9,8},{10,11... | collective-permute-start | bytes 786440 | tf_op jit(solution)/shard_map/ppermute | solution.py:200
  102.2 3.1 %collective-permute-start.16 = (f32[32,2048]{1,0:T(8,128)S(1)}, f32[32,2048]{1,0:T(8,128)}, u32[]{:S(2)}, u32[]{:S(2)}) collective-permute-start(f32[32,2048]{1,0:T(8,128)S(1)} %constant_dynamic-update-slice_fusion), channel_id=1, source_target_pairs={{0,1},{1,0},{2,3},{3,2},{4,5},{5,4},{6,7},{7,6},{8,9},{9,8},{10,11... | collective-permute-start | bytes 786440 | tf_op jit(solution)/shard_map/ppermute | solution.py:200
  143.9 3.9 %collective-permute-start.17 = (f32[8,16,640]{2,1,0:T(8,128)S(1)}, f32[8,16,640]{2,1,0:T(8,128)S(1)}, u32[]{:S(2)}, u32[]{:S(2)}) collective-permute-start(f32[8,16,640]{2,1,0:T(8,128)S(1)} %slice.12), channel_id=1, source_target_pairs={{0,1},{1,0},{2,3},{3,2},{4,5},{5,4},{6,7},{7,6},{8,9},{9,8},{10,11... | collective-permute-start | bytes 983048 | tf_op jit(solution)/shard_map/ppermute | solution.py:433
  (10 other events, 115.3 us)

commit v12 on v11

--- a/solution.py
+++ b/solution.py
@@ -390,10 +390,10 @@
         for copy in copies:
             copy.wait()
 
-    keep = lax.broadcasted_iota(jnp.int32, (128, 512), 0) >= 16
-    points = pl.ds(pl.multiple_of(pl.program_id(0) * 512, 512), 512)
+    keep = lax.broadcasted_iota(jnp.int32, (128, 1024), 0) >= 16
+    points = pl.ds(pl.multiple_of(pl.program_id(0) * 1024, 1024), 1024)
     moved = (dot_nn(mixer[...], held[:, points]) + jnp.where(keep, field_ref[...], 0.0)).T
-    for low in range(2):
+    for low in range(4):
         for xp in range(4):
             for yh in range(2):
                 first = low * 256 + xp * 64 + yh * 32
@@ -403,15 +403,15 @@
 def update(place, sums, by_core, panel, field):
     out = pl.pallas_call(
         update_kernel,
-        grid=(4,),
+        grid=(2,),
         in_specs=[
             pl.BlockSpec(memory_space=pltpu.SMEM),
             pl.BlockSpec((8, 16, 1152), lambda i: (0, 0, 0)),
             pl.BlockSpec((8, 16, 640), lambda i: (0, 0, 0)),
             pl.BlockSpec(memory_space=pl.ANY),
-            pl.BlockSpec((128, 512), lambda i: (0, i)),
+            pl.BlockSpec((128, 1024), lambda i: (0, i)),
         ],
-        out_specs=pl.BlockSpec((4, 2, 2, 32, 128), lambda i: (0, 0, i, 0, 0)),
+        out_specs=pl.BlockSpec((4, 2, 4, 32, 128), lambda i: (0, 0, i, 0, 0)),
         out_shape=jax.ShapeDtypeStruct((4, 2, 8, 32, 128), jnp.float32),
         scratch_shapes=[pltpu.VMEM((PANEL, PANEL), jnp.float32)] * 2
         + [pltpu.VMEM((128, PANEL), jnp.float32)] * 2

time: 176 us -> 176 us (level)
  no operation moved by 1% of the time
where the time goes in v12:
time: 176 us; the launch traced here: 175 us
  blocking collectives  71.2 us (40%)
  Pallas kernels  52.3 us (30%)
  starting transfers between devices  28.5 us (16%)
  waiting for transfers between devices  21 us (12%)
    pallas_call x1, Pallas kernels, update(): pl.pallas_call(update_kernel, grid=(2,), in_specs=[pl.BlockSpec(memory_sp...  27.3 us
    all_to_all x1, blocking collectives, per_device(): lax.all_to_all(pack(orbitals, potential), SPACE, 0, 0, tiled=True)  24.2 us
    all_to_all x1, blocking collectives, per_device(): back = lax.all_to_all(chebyshev(received), SPACE, 0, 0, tiled=True)  17.8 us
    ppermute x4, waiting for transfers between devices, right(): return lax.ppermute(block, 'z', ring(8, 1))  17.4 us
    all_to_all x1, blocking collectives, per_device(): mine = jnp.sum(lax.all_to_all(terms, SPACE, 0, 0, tiled=True), axis=0)  15.3 us
    all_to_all x1, blocking collectives, per_device(): lax.all_to_all(jnp.broadcast_to(mine, (8, 16, 1152)), SPACE, 0, 0, tiled=...  13.9 us
    ppermute x4, starting transfers between devices, left(): return lax.ppermute(block, 'z', ring(8, -1))  12.5 us
    pallas_call x1, Pallas kernels, chebyshev(): pl.pallas_call(filter_kernel, out_shape=jax.ShapeDtypeStruct((64, 32, 128...  11.3 us
  transfers between devices with their start and end apart: 18, of which 7 were waited for; matrix products, arithmetic and copies ran while one was open for 0% of the time, Pallas kernels for 0%

profile of v12, /device:TPU:1, one launch (start us, length us, event | category | flops | bytes accessed | tf_op | source)
XLA Modules:
  0.0 175.4 jit_solution(4100776557037968592)
XLA Ops:
  0.0 3.6 %shard_map.28 = f32[8,272,128]{2,1,0:T(8,128)} custom-call(f32[4,16,32,128]{3,2,1,0:T(8,128)} %orb_ref.1, f32[4,16,32]{2,1,0:T(8,128)} %pot_ref.1), custom_call_target="tpu_custom_call" | custom-call | tf_op jit(solution)/shard_map/pallas_call | solution.py:75
  3.6 24.2 %all_to_all.20.in_ref = f32[8,272,128]{2,1,0:T(8,128)S(1)} all-to-all(f32[8,272,128]{2,1,0:T(8,128)} %shard_map.28), channel_id=1, replica_groups=mesh['y'=4,'xh'=2,'xl'=2,'z'=8,'c'=2] {'y','xh'}, dimensions={0} | all-to-all | bytes 2228224 | tf_op jit(solution)/shard_map/all_to_all | solution.py:427
  27.8 11.3 %shard_map.29 = f32[64,32,128]{2,1,0:T(8,128)S(1)} custom-call(f32[8,272,128]{2,1,0:T(8,128)S(1)} %all_to_all.20.in_ref), custom_call_target="tpu_custom_call" | custom-call | tf_op jit(solution)/shard_map/pallas_call | solution.py:161
  39.1 17.8 %all_to_all.21.in_ref = f32[8,256,128]{2,1,0:T(8,128)S(1)} all-to-all(f32[8,256,128]{2,1,0:T(8,128)S(1)} %bitcast.22), channel_id=1, replica_groups=mesh['y'=4,'xh'=2,'xl'=2,'z'=8,'c'=2] {'y','xh'}, dimensions={0} | all-to-all | bytes 2097152 | tf_op jit(solution)/shard_map/all_to_all | solution.py:428
  59.2 1.7 collective-permute-done
  61.0 4.4 %collective-permute-start.3 = (f32[32,2048]{1,0:T(8,128)S(1)}, f32[32,2048]{1,0:T(8,128)S(1)}, u32[]{:S(2)}, u32[]{:S(2)}) collective-permute-start(f32[32,2048]{1,0:T(8,128)S(1)} %pad_maximum_fusion), channel_id=1, source_target_pairs={{0,1},{1,0},{2,3},{3,2},{4,5},{5,4},{6,7},{7,6},{8,9},{9,8},{10,11... | collective-permute-start | bytes 786440 | tf_op jit(solution)/shard_map/ppermute | solution.py:200
  65.4 1.7 collective-permute-start.1
  67.0 3.9 %collective-permute-start.2 = (f32[32,2048]{1,0:T(8,128)S(1)}, f32[32,2048]{1,0:T(8,128)S(1)}, u32[]{:S(2)}, u32[]{:S(2)}) collective-permute-start(f32[32,2048]{1,0:T(8,128)S(1)} %pad_maximum_fusion), channel_id=1, source_target_pairs={{0,14},{2,0},{4,2},{6,4},{8,6},{10,8},{12,10},{14,12},{1,15},{3,1}... | collective-permute-start | bytes 786440 | tf_op jit(solution)/shard_map/ppermute | solution.py:197
  71.0 6.6 %collective-permute-done.1 = f32[32,2048]{1,0:T(8,128)S(1)} collective-permute-done((f32[32,2048]{1,0:T(8,128)S(1)}, f32[32,2048]{1,0:T(8,128)S(1)}, u32[]{:S(2)}, u32[]{:S(2)}) %collective-permute-start.1) | collective-permute-done | bytes 262176 | tf_op jit(solution)/shard_map/ppermute | solution.py:194
  78.3 2.9 %collective-permute-start.5 = (f32[32,2048]{1,0:T(8,128)S(1)}, f32[32,2048]{1,0:T(8,128)S(1)}, u32[]{:S(2)}, u32[]{:S(2)}) collective-permute-start(f32[32,2048]{1,0:T(8,128)S(1)} %collective-permute-done.2), channel_id=1, source_target_pairs={{0,14},{2,0},{4,2},{6,4},{8,6},{10,8},{12,10},{14,12},{1,15},{3,1}... | collective-permute-start | bytes 786440 | tf_op jit(solution)/shard_map/ppermute | solution.py:197
  81.3 4.7 %collective-permute-done.4 = f32[32,2048]{1,0:T(8,128)S(1)} collective-permute-done((f32[32,2048]{1,0:T(8,128)S(1)}, f32[32,2048]{1,0:T(8,128)S(1)}, u32[]{:S(2)}, u32[]{:S(2)}) %collective-permute-start.4) | collective-permute-done | bytes 262176 | tf_op jit(solution)/shard_map/ppermute | solution.py:194
  86.0 1.6 collective-permute-start.10
  87.6 2.8 %collective-permute-start.9 = (f32[32,2048]{1,0:T(8,128)S(1)}, f32[32,2048]{1,0:T(8,128)S(1)}, u32[]{:S(2)}, u32[]{:S(2)}) collective-permute-start(f32[32,2048]{1,0:T(8,128)S(1)} %collective-permute-done.5), channel_id=1, source_target_pairs={{0,14},{2,0},{4,2},{6,4},{8,6},{10,8},{12,10},{14,12},{1,15},{3,1}... | collective-permute-start | bytes 786440 | tf_op jit(solution)/shard_map/ppermute | solution.py:197
  90.4 1.1 collective-permute-start.12
  91.5 5.2 %collective-permute-done.7 = f32[32,2048]{1,0:T(8,128)S(1)} collective-permute-done((f32[32,2048]{1,0:T(8,128)S(1)}, f32[32,2048]{1,0:T(8,128)S(1)}, u32[]{:S(2)}, u32[]{:S(2)}) %collective-permute-start.7) | collective-permute-done | bytes 262176 | tf_op jit(solution)/shard_map/ppermute | solution.py:194
  96.8 2.9 %collective-permute-start.13 = (f32[16,2048]{1,0:T(8,128)S(1)}, f32[16,2048]{1,0:T(8,128)S(1)}, u32[]{:S(2)}, u32[]{:S(2)}) collective-permute-start(f32[16,2048]{1,0:T(8,128)S(1)} %slice.10), channel_id=1, source_target_pairs={{0,14},{2,0},{4,2},{6,4},{8,6},{10,8},{12,10},{14,12},{1,15},{3,1}... | collective-permute-start | bytes 393224 | tf_op jit(solution)/shard_map/ppermute | solution.py:197
  99.7 1.4 collective-permute-start.15
  102.2 1.9 %collective-permute-start.16 = (f32[32,2048]{1,0:T(8,128)S(1)}, f32[32,2048]{1,0:T(8,128)}, u32[]{:S(2)}, u32[]{:S(2)}) collective-permute-start(f32[32,2048]{1,0:T(8,128)S(1)} %constant_dynamic-update-slice_fusion), channel_id=1, source_target_pairs={{0,1},{1,0},{2,3},{3,2},{4,5},{5,4},{6,7},{7,6},{8,9},{9,8},{10,11... | collective-permute-start | bytes 786440 | tf_op jit(solution)/shard_map/ppermute | solution.py:200
  105.4 9.2 %shard_map.32 = (f32[2,256,2048]{2,1,0:T(8,128)}, f32[8,16,1152]{2,1,0:T(8,128)}) custom-call(s32[3]{0:T(128)} %pad_add_fusion.place_ref, f32[2,16,2048]{2,1,0:T(8,128)} %bitcast.24, f32[2,16,2048]{2,1,0:T(8,128)} %bitcast.29, f32[2,16,2048]{2,1,0:T(8,128)} %bitcast.30, f32[2,16,2048]{2,1,0:T(8,128)} %bitcast.31, f32[2,16,2048]{2,1,0:T(8,128)} %bitcast.34, ...), custom_call_target="tpu_custom_call" | custom-call | tf_op jit(solution)/shard_map/pallas_call | solution.py:267
  114.6 15.3 %all_to_all.22 = f32[8,16,1152]{2,1,0:T(8,128)S(1)} all-to-all(f32[8,16,1152]{2,1,0:T(8,128)} %get-tuple-element.31), channel_id=1, replica_groups=mesh['y'=4,'xh'=2,'xl'=2,'z'=8,'c'=2] {'y','xh'}, dimensions={0} | all-to-all | bytes 1179648 | tf_op jit(solution)/shard_map/all_to_all | solution.py:431
  130.0 13.9 %all_to_all.23.sums_ref = f32[8,16,1152]{2,1,0:T(8,128)S(1)} all-to-all(f32[8,16,1152]{2,1,0:T(8,128)S(1)} %broadcast_in_dim.3), channel_id=1, replica_groups=mesh['y'=4,'xh'=2,'xl'=2,'z'=8,'c'=2] {'y','xh'}, dimensions={0} | all-to-all | bytes 1179648 | tf_op jit(solution)/shard_map/all_to_all | solution.py:432
  143.9 2.6 %collective-permute-start.17 = (f32[8,16,640]{2,1,0:T(8,128)S(1)}, f32[8,16,640]{2,1,0:T(8,128)S(1)}, u32[]{:S(2)}, u32[]{:S(2)}) collective-permute-start(f32[8,16,640]{2,1,0:T(8,128)S(1)} %slice.12), channel_id=1, source_target_pairs={{0,1},{1,0},{2,3},{3,2},{4,5},{5,4},{6,7},{7,6},{8,9},{9,8},{10,11... | collective-permute-start | bytes 983048 | tf_op jit(solution)/shard_map/ppermute | solution.py:433
  146.6 1.3 collective-permute-done.17.by_core_ref
  147.8 27.3 %shard_map.33 = f32[4,2,8,32,128]{4,3,2,1,0:T(8,128)} custom-call(s32[3]{0:T(128)S(1)} %copy-done.2, f32[8,16,1152]{2,1,0:T(8,128)S(1)} %all_to_all.23.sums_ref, f32[8,16,640]{2,1,0:T(8,128)S(1)} %collective-permute-done.17.by_core_ref, f32[512,2048]{1,0:T(8,128)} %bitcast.23, f32[128,2048]{1,0:T(8,128)S(1)} %copy-done.1), custom_call_target="tpu_custom_call" | custom-call | tf_op jit(solution)/shard_map/pallas_call | solution.py:404
  (64 shorter events, 5.7 us)
Async XLA Ops:
  57.0 3.9 %collective-permute-start = (f32[16,2048]{1,0:T(8,128)S(1)}, f32[16,2048]{1,0:T(8,128)S(1)}, u32[]{:S(2)}, u32[]{:S(2)}) collective-permute-start(f32[16,2048]{1,0:T(8,128)S(1)} %shard_map.30), channel_id=1, source_target_pairs={{0,16},{16,0},{1,17},{17,1},{2,18},{18,2},{3,19},{19,3},{4,20},{20... | collective-permute-start | bytes 393224 | tf_op jit(solution)/shard_map/ppermute | solution.py:203
  61.0 44.3 %copy-start.3 = (f32[32,2048]{1,0:T(8,128)}, f32[32,2048]{1,0:T(8,128)S(1)}, u32[]{:S(2)}) copy-start(f32[32,2048]{1,0:T(8,128)S(1)} %pad_maximum_fusion) | copy-start | bytes 786436
  61.0 10.0 %collective-permute-start.3 = (f32[32,2048]{1,0:T(8,128)S(1)}, f32[32,2048]{1,0:T(8,128)S(1)}, u32[]{:S(2)}, u32[]{:S(2)}) collective-permute-start(f32[32,2048]{1,0:T(8,128)S(1)} %pad_maximum_fusion), channel_id=1, source_target_pairs={{0,1},{1,0},{2,3},{3,2},{4,5},{5,4},{6,7},{7,6},{8,9},{9,8},{10,11... | collective-permute-start | bytes 786440 | tf_op jit(solution)/shard_map/ppermute | solution.py:200
  65.4 12.2 %collective-permute-start.1 = (f32[32,2048]{1,0:T(8,128)S(1)}, f32[32,2048]{1,0:T(8,128)S(1)}, u32[]{:S(2)}, u32[]{:S(2)}) collective-permute-start(f32[32,2048]{1,0:T(8,128)S(1)} %pad_maximum_fusion), channel_id=1, source_target_pairs={{0,2},{2,4},{4,6},{6,8},{8,10},{10,12},{12,14},{14,0},{1,3},{3,5},... | collective-permute-start | bytes 786440 | tf_op jit(solution)/shard_map/ppermute | solution.py:194
  67.0 11.2 %collective-permute-start.2 = (f32[32,2048]{1,0:T(8,128)S(1)}, f32[32,2048]{1,0:T(8,128)S(1)}, u32[]{:S(2)}, u32[]{:S(2)}) collective-permute-start(f32[32,2048]{1,0:T(8,128)S(1)} %pad_maximum_fusion), channel_id=1, source_target_pairs={{0,14},{2,0},{4,2},{6,4},{8,6},{10,8},{12,10},{14,12},{1,15},{3,1}... | collective-permute-start | bytes 786440 | tf_op jit(solution)/shard_map/ppermute | solution.py:197
  71.0 34.3 %copy-start.7 = (f32[32,2048]{1,0:T(8,128)}, f32[32,2048]{1,0:T(8,128)S(1)}, u32[]{:S(2)}) copy-start(f32[32,2048]{1,0:T(8,128)S(1)} %collective-permute-done.3) | copy-start | bytes 786436
  77.6 27.8 %copy-start.8 = (f32[32,2048]{1,0:T(8,128)}, f32[32,2048]{1,0:T(8,128)S(1)}, u32[]{:S(2)}) copy-start(f32[32,2048]{1,0:T(8,128)S(1)} %collective-permute-done.1) | copy-start | bytes 786436
  77.6 8.4 %collective-permute-start.4 = (f32[32,2048]{1,0:T(8,128)S(1)}, f32[32,2048]{1,0:T(8,128)S(1)}, u32[]{:S(2)}, u32[]{:S(2)}) collective-permute-start(f32[32,2048]{1,0:T(8,128)S(1)} %collective-permute-done.1), channel_id=1, source_target_pairs={{0,2},{2,4},{4,6},{6,8},{8,10},{10,12},{12,14},{14,0},{1,3},{3,5},... | collective-permute-start | bytes 786440 | tf_op jit(solution)/shard_map/ppermute | solution.py:194
  77.6 8.4 %collective-permute-start.6 = (f32[32,2048]{1,0:T(8,128)S(1)}, f32[32,2048]{1,0:T(8,128)S(1)}, u32[]{:S(2)}, u32[]{:S(2)}) collective-permute-start(f32[32,2048]{1,0:T(8,128)S(1)} %collective-permute-done.1), channel_id=1, source_target_pairs={{0,1},{1,0},{2,3},{3,2},{4,5},{5,4},{6,7},{7,6},{8,9},{9,8},{10,11... | collective-permute-start | bytes 786440 | tf_op jit(solution)/shard_map/ppermute | solution.py:200
  78.2 27.1 %copy-start.9 = (f32[32,2048]{1,0:T(8,128)}, f32[32,2048]{1,0:T(8,128)S(1)}, u32[]{:S(2)}) copy-start(f32[32,2048]{1,0:T(8,128)S(1)} %collective-permute-done.2) | copy-start | bytes 786436
  78.2 9.3 %collective-permute-start.8 = (f32[32,2048]{1,0:T(8,128)S(1)}, f32[32,2048]{1,0:T(8,128)S(1)}, u32[]{:S(2)}, u32[]{:S(2)}) collective-permute-start(f32[32,2048]{1,0:T(8,128)S(1)} %collective-permute-done.2), channel_id=1, source_target_pairs={{0,1},{1,0},{2,3},{3,2},{4,5},{5,4},{6,7},{7,6},{8,9},{9,8},{10,11... | collective-permute-start | bytes 786440 | tf_op jit(solution)/shard_map/ppermute | solution.py:200
  78.3 9.2 %collective-permute-start.5 = (f32[32,2048]{1,0:T(8,128)S(1)}, f32[32,2048]{1,0:T(8,128)S(1)}, u32[]{:S(2)}, u32[]{:S(2)}) collective-permute-start(f32[32,2048]{1,0:T(8,128)S(1)} %collective-permute-done.2), channel_id=1, source_target_pairs={{0,14},{2,0},{4,2},{6,4},{8,6},{10,8},{12,10},{14,12},{1,15},{3,1}... | collective-permute-start | bytes 786440 | tf_op jit(solution)/shard_map/ppermute | solution.py:197
  86.0 19.4 %copy-start.10 = (f32[32,2048]{1,0:T(8,128)}, f32[32,2048]{1,0:T(8,128)S(1)}, u32[]{:S(2)}) copy-start(f32[32,2048]{1,0:T(8,128)S(1)} %collective-permute-done.4) | copy-start | bytes 786436
  86.0 19.4 %copy-start.11 = (f32[32,2048]{1,0:T(8,128)}, f32[32,2048]{1,0:T(8,128)S(1)}, u32[]{:S(2)}) copy-start(f32[32,2048]{1,0:T(8,128)S(1)} %collective-permute-done.6) | copy-start | bytes 786436
  86.0 5.5 %collective-permute-start.10 = (f32[32,2048]{1,0:T(8,128)S(1)}, f32[32,2048]{1,0:T(8,128)S(1)}, u32[]{:S(2)}, u32[]{:S(2)}) collective-permute-start(f32[32,2048]{1,0:T(8,128)S(1)} %collective-permute-done.4), channel_id=1, source_target_pairs={{0,1},{1,0},{2,3},{3,2},{4,5},{5,4},{6,7},{7,6},{8,9},{9,8},{10,11... | collective-permute-start | bytes 786440 | tf_op jit(solution)/shard_map/ppermute | solution.py:200
  87.6 9.1 %collective-permute-start.7 = (f32[32,2048]{1,0:T(8,128)S(1)}, f32[32,2048]{1,0:T(8,128)S(1)}, u32[]{:S(2)}, u32[]{:S(2)}) collective-permute-start(f32[32,2048]{1,0:T(8,128)S(1)} %collective-permute-done.4), channel_id=1, source_target_pairs={{0,2},{2,4},{4,6},{6,8},{8,10},{10,12},{12,14},{14,0},{1,3},{3,5},... | collective-permute-start | bytes 786440 | tf_op jit(solution)/shard_map/ppermute | solution.py:194
  87.6 9.2 %collective-permute-start.9 = (f32[32,2048]{1,0:T(8,128)S(1)}, f32[32,2048]{1,0:T(8,128)S(1)}, u32[]{:S(2)}, u32[]{:S(2)}) collective-permute-start(f32[32,2048]{1,0:T(8,128)S(1)} %collective-permute-done.5), channel_id=1, source_target_pairs={{0,14},{2,0},{4,2},{6,4},{8,6},{10,8},{12,10},{14,12},{1,15},{3,1}... | collective-permute-start | bytes 786440 | tf_op jit(solution)/shard_map/ppermute | solution.py:197
  90.4 6.4 %collective-permute-start.12 = (f32[32,2048]{1,0:T(8,128)S(1)}, f32[32,2048]{1,0:T(8,128)S(1)}, u32[]{:S(2)}, u32[]{:S(2)}) collective-permute-start(f32[32,2048]{1,0:T(8,128)S(1)} %collective-permute-done.5), channel_id=1, source_target_pairs={{0,1},{1,0},{2,3},{3,2},{4,5},{5,4},{6,7},{7,6},{8,9},{9,8},{10,11... | collective-permute-start | bytes 786440 | tf_op jit(solution)/shard_map/ppermute | solution.py:200
  96.7 5.4 %collective-permute-start.11 = (f32[16,2048]{1,0:T(8,128)S(1)}, f32[16,2048]{1,0:T(8,128)S(1)}, u32[]{:S(2)}, u32[]{:S(2)}) collective-permute-start(f32[16,2048]{1,0:T(8,128)S(1)} %slice.9), channel_id=1, source_target_pairs={{0,2},{2,4},{4,6},{6,8},{8,10},{10,12},{12,14},{14,0},{1,3},{3,5},... | collective-permute-start | bytes 393224 | tf_op jit(solution)/shard_map/ppermute | solution.py:194
  96.8 5.3 %collective-permute-start.13 = (f32[16,2048]{1,0:T(8,128)S(1)}, f32[16,2048]{1,0:T(8,128)S(1)}, u32[]{:S(2)}, u32[]{:S(2)}) collective-permute-start(f32[16,2048]{1,0:T(8,128)S(1)} %slice.10), channel_id=1, source_target_pairs={{0,14},{2,0},{4,2},{6,4},{8,6},{10,8},{12,10},{14,12},{1,15},{3,1}... | collective-permute-start | bytes 393224 | tf_op jit(solution)/shard_map/ppermute | solution.py:197
  99.7 4.9 %collective-permute-start.15 = (f32[32,2048]{1,0:T(8,128)S(1)}, f32[32,2048]{1,0:T(8,128)}, u32[]{:S(2)}, u32[]{:S(2)}) collective-permute-start(f32[32,2048]{1,0:T(8,128)S(1)} %collective-permute-done.9), channel_id=1, source_target_pairs={{0,1},{1,0},{2,3},{3,2},{4,5},{5,4},{6,7},{7,6},{8,9},{9,8},{10,11... | collective-permute-start | bytes 786440 | tf_op jit(solution)/shard_map/ppermute | solution.py:200
  101.2 3.5 %collective-permute-start.14 = (f32[32,2048]{1,0:T(8,128)S(1)}, f32[32,2048]{1,0:T(8,128)}, u32[]{:S(2)}, u32[]{:S(2)}) collective-permute-start(f32[32,2048]{1,0:T(8,128)S(1)} %collective-permute-done.7), channel_id=1, source_target_pairs={{0,1},{1,0},{2,3},{3,2},{4,5},{5,4},{6,7},{7,6},{8,9},{9,8},{10,11... | collective-permute-start | bytes 786440 | tf_op jit(solution)/shard_map/ppermute | solution.py:200
  102.2 3.1 %collective-permute-start.16 = (f32[32,2048]{1,0:T(8,128)S(1)}, f32[32,2048]{1,0:T(8,128)}, u32[]{:S(2)}, u32[]{:S(2)}) collective-permute-start(f32[32,2048]{1,0:T(8,128)S(1)} %constant_dynamic-update-slice_fusion), channel_id=1, source_target_pairs={{0,1},{1,0},{2,3},{3,2},{4,5},{5,4},{6,7},{7,6},{8,9},{9,8},{10,11... | collective-permute-start | bytes 786440 | tf_op jit(solution)/shard_map/ppermute | solution.py:200
  143.9 3.9 %collective-permute-start.17 = (f32[8,16,640]{2,1,0:T(8,128)S(1)}, f32[8,16,640]{2,1,0:T(8,128)S(1)}, u32[]{:S(2)}, u32[]{:S(2)}) collective-permute-start(f32[8,16,640]{2,1,0:T(8,128)S(1)} %slice.12), channel_id=1, source_target_pairs={{0,1},{1,0},{2,3},{3,2},{4,5},{5,4},{6,7},{7,6},{8,9},{9,8},{10,11... | collective-permute-start | bytes 983048 | tf_op jit(solution)/shard_map/ppermute | solution.py:433
  (10 other events, 115.3 us)
